TPU v7x, 32 devices: a whole 2x2x4 slice. The times are simulated.
32 devices in a mesh: dp: 8 (over z, x), mp: 4 (over y, core).
Axes of the slice: x: 2, y: 2, z: 4, core: 2. Of those that a mesh axis runs over, the one named last changes fastest.
Arguments:
- tokens: bfloat16 [8, 2048, 768], P('dp'), may hold values from -6 to 6
- segment_ids: int32 [8, 2048], P('dp'), may hold values from 0 to 7, never falling along the last dimension, each value on 1 to 1024 neighbouring positions
- gain_one: float32 [768], replicated, may hold values from 0.5 to 1.5
- bias_one: float32 [768], replicated, may hold values from -1.75 to 1.75
- query_weight: bfloat16 [768, 768], P(None, 'mp'), may hold values from -0.3125 to 0.3125
- query_bias: float32 [768], P('mp'), may hold values from -3 to 3
- key_weight: bfloat16 [768, 768], P(None, 'mp'), may hold values from -0.21875 to 0.21875
- value_weight: bfloat16 [768, 768], P(None, 'mp'), may hold values from -0.21875 to 0.21875
- value_bias: float32 [768], P('mp'), may hold values from -3 to 3
- output_weight: bfloat16 [768, 768], P('mp'), may hold values from -0.875 to 0.875
- output_bias: float32 [768], replicated, may hold values from -3 to 3
- gain_two: float32 [768], replicated, may hold values from 0.5 to 1.5
- bias_two: float32 [768], replicated, may hold values from -1.75 to 1.75
- inner_weight: bfloat16 [768, 3072], P(None, 'mp'), may hold values from -0.21875 to 0.21875
- inner_bias: float32 [3072], P('mp'), may hold values from -3 to 3
- outer_weight: bfloat16 [3072, 768], P('mp'), may hold values from -0.109375 to 0.109375
- outer_bias: float32 [768], replicated, may hold values from -3 to 3
- cotangent: bfloat16 [8, 2048, 768], P('dp'), may hold values from -6 to 6
Outputs:
- layer_out: bfloat16 [8, 2048, 768], P('dp')
- input_grad: float32 [8, 2048, 768], P('dp')
- grad_gain_one: float32 [768], replicated
- grad_bias_one: float32 [768], replicated
- grad_query_weight: float32 [768, 768], P(None, 'mp')
- grad_query_bias: float32 [768], P('mp')
- grad_key_weight: float32 [768, 768], P(None, 'mp')
- grad_value_weight: float32 [768, 768], P(None, 'mp')
- grad_value_bias: float32 [768], P('mp')
- grad_output_weight: float32 [768, 768], P('mp')
- grad_output_bias: float32 [768], replicated
- grad_gain_two: float32 [768], replicated
- grad_bias_two: float32 [768], replicated
- grad_inner_weight: float32 [768, 3072], P(None, 'mp')
- grad_inner_bias: float32 [3072], P('mp')
- grad_outer_weight: float32 [3072, 768], P('mp')
- grad_outer_bias: float32 [768], replicated
Inputs may be any that keep to these rules, and one draw needn't show every extreme that they name: `segment_ids`: ids never fall along a row; a document holds at most 1024 characters and some document holds exactly that many.
All inputs are finite; a program needn't handle non-finite values.
Results may differ from a plain program's by a relative error of at most 0.013.
Values may be sent and summed in bfloat16 or wider, within the bound.
No kernel may reach another device: no remote copies, remote signals or barrier semaphores. Data moves between devices by JAX's collectives and lax.ppermute only.
A program may use at most 192 MiB of HBM per device.

v0:
```python
import jax
import jax.numpy as jnp
from jax import lax
from jax.sharding import PartitionSpec as P

HEAD = 64


def layer_norm(values, gain, shift):
    center = values - jnp.mean(values, axis=-1, keepdims=True)
    scale = lax.rsqrt(jnp.mean(center * center, axis=-1, keepdims=True) + 1e-05)
    normed = center * scale
    return (normed * gain + shift, normed, scale)


def norm_back(grad_out, normed, scale, gain):
    upstream = grad_out * gain
    return scale * (
        upstream
        - jnp.mean(upstream, axis=-1, keepdims=True)
        - normed * jnp.mean(upstream * normed, axis=-1, keepdims=True)
    )


def gelu_exact(values):
    return jax.nn.gelu(values, approximate=False)


def across(left, right):
    return lax.dot_general(
        left, right, (((0,), (0,)), ((), ())), preferred_element_type=jnp.float32
    )


def against(left, right):
    return lax.dot_general(
        left, right, (((1,), (1,)), ((), ())), preferred_element_type=jnp.float32
    )


def masked_scores(query_block, key_block, segment_row, offset, block):
    scores = jnp.einsum(
        "qhd,khd->hqk", query_block, key_block, preferred_element_type=jnp.float32
    ) * HEAD ** (-0.5)
    allowed = segment_row[offset : offset + block][:, None] == segment_row[None, :]
    return jnp.where(allowed[None], scores, -1e30)


def attend_forward(queries, key_local, values_local, segment_ids):
    rows_here, length = segment_ids.shape
    width = queries.shape[1]
    heads = width // HEAD
    block = min(512, length)
    outputs = []
    log_totals = []
    key_block = key_local.reshape(length, heads, HEAD)
    value_block = values_local.reshape(length, heads, HEAD)
    segment_row = segment_ids[0]
    for offset in range(0, length, block):
        query_block = queries[offset : offset + block].reshape(block, heads, HEAD)
        scores = masked_scores(query_block, key_block, segment_row, offset, block)
        highest = jnp.max(scores, axis=-1, keepdims=True)
        powered = jnp.exp(scores - highest)
        denominator = jnp.sum(powered, axis=-1, keepdims=True)
        softmax_block = (powered / denominator).astype(jnp.bfloat16)
        context = jnp.einsum(
            "hqk,khd->qhd", softmax_block, value_block, preferred_element_type=jnp.float32
        )
        outputs.append(context.reshape(block, width))
        log_totals.append(highest + jnp.log(denominator))
    return (jnp.concatenate(outputs, axis=0).astype(jnp.bfloat16), log_totals)


def attend_backward(queries, key_local, values_local, segment_ids, grad_attended, log_totals):
    rows_here, length = segment_ids.shape
    width = queries.shape[1]
    heads = width // HEAD
    block = min(512, length)
    factor = HEAD ** (-0.5)
    query_grads = []
    position = 0
    key_block = key_local.reshape(length, heads, HEAD)
    value_block = values_local.reshape(length, heads, HEAD)
    segment_row = segment_ids[0]
    key_total = jnp.zeros((length, heads, HEAD), jnp.float32)
    value_total = jnp.zeros((length, heads, HEAD), jnp.float32)
    for offset in range(0, length, block):
        query_block = queries[offset : offset + block].reshape(block, heads, HEAD)
        grad_context = grad_attended[offset : offset + block].reshape(block, heads, HEAD)
        scores = masked_scores(query_block, key_block, segment_row, offset, block)
        softmax_block = jnp.exp(scores - log_totals[position])
        position = position + 1
        grad_softmax = jnp.einsum(
            "qhd,khd->hqk", grad_context, value_block, preferred_element_type=jnp.float32
        )
        inner_sum = jnp.sum(softmax_block * grad_softmax, axis=-1, keepdims=True)
        grad_scores = (softmax_block * (grad_softmax - inner_sum)).astype(jnp.bfloat16)
        grad_query = (
            jnp.einsum("hqk,khd->qhd", grad_scores, key_block, preferred_element_type=jnp.float32)
            * factor
        )
        query_grads.append(grad_query.reshape(block, width))
        key_total = (
            key_total
            + jnp.einsum(
                "hqk,qhd->khd", grad_scores, query_block, preferred_element_type=jnp.float32
            )
            * factor
        )
        value_total = value_total + jnp.einsum(
            "hqk,qhd->khd",
            softmax_block.astype(jnp.bfloat16),
            grad_context,
            preferred_element_type=jnp.float32,
        )
    key_grads = key_total.reshape(length, width)
    value_grads = value_total.reshape(length, width)
    return (
        jnp.concatenate(query_grads, axis=0).astype(jnp.bfloat16),
        key_grads.astype(jnp.bfloat16),
        value_grads.astype(jnp.bfloat16),
    )


def local(
    tokens,
    segment_ids,
    gain_one,
    bias_one,
    query_weight,
    query_bias,
    key_weight,
    value_weight,
    value_bias,
    output_weight,
    output_bias,
    gain_two,
    bias_two,
    inner_weight,
    inner_bias,
    outer_weight,
    outer_bias,
    cotangent,
):
    rows_here, length, features = tokens.shape
    total_rows = rows_here * length
    share = total_rows // lax.axis_size("mp")
    begin = lax.axis_index("mp") * share
    inputs = tokens.reshape(total_rows, features).astype(jnp.float32)
    attend_full, normed_one, scale_one = layer_norm(inputs, gain_one, bias_one)
    attend_in = attend_full.astype(jnp.bfloat16)
    queries = (
        jnp.dot(attend_in, query_weight, preferred_element_type=jnp.float32) + query_bias
    ).astype(jnp.bfloat16)
    key_local = jnp.dot(attend_in, key_weight, preferred_element_type=jnp.float32).astype(
        jnp.bfloat16
    )
    values_local = (
        jnp.dot(attend_in, value_weight, preferred_element_type=jnp.float32) + value_bias
    ).astype(jnp.bfloat16)
    attended, log_totals = attend_forward(queries, key_local, values_local, segment_ids)
    attend_part = lax.psum_scatter(
        jnp.dot(attended, output_weight, preferred_element_type=jnp.float32),
        "mp",
        scatter_dimension=0,
        tiled=True,
    )
    residual = lax.dynamic_slice_in_dim(inputs, begin, share, 0) + attend_part + output_bias
    expand_part, normed_two, scale_two = layer_norm(residual, gain_two, bias_two)
    expand_in = lax.all_gather(expand_part.astype(jnp.bfloat16), "mp", axis=0, tiled=True)
    hidden_pre = jnp.dot(expand_in, inner_weight, preferred_element_type=jnp.float32) + inner_bias
    activated = gelu_exact(hidden_pre).astype(jnp.bfloat16)
    result = (
        residual
        + lax.psum_scatter(
            jnp.dot(activated, outer_weight, preferred_element_type=jnp.float32).astype(
                jnp.bfloat16
            ),
            "mp",
            scatter_dimension=0,
            tiled=True,
        ).astype(jnp.float32)
        + outer_bias
    )
    layer_out = lax.all_gather(result.astype(jnp.bfloat16), "mp", axis=0, tiled=True).reshape(
        tokens.shape
    )
    cot_low = cotangent.reshape(total_rows, features)
    cot_share = lax.dynamic_slice_in_dim(cot_low, begin, share, 0).astype(jnp.float32)
    grad_outer_weight = across(activated, cot_low)
    grad_activated = against(cot_low, outer_weight)
    grad_hidden = jax.vjp(gelu_exact, hidden_pre)[1](grad_activated)[0].astype(jnp.bfloat16)
    grad_inner_bias = jnp.sum(grad_hidden.astype(jnp.float32), axis=0)
    grad_inner_weight = across(expand_in, grad_hidden)
    grad_mid = lax.psum_scatter(
        against(grad_hidden, inner_weight), "mp", scatter_dimension=0, tiled=True
    )
    gain_two_part = jnp.sum(grad_mid * normed_two, axis=0)
    bias_two_part = jnp.sum(grad_mid, axis=0)
    grad_residual = cot_share + norm_back(grad_mid, normed_two, scale_two, gain_two)
    residual_low = lax.all_gather(grad_residual.astype(jnp.bfloat16), "mp", axis=0, tiled=True)
    grad_output_weight = across(attended, residual_low)
    grad_attended = against(residual_low, output_weight).astype(jnp.bfloat16)
    grad_queries, grad_keys, grad_values = attend_backward(
        queries, key_local, values_local, segment_ids, grad_attended, log_totals
    )
    grad_query_bias = jnp.sum(grad_queries.astype(jnp.float32), axis=0)
    grad_value_bias = jnp.sum(grad_values.astype(jnp.float32), axis=0)
    grad_query_weight = across(attend_in, grad_queries)
    grad_key_weight = across(attend_in, grad_keys)
    grad_value_weight = across(attend_in, grad_values)
    total = against(grad_queries, query_weight)
    total = total + against(grad_keys, key_weight)
    grad_attend = lax.psum_scatter(
        total + against(grad_values, value_weight), "mp", scatter_dimension=0, tiled=True
    )
    normed_share = lax.dynamic_slice_in_dim(normed_one, begin, share, 0)
    scale_share = lax.dynamic_slice_in_dim(scale_one, begin, share, 0)
    gain_one_part = jnp.sum(grad_attend * normed_share, axis=0)
    bias_one_part = jnp.sum(grad_attend, axis=0)
    input_share = grad_residual + norm_back(grad_attend, normed_share, scale_share, gain_one)
    input_grad = lax.all_gather(input_share, "mp", axis=0, tiled=True).reshape(tokens.shape)
    (
        grad_gain_one,
        grad_bias_one,
        grad_output_bias,
        grad_gain_two,
        grad_bias_two,
        grad_outer_bias,
    ) = lax.psum(
        (
            gain_one_part,
            bias_one_part,
            jnp.sum(grad_residual, axis=0),
            gain_two_part,
            bias_two_part,
            jnp.sum(cot_share, axis=0),
        ),
        ("dp", "mp"),
    )
    (
        grad_query_weight,
        grad_query_bias,
        grad_key_weight,
        grad_value_weight,
        grad_value_bias,
        grad_output_weight,
        grad_inner_weight,
        grad_inner_bias,
        grad_outer_weight,
    ) = lax.psum(
        (
            grad_query_weight,
            grad_query_bias,
            grad_key_weight,
            grad_value_weight,
            grad_value_bias,
            grad_output_weight,
            grad_inner_weight,
            grad_inner_bias,
            grad_outer_weight,
        ),
        "dp",
    )
    return (
        layer_out,
        input_grad,
        grad_gain_one,
        grad_bias_one,
        grad_query_weight,
        grad_query_bias,
        grad_key_weight,
        grad_value_weight,
        grad_value_bias,
        grad_output_weight,
        grad_output_bias,
        grad_gain_two,
        grad_bias_two,
        grad_inner_weight,
        grad_inner_bias,
        grad_outer_weight,
        grad_outer_bias,
    )


def solution(mesh):
    placed = (
        P("dp", None, None),
        P("dp", None),
        P(),
        P(),
        P(None, "mp"),
        P("mp"),
        P(None, "mp"),
        P(None, "mp"),
        P("mp"),
        P("mp", None),
        P(),
        P(),
        P(),
        P(None, "mp"),
        P("mp"),
        P("mp", None),
        P(),
        P("dp", None, None),
    )
    return jax.shard_map(
        local,
        mesh=mesh,
        in_specs=placed,
        out_specs=(
            P("dp", None, None),
            P("dp", None, None),
            P(),
            P(),
            P(None, "mp"),
            P("mp"),
            P(None, "mp"),
            P(None, "mp"),
            P("mp"),
            P("mp", None),
            P(),
            P(),
            P(),
            P(None, "mp"),
            P("mp"),
            P("mp", None),
            P(),
        ),
        check_vma=False,
    )
```

profile of v0, /device:TPU:0, one launch (start us, length us, event | category | flops | bytes accessed | tf_op | source)
XLA Modules:
  0.0 874.9 jit_solution(4931055691356864238)
XLA Ops:
  71.7 5.0 convert_element_type.123
  76.7 56.1 %reduce-scatter.5.cloned.1.call-done = f32[512,768]{1,0:T(8,128)} async-done(((f32[2048,768]{1,0:T(8,128)}), f32[512,768]{1,0:T(8,128)}) %reduce-scatter.5.cloned.1.call-update) | async-done | bytes 1572880 | tf_op jit(solution)/shard_map/reduce_scatter | solution.py:162
  136.5 28.6 %all-gather.5.cloned.1.call-done = bf16[2048,768]{1,0:T(8,128)(2,1)} async-done(((bf16[512,768]{1,0:T(8,128)(2,1)}), bf16[2048,768]{1,0:T(8,128)(2,1)}) %all-gather.5.cloned.1.call-update) | async-done | bytes 3145744 | tf_op jit(solution)/shard_map/all_gather | solution.py:170
  165.2 18.0 %multiply_convert_fusion.4 = (bf16[2048,768]{1,0:T(8,128)(2,1)}, f32[2048,768]{1,0:T(8,128)S(1)}, f32[2048,768]{1,0:T(8,128)S(1)}) fusion(f32[768]{0:T(1024)} %param.32, bf16[2048,768]{1,0:T(8,128)(2,1)} %all-gather.5.cloned.1.call-done, bf16[768,768]{1,0:T(8,128)(2,1)S(1)} %copy-done), kind=kOutput, calls=%fused_computation.47 | convolution fusion | flops 2519728128 | bytes 20057088 | tf_op jit(solution)/shard_map/dot_general | solution.py:171
  183.2 5.0 convert_reduce_fusion
  195.6 6.2 convolution_convert_fusion
  201.9 50.9 %reduce-scatter.9.cloned.1.call-done = f32[512,768]{1,0:T(8,128)} async-done(((f32[2048,768]{1,0:T(8,128)}), f32[512,768]{1,0:T(8,128)}) %reduce-scatter.9.cloned.1.call-update) | async-done | bytes 1572880 | tf_op jit(solution)/shard_map/reduce_scatter | solution.py:195
  255.5 37.6 %reduce-scatter.7.cloned.1.call-done = bf16[512,768]{1,0:T(8,128)(2,1)} async-done(((bf16[2048,768]{1,0:T(8,128)(2,1)}), bf16[512,768]{1,0:T(8,128)(2,1)}) %reduce-scatter.7.cloned.1.call-update) | async-done | bytes 786448 | tf_op jit(solution)/shard_map/reduce_scatter | solution.py:175
  299.6 28.5 %all-gather.9.cloned.1.call-done = bf16[2048,768]{1,0:T(8,128)(2,1)} async-done(((bf16[512,768]{1,0:T(8,128)(2,1)}), bf16[2048,768]{1,0:T(8,128)(2,1)}) %all-gather.9.cloned.1.call-update) | async-done | bytes 3145744 | tf_op jit(solution)/shard_map/all_gather | solution.py:201
  331.9 11.1 %multiply_reduce_fusion.3 = (f32[3,512]{1,0:T(4,128)S(1)}, f32[3,512,2048]{2,1,0:T(8,128)}) fusion(f32[3,512,2048]{2,1,0:T(8,128)} %copy-done.2, f32[3,512]{1,0:T(4,128)S(1)} %log_add_fusion.3, bf16[512,3,64]{0,2,1:T(8,128)(2,1)S(1)} %bitcast.175, bf16[2048,3,64]{0,2,1:T(8,128)(2,1)S(1)} %bitcast.157), kind=kOutput, calls=%fused_computation.10 | convolution fusion | flops 412088832 | bytes 26161152 | tf_op jit(solution)/shard_map/qhd,khd->hqk/dot_general | solution.py:93
  344.5 11.0 %multiply_convert_fusion.3 = bf16[3,512,2048]{2,1,0:T(8,128)(2,1)} fusion(f32[3,512,2048]{2,1,0:T(8,128)} %get-tuple-element.81, f32[3,512,2048]{2,1,0:T(8,128)S(1)} %bitcast.148, f32[3,512]{1,0:T(4,128)S(1)} %get-tuple-element.80, f32[3,512]{1,0:T(4,128)S(1)} %log_add_fusion.3), kind=kLoop, calls=%fused_computation.9 | loop fusion | flops 12582912 | bytes 31469568 | tf_op jit(solution)/shard_map/convert_element_type | solution.py:97
  355.5 5.6 fusion.56
  366.6 7.7 multiply_reduce_fusion.2
  374.2 8.0 fusion.11
  382.2 11.1 %multiply_reduce_fusion.1 = (f32[3,512]{1,0:T(4,128)}, f32[3,512,2048]{2,1,0:T(8,128)}) fusion(f32[3,512,2048]{2,1,0:T(8,128)} %copy-done.4, f32[3,512]{1,0:T(4,128)S(1)} %log_add_fusion.1, bf16[512,3,64]{0,2,1:T(8,128)(2,1)S(1)} %bitcast.180, bf16[2048,3,64]{0,2,1:T(8,128)(2,1)S(1)} %bitcast.159), kind=kOutput, calls=%fused_computation.4 | convolution fusion | flops 412088832 | bytes 26161152 | tf_op jit(solution)/shard_map/qhd,khd->hqk/dot_general | solution.py:93
  396.7 6.3 multiply_reduce_fusion
  403.0 12.1 %multiply_convert_fusion.2 = bf16[3,512,2048]{2,1,0:T(8,128)(2,1)} fusion(f32[3,512,2048]{2,1,0:T(8,128)} %get-tuple-element.79, f32[3,512,2048]{2,1,0:T(8,128)} %copy-done.5, f32[3,512]{1,0:T(4,128)S(1)} %copy-done.82, f32[3,512]{1,0:T(4,128)S(1)} %log_add_fusion.2), kind=kLoop, calls=%fused_computation.6 | loop fusion | flops 12582912 | bytes 31469568 | tf_op jit(solution)/shard_map/convert_element_type | solution.py:97
  423.9 12.0 %multiply_convert_fusion.1 = bf16[3,512,2048]{2,1,0:T(8,128)(2,1)} fusion(f32[3,512,2048]{2,1,0:T(8,128)} %get-tuple-element.77, f32[3,512,2048]{2,1,0:T(8,128)} %copy-done.4, f32[3,512]{1,0:T(4,128)S(1)} %copy-done.81, f32[3,512]{1,0:T(4,128)S(1)} %log_add_fusion.1), kind=kLoop, calls=%fused_computation.3 | loop fusion | flops 12582912 | bytes 31469568 | tf_op jit(solution)/shard_map/convert_element_type | solution.py:97
  435.9 5.6 fusion.58
  445.4 9.3 %multiply_convert_fusion = bf16[3,512,2048]{2,1,0:T(8,128)(2,1)} fusion(f32[3,512,2048]{2,1,0:T(8,128)} %get-tuple-element.75, f32[3,512,2048]{2,1,0:T(8,128)S(1)} %bitcast.150, f32[3,512]{1,0:T(4,128)S(1)} %get-tuple-element.74, f32[3,512]{1,0:T(4,128)S(1)} %log_add_fusion), kind=kLoop, calls=%fused_computation | loop fusion | flops 12582912 | bytes 31469568 | tf_op jit(solution)/shard_map/convert_element_type | solution.py:97
  474.1 57.1 %reduce-scatter.11.cloned.1.call-done = f32[512,768]{1,0:T(8,128)} async-done(((f32[2048,768]{1,0:T(8,128)}), f32[512,768]{1,0:T(8,128)}) %reduce-scatter.11.cloned.1.call-update) | async-done | bytes 1572880 | tf_op jit(solution)/shard_map/reduce_scatter | solution.py:214
  561.6 22.2 %all-reduce.1 = (f32[192]{0:T(256)}, f32[192]{0:T(256)}, f32[768]{0:T(1024)}) all-reduce(f32[192]{0:T(256)S(1)} %convert_reduce_fusion.4, f32[192]{0:T(256)S(1)} %reduce_sum.247, f32[768]{0:T(1024)S(1)} %copy-done.92), channel_id=1, replica_groups=mesh['dp'=8,'mp'=4] {'dp'}, use_global_device_ids=true, to_apply=%region_30.31 | all-reduce | flops 1152 | bytes 9216 | tf_op jit(solution)/shard_map/psum | solution.py:251
  583.8 37.8 %all-reduce = (f32[768]{0:T(1024)}, f32[768]{0:T(1024)}, f32[768]{0:T(1024)}, f32[768]{0:T(1024)}, f32[768]{0:T(1024)}, /*index=5*/f32[768]{0:T(1024)}) all-reduce(f32[768]{0:T(1024)S(1)} %copy-done.87, f32[768]{0:T(1024)S(1)} %copy-done.88, f32[768]{0:T(1024)S(1)} %copy-done.86, ...), channel_id=1, replica_groups=mesh['dp'=8,'mp'=4] {'dp','mp'}, use_global_device_ids=true, to_apply=%region_25.26 | all-reduce | flops 4608 | bytes 36864 | tf_op jit(solution)/shard_map/psum | solution.py:230
  621.6 232.2 %all-reduce.5.cloned.1.call-done = (f32[768,192]{0,1:T(8,128)}, f32[768,192]{0,1:T(8,128)}, f32[768,192]{0,1:T(8,128)}, f32[192,768]{1,0:T(8,128)}, f32[768,768]{1,0:T(8,128)}, /*index=5*/f32[768,768]{1,0:T(8,128)}) async-done(((f32[768,192]{0,1:T(8,128)}, f32[768,192]{0,1:T(8,128)}, f32[768,192]{0,1:T(8,128)}, f32[192,768]{1,0:T(8,128)}, f32[768,768]{1,0:T(8,128)}, /*index=5*/f32[768,768]{1,0:T(8,128)}), ...) | async-done | bytes 7077904 | tf_op jit(solution)/shard_map/psum | solution.py:251
  (324 shorter events, 174.6 us)
Async XLA Ops:
  7.2 158.0 %copy-start = (bf16[768,768]{1,0:T(8,128)(2,1)S(1)}, bf16[768,768]{1,0:T(8,128)(2,1)}, u32[]{:S(2)}) copy-start(bf16[768,768]{1,0:T(8,128)(2,1)} %param.31) | copy-start | bytes 3538948
  7.2 125.6 %reduce-scatter.5.cloned.1.call-start = ((), (), s32[]{:S(2)}) async-start(), calls=%async_computation.4 | async-start | bytes 7864320 | tf_op jit(solution)/shard_map/reduce_scatter | solution.py:162
  71.6 93.6 %all-gather.5.cloned.1.call-start = ((), (), s32[]{:S(2)}) async-start(), calls=%async_computation.5 | async-start | bytes 3932160 | tf_op jit(solution)/shard_map/all_gather | solution.py:170
  71.7 63.6 %copy-start.63 = (f32[768]{0:T(1024)S(1)}, f32[768]{0:T(1024)}, u32[]{:S(2)}) copy-start(f32[768]{0:T(1024)} %param.29) | copy-start | bytes 9220
  71.7 63.6 %copy-start.90 = (f32[768]{0:T(1024)S(1)}, f32[768]{0:T(1024)}, u32[]{:S(2)}) copy-start(f32[768]{0:T(1024)} %param.30) | copy-start | bytes 9220
  136.5 116.3 %reduce-scatter.9.cloned.1.call-start = ((), (), s32[]{:S(2)}) async-start(), calls=%async_computation.8 | async-start | bytes 7864320 | tf_op jit(solution)/shard_map/reduce_scatter | solution.py:195
  194.3 98.9 %reduce-scatter.7.cloned.1.call-start = ((), (), s32[]{:S(2)}) async-start(), calls=%async_computation.6 | async-start | bytes 3932160 | tf_op jit(solution)/shard_map/reduce_scatter | solution.py:175
  201.7 91.5 %copy-start.91 = (f32[768]{0:T(1024)S(1)}, f32[768]{0:T(1024)}, u32[]{:S(2)}) copy-start(f32[768]{0:T(1024)} %param.34) | copy-start | bytes 9220
  201.8 97.7 %copy-start.65 = (f32[3,512]{1,0:T(4,128)S(1)}, f32[3,512]{1,0:T(4,128)}, u32[]{:S(2)}) copy-start(f32[3,512]{1,0:T(4,128)} %copy-done.64) | copy-start | bytes 18436
  201.8 97.7 %copy-start.67 = (f32[3,512]{1,0:T(4,128)S(1)}, f32[3,512]{1,0:T(4,128)}, u32[]{:S(2)}) copy-start(f32[3,512]{1,0:T(4,128)} %copy-done.66) | copy-start | bytes 18436
  201.8 97.7 %copy-start.69 = (f32[3,512]{1,0:T(4,128)S(1)}, f32[3,512]{1,0:T(4,128)}, u32[]{:S(2)}) copy-start(f32[3,512]{1,0:T(4,128)} %copy-done.68) | copy-start | bytes 18436
  201.8 97.7 %copy-start.71 = (f32[3,512]{1,0:T(4,128)S(1)}, f32[3,512]{1,0:T(4,128)}, u32[]{:S(2)}) copy-start(f32[3,512]{1,0:T(4,128)} %copy-done.70) | copy-start | bytes 18436
  201.8 97.7 %copy-start.73 = (f32[3,512]{1,0:T(4,128)S(1)}, f32[3,512]{1,0:T(4,128)}, u32[]{:S(2)}) copy-start(f32[3,512]{1,0:T(4,128)} %copy-done.72) | copy-start | bytes 18436
  201.8 97.7 %copy-start.75 = (f32[3,512]{1,0:T(4,128)S(1)}, f32[3,512]{1,0:T(4,128)}, u32[]{:S(2)}) copy-start(f32[3,512]{1,0:T(4,128)} %copy-done.74) | copy-start | bytes 18436
  201.8 97.7 %copy-start.77 = (f32[3,512]{1,0:T(4,128)S(1)}, f32[3,512]{1,0:T(4,128)}, u32[]{:S(2)}) copy-start(f32[3,512]{1,0:T(4,128)} %copy-done.76) | copy-start | bytes 18436
  201.8 97.7 %copy-start.79 = (f32[3,512]{1,0:T(4,128)S(1)}, f32[3,512]{1,0:T(4,128)}, u32[]{:S(2)}) copy-start(f32[3,512]{1,0:T(4,128)} %copy-done.78) | copy-start | bytes 18436
  201.8 126.3 %copy-start.43 = (bf16[192,768]{1,0:T(8,128)(2,1)S(1)}, bf16[192,768]{1,0:T(8,128)(2,1)}, u32[]{:S(2)}) copy-start(bf16[192,768]{1,0:T(8,128)(2,1)} %param.27) | copy-start | bytes 884740
  201.9 126.2 %all-gather.9.cloned.1.call-start = ((), (), s32[]{:S(2)}) async-start(), calls=%async_computation.9 | async-start | bytes 3932160 | tf_op jit(solution)/shard_map/all_gather | solution.py:201
  299.4 231.8 %reduce-scatter.11.cloned.1.call-start = ((), (), s32[]{:S(2)}) async-start(), calls=%async_computation.10 | async-start | bytes 7864320 | tf_op jit(solution)/shard_map/reduce_scatter | solution.py:214
  472.6 61.5 %copy-start.12 = (f32[512,768]{1,0:T(8,128)S(1)}, f32[512,768]{1,0:T(8,128)}, u32[]{:S(2)}) copy-start(f32[512,768]{1,0:T(8,128)} %copy-done.11) | copy-start | bytes 4718596
  472.6 65.0 %copy-start.59 = (f32[2048]{0:T(1024)S(1)}, f32[2048]{0:T(1024)}, u32[]{:S(2)}) copy-start(f32[2048]{0:T(1024)} %copy-done.58) | copy-start | bytes 24580
  472.6 88.6 %all-gather.7.cloned.1.call-start = ((), (), s32[]{:S(2)}) async-start(), calls=%async_computation.7 | async-start | bytes 3932160 | tf_op jit(solution)/shard_map/all_gather | solution.py:185
  473.4 148.2 %all-gather.11.cloned.1.call-start = ((), (), s32[]{:S(2)}) async-start(), calls=%async_computation.11 | async-start | bytes 7864320 | tf_op jit(solution)/shard_map/all_gather | solution.py:222
  537.6 316.1 %all-reduce.5.cloned.1.call-start = ((), (), s32[]{:S(2)}) async-start(), calls=%async_computation.12 | async-start | bytes 14155776 | tf_op jit(solution)/shard_map/psum | solution.py:251
  (98 other events, 820.5 us)
Sparse Core Ops, SparseCore 0:
  71.7 61.0 reduce-scatter.4
  136.6 28.5 all-gather.4
  194.4 58.3 reduce-scatter.8
  255.2 37.9 reduce-scatter.6
  299.5 28.5 all-gather.8
  472.8 58.3 reduce-scatter.10
  532.7 28.5 all-gather.6
  562.9 47.0 all-gather.10
  616.2 237.4 all-reduce.4
where the time goes:
time: 883 us; the launch traced here: 875 us
  waiting for transfers between devices  494 us (56%)
  matrix products  177 us (20%)
  other arithmetic  91.7 us (10%)
  blocking collectives  60 us (7%)
  local copies, waits for them, and re-layouts  35.9 us (4%)
  between operations  15.3 us (2%)
    psum x1, waiting for transfers between devices, local(): lax.psum((grad_query_weight, grad_query_bias, grad_key_weight, grad_value...  232 us
    reduce_scatter x1, waiting for transfers between devices, local(): lax.psum_scatter(total + against(grad_values, value_weight), 'mp', scatte...  57.1 us
    reduce_scatter x1, waiting for transfers between devices, local(): lax.psum_scatter(jnp.dot(attended, output_weight, preferred_element_type=...  56.1 us
    reduce_scatter x1, waiting for transfers between devices, local(): lax.psum_scatter(against(grad_hidden, inner_weight), 'mp', scatter_dimens...  50.9 us
    convert_element_type x4, other arithmetic, attend_backward(): (softmax_block * (grad_softmax - inner_sum)).astype(jnp.bfloat16)  44.4 us
    psum x1, blocking collectives, local(): lax.psum((gain_one_part, bias_one_part, jnp.sum(grad_residual, axis=0), g...  37.8 us
    reduce_scatter x1, waiting for transfers between devices, local(): lax.psum_scatter(jnp.dot(activated, outer_weight, preferred_element_type=...  37.6 us
    dot_general x4, matrix products, attend_backward(): jnp.einsum('qhd,khd->hqk', grad_context, value_block, preferred_element_t...  36.2 us
  transfers between devices with their start and end apart: 9, of which 8 were waited for; matrix products, arithmetic and copies ran while one was open for 5% of the time, Pallas kernels for 0%

commit v1 on v0

v1 whole, which is shorter than its diff:
```python
import functools

import jax
import jax.numpy as jnp
from jax import lax
from jax.experimental import pallas as pl
from jax.experimental.pallas import tpu as pltpu
from jax.sharding import Mesh
from jax.sharding import PartitionSpec as P

HEAD = 64
WIDE = 128
TILE = 256
MASKED = 1e30
F32 = jnp.float32
BF16 = jnp.bfloat16
MP = ("y", "core")
SWAP = [(0, 1), (1, 0)]


def nn(left, right):
    return lax.dot_general(left, right, (((1,), (0,)), ((), ())), preferred_element_type=F32)


def nt(left, right):
    return lax.dot_general(left, right, (((1,), (1,)), ((), ())), preferred_element_type=F32)


def tn(left, right):
    return lax.dot_general(left, right, (((0,), (0,)), ((), ())), preferred_element_type=F32)


def stats(values):
    center = values - jnp.mean(values, axis=-1, keepdims=True)
    scale = lax.rsqrt(jnp.mean(center * center, axis=-1, keepdims=True) + 1e-05)
    return center * scale, scale


def norm_back(grad_out, normed, scale, gain):
    upstream = grad_out * gain
    return scale * (
        upstream
        - jnp.mean(upstream, axis=-1, keepdims=True)
        - normed * jnp.mean(upstream * normed, axis=-1, keepdims=True)
    )


def project_body(x_ref, seg_ref, gain_ref, bias_ref, wt_ref, wn_ref, qb_ref, vb_ref, vbn_ref,
                 ai_ref, qt_ref, kt_ref, vt_ref, kn_ref, vn_ref):
    heads = kn_ref.shape[0]
    width = heads * HEAD
    normed, _ = stats(x_ref[...].astype(F32))
    ai = (normed * gain_ref[...] + bias_ref[...]).astype(BF16)
    ai_ref[...] = ai
    low = nt(wt_ref[...], ai)
    queries = ((low[:width] + qb_ref[...]).astype(BF16)).astype(F32) * HEAD ** -0.5
    kt_ref[...] = low[width:2 * width].astype(BF16)
    vt_ref[...] = (low[2 * width:] + vb_ref[...]).astype(BF16)
    tile = x_ref.shape[0]
    row = lax.broadcasted_iota(jnp.int32, (WIDE, tile), 0) - HEAD
    same = jnp.where(row == seg_ref[...], 1.0, 0.0)
    same = jnp.where(row >= 0, same, 0.0)
    for h in range(heads):
        qt_ref[h, :HEAD, :] = queries[h * HEAD:(h + 1) * HEAD].astype(BF16)
        qt_ref[h, HEAD:, :] = same[HEAD:].astype(BF16)
    lane = lax.broadcasted_iota(jnp.int32, (tile, WIDE), 1)
    mask = jnp.where((lane >= HEAD) & (lane < HEAD + 8), (same.T - 1.0) * MASKED, 0.0)
    mask = jnp.where((lane >= HEAD + 8) & (lane < HEAD + 11), 1.0, mask)
    ones = jnp.where((lane >= HEAD) & (lane < HEAD + 2), 1.0, 0.0)
    natural = nn(ai, wn_ref[...])
    for h in range(heads):
        kn_ref[h] = (natural[:, h * WIDE:(h + 1) * WIDE] + mask).astype(BF16)
        at = (heads + h) * WIDE
        vn_ref[h] = (natural[:, at:at + WIDE] + vbn_ref[:, h * WIDE:(h + 1) * WIDE] + ones).astype(BF16)


def project(tokens, seg_row, gain, bias, wt, wn, qb, vb, vbn, heads):
    length, features = tokens.shape
    width = heads * HEAD
    const = lambda shape: pl.BlockSpec(shape, lambda i: (0,) * len(shape))
    return pl.pallas_call(
        project_body,
        grid=(length // TILE,),
        in_specs=[
            pl.BlockSpec((TILE, features), lambda i: (i, 0)),
            pl.BlockSpec((1, TILE), lambda i: (0, i)),
            const((1, features)), const((1, features)),
            const(wt.shape), const(wn.shape), const(qb.shape), const(vb.shape), const(vbn.shape),
        ],
        out_specs=[
            pl.BlockSpec((TILE, features), lambda i: (i, 0)),
            pl.BlockSpec((heads, WIDE, TILE), lambda i: (0, 0, i)),
            pl.BlockSpec((width, TILE), lambda i: (0, i)),
            pl.BlockSpec((width, TILE), lambda i: (0, i)),
            pl.BlockSpec((heads, TILE, WIDE), lambda i: (0, i, 0)),
            pl.BlockSpec((heads, TILE, WIDE), lambda i: (0, i, 0)),
        ],
        out_shape=[
            jax.ShapeDtypeStruct((length, features), BF16),
            jax.ShapeDtypeStruct((heads, WIDE, length), BF16),
            jax.ShapeDtypeStruct((width, length), BF16),
            jax.ShapeDtypeStruct((width, length), BF16),
            jax.ShapeDtypeStruct((heads, length, WIDE), BF16),
            jax.ShapeDtypeStruct((heads, length, WIDE), BF16),
        ],
        compiler_params=pltpu.CompilerParams(vmem_limit_bytes=48 << 20),
        name="project",
    )(tokens, seg_row, gain, bias, wt, wn, qb, vb, vbn)


def key_range(seg_ref, seg_all, i):
    first = seg_ref[0, i * TILE]
    last = seg_ref[0, i * TILE + TILE - 1]
    before = jnp.sum(jnp.where(seg_all < first, 1.0, 0.0)).astype(jnp.int32)
    until = jnp.sum(jnp.where(seg_all <= last, 1.0, 0.0)).astype(jnp.int32)
    return before // TILE, (until + TILE - 1) // TILE


def split(value, parts):
    out = []
    for _ in range(parts):
        piece = value.astype(BF16).astype(F32)
        out.append(piece)
        value = value - piece
    return out


def forward_body(segs_ref, seg_ref, qt_ref, kn_ref, vt_ref, out_ref, extra_ref, acc_ref):
    heads = qt_ref.shape[0]
    low, high = key_range(segs_ref, seg_ref[...], pl.program_id(0))
    acc_ref[...] = jnp.zeros_like(acc_ref)

    def step(kb, carry):
        at = pl.multiple_of(kb * TILE, TILE)
        result = []
        for h in range(heads):
            top, total = carry[2 * h], carry[2 * h + 1]
            scores = nn(kn_ref[h, pl.ds(at, TILE), :], qt_ref[h])
            new_top = jnp.maximum(top, jnp.max(scores, axis=0, keepdims=True))
            powered = jnp.exp(scores - new_top)
            fade = jnp.exp(top - new_top)
            result += [new_top, total * fade + jnp.sum(powered, axis=0, keepdims=True)]
            rows = slice(h * HEAD, (h + 1) * HEAD)
            acc_ref[rows] = acc_ref[rows] * fade + nn(vt_ref[rows, pl.ds(at, TILE)], powered.astype(BF16))
        return tuple(result)

    tile = qt_ref.shape[2]
    start = (jnp.full((1, tile), -jnp.inf, F32), jnp.zeros((1, tile), F32)) * heads
    carry = lax.fori_loop(low, high, step, start)
    for h in range(heads):
        top, total = carry[2 * h], carry[2 * h + 1]
        rows = slice(h * HEAD, (h + 1) * HEAD)
        out_ref[rows] = (acc_ref[rows] / total).astype(BF16)
        pieces = split(-(top + jnp.log(total)), 3)
        one_hot = qt_ref[h, HEAD:HEAD + 16, :].astype(F32)
        row = lax.broadcasted_iota(jnp.int32, (16, tile), 0)
        value = one_hot
        for n, piece in enumerate(pieces):
            value = jnp.where(row == 8 + n, piece, value)
        extra_ref[h] = value.astype(BF16)


def attend_forward(seg_row, qt, kn, vt):
    heads, _, length = qt.shape
    width = heads * HEAD
    const = lambda shape: pl.BlockSpec(shape, lambda i: (0,) * len(shape))
    return pl.pallas_call(
        forward_body,
        grid=(length // TILE,),
        in_specs=[
            pl.BlockSpec(memory_space=pltpu.SMEM),
            const((1, length)),
            pl.BlockSpec((heads, WIDE, TILE), lambda i: (0, 0, i)),
            const(kn.shape), const(vt.shape),
        ],
        out_specs=[
            pl.BlockSpec((width, TILE), lambda i: (0, i)),
            pl.BlockSpec((heads, 16, TILE), lambda i: (0, 0, i)),
        ],
        out_shape=[
            jax.ShapeDtypeStruct((width, length), BF16),
            jax.ShapeDtypeStruct((heads, 16, length), BF16),
        ],
        scratch_shapes=[pltpu.VMEM((width, TILE), F32)],
        compiler_params=pltpu.CompilerParams(vmem_limit_bytes=48 << 20),
        name="attend_forward",
    )(seg_row, seg_row, qt, kn, vt)


def backward_body(segs_ref, seg_ref, qt_ref, extra_ref, kn_ref, kt_ref, vn_ref, out_ref, grad_ref,
                  grads_ref, qa_ref, da_ref, dq_ref, dk_ref, dv_ref):
    heads = qt_ref.shape[0]
    width = heads * HEAD
    tile = qt_ref.shape[2]
    i = pl.program_id(0)
    low, high = key_range(segs_ref, seg_ref[...], i)

    @pl.when(i == 0)
    def _():
        dk_ref[...] = jnp.zeros_like(dk_ref)
        dv_ref[...] = jnp.zeros_like(dv_ref)
        qa_ref[...] = jnp.zeros_like(qa_ref)
        da_ref[...] = jnp.zeros_like(da_ref)

    dq_ref[...] = jnp.zeros_like(dq_ref)
    row = lax.broadcasted_iota(jnp.int32, (16, tile), 0)
    for h in range(heads):
        rows = slice(h * HEAD, (h + 1) * HEAD)
        qa_ref[h, :HEAD, :] = qt_ref[h, :HEAD, :]
        qa_ref[h, HEAD:HEAD + 16, :] = extra_ref[h]
        grad = grad_ref[rows]
        da_ref[h, :HEAD, :] = grad
        inner = jnp.sum(grad.astype(F32) * out_ref[rows].astype(F32), axis=0, keepdims=True)
        first, second = split(-inner, 2)
        value = jnp.where(row == 0, first, jnp.where(row == 1, second, 0.0))
        da_ref[h, HEAD:HEAD + 16, :] = value.astype(BF16)

    def step(kb, carry):
        at = pl.multiple_of(kb * TILE, TILE)
        keys = pl.ds(at, TILE)
        for h in range(heads):
            rows = slice(h * HEAD, (h + 1) * HEAD)
            probs = jnp.exp(nn(kn_ref[h, keys, :], qa_ref[h]))
            ds = (probs * nn(vn_ref[h, keys, :], da_ref[h])).astype(BF16)
            dv_ref[rows, keys] += nt(grad_ref[rows], probs.astype(BF16))
            dk_ref[rows, keys] += nt(qa_ref[h, :HEAD, :], ds)
            dq_ref[rows] += nn(kt_ref[rows, keys], ds)
        return carry

    lax.fori_loop(low, high, step, 0)
    here = pl.ds(pl.multiple_of(i * TILE, TILE), TILE)
    grads_ref[:width, here] = (dq_ref[...] * HEAD ** -0.5).astype(BF16)

    @pl.when(i == pl.num_programs(0) - 1)
    def _():
        grads_ref[width:2 * width] = dk_ref[...].astype(BF16)
        grads_ref[2 * width:] = dv_ref[...].astype(BF16)


def attend_backward(seg_row, qt, extra, kn, kt, vn, out, grad):
    heads, _, length = qt.shape
    width = heads * HEAD
    const = lambda shape: pl.BlockSpec(shape, lambda i: (0,) * len(shape))
    return pl.pallas_call(
        backward_body,
        grid=(length // TILE,),
        in_specs=[
            pl.BlockSpec(memory_space=pltpu.SMEM),
            const((1, length)),
            pl.BlockSpec((heads, WIDE, TILE), lambda i: (0, 0, i)),
            pl.BlockSpec((heads, 16, TILE), lambda i: (0, 0, i)),
            const(kn.shape), const(kt.shape), const(vn.shape),
            pl.BlockSpec((width, TILE), lambda i: (0, i)),
            pl.BlockSpec((width, TILE), lambda i: (0, i)),
        ],
        out_specs=const((3 * width, length)),
        out_shape=jax.ShapeDtypeStruct((3 * width, length), BF16),
        scratch_shapes=[
            pltpu.VMEM((heads, WIDE, TILE), BF16),
            pltpu.VMEM((heads, WIDE, TILE), BF16),
            pltpu.VMEM((width, TILE), F32),
            pltpu.VMEM((width, length), F32),
            pltpu.VMEM((width, length), F32),
        ],
        compiler_params=pltpu.CompilerParams(vmem_limit_bytes=48 << 20),
        name="attend_backward",
    )(seg_row, seg_row, qt, extra, kn, kt, vn, out, grad)


def feed_body(order_ref, x_ref, g_ref, inner_ref, bias_ref, outer_ref, act_ref, dh_ref, out_ref, back_ref):
    hidden = nn(x_ref[...], inner_ref[...]) + bias_ref[...]
    half = 0.5 + 0.5 * lax.erf(hidden * 0.5 ** 0.5)
    act = (hidden * half).astype(BF16)
    act_ref[...] = act
    slope = half + hidden * (jnp.exp(-0.5 * hidden * hidden) * 0.3989422804014327)
    dh = (nt(g_ref[...], outer_ref[...]) * slope).astype(BF16)
    dh_ref[...] = dh
    out_ref[...] = nn(act, outer_ref[...]).astype(BF16)
    back_ref[...] = nt(dh, inner_ref[...]).astype(BF16)


def feed(order, x, cot, inner, bias, outer):
    total, features = x.shape
    units = inner.shape[1]
    const = lambda shape: pl.BlockSpec(shape, lambda i, o: (0,) * len(shape))
    rows = lambda n: pl.BlockSpec((TILE, n), lambda i, o: (i, 0))
    shape = lambda n: jax.ShapeDtypeStruct((total, n), BF16)
    return pl.pallas_call(
        feed_body,
        grid_spec=pltpu.PrefetchScalarGridSpec(
            num_scalar_prefetch=1,
            grid=(total // TILE,),
            in_specs=[
                rows(features),
                pl.BlockSpec((TILE, features), lambda i, o: (o[i], 0)),
                const(inner.shape), const(bias.shape), const(outer.shape),
            ],
            out_specs=[rows(units), rows(units), rows(features), rows(features)],
        ),
        out_shape=[shape(units), shape(units), shape(features), shape(features)],
        compiler_params=pltpu.CompilerParams(vmem_limit_bytes=48 << 20),
        name="feed",
    )(order, x, cot, inner, bias, outer)


def other_core(value):
    return lax.ppermute(value, "core", SWAP)


def other_chip(value):
    return lax.ppermute(value, "y", SWAP)


def local(
    tokens,
    segment_ids,
    gain_one,
    bias_one,
    query_weight,
    query_bias,
    key_weight,
    value_weight,
    value_bias,
    output_weight,
    output_bias,
    gain_two,
    bias_two,
    inner_weight,
    inner_bias,
    outer_weight,
    outer_bias,
    cotangent,
):
    _, length, features = tokens.shape
    width = query_weight.shape[1]
    heads = width // HEAD
    tokens = tokens.reshape(length, features)
    cot = cotangent.reshape(length, features)
    share = length // 4
    me = lax.axis_index(MP)
    begin = me * share

    output_full = lax.all_gather(output_weight, MP, axis=0, tiled=True)
    pad = lambda w: jnp.pad(w.reshape(-1, heads, HEAD), ((0, 0), (0, 0), (0, WIDE - HEAD))).reshape(-1, heads * WIDE)
    wt = jnp.concatenate([query_weight, key_weight, value_weight], axis=1).T
    wn = jnp.concatenate([pad(key_weight), pad(value_weight)], axis=1)
    attend_in, qt, kt, vt, kn, vn = project(
        tokens, segment_ids, gain_one[None], bias_one[None], wt, wn,
        query_bias[:, None], value_bias[:, None], pad(value_bias[None]), heads,
    )
    attended, extra = attend_forward(segment_ids, qt, kn, vt)

    mine = lax.all_to_all(attended, MP, 1, 0, tiled=True)
    inputs = lax.dynamic_slice_in_dim(tokens, begin, share, 0).astype(F32)
    residual = inputs + tn(mine, output_full) + output_bias
    normed_two, scale_two = stats(residual)
    own = (normed_two * gain_two + bias_two).astype(BF16)
    near = other_core(own)
    far = other_chip(own)
    across = other_core(far)

    blocks = share // TILE
    order = lambda who: who * blocks + jnp.arange(blocks, dtype=jnp.int32)
    x_one = jnp.concatenate([own, near], axis=0)
    x_two = jnp.concatenate([far, across], axis=0)
    cot_one = jnp.concatenate([order(me), order(me ^ 1)])
    cot_two = jnp.concatenate([order(me ^ 2), order(me ^ 3)])
    inner_row = inner_bias[None]
    act_one, dh_one, out_one, back_one = feed(cot_one, x_one, cot, inner_weight, inner_row, outer_weight)
    act_two, dh_two, out_two, back_two = feed(cot_two, x_two, cot, inner_weight, inner_row, outer_weight)

    def gather_sum(one, two):
        low = lambda v: v.astype(BF16)
        wide = lambda v: v.astype(F32)
        far_sum = low(wide(two[:share]) + wide(other_core(two[share:])))
        near_sum = wide(one[:share]) + wide(other_core(one[share:]))
        return near_sum + wide(other_chip(far_sum))

    grad_mid = gather_sum(back_one, back_two)
    cot_share = lax.dynamic_slice_in_dim(cot, begin, share, 0).astype(F32)
    grad_residual = cot_share + norm_back(grad_mid, normed_two, scale_two, gain_two)
    residual_low = grad_residual.astype(BF16)
    grad_attended = lax.all_to_all(nt(output_full, residual_low).astype(BF16), MP, 0, 1, tiled=True)

    cot_of = lambda who: lax.dynamic_slice_in_dim(cot, who * share, share, 0)
    g_one = jnp.concatenate([cot_of(me), cot_of(me ^ 1)], axis=0)
    g_two = jnp.concatenate([cot_of(me ^ 2), cot_of(me ^ 3)], axis=0)
    grad_outer = (tn(act_one, g_one) + tn(act_two, g_two)).astype(BF16)
    grad_inner = (tn(x_one, dh_one) + tn(x_two, dh_two)).astype(BF16)
    colsum = lambda v: jnp.sum(v.astype(F32), axis=0)
    vectors = jnp.stack([
        colsum(dh_one) + colsum(dh_two),
        jnp.sum(grad_mid * normed_two, axis=0),
        jnp.sum(grad_mid, axis=0),
        colsum(grad_residual),
        colsum(cot_share),
    ]).astype(BF16)
    grad_outer, grad_inner, vectors = lax.psum((grad_outer, grad_inner, vectors), "dp")

    result = residual + gather_sum(out_one, out_two) + outer_bias

    def spread(value):
        near, far = other_core(value), other_chip(value)
        across = other_core(far)
        whole = jnp.zeros((length, features), value.dtype)
        for n, part in enumerate((value, near, far, across)):
            whole = lax.dynamic_update_slice_in_dim(whole, part, (me ^ n) * share, 0)
        return whole

    layer_out = spread(result.astype(BF16))

    grads = attend_backward(segment_ids, qt, extra, kn, kt, vn, attended, grad_attended)
    part_of = lambda who: tn(lax.dynamic_slice_in_dim(grads, who * share, share, 1), wt)
    piece = [part_of(me ^ n) for n in (2, 3, 0, 1)]
    far_sum = (piece[0] + other_core(piece[1].astype(BF16)).astype(F32)).astype(BF16)
    grad_attend = piece[2] + other_core(piece[3].astype(BF16)).astype(F32) + other_chip(far_sum).astype(F32)
    normed_one, scale_one = stats(inputs)
    input_share = grad_residual + norm_back(grad_attend, normed_one, scale_one, gain_one)
    input_grad = spread(input_share.astype(BF16)).astype(F32)

    grad_weights = nn(grads, attend_in).astype(BF16)
    low_all = spread(residual_low)
    grad_output = nn(attended, low_all).astype(BF16)
    rowsum = jnp.sum(grads.astype(F32), axis=1).reshape(3, width)
    more = jnp.stack([
        jnp.pad(rowsum[0], (0, features - width)),
        jnp.pad(rowsum[2], (0, features - width)),
        jnp.sum(grad_attend * normed_one, axis=0),
        jnp.sum(grad_attend, axis=0),
    ]).astype(BF16)
    grad_weights, grad_output, more = lax.psum((grad_weights, grad_output, more), "dp")

    vectors, more = vectors.astype(F32), more.astype(F32)
    shared = lax.psum(jnp.concatenate([vectors[1:], more[2:]]), MP)
    weights = grad_weights.astype(F32).T
    return (
        layer_out.reshape(1, length, features),
        input_grad.reshape(1, length, features),
        shared[4],
        shared[5],
        weights[:, :width],
        more[0, :width],
        weights[:, width:2 * width],
        weights[:, 2 * width:],
        more[1, :width],
        grad_output.astype(F32),
        shared[2],
        shared[0],
        shared[1],
        grad_inner.astype(F32),
        vectors[0],
        grad_outer.astype(F32),
        shared[3],
    )


def solution(mesh):
    rows = mesh.shape["dp"]
    inner = Mesh(mesh.devices.reshape(rows, 2, 2), ("dp", "y", "core"))
    placed = (
        P("dp", None, None),
        P("dp", None),
        P(),
        P(),
        P(None, MP),
        P(MP),
        P(None, MP),
        P(None, MP),
        P(MP),
        P(MP, None),
        P(),
        P(),
        P(),
        P(None, MP),
        P(MP),
        P(MP, None),
        P(),
        P("dp", None, None),
    )
    return jax.shard_map(
        local,
        mesh=inner,
        in_specs=placed,
        out_specs=(
            P("dp", None, None),
            P("dp", None, None),
            P(),
            P(),
            P(None, MP),
            P(MP),
            P(None, MP),
            P(None, MP),
            P(MP),
            P(MP, None),
            P(),
            P(),
            P(),
            P(None, MP),
            P(MP),
            P(MP, None),
            P(),
        ),
        check_vma=False,
    )
```

time: 883 us -> 435 us (0.49)
  waiting for transfers between devices: 494 us -> 143 us
  matrix products: 177 us -> 37.3 us
  Pallas kernels: 0 us -> 82.1 us
  other arithmetic: 91.7 us -> 36.7 us
  starting transfers between devices: 0.37 us -> 15.2 us
    reduce_scatter x4 -> x0, waiting for transfers between devices: 202 us -> none  [the longest x1 57.1 us: local(): lax.psum_scatter(total + against(grad_values, value_weight), 'mp', scatte...]
    psum x1, waiting for transfers between devices: 232 us -> 55.5 us  [local(): lax.psum((grad_weights, grad_output, more), 'dp')]
    dot_general x42 -> x12, matrix products: 177 us -> 37.3 us  [the longest x9 28.3 us: tn(): lax.dot_general(left, right, (((0,), (0,)), ((), ())), preferred_element_...]
    pallas_call x0 -> x5, Pallas kernels: none -> 82.1 us  [the longest x1 28.2 us: attend_backward(): pl.pallas_call(backward_body, grid=(length // TILE,), in_specs=[pl.BlockS...]
    all_gather x4 -> x1, waiting for transfers between devices: 59.6 us -> 0.01 us  [local(): output_full = lax.all_gather(output_weight, MP, axis=0, tiled=True)]
    ppermute x0 -> x21, waiting for transfers between devices: none -> 57.2 us  [the longest x7 57.2 us: other_chip(): return lax.ppermute(value, 'y', SWAP)]
    convert_element_type x8 -> x7, other arithmetic: 54.9 us -> 8.17 us  [the longest x1 2.94 us: local(): grad_inner.astype(F32)]
    all_to_all x0 -> x2, waiting for transfers between devices: none -> 29.5 us  [the longest x1 17.1 us: local(): lax.all_to_all(nt(output_full, residual_low).astype(BF16), MP, 0, 1, tile...]
  transfers between devices with their start and end apart: 9 -> 25, of which waited for: 8 -> 7; matrix products, arithmetic and copies ran while one was open for 5% -> 21% of each run, Pallas kernels for 0% -> 19%
where the time goes in v1:
time: 435 us; the launch traced here: 434 us
  waiting for transfers between devices  143 us (33%)
  Pallas kernels  82.1 us (19%)
  blocking collectives  68.5 us (16%)
  matrix products  37.3 us (9%)
  other arithmetic  36.7 us (8%)
  local copies, waits for them, and re-layouts  36.6 us (8%)
  starting transfers between devices  15.2 us (3%)
  between operations  14.8 us (3%)
    psum x1, blocking collectives, local(): lax.psum((grad_weights, grad_output, more), 'dp')  57.8 us
    ppermute x7, waiting for transfers between devices, other_chip(): return lax.ppermute(value, 'y', SWAP)  57.2 us
    psum x1, waiting for transfers between devices, local(): lax.psum((grad_weights, grad_output, more), 'dp')  55.5 us
    dot_general x9, matrix products, tn(): lax.dot_general(left, right, (((0,), (0,)), ((), ())), preferred_element_...  28.3 us
    pallas_call x1, Pallas kernels, attend_backward(): pl.pallas_call(backward_body, grid=(length // TILE,), in_specs=[pl.BlockS...  28.2 us
    pallas_call x1, Pallas kernels, attend_forward(): pl.pallas_call(forward_body, grid=(length // TILE,), in_specs=[pl.BlockSp...  26.5 us
    all_to_all x1, waiting for transfers between devices, local(): lax.all_to_all(nt(output_full, residual_low).astype(BF16), MP, 0, 1, tile...  17.1 us
    pallas_call x2, Pallas kernels, feed(): pl.pallas_call(feed_body, grid_spec=pltpu.PrefetchScalarGridSpec(num_scal...  17 us
  transfers between devices with their start and end apart: 25, of which 7 were waited for; matrix products, arithmetic and copies ran while one was open for 21% of the time, Pallas kernels for 19%

profile of v1, /device:TPU:0, one launch (start us, length us, event | category | flops | bytes accessed | tf_op | source)
XLA Modules:
  0.0 434.1 jit_solution(8404541963161439299)
XLA Ops:
  11.0 10.5 %project.1 = (bf16[2048,768]{1,0:T(8,128)(2,1)}, bf16[3,128,2048]{2,1,0:T(8,128)(2,1)S(1)}, bf16[192,2048]{1,0:T(8,128)(2,1)S(1)}, bf16[192,2048]{1,0:T(8,128)(2...) custom-call(bf16[2048,768]{1,0:T(8,128)(2,1)} %bitcast.112, s32[1,2048]{1,0:T(1,128)S(1)} %copy-done.6, ...), custom_call_target="tpu_custom_call" | custom-call | tf_op jit(solution)/shard_map/project/pallas_call | solution.py:81
  23.2 26.5 %attend_forward.1 = (bf16[192,2048]{1,0:T(8,128)(2,1)S(1)}, bf16[3,16,2048]{2,1,0:T(8,128)(2,1)S(1)}) custom-call(s32[1,2048]{1,0:T(1,128)S(1)} %copy-done.6, s32[1,2048]{1,0:T(1,128)S(1)} %copy-done.6, bf16[3,128,2048]{2,1,0:T(8,128)(2,1)S(1)} %get-tuple-element.33.qt_ref, bf16[3,2048,128]{2,1,0:T(8,128)(2,1)S(1)} %copy-done, ...), custom_call_target="tpu_custom_call" | custom-call | tf_op jit(solution)/shard_map/attend_forward/pallas_call | solution.py:167
  50.6 4.2 all-to-all-start
  54.9 12.3 %all-to-all-done = bf16[192,4,512]{2,0,1:T(8,128)(2,1)} async-done(((bf16[192,4,512]{2,0,1:T(8,128)(2,1)}), bf16[192,4,512]{2,0,1:T(8,128)(2,1)}, u32[]{:S(2)}, u32[]{:S(2)}) %all-to-all-start) | async-done | bytes 786464 | tf_op jit(solution)/shard_map/all_to_all | solution.py:353
  73.2 3.3 dynamic-slice_bitcast_fusion.1
  76.5 14.4 %collective-permute-done.2 = bf16[512,768]{1,0:T(8,128)(2,1)} collective-permute-done((bf16[512,768]{1,0:T(8,128)(2,1)}, bf16[512,768]{1,0:T(8,128)(2,1)}, u32[]{:S(2)}, u32[]{:S(2)}) %collective-permute-start.2) | collective-permute-done | bytes 786464 | tf_op jit(solution)/shard_map/ppermute | solution.py:311
  95.7 8.5 %feed.3 = (bf16[1024,768]{1,0:T(8,128)(2,1)S(1)}, bf16[1024,768]{1,0:T(8,128)(2,1)S(1)}, bf16[1024,768]{1,0:T(8,128)(2,1)}, bf16[1024,768]{1,0:T(8,128)(2,1)}) custom-call(s32[4]{0:T(128)S(1)} %pad_add_fusion.1.order_ref, bf16[1024,768]{1,0:T(8,128)(2,1)} %copy-done.17, bf16[2048,768]{1,0:T(8,128)(2,1)} %bitcast.110, bf16[768,768]{1,0:T(8,128)(2,1)S(1)} %copy-done.2, ...), custom_call_target="tpu_custom_call" | custom-call | tf_op jit(solution)/shard_map/feed/pallas_call | solution.py:288
  109.4 8.5 %feed.2 = (bf16[1024,768]{1,0:T(8,128)(2,1)S(1)}, bf16[1024,768]{1,0:T(8,128)(2,1)S(1)}, bf16[1024,768]{1,0:T(8,128)(2,1)}, bf16[1024,768]{1,0:T(8,128)(2,1)}) custom-call(s32[4]{0:T(128)S(1)} %pad_add_fusion.order_ref, bf16[1024,768]{1,0:T(8,128)(2,1)} %pad_maximum_fusion.x_ref, bf16[2048,768]{1,0:T(8,128)(2,1)} %bitcast.111, ...), custom_call_target="tpu_custom_call" | custom-call | tf_op jit(solution)/shard_map/feed/pallas_call | solution.py:288
  131.8 15.5 %collective-permute-done.11 = bf16[512,768]{1,0:T(8,128)(2,1)S(1)} collective-permute-done((bf16[512,768]{1,0:T(8,128)(2,1)S(1)}, bf16[512,768]{1,0:T(8,128)(2,1)S(1)}, u32[]{:S(2)}, u32[]{:S(2)}) %collective-permute-start.11) | collective-permute-done | bytes 786464 | tf_op jit(solution)/shard_map/ppermute | solution.py:311
  148.5 3.7 constant_dynamic-update-slice_fusion.8
  152.7 11.5 %collective-permute-done.5 = bf16[512,768]{1,0:T(8,128)(2,1)S(1)} collective-permute-done((bf16[512,768]{1,0:T(8,128)(2,1)S(1)}, bf16[512,768]{1,0:T(8,128)(2,1)S(1)}, u32[]{:S(2)}, u32[]{:S(2)}) %collective-permute-start.5) | collective-permute-done | bytes 786464 | tf_op jit(solution)/shard_map/ppermute | solution.py:311
  173.0 4.2 all-to-all-start.1
  177.2 4.7 %fusion.15 = f32[768,768]{1,0:T(8,128)} fusion(bf16[1024,768]{1,0:T(8,128)(2,1)} %copy-done.8, bf16[512,768]{1,0:T(8,128)(2,1)} %get-tuple-element.80, bf16[512,768]{1,0:T(8,128)(2,1)} %get-tuple-element.72), kind=kOutput, calls=%fused_computation.22 | convolution fusion | flops 1211105280 | bytes 5505024 | tf_op jit(solution)/shard_map/dot_general | solution.py:30
  183.5 5.2 %add_convert_fusion = bf16[768,768]{1,0:T(8,128)(2,1)} fusion(f32[768,768]{1,0:T(8,128)} %fusion.15, bf16[1024,768]{1,0:T(8,128)(2,1)} %copy-done.7, bf16[512,768]{1,0:T(8,128)(2,1)} %get-tuple-element.81, bf16[512,768]{1,0:T(8,128)(2,1)} %get-tuple-element.78), kind=kOutput, calls=%fused_computation.2 | convolution fusion | flops 1212284928 | bytes 6684672 | tf_op jit(solution)/shard_map/dot_general | solution.py:30
  188.7 17.1 %all-to-all-done.1 = bf16[4,192,512]{2,1,0:T(8,128)(2,1)} async-done(((bf16[4,192,512]{2,1,0:T(8,128)(2,1)}), bf16[4,192,512]{2,1,0:T(8,128)(2,1)}, u32[]{:S(2)}, u32[]{:S(2)}) %all-to-all-start.1) | async-done | bytes 786464 | tf_op jit(solution)/shard_map/all_to_all | solution.py:383
  208.6 28.2 %attend_backward.1 = bf16[576,2048]{1,0:T(8,128)(2,1)} custom-call(s32[1,2048]{1,0:T(1,128)S(1)} %copy-done.6, s32[1,2048]{1,0:T(1,128)S(1)} %copy-done.6, bf16[3,128,2048]{2,1,0:T(8,128)(2,1)S(1)} %get-tuple-element.33.qt_ref, bf16[3,16,2048]{2,1,0:T(8,128)(2,1)S(1)} %get-tuple-element.41.extra_ref, bf16[3,2048,128]{2,1,0:T(8,128)(2,1)S(1)} %copy-done.1, ...), custom_call_target="tpu_custom_call" | custom-call | tf_op jit(solution)/shard_map/attend_backward/pallas_call | solution.py:244
  236.9 4.6 %fusion.25 = bf16[768,576]{0,1:T(8,128)(2,1)} fusion(bf16[576,2048]{1,0:T(8,128)(2,1)} %attend_backward.1, bf16[2048,768]{1,0:T(8,128)(2,1)S(1)} %copy-done.38), kind=kOutput, calls=%fused_computation.48 | convolution fusion | flops 1812381696 | bytes 6389760 | tf_op jit(solution)/shard_map/dot_general | solution.py:22
  254.1 3.0 add_convert_fusion.2
  261.6 15.7 %collective-permute-done.14 = bf16[512,768]{1,0:T(8,128)(2,1)S(1)} collective-permute-done((bf16[512,768]{1,0:T(8,128)(2,1)}, bf16[512,768]{1,0:T(8,128)(2,1)S(1)}, u32[]{:S(2)}, u32[]{:S(2)}) %collective-permute-start.14) | collective-permute-done | bytes 786464 | tf_op jit(solution)/shard_map/ppermute | solution.py:311
  286.9 57.8 %all-reduce.5 = (bf16[4,768]{1,0:T(4,128)(2,1)S(1)}, bf16[5,768]{1,0:T(8,128)(2,1)S(1)}) all-reduce(bf16[4,768]{1,0:T(4,128)(2,1)S(1)} %pad_maximum_fusion.3, bf16[5,768]{1,0:T(8,128)(2,1)S(1)} %stack.45), channel_id=1, replica_groups=mesh['dp'=8,'y'=2,'core'=2] {'dp'}, use_global_device_ids=true, to_apply=%region_18.19 | all-reduce | flops 6912 | bytes 27648 | tf_op jit(solution)/shard_map/psum | solution.py:431
  344.8 10.7 %psum.51 = f32[6,768]{1,0:T(8,128)S(1)} all-reduce(f32[6,768]{1,0:T(8,128)S(1)} %pad_maximum_fusion.2), channel_id=1, replica_groups=mesh['dp'=8,'y'=2,'core'=2] {'y','core'}, use_global_device_ids=true, to_apply=%region_19.20 | all-reduce | flops 4608 | bytes 36864 | tf_op jit(solution)/shard_map/psum | solution.py:434
  360.1 5.1 %reshape.185 = f32[1,2048,768]{2,1,0:T(8,128)} convert(bf16[1,2048,768]{2,1,0:T(8,128)(2,1)} %bitcast_dynamic-update-slice_fusion) | non-fusion elementwise | flops 1572864 | bytes 9437184 | tf_op jit(solution)/shard_map/reshape | solution.py:438
  365.2 55.5 %all-reduce.9.cloned.1.call-done = (bf16[768,576]{0,1:T(8,128)(2,1)}, bf16[192,768]{1,0:T(8,128)(2,1)}, bf16[768,768]{1,0:T(8,128)(2,1)}, bf16[768,768]{1,0:T(8,128)(2,1)}) async-done(((bf16[768,576]{0,1:T(8,128)(2,1)}, bf16[192,768]{1,0:T(8,128)(2,1)}, bf16[768,768]{1,0:T(8,128)(2,1)}, bf16[768,768]{1,0:T(8,128)(2,1)}), (bf16[768,576]{0,1:T(8,128)(2,1)}, bf16[192,768]{1,0:T(8,128)(2,1)}, ...) | async-done | bytes 3538960 | tf_op jit(solution)/shard_map/psum | solution.py:431
  420.6 2.9 convert_element_type.165
  (222 shorter events, 85.7 us)
Async XLA Ops:
  7.2 60.0 %all-gather.2.cloned.1.call-start = ((), (), s32[]{:S(2)}) async-start(), calls=%async_computation.2 | async-start | bytes 1474560 | tf_op jit(solution)/shard_map/all_gather | solution.py:343
  50.6 16.6 %all-to-all-start = ((bf16[192,4,512]{2,0,1:T(8,128)(2,1)}), bf16[192,4,512]{2,0,1:T(8,128)(2,1)}, u32[]{:S(2)}, u32[]{:S(2)}) async-start(bf16[192,4,512]{2,0,1:T(8,128)(2,1)} %bitcast.114), calls=%async_computation | async-start | bytes 1572864 | tf_op jit(solution)/shard_map/all_to_all | solution.py:353
  71.8 19.1 %collective-permute-start.2 = (bf16[512,768]{1,0:T(8,128)(2,1)}, bf16[512,768]{1,0:T(8,128)(2,1)}, u32[]{:S(2)}, u32[]{:S(2)}) collective-permute-start(bf16[512,768]{1,0:T(8,128)(2,1)} %add_convert_fusion.6), channel_id=1, source_target_pairs={{0,2},{2,0},{1,3},{3,1},{4,6},{6,4},{5,7},{7,5},{8,10},{10,8},{9,1... | collective-permute-start | bytes 2359304 | tf_op jit(solution)/shard_map/ppermute | solution.py:311
  90.9 3.5 collective-permute-start.3
  90.9 15.1 %collective-permute-start = (bf16[512,768]{1,0:T(8,128)(2,1)}, bf16[512,768]{1,0:T(8,128)(2,1)S(1)}, u32[]{:S(2)}, u32[]{:S(2)}) collective-permute-start(bf16[512,768]{1,0:T(8,128)(2,1)} %add_convert_fusion.6), channel_id=1, source_target_pairs={{0,1},{1,0},{2,3},{3,2},{4,5},{5,4},{6,7},{7,6},{8,9},{9,8},{10,11... | collective-permute-start | bytes 2359304 | tf_op jit(solution)/shard_map/ppermute | solution.py:307
  105.9 19.0 %collective-permute-start.10 = (bf16[512,768]{1,0:T(8,128)(2,1)S(1)}, bf16[512,768]{1,0:T(8,128)(2,1)}, u32[]{:S(2)}, u32[]{:S(2)}) collective-permute-start(bf16[512,768]{1,0:T(8,128)(2,1)S(1)} %slice.83), channel_id=1, source_target_pairs={{0,1},{1,0},{2,3},{3,2},{4,5},{5,4},{6,7},{7,6},{8,9},{9,8},{10,11... | collective-permute-start | bytes 2359304 | tf_op jit(solution)/shard_map/ppermute | solution.py:307
  119.7 12.1 %collective-permute-start.9 = (bf16[512,768]{1,0:T(8,128)(2,1)S(1)}, bf16[512,768]{1,0:T(8,128)(2,1)S(1)}, u32[]{:S(2)}, u32[]{:S(2)}) collective-permute-start(bf16[512,768]{1,0:T(8,128)(2,1)S(1)} %slice.81), channel_id=1, source_target_pairs={{0,1},{1,0},{2,3},{3,2},{4,5},{5,4},{6,7},{7,6},{8,9},{9,8},{10,11... | collective-permute-start | bytes 2359304 | tf_op jit(solution)/shard_map/ppermute | solution.py:307
  120.3 32.4 %collective-permute-start.1 = (bf16[512,768]{1,0:T(8,128)(2,1)S(1)}, bf16[512,768]{1,0:T(8,128)(2,1)S(1)}, u32[]{:S(2)}, u32[]{:S(2)}) collective-permute-start(bf16[512,768]{1,0:T(8,128)(2,1)S(1)} %slice.77), channel_id=1, source_target_pairs={{0,1},{1,0},{2,3},{3,2},{4,5},{5,4},{6,7},{7,6},{8,9},{9,8},{10,11... | collective-permute-start | bytes 2359304 | tf_op jit(solution)/shard_map/ppermute | solution.py:307
  124.2 5.7 %collective-permute-start.4 = (bf16[512,768]{1,0:T(8,128)(2,1)S(1)}, bf16[512,768]{1,0:T(8,128)(2,1)S(1)}, u32[]{:S(2)}, u32[]{:S(2)}) collective-permute-start(bf16[512,768]{1,0:T(8,128)(2,1)S(1)} %slice.79), channel_id=1, source_target_pairs={{0,1},{1,0},{2,3},{3,2},{4,5},{5,4},{6,7},{7,6},{8,9},{9,8},{10,11... | collective-permute-start | bytes 2359304 | tf_op jit(solution)/shard_map/ppermute | solution.py:307
  126.9 20.4 %collective-permute-start.11 = (bf16[512,768]{1,0:T(8,128)(2,1)S(1)}, bf16[512,768]{1,0:T(8,128)(2,1)S(1)}, u32[]{:S(2)}, u32[]{:S(2)}) collective-permute-start(bf16[512,768]{1,0:T(8,128)(2,1)S(1)} %add_convert_fusion.3), channel_id=1, source_target_pairs={{0,2},{2,0},{1,3},{3,1},{4,6},{6,4},{5,7},{7,5},{8,10},{10,8},{9,1... | collective-permute-start | bytes 2359304 | tf_op jit(solution)/shard_map/ppermute | solution.py:311
  130.1 34.1 %collective-permute-start.5 = (bf16[512,768]{1,0:T(8,128)(2,1)S(1)}, bf16[512,768]{1,0:T(8,128)(2,1)S(1)}, u32[]{:S(2)}, u32[]{:S(2)}) collective-permute-start(bf16[512,768]{1,0:T(8,128)(2,1)S(1)} %add_convert_fusion.5), channel_id=1, source_target_pairs={{0,2},{2,0},{1,3},{3,1},{4,6},{6,4},{5,7},{7,5},{8,10},{10,8},{9,1... | collective-permute-start | bytes 2359304 | tf_op jit(solution)/shard_map/ppermute | solution.py:311
  152.2 99.5 %collective-permute-start.18 = (bf16[512,768]{1,0:T(8,128)(2,1)}, bf16[512,768]{1,0:T(8,128)(2,1)}, u32[]{:S(2)}, u32[]{:S(2)}) collective-permute-start(bf16[512,768]{1,0:T(8,128)(2,1)} %get-tuple-element.70), channel_id=1, source_target_pairs={{0,1},{1,0},{2,3},{3,2},{4,5},{5,4},{6,7},{7,6},{8,9},{9,8},{10,11... | collective-permute-start | bytes 2359304 | tf_op jit(solution)/shard_map/ppermute | solution.py:307
  152.2 96.1 %collective-permute-start.19 = (bf16[512,768]{1,0:T(8,128)(2,1)}, bf16[512,768]{1,0:T(8,128)(2,1)}, u32[]{:S(2)}, u32[]{:S(2)}) collective-permute-start(bf16[512,768]{1,0:T(8,128)(2,1)} %get-tuple-element.70), channel_id=1, source_target_pairs={{0,2},{2,0},{1,3},{3,1},{4,6},{6,4},{5,7},{7,5},{8,10},{10,8},{9,1... | collective-permute-start | bytes 2359304 | tf_op jit(solution)/shard_map/ppermute | solution.py:311
  167.5 92.0 %collective-permute-start.6 = (bf16[512,768]{1,0:T(8,128)(2,1)}, bf16[512,768]{1,0:T(8,128)(2,1)}, u32[]{:S(2)}, u32[]{:S(2)}) collective-permute-start(bf16[512,768]{1,0:T(8,128)(2,1)} %get-tuple-element.77), channel_id=1, source_target_pairs={{0,1},{1,0},{2,3},{3,2},{4,5},{5,4},{6,7},{7,6},{8,9},{9,8},{10,11... | collective-permute-start | bytes 2359304 | tf_op jit(solution)/shard_map/ppermute | solution.py:307
  167.5 91.7 %collective-permute-start.7 = (bf16[512,768]{1,0:T(8,128)(2,1)}, bf16[512,768]{1,0:T(8,128)(2,1)}, u32[]{:S(2)}, u32[]{:S(2)}) collective-permute-start(bf16[512,768]{1,0:T(8,128)(2,1)} %get-tuple-element.77), channel_id=1, source_target_pairs={{0,2},{2,0},{1,3},{3,1},{4,6},{6,4},{5,7},{7,5},{8,10},{10,8},{9,1... | collective-permute-start | bytes 2359304 | tf_op jit(solution)/shard_map/ppermute | solution.py:311
  173.0 32.9 %all-to-all-start.1 = ((bf16[4,192,512]{2,1,0:T(8,128)(2,1)}), bf16[4,192,512]{2,1,0:T(8,128)(2,1)}, u32[]{:S(2)}, u32[]{:S(2)}) async-start(bf16[4,192,512]{2,1,0:T(8,128)(2,1)} %bitcast.113), calls=%async_computation.1 | async-start | bytes 1572864 | tf_op jit(solution)/shard_map/all_to_all | solution.py:383
  177.2 243.4 %all-reduce.9.cloned.1.call-start = ((), (), s32[]{:S(2)}) async-start(), calls=%async_computation.3 | async-start | bytes 7077888 | tf_op jit(solution)/shard_map/psum | solution.py:431
  244.2 9.9 %collective-permute-start.13 = (bf16[512,768]{1,0:T(8,128)(2,1)}, bf16[512,768]{1,0:T(8,128)(2,1)}, u32[]{:S(2)}, u32[]{:S(2)}) collective-permute-start(bf16[512,768]{1,0:T(8,128)(2,1)} %convolution_convert_fusion.2), channel_id=1, source_target_pairs={{0,1},{1,0},{2,3},{3,2},{4,5},{5,4},{6,7},{7,6},{8,9},{9,8},{10,11... | collective-permute-start | bytes 2359304 | tf_op jit(solution)/shard_map/ppermute | solution.py:307
  248.3 9.2 %collective-permute-start.20 = (bf16[512,768]{1,0:T(8,128)(2,1)}, bf16[512,768]{1,0:T(8,128)(2,1)S(1)}, u32[]{:S(2)}, u32[]{:S(2)}) collective-permute-start(bf16[512,768]{1,0:T(8,128)(2,1)} %collective-permute-done.19), channel_id=1, source_target_pairs={{0,1},{1,0},{2,3},{3,2},{4,5},{5,4},{6,7},{7,6},{8,9},{9,8},{10,11... | collective-permute-start | bytes 2359304 | tf_op jit(solution)/shard_map/ppermute | solution.py:307
  251.7 9.9 %collective-permute-start.12 = (bf16[512,768]{1,0:T(8,128)(2,1)}, bf16[512,768]{1,0:T(8,128)(2,1)}, u32[]{:S(2)}, u32[]{:S(2)}) collective-permute-start(bf16[512,768]{1,0:T(8,128)(2,1)} %convolution_convert_fusion.3), channel_id=1, source_target_pairs={{0,1},{1,0},{2,3},{3,2},{4,5},{5,4},{6,7},{7,6},{8,9},{9,8},{10,11... | collective-permute-start | bytes 2359304 | tf_op jit(solution)/shard_map/ppermute | solution.py:307
  257.1 20.1 %collective-permute-start.14 = (bf16[512,768]{1,0:T(8,128)(2,1)}, bf16[512,768]{1,0:T(8,128)(2,1)S(1)}, u32[]{:S(2)}, u32[]{:S(2)}) collective-permute-start(bf16[512,768]{1,0:T(8,128)(2,1)} %add_convert_fusion.2), channel_id=1, source_target_pairs={{0,2},{2,0},{1,3},{3,1},{4,6},{6,4},{5,7},{7,5},{8,10},{10,8},{9,1... | collective-permute-start | bytes 2359304 | tf_op jit(solution)/shard_map/ppermute | solution.py:311
  259.2 26.7 %collective-permute-start.8 = (bf16[512,768]{1,0:T(8,128)(2,1)}, bf16[512,768]{1,0:T(8,128)(2,1)S(1)}, u32[]{:S(2)}, u32[]{:S(2)}) collective-permute-start(bf16[512,768]{1,0:T(8,128)(2,1)} %collective-permute-done.7), channel_id=1, source_target_pairs={{0,1},{1,0},{2,3},{3,2},{4,5},{5,4},{6,7},{7,6},{8,9},{9,8},{10,11... | collective-permute-start | bytes 2359304 | tf_op jit(solution)/shard_map/ppermute | solution.py:307
  282.8 73.3 %collective-permute-start.16 = (bf16[512,768]{1,0:T(8,128)(2,1)S(1)}, bf16[512,768]{1,0:T(8,128)(2,1)S(1)}, u32[]{:S(2)}, u32[]{:S(2)}) collective-permute-start(bf16[512,768]{1,0:T(8,128)(2,1)S(1)} %get-tuple-element.74), channel_id=1, source_target_pairs={{0,2},{2,0},{1,3},{3,1},{4,6},{6,4},{5,7},{7,5},{8,10},{10,8},{9,1... | collective-permute-start | bytes 2359304 | tf_op jit(solution)/shard_map/ppermute | solution.py:311
  285.9 71.4 %collective-permute-start.15 = (bf16[512,768]{1,0:T(8,128)(2,1)S(1)}, bf16[512,768]{1,0:T(8,128)(2,1)S(1)}, u32[]{:S(2)}, u32[]{:S(2)}) collective-permute-start(bf16[512,768]{1,0:T(8,128)(2,1)S(1)} %get-tuple-element.74), channel_id=1, source_target_pairs={{0,1},{1,0},{2,3},{3,2},{4,5},{5,4},{6,7},{7,6},{8,9},{9,8},{10,11... | collective-permute-start | bytes 2359304 | tf_op jit(solution)/shard_map/ppermute | solution.py:307
  (42 other events, 217.2 us)
Sparse Core Ops, SparseCore 0:
  9.6 20.1 all-gather.1
  259.3 161.3 all-reduce.8

commit v2 on v1

v2 whole, which is shorter than its diff:
```python
import jax
import jax.numpy as jnp
from jax import lax
from jax.experimental import pallas as pl
from jax.experimental.pallas import tpu as pltpu
from jax.sharding import Mesh
from jax.sharding import PartitionSpec as P

HEAD = 64
WIDE = 128
TILE = 256
PARTS = 2
MASKED = 1e30
F32 = jnp.float32
BF16 = jnp.bfloat16
DP = ("z", "x")
MP = ("y", "core")
SWAP = [(0, 1), (1, 0)]


def nn(left, right):
    return lax.dot_general(left, right, (((1,), (0,)), ((), ())), preferred_element_type=F32)


def nt(left, right):
    return lax.dot_general(left, right, (((1,), (1,)), ((), ())), preferred_element_type=F32)


def tn(left, right):
    return lax.dot_general(left, right, (((0,), (0,)), ((), ())), preferred_element_type=F32)


def stats(values):
    center = values - jnp.mean(values, axis=-1, keepdims=True)
    scale = lax.rsqrt(jnp.mean(center * center, axis=-1, keepdims=True) + 1e-05)
    return center * scale, scale


def norm_back(grad_out, normed, scale, gain):
    upstream = grad_out * gain
    return scale * (
        upstream
        - jnp.mean(upstream, axis=-1, keepdims=True)
        - normed * jnp.mean(upstream * normed, axis=-1, keepdims=True)
    )


def fold(values):
    return jnp.sum(values.reshape(-1, 8, values.shape[-1]), axis=0)


def split(value, parts):
    out = []
    for _ in range(parts):
        piece = value.astype(BF16).astype(F32)
        out.append(piece)
        value = value - piece
    return out


def const(shape):
    return pl.BlockSpec(shape, lambda *_: (0,) * len(shape))


def shape_of(*dims, dtype=BF16):
    return jax.ShapeDtypeStruct(dims, dtype)


def params():
    return pltpu.CompilerParams(vmem_limit_bytes=48 << 20)


def cost(flops, moved, special=0):
    return pl.CostEstimate(flops=int(flops), bytes_accessed=int(moved), transcendentals=int(special))


def project_body(x_ref, seg_ref, gain_ref, bias_ref, wt_ref, wn_ref, qb_ref, vb_ref, vbn_ref,
                 ai_ref, qt_ref, kt_ref, vt_ref, kn_ref, vn_ref):
    heads = kn_ref.shape[0]
    width = heads * HEAD
    normed, _ = stats(x_ref[...].astype(F32))
    ai = (normed * gain_ref[...] + bias_ref[...]).astype(BF16)
    ai_ref[...] = ai
    low = nt(wt_ref[...], ai)
    queries = ((low[:width] + qb_ref[...]).astype(BF16)).astype(F32) * HEAD ** -0.5
    kt_ref[...] = low[width:2 * width].astype(BF16)
    values = (low[2 * width:] + vb_ref[...]).astype(BF16)
    tile = x_ref.shape[0]
    row = lax.broadcasted_iota(jnp.int32, (WIDE, tile), 0) - HEAD
    same = jnp.where(row == seg_ref[...], 1.0, 0.0)
    same = jnp.where(row >= 0, same, 0.0)
    first = jnp.where(lax.broadcasted_iota(jnp.int32, (16, tile), 0) == 0, 1.0, 0.0).astype(BF16)
    for h in range(heads):
        rows = slice(h * HEAD, (h + 1) * HEAD)
        qt_ref[h, :HEAD, :] = queries[rows].astype(BF16)
        qt_ref[h, HEAD:, :] = same[HEAD:].astype(BF16)
        vt_ref[h, :HEAD, :] = values[rows]
        vt_ref[h, HEAD:, :] = first
    lane = lax.broadcasted_iota(jnp.int32, (tile, WIDE), 1)
    mask = jnp.where((lane >= HEAD) & (lane < HEAD + 8), (same.T - 1.0) * MASKED, 0.0)
    mask = jnp.where((lane >= HEAD + 8) & (lane < HEAD + 11), 1.0, mask)
    ones = jnp.where((lane >= HEAD) & (lane < HEAD + 2), 1.0, 0.0)
    natural = nn(ai, wn_ref[...])
    for h in range(heads):
        kn_ref[h] = (natural[:, h * WIDE:(h + 1) * WIDE] + mask).astype(BF16)
        at = (heads + h) * WIDE
        vn_ref[h] = (natural[:, at:at + WIDE] + vbn_ref[:, h * WIDE:(h + 1) * WIDE] + ones).astype(BF16)


def project(tokens, seg_row, gain, bias, wt, wn, qb, vb, vbn, heads):
    length, features = tokens.shape
    width = heads * HEAD
    return pl.pallas_call(
        project_body,
        grid=(length // TILE,),
        in_specs=[
            pl.BlockSpec((TILE, features), lambda i: (i, 0)),
            pl.BlockSpec((1, TILE), lambda i: (0, i)),
            const((1, features)), const((1, features)),
            const(wt.shape), const(wn.shape), const(qb.shape), const(vb.shape), const(vbn.shape),
        ],
        out_specs=[
            pl.BlockSpec((TILE, features), lambda i: (i, 0)),
            pl.BlockSpec((heads, WIDE, TILE), lambda i: (0, 0, i)),
            pl.BlockSpec((width, TILE), lambda i: (0, i)),
            pl.BlockSpec((heads, HEAD + 16, TILE), lambda i: (0, 0, i)),
            pl.BlockSpec((heads, TILE, WIDE), lambda i: (0, i, 0)),
            pl.BlockSpec((heads, TILE, WIDE), lambda i: (0, i, 0)),
        ],
        out_shape=[
            shape_of(length, features),
            shape_of(heads, WIDE, length),
            shape_of(width, length),
            shape_of(heads, HEAD + 16, length),
            shape_of(heads, length, WIDE),
            shape_of(heads, length, WIDE),
        ],
        compiler_params=params(),
        cost_estimate=cost(6e9, 14e6),
        name="project",
    )(tokens, seg_row, gain, bias, wt, wn, qb, vb, vbn)


def key_range(seg_ref, seg_all, i):
    first = seg_ref[0, i * TILE]
    last = seg_ref[0, i * TILE + TILE - 1]
    before = jnp.sum(jnp.where(seg_all < first, 1.0, 0.0)).astype(jnp.int32)
    until = jnp.sum(jnp.where(seg_all <= last, 1.0, 0.0)).astype(jnp.int32)
    return before // TILE, (until + TILE - 1) // TILE


def shifted(one_hot, pieces):
    row = lax.broadcasted_iota(jnp.int32, one_hot.shape, 0)
    value = one_hot
    for n, piece in enumerate(pieces):
        value = jnp.where(row == 8 + n, piece, value)
    return value.astype(BF16)


def forward_body(offset, segs_ref, seg_ref, qt_ref, kn_ref, vt_ref, out_ref, extra_ref, qa_ref, acc_ref):
    heads, _, tile = qt_ref.shape
    low, high = key_range(segs_ref, seg_ref[...], pl.program_id(0) + offset)
    acc_ref[...] = jnp.zeros_like(acc_ref)
    qa_ref[...] = qt_ref[...]

    def look(kb, tops):
        keys = pl.ds(pl.multiple_of(kb * TILE, TILE), TILE)
        return tuple(
            jnp.maximum(tops[h], jnp.max(nn(kn_ref[h, keys, :], qa_ref[h]).reshape(-1, 8, tile), axis=0))
            for h in range(heads)
        )

    tops = lax.fori_loop(low, high, look, (jnp.full((8, tile), -jnp.inf, F32),) * heads)
    tops = [jnp.max(top, axis=0, keepdims=True) for top in tops]
    one_hots = [qt_ref[h, HEAD:HEAD + 16, :].astype(F32) for h in range(heads)]
    for h in range(heads):
        qa_ref[h, HEAD:HEAD + 16, :] = shifted(one_hots[h], split(-tops[h], 3))

    def step(kb, carry):
        keys = pl.ds(pl.multiple_of(kb * TILE, TILE), TILE)
        for h in range(heads):
            powered = jnp.exp(nn(kn_ref[h, keys, :], qa_ref[h])).astype(BF16)
            acc_ref[h] += nn(vt_ref[h, :, keys], powered)
        return carry

    lax.fori_loop(low, high, step, 0)
    for h in range(heads):
        total = acc_ref[h, HEAD:HEAD + 1, :]
        out_ref[0, h * HEAD:(h + 1) * HEAD, :] = (acc_ref[h, :HEAD, :] / total).astype(BF16)
        extra_ref[h] = shifted(one_hots[h], split(-(tops[h] + jnp.log(total)), 3))


def attend_forward(part, seg_row, qt, kn, vt):
    heads, _, length = qt.shape
    width = heads * HEAD
    count = length // TILE // PARTS
    offset = part * count

    def body(*refs):
        forward_body(offset, *refs)

    return pl.pallas_call(
        body,
        grid=(count,),
        in_specs=[
            pl.BlockSpec(memory_space=pltpu.SMEM),
            const((1, length)),
            pl.BlockSpec((heads, WIDE, TILE), lambda i: (0, 0, i + offset)),
            const(kn.shape), const(vt.shape),
        ],
        out_specs=[
            pl.BlockSpec((1, width, TILE), lambda i: (i, 0, 0)),
            pl.BlockSpec((heads, 16, TILE), lambda i: (0, 0, i)),
        ],
        out_shape=[
            shape_of(count, width, TILE),
            shape_of(heads, 16, count * TILE),
        ],
        scratch_shapes=[
            pltpu.VMEM((heads, WIDE, TILE), BF16),
            pltpu.VMEM((heads, HEAD + 16, TILE), F32),
        ],
        compiler_params=params(),
        cost_estimate=cost(9e9, 5e6, 4e6),
        name="attend_forward",
    )(seg_row, seg_row, qt, kn, vt)


def backward_body(part, me_ref, segs_ref, seg_ref, qt_ref, extra_ref, kn_ref, kt_ref, vn_ref, out_ref,
                  g0_ref, g1_ref, g2_ref, g3_ref, *rest):
    heads, _, tile = qt_ref.shape
    width = heads * HEAD
    length = kt_ref.shape[1]
    if part == 0:
        dq_out, dk_ref, dv_ref, qa_ref, da_ref, dq_ref = rest
    else:
        dq_in, dk_in, dv_in, grads_ref, qa_ref, da_ref, dq_ref, dk_ref, dv_ref = rest
    i = pl.program_id(0)
    count = length // TILE // PARTS
    at_here = i + part * count
    low, high = key_range(segs_ref, seg_ref[...], at_here)

    @pl.when(i == 0)
    def _():
        if part == 0:
            dk_ref[...] = jnp.zeros_like(dk_ref)
            dv_ref[...] = jnp.zeros_like(dv_ref)
        else:
            dk_ref[...] = dk_in[...]
            dv_ref[...] = dv_in[...]
            grads_ref[:width, :count * TILE] = dq_in[...]
        qa_ref[...] = jnp.zeros_like(qa_ref)
        da_ref[...] = jnp.zeros_like(da_ref)

    source = i ^ me_ref[0]
    for n, g_ref in enumerate((g0_ref, g1_ref, g2_ref, g3_ref)):
        @pl.when(source == n)
        def _(g_ref=g_ref):
            for h in range(heads):
                da_ref[h, :HEAD, :] = g_ref[h * HEAD:(h + 1) * HEAD]

    dq_ref[...] = jnp.zeros_like(dq_ref)
    row = lax.broadcasted_iota(jnp.int32, (16, tile), 0)
    for h in range(heads):
        rows = slice(h * HEAD, (h + 1) * HEAD)
        qa_ref[h, :HEAD, :] = qt_ref[h, :HEAD, :]
        qa_ref[h, HEAD:HEAD + 16, :] = extra_ref[h]
        inner = jnp.sum(da_ref[h, :HEAD, :].astype(F32) * out_ref[0, rows].astype(F32), axis=0, keepdims=True)
        first, second = split(-inner, 2)
        value = jnp.where(row == 0, first, jnp.where(row == 1, second, 0.0))
        da_ref[h, HEAD:HEAD + 16, :] = value.astype(BF16)

    def step(kb, carry):
        keys = pl.ds(pl.multiple_of(kb * TILE, TILE), TILE)
        for h in range(heads):
            rows = slice(h * HEAD, (h + 1) * HEAD)
            probs = jnp.exp(nn(kn_ref[h, keys, :], qa_ref[h]))
            ds = (probs * nn(vn_ref[h, keys, :], da_ref[h])).astype(BF16)
            dv_ref[rows, keys] += nt(da_ref[h, :HEAD, :], probs.astype(BF16))
            dk_ref[rows, keys] += nt(qa_ref[h, :HEAD, :], ds)
            dq_ref[rows] += nn(kt_ref[rows, keys], ds)
        return carry

    lax.fori_loop(low, high, step, 0)
    dq = (dq_ref[...] * HEAD ** -0.5).astype(BF16)
    if part == 0:
        dq_out[...] = dq
    else:
        grads_ref[:width, pl.ds(pl.multiple_of(at_here * TILE, TILE), TILE)] = dq

        @pl.when(i == pl.num_programs(0) - 1)
        def _():
            grads_ref[width:2 * width] = dk_ref[...].astype(BF16)
            grads_ref[2 * width:] = dv_ref[...].astype(BF16)


def attend_backward(part, me, seg_row, qt, extra, kn, kt, vn, out, grad, earlier):
    heads, _, length = qt.shape
    width = heads * HEAD
    count = length // TILE // PARTS
    offset = part * count

    def body(*refs):
        backward_body(part, *refs)

    in_specs = [
        pl.BlockSpec(memory_space=pltpu.SMEM),
        const((1, length)),
        pl.BlockSpec((heads, WIDE, TILE), lambda i, m: (0, 0, i + offset)),
        pl.BlockSpec((heads, 16, TILE), lambda i, m: (0, 0, i)),
        const(kn.shape), const(kt.shape), const(vn.shape),
        pl.BlockSpec((1, width, TILE), lambda i, m: (i, 0, 0)),
        const(grad[0].shape), const(grad[1].shape), const(grad[2].shape), const(grad[3].shape),
    ]
    scratch = [
        pltpu.VMEM((heads, WIDE, TILE), BF16),
        pltpu.VMEM((heads, WIDE, TILE), BF16),
        pltpu.VMEM((width, TILE), F32),
    ]
    if part == 0:
        out_specs = [pl.BlockSpec((width, TILE), lambda i, m: (0, i)), const((width, length)), const((width, length))]
        out_shape = [shape_of(width, count * TILE), shape_of(width, length, dtype=F32), shape_of(width, length, dtype=F32)]
    else:
        in_specs += [const(v.shape) for v in earlier]
        out_specs = const((3 * width, length))
        out_shape = shape_of(3 * width, length)
        scratch += [pltpu.VMEM((width, length), F32), pltpu.VMEM((width, length), F32)]
    return pl.pallas_call(
        body,
        grid_spec=pltpu.PrefetchScalarGridSpec(
            num_scalar_prefetch=1, grid=(count,), in_specs=in_specs, out_specs=out_specs, scratch_shapes=scratch,
        ),
        out_shape=out_shape,
        compiler_params=params(),
        cost_estimate=cost(16e9, 10e6, 4e6),
        name="attend_backward",
    )(me, seg_row, seg_row, qt, extra, kn, kt, vn, out, *grad, *earlier)


def middle_body(me_ref, x_ref, m0_ref, m1_ref, m2_ref, m3_ref, w0_ref, w1_ref, w2_ref, w3_ref,
                ob_ref, gain_ref, bias_ref, residual_ref, own_ref):
    total = x_ref[...].astype(F32) + ob_ref[...]
    for m_ref, w_ref in ((m0_ref, w0_ref), (m1_ref, w1_ref), (m2_ref, w2_ref), (m3_ref, w3_ref)):
        total = total + tn(m_ref[...], w_ref[...])
    residual_ref[...] = total
    normed, _ = stats(total)
    own_ref[...] = (normed * gain_ref[...] + bias_ref[...]).astype(BF16)


def middle(part, me, tokens, mixed, weights, output_bias, gain, bias):
    features = tokens.shape[1]
    vector = const((1, features))
    return pl.pallas_call(
        middle_body,
        grid_spec=pltpu.PrefetchScalarGridSpec(
            num_scalar_prefetch=1,
            grid=(1,),
            in_specs=[pl.BlockSpec((TILE, features), lambda i, m: (4 * part + m[0], 0))]
            + [const(v.shape) for v in mixed] + [const(v.shape) for v in weights] + [vector] * 3,
            out_specs=[const((TILE, features)), const((TILE, features))],
        ),
        out_shape=[shape_of(TILE, features, dtype=F32), shape_of(TILE, features)],
        compiler_params=params(),
        cost_estimate=cost(2e9, 3e6),
        name="middle",
    )(me, tokens, *mixed, *weights, output_bias, gain, bias)


def feed_body(me_ref, x0_ref, x1_ref, g_ref, inner_ref, bias_ref, outer_ref, *rest):
    act_ref, dh_ref, xs_ref, gs_ref, out0_ref, out1_ref, back0_ref, back1_ref, sum_ref = rest[-9:]
    i = pl.program_id(0)

    @pl.when(i == 0)
    def _():
        xs_ref[...] = x0_ref[...]

    @pl.when(i == 1)
    def _():
        xs_ref[...] = x1_ref[...]

    gs_ref[...] = g_ref[...]
    hidden = nn(xs_ref[...], inner_ref[...]) + bias_ref[...]
    half = 0.5 + 0.5 * lax.erf(hidden * 0.5 ** 0.5)
    act = (hidden * half).astype(BF16)
    act_ref[...] = act
    slope = half + hidden * (jnp.exp(-0.5 * hidden * hidden) * 0.3989422804014327)
    dh = (nt(g_ref[...], outer_ref[...]) * slope).astype(BF16)
    dh_ref[...] = dh
    sums = fold(dh.astype(F32))
    out = nn(act, outer_ref[...]).astype(BF16)
    back = nt(dh, inner_ref[...]).astype(BF16)

    @pl.when(i == 0)
    def _():
        sum_ref[...] = sums
        out0_ref[...] = out
        back0_ref[...] = back

    @pl.when(i == 1)
    def _():
        sum_ref[...] += sums
        out1_ref[...] = out
        back1_ref[...] = back


def feed(part, base, me, first, second, cot, inner, bias, outer, kept):
    length, features = cot.shape
    units = inner.shape[1]
    at = 4 * part + base
    rows = lambda n: pl.BlockSpec((TILE, n), lambda i, m: (at + i, 0))
    piece = const((TILE, features))
    return pl.pallas_call(
        feed_body,
        grid_spec=pltpu.PrefetchScalarGridSpec(
            num_scalar_prefetch=1,
            grid=(2,),
            in_specs=[
                piece, piece,
                pl.BlockSpec((TILE, features), lambda i, m: (4 * part + (m[0] ^ (base + i)), 0)),
                const(inner.shape), const(bias.shape), const(outer.shape),
            ] + [pl.BlockSpec(memory_space=pl.ANY)] * len(kept),
            out_specs=[rows(units), rows(units), rows(features), rows(features)] + [piece] * 4 + [const((8, units))],
        ),
        out_shape=[shape_of(length, units), shape_of(length, units), shape_of(length, features),
                   shape_of(length, features)] + [shape_of(TILE, features)] * 4 + [shape_of(8, units, dtype=F32)],
        input_output_aliases={7 + n: n for n in range(len(kept))},
        compiler_params=params(),
        cost_estimate=cost(5e9, 8e6, 1e6),
        name="feed",
    )(me, first, second, cot, inner, bias, outer, *kept)


def back_body(me_ref, b0_ref, b1_ref, b2_ref, residual_ref, g_ref, gain_ref, w0_ref, w1_ref, w2_ref, w3_ref,
              grad_ref, low_ref, a0_ref, a1_ref, a2_ref, a3_ref, sum_ref):
    grad_mid = b0_ref[...].astype(F32) + b1_ref[...].astype(F32) + b2_ref[...].astype(F32)
    normed, scale = stats(residual_ref[...])
    upstream = g_ref[...].astype(F32)
    grad = upstream + norm_back(grad_mid, normed, scale, gain_ref[...])
    grad_ref[...] = grad
    low = grad.astype(BF16)
    low_ref[...] = low
    for w_ref, a_ref in ((w0_ref, a0_ref), (w1_ref, a1_ref), (w2_ref, a2_ref), (w3_ref, a3_ref)):
        a_ref[...] = nt(w_ref[...], low).astype(BF16)
    for n, value in enumerate((grad_mid * normed, grad_mid, grad, upstream)):
        sum_ref[8 * n:8 * n + 8] = fold(value)


def middle_back(part, me, sums, residual, cot, gain, weights):
    features = cot.shape[1]
    piece = const((TILE, features))
    width = weights[0].shape[0]
    return pl.pallas_call(
        back_body,
        grid_spec=pltpu.PrefetchScalarGridSpec(
            num_scalar_prefetch=1,
            grid=(1,),
            in_specs=[piece] * 4
            + [pl.BlockSpec((TILE, features), lambda i, m: (4 * part + m[0], 0)), const((1, features))]
            + [const(v.shape) for v in weights],
            out_specs=[piece, piece] + [const((width, TILE))] * 4 + [const((32, features))],
        ),
        out_shape=[shape_of(TILE, features, dtype=F32), shape_of(TILE, features)]
        + [shape_of(width, TILE)] * 4 + [shape_of(32, features, dtype=F32)],
        compiler_params=params(),
        cost_estimate=cost(2e9, 4e6),
        name="middle_back",
    )(me, *sums, residual, cot, gain, *weights)


def output_body(*refs):
    mixed, lows, outs = refs[:4 * PARTS], refs[4 * PARTS:5 * PARTS], refs[5 * PARTS:]
    for n in range(4):
        total = nn(mixed[n][...], lows[0][...])
        for p in range(1, PARTS):
            total = total + nn(mixed[4 * p + n][...], lows[p][...])
        outs[n][...] = total.astype(BF16)


def output_grad(mixed, lows):
    width, features = mixed[0].shape[0], lows[0].shape[1]
    return pl.pallas_call(
        output_body,
        out_shape=[shape_of(width, features)] * 4,
        compiler_params=params(),
        cost_estimate=cost(2e9, 4e6),
        name="output_grad",
    )(*mixed, *lows)


def tail_body(me_ref, g_ref, wt_ref, o0_ref, o1_ref, o2_ref, o3_ref, sum_ref):
    i = pl.program_id(0)
    grads = g_ref[...]
    value = tn(grads, wt_ref[...]).astype(BF16)
    sums = nt(jnp.ones((8, grads.shape[1]), BF16), grads)
    for step, o_ref in enumerate((o3_ref, o2_ref, o1_ref, o0_ref)):
        @pl.when(i == step)
        def _(o_ref=o_ref, step=step):
            o_ref[...] = value
            sum_ref[...] = sums if step == 0 else sum_ref[...] + sums


def tail(part, me, grads, wt):
    deep = grads.shape[0]
    features = wt.shape[1]
    piece = const((TILE, features))
    return pl.pallas_call(
        tail_body,
        grid_spec=pltpu.PrefetchScalarGridSpec(
            num_scalar_prefetch=1,
            grid=(4,),
            in_specs=[pl.BlockSpec((deep, TILE), lambda i, m: (0, 4 * part + (m[0] ^ (3 - i)))), const(wt.shape)],
            out_specs=[piece] * 4 + [const((8, deep))],
        ),
        out_shape=[shape_of(TILE, features)] * 4 + [shape_of(8, deep, dtype=F32)],
        compiler_params=params(),
        cost_estimate=cost(2e9, 4e6),
        name="tail",
    )(me, grads, wt)


def final_body(me_ref, b0_ref, b1_ref, b2_ref, x_ref, grad_ref, gain_ref, out_ref, sum_ref):
    grad_attend = b0_ref[...].astype(F32) + b1_ref[...].astype(F32) + b2_ref[...].astype(F32)
    normed, scale = stats(x_ref[...].astype(F32))
    out_ref[...] = (grad_ref[...] + norm_back(grad_attend, normed, scale, gain_ref[...])).astype(BF16)
    sum_ref[:8] = fold(grad_attend * normed)
    sum_ref[8:] = fold(grad_attend)


def final(part, me, sums, tokens, grad, gain):
    features = tokens.shape[1]
    piece = const((TILE, features))
    return pl.pallas_call(
        final_body,
        grid_spec=pltpu.PrefetchScalarGridSpec(
            num_scalar_prefetch=1,
            grid=(1,),
            in_specs=[piece] * 3
            + [pl.BlockSpec((TILE, features), lambda i, m: (4 * part + m[0], 0)), piece, const((1, features))],
            out_specs=[piece, const((16, features))],
        ),
        out_shape=[shape_of(TILE, features), shape_of(16, features, dtype=F32)],
        compiler_params=params(),
        cost_estimate=cost(1e8, 3e6),
        name="final",
    )(me, *sums, tokens, grad, gain)


def place_body(me_ref, p0_ref, p1_ref, p2_ref, p3_ref, *rest):
    out_ref = rest[-1]
    for step, p_ref in enumerate((p0_ref, p1_ref, p2_ref, p3_ref)):
        @pl.when(pl.program_id(0) == step)
        def _(p_ref=p_ref):
            out_ref[...] = p_ref[...].astype(out_ref.dtype)


def place(part, me, pieces, length, dtype, kept):
    features = pieces[0].shape[1]
    return pl.pallas_call(
        place_body,
        grid_spec=pltpu.PrefetchScalarGridSpec(
            num_scalar_prefetch=1,
            grid=(4,),
            in_specs=[const((TILE, features))] * 4 + [pl.BlockSpec(memory_space=pl.ANY)] * len(kept),
            out_specs=pl.BlockSpec((TILE, features), lambda i, m: (4 * part + (m[0] ^ i), 0)),
        ),
        out_shape=shape_of(length, features, dtype=dtype),
        input_output_aliases={5 + n: n for n in range(len(kept))},
        compiler_params=params(),
        cost_estimate=cost(1e6, 5e6),
        name="place",
    )(me, *pieces, *kept)


def other_core(value):
    return lax.ppermute(value, "core", SWAP)


def other_chip(value):
    return lax.ppermute(value, "y", SWAP)


def crosswise(value):
    return lax.ppermute(value, MP, [(n, n ^ 3) for n in range(4)])


def exchange(pieces):
    return [pieces[0], other_core(pieces[1]), other_chip(pieces[2]), crosswise(pieces[3])]


def gather_sum(pieces):
    near = other_core(pieces[1])
    far = (pieces[2].astype(F32) + other_core(pieces[3]).astype(F32)).astype(BF16)
    return [pieces[0], near, other_chip(far)]


def spread(value):
    far = other_chip(value)
    return [value, other_core(value), far, other_core(far)]


def pick(values, at):
    return lax.dynamic_index_in_dim(values, at, 0, keepdims=False)


def turned(values, way):
    size = lax.axis_size("z")
    return lax.ppermute(values, "z", [(n, (n + way) % size) for n in range(size)])


def sum_rows(value):
    size = lax.axis_size("z")
    if size > 4:
        return lax.psum(value, DP)
    rows, features = value.shape
    x, z = lax.axis_index("x"), lax.axis_index("z")
    halves = value.reshape(2, rows // 2, features)
    got = lax.ppermute(pick(halves, 1 - x), "x", SWAP)
    half = (pick(halves, x).astype(F32) + got.astype(F32)).astype(BF16)
    parts = half.reshape(size, -1, features)
    total = pick(parts, z).astype(F32)
    for way in range(1, size):
        total = total + turned(pick(parts, (z + way) % size), way).astype(F32)
    total = total.astype(BF16)
    whole = jnp.zeros_like(parts)
    for way in range(size):
        part = turned(total, way) if way else total
        whole = lax.dynamic_update_index_in_dim(whole, part, (z - way) % size, 0)
    half = whole.reshape(rows // 2, features)
    other = lax.ppermute(half, "x", SWAP)
    return jnp.where(x == 0, jnp.concatenate([half, other]), jnp.concatenate([other, half]))


def sum_small(value):
    size = lax.axis_size("z")
    if size > 4:
        return lax.psum(value, DP)
    value = value + lax.ppermute(value, "x", SWAP)
    total = value
    for way in range(1, size):
        total = total + turned(value, way)
    return total


def local(
    tokens,
    segment_ids,
    gain_one,
    bias_one,
    query_weight,
    query_bias,
    key_weight,
    value_weight,
    value_bias,
    output_weight,
    output_bias,
    gain_two,
    bias_two,
    inner_weight,
    inner_bias,
    outer_weight,
    outer_bias,
    cotangent,
):
    _, length, features = tokens.shape
    width = query_weight.shape[1]
    heads = width // HEAD
    tokens = tokens.reshape(length, features)
    cot = cotangent.reshape(length, features)
    at = lax.axis_index(MP).astype(jnp.int32)
    me = at[None]
    gain_one, bias_one, gain_two, bias_two = gain_one[None], bias_one[None], gain_two[None], bias_two[None]

    output_weights = exchange([output_weight] * 4)
    pad = lambda w: jnp.pad(w.reshape(-1, heads, HEAD), ((0, 0), (0, 0), (0, WIDE - HEAD))).reshape(-1, heads * WIDE)
    wt = jnp.concatenate([query_weight, key_weight, value_weight], axis=1).T
    wn = jnp.concatenate([pad(key_weight), pad(value_weight)], axis=1)
    attend_in, qt, kt, vt, kn, vn = project(
        tokens, segment_ids, gain_one, bias_one, wt, wn,
        query_bias[:, None], value_bias[:, None], pad(value_bias[None]), heads,
    )

    parts = range(PARTS)
    attended, extras, mixed, residuals, pieces = [], [], [], [], []
    for p in parts:
        out, extra = attend_forward(p, segment_ids, qt, kn, vt)
        attended.append(out)
        extras.append(extra)
        mixed.append(exchange([pick(out, at ^ n) for n in range(4)]))
        residual, own = middle(p, me, tokens, mixed[p], output_weights, output_bias[None], gain_two, bias_two)
        residuals.append(residual)
        pieces.append(spread(own))

    outs, backs, sums, kept = {}, {}, [], ()
    for base in (0, 2):
        for p in parts:
            result = feed(p, base, me, pieces[p][base], pieces[p][base + 1], cot,
                          inner_weight, inner_bias[None], outer_weight, kept)
            kept = result[:4]
            outs[p, base], outs[p, base + 1] = result[4:6]
            backs[p, base], backs[p, base + 1] = result[6:8]
            sums.append(result[8])
    acts, dhs, xs, gs = kept

    grad_residuals, lows, grads_attended, vectors = [], [], [], []
    for p in parts:
        grad, low, a0, a1, a2, a3, vector = middle_back(
            p, me, gather_sum([backs[p, n] for n in range(4)]), residuals[p], cot, gain_two, output_weights
        )
        grad_residuals.append(grad)
        lows.append(low)
        vectors.append(vector)
        grads_attended.append(exchange([a0, a1, a2, a3]))

    grad_outer = tn(acts, gs).astype(BF16)
    grad_inner = tn(xs, dhs).astype(BF16)
    grad_outer, grad_inner = lax.psum((grad_outer, grad_inner), DP)

    earlier = ()
    for p in parts:
        earlier = attend_backward(p, me, segment_ids, qt, extras[p], kn, kt, vn, attended[p], grads_attended[p], earlier)
    grads = earlier

    held, _ = lax.optimization_barrier((outs, grads_attended))
    layer_out = ()
    for p in parts:
        one, two, three = gather_sum([held[p, n] for n in range(4)])
        result = residuals[p] + one.astype(F32) + two.astype(F32) + three.astype(F32) + outer_bias
        layer_out = (place(p, me, spread(result.astype(BF16)), length, BF16, layer_out),)
    one, two, three = gather_sum(output_grad([m for p in parts for m in mixed[p]], lows))
    grad_output = (one.astype(F32) + two.astype(F32) + three.astype(F32)).astype(BF16)

    input_grad, finals, row_sums = (), [], []
    tails = [tail(p, me, grads, wt) for p in parts]
    grad_weights = nn(grads, attend_in).astype(BF16)
    for p in parts:
        share, vector = final(p, me, gather_sum(tails[p][:4]), tokens, grad_residuals[p], gain_one)
        finals.append(vector)
        row_sums.append(tails[p][4])
        input_grad = (place(p, me, spread(share), length, F32, input_grad),)

    weights = sum_rows(jnp.concatenate([grad_weights, grad_output], axis=0)).astype(F32)

    fold_rows = lambda v: jnp.sum(v.reshape(-1, 8, v.shape[-1]), axis=1)
    shared = jnp.concatenate([fold_rows(sum(vectors)), fold_rows(sum(finals)), jnp.zeros((2, features), F32)])
    shared = shared + other_core(shared)
    shared = shared + other_chip(shared)
    row_sum = sum(row_sums)[:1]
    apart = jnp.concatenate([
        jnp.sum(sum(sums), axis=0, keepdims=True),
        jnp.pad(row_sum, ((0, 0), (0, features - row_sum.shape[1]))),
        jnp.zeros((6, features), F32),
    ])
    small = sum_small(jnp.concatenate([shared, apart]))
    turned_weights = weights[:3 * width].T
    return (
        layer_out[0].reshape(1, length, features),
        input_grad[0].reshape(1, length, features),
        small[4],
        small[5],
        turned_weights[:, :width],
        small[9, :width],
        turned_weights[:, width:2 * width],
        turned_weights[:, 2 * width:],
        small[9, 2 * width:3 * width],
        weights[3 * width:],
        small[2],
        small[0],
        small[1],
        grad_inner.astype(F32),
        small[8],
        grad_outer.astype(F32),
        small[3],
    )


def solution(mesh):
    rows = mesh.shape["dp"]
    inner = Mesh(mesh.devices.reshape(rows // 2, 2, 2, 2), DP + MP)
    placed = (
        P(DP, None, None),
        P(DP, None),
        P(),
        P(),
        P(None, MP),
        P(MP),
        P(None, MP),
        P(None, MP),
        P(MP),
        P(MP, None),
        P(),
        P(),
        P(),
        P(None, MP),
        P(MP),
        P(MP, None),
        P(),
        P(DP, None, None),
    )
    return jax.shard_map(
        local,
        mesh=inner,
        in_specs=placed,
        out_specs=(
            P(DP, None, None),
            P(DP, None, None),
            P(),
            P(),
            P(None, MP),
            P(MP),
            P(None, MP),
            P(None, MP),
            P(MP),
            P(MP, None),
            P(),
            P(),
            P(),
            P(None, MP),
            P(MP),
            P(MP, None),
            P(),
        ),
        check_vma=False,
    )
```

time: 435 us -> 367 us (0.84)
  blocking collectives: 68.5 us -> 0 us
  waiting for transfers between devices: 143 us -> 86.1 us
  Pallas kernels: 82.1 us -> 137 us
  starting transfers between devices: 15.2 us -> 55.9 us
  matrix products: 37.3 us -> 14.3 us
  other arithmetic: 36.7 us -> 14.1 us
  local copies, waits for them, and re-layouts: 36.6 us -> 41.7 us
    psum x2 -> x0, blocking collectives: 68.5 us -> none  [the longest x1 57.8 us: local(): lax.psum((grad_weights, grad_output, more), 'dp')]
    psum x1, waiting for transfers between devices: 55.5 us -> 0.01 us  [local(): grad_outer, grad_inner = lax.psum((grad_outer, grad_inner), DP)]
    pallas_call x2 -> x17, Pallas kernels: 54.7 us -> 104 us  [the longest x2 38.4 us: attend_backward(): pl.pallas_call(body, grid_spec=pltpu.PrefetchScalarGridSpec(num_scalar_pr...]
    all_to_all x2 -> x0, waiting for transfers between devices: 29.5 us -> none  [the longest x1 17.1 us: local(): lax.all_to_all(nt(output_full, residual_low).astype(BF16), MP, 0, 1, tile...]
    ppermute x0 -> x17, starting transfers between devices: none -> 24.9 us  [the longest x9 16.5 us: turned(): lax.ppermute(values, 'z', [(n, (n + way) % size) for n in range(size)])]
    ppermute x7 -> x19, starting transfers between devices: 3.85 us -> 23.5 us  [other_chip(): return lax.ppermute(value, 'y', SWAP)]
    unnamed x87 -> x202, local copies, waits for them, and re-layouts: 11.7 us -> 30 us
    dot_general x9 -> x2, matrix products: 28.3 us -> 10.4 us  [tn(): lax.dot_general(left, right, (((0,), (0,)), ((), ())), preferred_element_...]
  transfers between devices with their start and end apart: 25 -> 69, of which waited for: 7 -> 24; matrix products, arithmetic and copies ran while one was open for 21% -> 8% of each run, Pallas kernels for 19% -> 28%
where the time goes in v2:
time: 367 us; the launch traced here: 364 us
  Pallas kernels  137 us (37%)
  waiting for transfers between devices  86.1 us (23%)
  starting transfers between devices  55.9 us (15%)
  local copies, waits for them, and re-layouts  41.7 us (11%)
  between operations  15.3 us (4%)
  matrix products  14.3 us (4%)
  other arithmetic  14.1 us (4%)
    ppermute x19, waiting for transfers between devices, other_chip(): return lax.ppermute(value, 'y', SWAP)  66.1 us
    pallas_call x2, Pallas kernels, attend_backward(): pl.pallas_call(body, grid_spec=pltpu.PrefetchScalarGridSpec(num_scalar_pr...  38.4 us
    pallas_call x2, Pallas kernels, attend_forward(): pl.pallas_call(body, grid=(count,), in_specs=[pl.BlockSpec(memory_space=p...  37.5 us
    unnamed x202, local copies, waits for them, and re-layouts  30 us
    ppermute x19, starting transfers between devices, other_chip(): return lax.ppermute(value, 'y', SWAP)  23.5 us
    pallas_call x4, Pallas kernels, feed(): pl.pallas_call(feed_body, grid_spec=pltpu.PrefetchScalarGridSpec(num_scal...  22.2 us
    ppermute x9, starting transfers between devices, turned(): lax.ppermute(values, 'z', [(n, (n + way) % size) for n in range(size)])  16.5 us
    ppermute x9, waiting for transfers between devices, turned(): lax.ppermute(values, 'z', [(n, (n + way) % size) for n in range(size)])  15.4 us
  transfers between devices with their start and end apart: 69, of which 24 were waited for; matrix products, arithmetic and copies ran while one was open for 8% of the time, Pallas kernels for 28%

profile of v2, /device:TPU:0, one launch (start us, length us, event | category | flops | bytes accessed | tf_op | source)
XLA Modules:
  0.0 364.5 jit_solution(17429061016392473786)
XLA Ops:
  13.3 10.4 %project.1 = (bf16[2048,768]{1,0:T(8,128)(2,1)}, bf16[3,128,2048]{2,1,0:T(8,128)(2,1)S(1)}, bf16[192,2048]{1,0:T(8,128)(2,1)S(1)}, bf16[3,80,2048]{2,1,0:T(8,128...) custom-call(bf16[2048,768]{1,0:T(8,128)(2,1)} %bitcast.74, s32[1,2048]{1,0:T(1,128)S(1)} %copy-done.63, ...), custom_call_target="tpu_custom_call" | custom-call | flops 6000000000 | bytes 14000000 | tf_op jit(solution)/shard_map/project/pallas_call | solution.py:113
  26.0 21.8 %attend_forward.3 = (bf16[4,192,256]{2,1,0:T(8,128)(2,1)S(1)}, bf16[3,16,1024]{2,1,0:T(8,128)(2,1)S(1)}) custom-call(s32[1,2048]{1,0:T(1,128)S(1)} %copy-done.63, s32[1,2048]{1,0:T(1,128)S(1)} %copy-done.63, bf16[3,128,2048]{2,1,0:T(8,128)(2,1)S(1)} %get-tuple-element.110.refs_2_.refs_3_, bf16[3,2048,128]{2,1,0:T(8,128)(2,1)S(1)} %copy-done.70, ...), custom_call_target="tpu_custom_call" | custom-call | flops 8999999488 | bytes 5000000 | tf_op jit(solution)/shard_map/attend_forward/pallas_call | solution.py:202
  53.2 15.8 %attend_forward.2 = (bf16[4,192,256]{2,1,0:T(8,128)(2,1)S(1)}, bf16[3,16,1024]{2,1,0:T(8,128)(2,1)S(1)}) custom-call(s32[1,2048]{1,0:T(1,128)S(1)} %copy-done.63, s32[1,2048]{1,0:T(1,128)S(1)} %copy-done.63, bf16[3,128,2048]{2,1,0:T(8,128)(2,1)S(1)} %get-tuple-element.110.refs_2_.refs_3_, bf16[3,2048,128]{2,1,0:T(8,128)(2,1)S(1)} %copy-done.71, ...), custom_call_target="tpu_custom_call" | custom-call | flops 8999999488 | bytes 5000000 | tf_op jit(solution)/shard_map/attend_forward/pallas_call | solution.py:202
  78.6 8.5 %collective-permute-done.1.m2_ref.refs_6_ = bf16[192,256]{1,0:T(8,128)(2,1)} collective-permute-done((bf16[192,256]{1,0:T(8,128)(2,1)}, bf16[192,256]{1,0:T(8,128)(2,1)}, u32[]{:S(2)}, u32[]{:S(2)}) %collective-permute-start.1) | collective-permute-done | bytes 98336 | tf_op jit(solution)/shard_map/ppermute | solution.py:579
  98.3 5.8 %feed.4 = (bf16[2048,768]{1,0:T(8,128)(2,1)}, bf16[2048,768]{1,0:T(8,128)(2,1)}, bf16[2048,768]{1,0:T(8,128)(2,1)}, bf16[2048,768]{1,0:T(8,128)(2,1)}, bf16[256,...) custom-call(s32[1]{0:T(128)} %bitcast.me_ref.refs_0_, ...), custom_call_target="tpu_custom_call" | custom-call | flops 5000000000 | bytes 8000000 | tf_op jit(solution)/shard_map/feed/pallas_call | solution.py:412
  106.4 5.5 %feed.5 = (bf16[2048,768]{1,0:T(8,128)(2,1)}, bf16[2048,768]{1,0:T(8,128)(2,1)}, bf16[2048,768]{1,0:T(8,128)(2,1)}, bf16[2048,768]{1,0:T(8,128)(2,1)}, bf16[256,...) custom-call(s32[1]{0:T(128)} %bitcast.me_ref.refs_0_, ...), custom_call_target="tpu_custom_call", output_to_operand_aliasing={{0}: (7, {}), {1}: (8, {}), {2}: (9, {}), {3}: (10, {})} | custom-call | flops 5000000000 | bytes 8000000 | tf_op jit(solution)/shard_map/feed/pallas_call | solution.py:412
  115.8 5.5 %feed.6 = (bf16[2048,768]{1,0:T(8,128)(2,1)}, bf16[2048,768]{1,0:T(8,128)(2,1)}, bf16[2048,768]{1,0:T(8,128)(2,1)}, bf16[2048,768]{1,0:T(8,128)(2,1)}, bf16[256,...) custom-call(s32[1]{0:T(128)} %bitcast.me_ref.refs_0_, ...), custom_call_target="tpu_custom_call", output_to_operand_aliasing={{0}: (7, {}), {1}: (8, {}), {2}: (9, {}), {3}: (10, {})} | custom-call | flops 5000000000 | bytes 8000000 | tf_op jit(solution)/shard_map/feed/pallas_call | solution.py:412
  122.8 5.4 %feed.7 = (bf16[2048,768]{1,0:T(8,128)(2,1)}, bf16[2048,768]{1,0:T(8,128)(2,1)}, bf16[2048,768]{1,0:T(8,128)(2,1)}, bf16[2048,768]{1,0:T(8,128)(2,1)}, bf16[256,...) custom-call(s32[1]{0:T(128)} %bitcast.me_ref.refs_0_, ...), custom_call_target="tpu_custom_call", output_to_operand_aliasing={{0}: (7, {}), {1}: (8, {}), {2}: (9, {}), {3}: (10, {})} | custom-call | flops 5000000000 | bytes 8000000 | tf_op jit(solution)/shard_map/feed/pallas_call | solution.py:412
  128.8 6.7 %convolution_convert_fusion = bf16[768,768]{1,0:T(8,128)(2,1)} fusion(bf16[2048,768]{1,0:T(8,128)(2,1)} %get-tuple-element.201, bf16[2048,768]{1,0:T(8,128)(2,1)} %get-tuple-element.202), kind=kOutput, calls=%fused_computation.1 | convolution fusion | flops 2416508928 | bytes 7471104 | tf_op jit(solution)/shard_map/dot_general | solution.py:30
  139.2 3.7 %convolution_convert_fusion.1 = bf16[768,768]{1,0:T(8,128)(2,1)} fusion(bf16[2048,768]{1,0:T(8,128)(2,1)S(1)} %copy-done.82, bf16[2048,768]{1,0:T(8,128)(2,1)S(1)} %copy-done.81), kind=kOutput, calls=%fused_computation.2 | convolution fusion | flops 2416508928 | bytes 7471104 | tf_op jit(solution)/shard_map/dot_general | solution.py:30
  143.7 4.9 %collective-permute-done.23.b2_ref = bf16[256,768]{1,0:T(8,128)(2,1)} collective-permute-done((bf16[256,768]{1,0:T(8,128)(2,1)}, bf16[256,768]{1,0:T(8,128)(2,1)}, u32[]{:S(2)}, u32[]{:S(2)}) %collective-permute-start.23) | collective-permute-done | bytes 393248 | tf_op jit(solution)/shard_map/ppermute | solution.py:579
  170.1 20.9 %attend_backward.2 = (bf16[192,1024]{1,0:T(8,128)(2,1)S(1)}, f32[192,2048]{1,0:T(8,128)S(1)}, f32[192,2048]{1,0:T(8,128)S(1)}) custom-call(s32[1]{0:T(128)} %bitcast.me_ref.refs_0_, s32[1,2048]{1,0:T(1,128)S(1)} %copy-done.64, s32[1,2048]{1,0:T(1,128)S(1)} %copy-done.64, bf16[3,128,2048]{2,1,0:T(8,128)(2,1)} %copy-done.68, ...), custom_call_target="tpu_custom_call" | custom-call | flops 16000000000 | bytes 10000000 | tf_op jit(solution)/shard_map/attend_backward/pallas_call | solution.py:328
  194.7 17.6 %attend_backward.3.g_ref = bf16[576,2048]{1,0:T(8,128)(2,1)} custom-call(s32[1]{0:T(128)} %bitcast.me_ref.refs_0_, s32[1,2048]{1,0:T(1,128)S(1)} %copy-done.64, s32[1,2048]{1,0:T(1,128)S(1)} %copy-done.64, bf16[3,128,2048]{2,1,0:T(8,128)(2,1)S(1)} %copy-done.69, bf16[3,16,1024]{2,1,0:T(8,128)(2,1)S(1)} %copy-done.80, bf16[3,2048,128]{2,1,0:T(8,128)(2,1)S(1)} %copy-done.72, ...), custom_call_target="tpu_custom_call" | custom-call | flops 16000000000 | bytes 10000000 | tf_op jit(solution)/shard_map/attend_backward/pallas_call | solution.py:328
  216.6 3.9 %convolution_convert_fusion.2 = bf16[576,768]{1,0:T(8,128)(2,1)S(1)} fusion(bf16[576,2048]{1,0:T(8,128)(2,1)S(1)} %copy-done.67, bf16[2048,768]{1,0:T(8,128)(2,1)} %get-tuple-element.192), kind=kOutput, calls=%fused_computation.3 | convolution fusion | flops 1812381696 | bytes 6389760 | tf_op jit(solution)/shard_map/dot_general | solution.py:22
  229.9 7.2 %collective-permute-done.59 = bf16[192,768]{1,0:T(8,128)(2,1)S(1)} collective-permute-done((bf16[192,768]{1,0:T(8,128)(2,1)S(1)}, bf16[192,768]{1,0:T(8,128)(2,1)S(1)}, u32[]{:S(2)}, u32[]{:S(2)}) %collective-permute-start.59) | collective-permute-done | bytes 294944 | tf_op jit(solution)/shard_map/ppermute | solution.py:579
  239.1 6.4 %collective-permute-done.47.b2_ref = bf16[256,768]{1,0:T(8,128)(2,1)S(1)} collective-permute-done((bf16[256,768]{1,0:T(8,128)(2,1)S(1)}, bf16[256,768]{1,0:T(8,128)(2,1)S(1)}, u32[]{:S(2)}, u32[]{:S(2)}) %collective-permute-start.47) | collective-permute-done | bytes 393248 | tf_op jit(solution)/shard_map/ppermute | solution.py:579
  248.4 5.6 %collective-permute-done.41.b2_ref = bf16[256,768]{1,0:T(8,128)(2,1)S(1)} collective-permute-done((bf16[256,768]{1,0:T(8,128)(2,1)S(1)}, bf16[256,768]{1,0:T(8,128)(2,1)S(1)}, u32[]{:S(2)}, u32[]{:S(2)}) %collective-permute-start.41) | collective-permute-done | bytes 393248 | tf_op jit(solution)/shard_map/ppermute | solution.py:579
  264.1 6.7 %collective-permute-done.35 = bf16[256,768]{1,0:T(8,128)(2,1)S(1)} collective-permute-done((bf16[256,768]{1,0:T(8,128)(2,1)S(1)}, bf16[256,768]{1,0:T(8,128)(2,1)S(1)}, u32[]{:S(2)}, u32[]{:S(2)}) %collective-permute-start.35) | collective-permute-done | bytes 393248 | tf_op jit(solution)/shard_map/ppermute | solution.py:579
  271.3 8.0 %collective-permute-done.52 = f32[8,768]{1,0:T(8,128)S(1)} collective-permute-done((f32[8,768]{1,0:T(8,128)S(1)}, f32[8,768]{1,0:T(8,128)S(1)}, u32[]{:S(2)}, u32[]{:S(2)}) %collective-permute-start.52) | collective-permute-done | bytes 24608 | tf_op jit(solution)/shard_map/ppermute | solution.py:579
  281.1 4.1 %collective-permute-start.62 = (bf16[96,768]{1,0:T(8,128)(2,1)S(1)}, bf16[96,768]{1,0:T(8,128)(2,1)S(1)}, u32[]{:S(2)}, u32[]{:S(2)}) collective-permute-start(bf16[96,768]{1,0:T(8,128)(2,1)S(1)} %get-tuple-element.219), channel_id=1, source_target_pairs={{0,16},{8,24},{16,0},{24,8},{1,17},{9,25},{17,1},{25,9},{2,18},{10... | collective-permute-start | bytes 442376 | tf_op jit(solution)/shard_map/ppermute | solution.py:607
  300.9 5.2 %collective-permute-done.55 = f32[16,768]{1,0:T(8,128)S(1)} collective-permute-done((f32[16,768]{1,0:T(8,128)S(1)}, f32[16,768]{1,0:T(8,128)S(1)}, u32[]{:S(2)}, u32[]{:S(2)}) %collective-permute-start.55) | collective-permute-done | bytes 49184 | tf_op jit(solution)/shard_map/ppermute | solution.py:607
  311.5 3.3 collective-permute-start.66
  321.4 6.2 %collective-permute-done.43.p2_ref = bf16[256,768]{1,0:T(8,128)(2,1)S(1)} collective-permute-done((bf16[256,768]{1,0:T(8,128)(2,1)S(1)}, bf16[256,768]{1,0:T(8,128)(2,1)S(1)}, u32[]{:S(2)}, u32[]{:S(2)}) %collective-permute-start.43) | collective-permute-done | bytes 393248 | tf_op jit(solution)/shard_map/ppermute | solution.py:579
  329.2 6.4 %collective-permute-done.31.p2_ref = bf16[256,768]{1,0:T(8,128)(2,1)S(1)} collective-permute-done((bf16[256,768]{1,0:T(8,128)(2,1)S(1)}, bf16[256,768]{1,0:T(8,128)(2,1)S(1)}, u32[]{:S(2)}, u32[]{:S(2)}) %collective-permute-start.31) | collective-permute-done | bytes 393248 | tf_op jit(solution)/shard_map/ppermute | solution.py:579
  (400 shorter events, 154.0 us)
Async XLA Ops:
  7.2 331.0 %all-reduce.7.cloned.1.call-start = ((), (), s32[]{:S(2)}) async-start(), calls=%async_computation | async-start | bytes 4718592 | tf_op jit(solution)/shard_map/psum | solution.py:716
  48.3 21.4 %collective-permute-start.3 = (bf16[192,768]{1,0:T(8,128)(2,1)S(1)}, bf16[192,768]{1,0:T(8,128)(2,1)S(1)}, u32[]{:S(2)}, u32[]{:S(2)}) collective-permute-start(bf16[192,768]{1,0:T(8,128)(2,1)S(1)} %copy-done.44), channel_id=1, source_target_pairs={{0,1},{1,0},{2,3},{3,2},{4,5},{5,4},{6,7},{7,6},{8,9},{9,8},{10,11... | collective-permute-start | bytes 884744 | tf_op jit(solution)/shard_map/ppermute | solution.py:575
  48.4 21.4 %collective-permute-start.4 = (bf16[192,768]{1,0:T(8,128)(2,1)S(1)}, bf16[192,768]{1,0:T(8,128)(2,1)S(1)}, u32[]{:S(2)}, u32[]{:S(2)}) collective-permute-start(bf16[192,768]{1,0:T(8,128)(2,1)S(1)} %copy-done.44), channel_id=1, source_target_pairs={{0,2},{2,0},{1,3},{3,1},{4,6},{6,4},{5,7},{7,5},{8,10},{10,8},{9,1... | collective-permute-start | bytes 884744 | tf_op jit(solution)/shard_map/ppermute | solution.py:579
  72.4 25.9 %collective-permute-start.9 = (bf16[256,768]{1,0:T(8,128)(2,1)}, bf16[256,768]{1,0:T(8,128)(2,1)}, u32[]{:S(2)}, u32[]{:S(2)}) collective-permute-start(bf16[256,768]{1,0:T(8,128)(2,1)} %get-tuple-element.116.x0_ref), channel_id=1, source_target_pairs={{0,1},{1,0},{2,3},{3,2},{4,5},{5,4},{6,7},{7,6},{8,9},{9,8},{10,11... | collective-permute-start | bytes 1179656 | tf_op jit(solution)/shard_map/ppermute | solution.py:575
  72.8 25.5 %collective-permute-start.10 = (bf16[256,768]{1,0:T(8,128)(2,1)}, bf16[256,768]{1,0:T(8,128)(2,1)}, u32[]{:S(2)}, u32[]{:S(2)}) collective-permute-start(bf16[256,768]{1,0:T(8,128)(2,1)} %get-tuple-element.116.x0_ref), channel_id=1, source_target_pairs={{0,2},{2,0},{1,3},{3,1},{4,6},{6,4},{5,7},{7,5},{8,10},{10,8},{9,1... | collective-permute-start | bytes 1179656 | tf_op jit(solution)/shard_map/ppermute | solution.py:579
  96.5 18.7 %collective-permute-start.13 = (bf16[256,768]{1,0:T(8,128)(2,1)S(1)}, bf16[256,768]{1,0:T(8,128)(2,1)S(1)}, u32[]{:S(2)}, u32[]{:S(2)}) collective-permute-start(bf16[256,768]{1,0:T(8,128)(2,1)S(1)} %get-tuple-element.119.x0_ref), channel_id=1, source_target_pairs={{0,2},{2,0},{1,3},{3,1},{4,6},{6,4},{5,7},{7,5},{8,10},{10,8},{9,1... | collective-permute-start | bytes 1179656 | tf_op jit(solution)/shard_map/ppermute | solution.py:579
  114.8 29.0 %collective-permute-start.21 = (bf16[256,768]{1,0:T(8,128)(2,1)}, bf16[256,768]{1,0:T(8,128)(2,1)}, u32[]{:S(2)}, u32[]{:S(2)}) collective-permute-start(bf16[256,768]{1,0:T(8,128)(2,1)} %get-tuple-element.148), channel_id=1, source_target_pairs={{0,1},{1,0},{2,3},{3,2},{4,5},{5,4},{6,7},{7,6},{8,9},{9,8},{10,11... | collective-permute-start | bytes 1179656 | tf_op jit(solution)/shard_map/ppermute | solution.py:575
  115.3 42.1 %collective-permute-start.15 = (bf16[256,768]{1,0:T(8,128)(2,1)}, bf16[256,768]{1,0:T(8,128)(2,1)}, u32[]{:S(2)}, u32[]{:S(2)}) collective-permute-start(bf16[256,768]{1,0:T(8,128)(2,1)} %get-tuple-element.139), channel_id=1, source_target_pairs={{0,1},{1,0},{2,3},{3,2},{4,5},{5,4},{6,7},{7,6},{8,9},{9,8},{10,11... | collective-permute-start | bytes 1179656 | tf_op jit(solution)/shard_map/ppermute | solution.py:575
  137.5 19.9 %collective-permute-start.17 = (bf16[256,768]{1,0:T(8,128)(2,1)}, bf16[256,768]{1,0:T(8,128)(2,1)}, u32[]{:S(2)}, u32[]{:S(2)}) collective-permute-start(bf16[256,768]{1,0:T(8,128)(2,1)} %add_convert_fusion.7), channel_id=1, source_target_pairs={{0,2},{2,0},{1,3},{3,1},{4,6},{6,4},{5,7},{7,5},{8,10},{10,8},{9,1... | collective-permute-start | bytes 1179656 | tf_op jit(solution)/shard_map/ppermute | solution.py:579
  162.0 62.2 %collective-permute-start.58 = (bf16[192,768]{1,0:T(8,128)(2,1)S(1)}, bf16[192,768]{1,0:T(8,128)(2,1)S(1)}, u32[]{:S(2)}, u32[]{:S(2)}) collective-permute-start(bf16[192,768]{1,0:T(8,128)(2,1)S(1)} %get-tuple-element.198), channel_id=1, source_target_pairs={{0,1},{1,0},{2,3},{3,2},{4,5},{5,4},{6,7},{7,6},{8,9},{9,8},{10,11... | collective-permute-start | bytes 884744 | tf_op jit(solution)/shard_map/ppermute | solution.py:575
  162.1 67.2 %collective-permute-start.57 = (bf16[192,768]{1,0:T(8,128)(2,1)S(1)}, bf16[192,768]{1,0:T(8,128)(2,1)S(1)}, u32[]{:S(2)}, u32[]{:S(2)}) collective-permute-start(bf16[192,768]{1,0:T(8,128)(2,1)S(1)} %get-tuple-element.196), channel_id=1, source_target_pairs={{0,1},{1,0},{2,3},{3,2},{4,5},{5,4},{6,7},{7,6},{8,9},{9,8},{10,11... | collective-permute-start | bytes 884744 | tf_op jit(solution)/shard_map/ppermute | solution.py:575
  164.5 28.7 %collective-permute-start.24 = (bf16[192,256]{1,0:T(8,128)(2,1)S(1)}, bf16[192,256]{1,0:T(8,128)(2,1)S(1)}, u32[]{:S(2)}, u32[]{:S(2)}) collective-permute-start(bf16[192,256]{1,0:T(8,128)(2,1)S(1)} %get-tuple-element.152), channel_id=1, source_target_pairs={{0,1},{1,0},{2,3},{3,2},{4,5},{5,4},{6,7},{7,6},{8,9},{9,8},{10,11... | collective-permute-start | bytes 294920 | tf_op jit(solution)/shard_map/ppermute | solution.py:575
  168.3 25.0 %collective-permute-start.25 = (bf16[192,256]{1,0:T(8,128)(2,1)S(1)}, bf16[192,256]{1,0:T(8,128)(2,1)S(1)}, u32[]{:S(2)}, u32[]{:S(2)}) collective-permute-start(bf16[192,256]{1,0:T(8,128)(2,1)S(1)} %get-tuple-element.153), channel_id=1, source_target_pairs={{0,2},{2,0},{1,3},{3,1},{4,6},{6,4},{5,7},{7,5},{8,10},{10,8},{9,1... | collective-permute-start | bytes 294920 | tf_op jit(solution)/shard_map/ppermute | solution.py:579
  169.5 23.8 %collective-permute-start.26 = (bf16[192,256]{1,0:T(8,128)(2,1)S(1)}, bf16[192,256]{1,0:T(8,128)(2,1)S(1)}, u32[]{:S(2)}, u32[]{:S(2)}) collective-permute-start(bf16[192,256]{1,0:T(8,128)(2,1)S(1)} %get-tuple-element.154), channel_id=1, source_target_pairs={{0,3},{1,2},{2,1},{3,0},{4,7},{5,6},{6,5},{7,4},{8,11},{9,10},{10,... | collective-permute-start | bytes 294920 | tf_op jit(solution)/shard_map/ppermute | solution.py:583
  224.2 23.8 %collective-permute-start.39 = (bf16[256,768]{1,0:T(8,128)(2,1)S(1)}, bf16[256,768]{1,0:T(8,128)(2,1)S(1)}, u32[]{:S(2)}, u32[]{:S(2)}) collective-permute-start(bf16[256,768]{1,0:T(8,128)(2,1)S(1)} %get-tuple-element.171), channel_id=1, source_target_pairs={{0,1},{1,0},{2,3},{3,2},{4,5},{5,4},{6,7},{7,6},{8,9},{9,8},{10,11... | collective-permute-start | bytes 1179656 | tf_op jit(solution)/shard_map/ppermute | solution.py:575
  229.1 28.6 %collective-permute-start.27 = (bf16[256,768]{1,0:T(8,128)(2,1)S(1)}, bf16[256,768]{1,0:T(8,128)(2,1)S(1)}, u32[]{:S(2)}, u32[]{:S(2)}) collective-permute-start(bf16[256,768]{1,0:T(8,128)(2,1)S(1)} %copy-done.37), channel_id=1, source_target_pairs={{0,1},{1,0},{2,3},{3,2},{4,5},{5,4},{6,7},{7,6},{8,9},{9,8},{10,11... | collective-permute-start | bytes 1179656 | tf_op jit(solution)/shard_map/ppermute | solution.py:575
  239.1 20.3 %collective-permute-start.33 = (bf16[256,768]{1,0:T(8,128)(2,1)S(1)}, bf16[256,768]{1,0:T(8,128)(2,1)S(1)}, u32[]{:S(2)}, u32[]{:S(2)}) collective-permute-start(bf16[256,768]{1,0:T(8,128)(2,1)S(1)} %copy-done.35), channel_id=1, source_target_pairs={{0,1},{1,0},{2,3},{3,2},{4,5},{5,4},{6,7},{7,6},{8,9},{9,8},{10,11... | collective-permute-start | bytes 1179656 | tf_op jit(solution)/shard_map/ppermute | solution.py:575
  248.0 22.8 %collective-permute-start.35 = (bf16[256,768]{1,0:T(8,128)(2,1)S(1)}, bf16[256,768]{1,0:T(8,128)(2,1)S(1)}, u32[]{:S(2)}, u32[]{:S(2)}) collective-permute-start(bf16[256,768]{1,0:T(8,128)(2,1)S(1)} %add_convert_fusion.3), channel_id=1, source_target_pairs={{0,2},{2,0},{1,3},{3,1},{4,6},{6,4},{5,7},{7,5},{8,10},{10,8},{9,1... | collective-permute-start | bytes 1179656 | tf_op jit(solution)/shard_map/ppermute | solution.py:579
  256.1 24.7 %collective-permute-start.60 = (bf16[384,768]{1,0:T(8,128)(2,1)S(1)}, bf16[384,768]{1,0:T(8,128)(2,1)S(1)}, u32[]{:S(2)}, u32[]{:S(2)}) collective-permute-start(bf16[384,768]{1,0:T(8,128)(2,1)S(1)} %dynamic-slice_bitcast_fusion), channel_id=1, source_target_pairs={{0,4},{4,0},{1,5},{5,1},{2,6},{6,2},{3,7},{7,3},{8,12},{12,8},{9,1... | collective-permute-start | bytes 1769480 | tf_op jit(solution)/shard_map/ppermute | solution.py:617
  257.7 57.8 %collective-permute-start.49 = (bf16[256,768]{1,0:T(8,128)(2,1)S(1)}, bf16[256,768]{1,0:T(8,128)(2,1)S(1)}, u32[]{:S(2)}, u32[]{:S(2)}) collective-permute-start(bf16[256,768]{1,0:T(8,128)(2,1)S(1)} %get-tuple-element.181.p0_ref), channel_id=1, source_target_pairs={{0,2},{2,0},{1,3},{3,1},{4,6},{6,4},{5,7},{7,5},{8,10},{10,8},{9,1... | collective-permute-start | bytes 1179656 | tf_op jit(solution)/shard_map/ppermute | solution.py:579
  259.3 56.2 %collective-permute-start.48 = (bf16[256,768]{1,0:T(8,128)(2,1)S(1)}, bf16[256,768]{1,0:T(8,128)(2,1)S(1)}, u32[]{:S(2)}, u32[]{:S(2)}) collective-permute-start(bf16[256,768]{1,0:T(8,128)(2,1)S(1)} %get-tuple-element.181.p0_ref), channel_id=1, source_target_pairs={{0,1},{1,0},{2,3},{3,2},{4,5},{5,4},{6,7},{7,6},{8,9},{9,8},{10,11... | collective-permute-start | bytes 1179656 | tf_op jit(solution)/shard_map/ppermute | solution.py:575
  289.7 26.0 %collective-permute-start.37 = (bf16[256,768]{1,0:T(8,128)(2,1)S(1)}, bf16[256,768]{1,0:T(8,128)(2,1)S(1)}, u32[]{:S(2)}, u32[]{:S(2)}) collective-permute-start(bf16[256,768]{1,0:T(8,128)(2,1)S(1)} %get-tuple-element.230.p0_ref), channel_id=1, source_target_pairs={{0,2},{2,0},{1,3},{3,1},{4,6},{6,4},{5,7},{7,5},{8,10},{10,8},{9,1... | collective-permute-start | bytes 1179656 | tf_op jit(solution)/shard_map/ppermute | solution.py:579
  316.5 19.0 %collective-permute-start.31 = (bf16[256,768]{1,0:T(8,128)(2,1)S(1)}, bf16[256,768]{1,0:T(8,128)(2,1)S(1)}, u32[]{:S(2)}, u32[]{:S(2)}) collective-permute-start(bf16[256,768]{1,0:T(8,128)(2,1)S(1)} %get-tuple-element.231.p0_ref), channel_id=1, source_target_pairs={{0,2},{2,0},{1,3},{3,1},{4,6},{6,4},{5,7},{7,5},{8,10},{10,8},{9,1... | collective-permute-start | bytes 1179656 | tf_op jit(solution)/shard_map/ppermute | solution.py:579
  327.5 26.4 %collective-permute-start.67 = (bf16[384,768]{1,0:T(8,128)(2,1)}, bf16[384,768]{1,0:T(8,128)(2,1)}, u32[]{:S(2)}, u32[]{:S(2)}) collective-permute-start(bf16[384,768]{1,0:T(8,128)(2,1)} %bitcast.94), channel_id=1, source_target_pairs={{0,4},{4,0},{1,5},{5,1},{2,6},{6,2},{3,7},{7,3},{8,12},{12,8},{9,1... | collective-permute-start | bytes 1769480 | tf_op jit(solution)/shard_map/ppermute | solution.py:629
  (145 other events, 1216.2 us)
Sparse Core Ops, SparseCore 0:
  143.9 109.3 all-reduce.6

commit v3 on v2

v3 whole, which is shorter than its diff:
```python
import jax
import jax.numpy as jnp
from jax import lax
from jax.experimental import pallas as pl
from jax.experimental.pallas import tpu as pltpu
from jax.sharding import Mesh
from jax.sharding import PartitionSpec as P

HEAD = 64
WIDE = 128
TILE = 256
PARTS = 2
MASKED = 1e30
SCALE = 1
F32 = jnp.float32
BF16 = jnp.bfloat16
DP = ("z", "x")
MP = ("y", "core")
SWAP = [(0, 1), (1, 0)]


def nn(left, right):
    return lax.dot_general(left, right, (((1,), (0,)), ((), ())), preferred_element_type=F32)


def nt(left, right):
    return lax.dot_general(left, right, (((1,), (1,)), ((), ())), preferred_element_type=F32)


def tn(left, right):
    return lax.dot_general(left, right, (((0,), (0,)), ((), ())), preferred_element_type=F32)


def stats(values):
    center = values - jnp.mean(values, axis=-1, keepdims=True)
    scale = lax.rsqrt(jnp.mean(center * center, axis=-1, keepdims=True) + 1e-05)
    return center * scale, scale


def norm_back(grad_out, normed, scale, gain):
    upstream = grad_out * gain
    return scale * (
        upstream
        - jnp.mean(upstream, axis=-1, keepdims=True)
        - normed * jnp.mean(upstream * normed, axis=-1, keepdims=True)
    )


def fold(values):
    return jnp.sum(values.reshape(-1, 8, values.shape[-1]), axis=0)


def split(value, parts):
    out = []
    for _ in range(parts):
        piece = value.astype(BF16).astype(F32)
        out.append(piece)
        value = value - piece
    return out


def const(shape):
    return pl.BlockSpec(shape, lambda *_: (0,) * len(shape))


def shape_of(*dims, dtype=BF16):
    return jax.ShapeDtypeStruct(dims, dtype)


def params():
    return pltpu.CompilerParams(vmem_limit_bytes=40 << 20)


def kernel_call(body, values, free_in=(), free_out=(), **options):
    shapes = options.pop("out_shape")
    many = isinstance(shapes, (list, tuple))
    shapes = [s if n in free_out else pltpu.HBM(s.shape, s.dtype) for n, s in enumerate(shapes if many else [shapes])]
    values = [
        v if n in free_in or v.dtype == jnp.int32 else pltpu.with_memory_space_constraint(v, pltpu.HBM)
        for n, v in enumerate(values)
    ]
    return pl.pallas_call(
        body, out_shape=shapes if many else shapes[0], compiler_params=params(), **options
    )(*values)


def cost(flops, moved, special=0):
    return pl.CostEstimate(flops=int(flops * SCALE), bytes_accessed=int(moved * SCALE), transcendentals=0)


def project_body(x_ref, seg_ref, vec_ref, wq_ref, wk_ref, wv_ref,
                 ai_ref, qt_ref, kt_ref, vt_ref, kn_ref, vn_ref):
    heads = kn_ref.shape[0]
    width = heads * HEAD
    tile = x_ref.shape[0]
    normed, _ = stats(x_ref[...].astype(F32))
    ai = (normed * vec_ref[0:1, :] + vec_ref[1:2, :]).astype(BF16)
    ai_ref[...] = ai
    column = vec_ref[...].T[:2 * width, 6:7]
    queries = ((nt(wq_ref[...], ai) + column[:width]).astype(BF16)).astype(F32) * HEAD ** -0.5
    keys = nt(wk_ref[...], ai)
    kt_ref[...] = keys.astype(BF16)
    values = nt(wv_ref[...], ai) + column[width:]
    row = lax.broadcasted_iota(jnp.int32, (HEAD, tile), 0)
    same = jnp.where(row == seg_ref[...], 1.0, 0.0)
    mask = jnp.where(row < 8, (same - 1.0) * MASKED, jnp.where(row < 11, 1.0, 0.0))
    ones = jnp.where(row < 2, 1.0, 0.0)
    first = jnp.where(row[:16] == 0, 1.0, 0.0).astype(BF16)
    for h in range(heads):
        rows = slice(h * HEAD, (h + 1) * HEAD)
        qt_ref[h, :HEAD, :] = queries[rows].astype(BF16)
        qt_ref[h, HEAD:, :] = same.astype(BF16)
        vt_ref[h, :HEAD, :] = values[rows].astype(BF16)
        vt_ref[h, HEAD:, :] = first
        kn_ref[h] = jnp.concatenate([keys[rows], mask], axis=0).T.astype(BF16)
        vn_ref[h] = jnp.concatenate([values[rows], ones], axis=0).T.astype(BF16)


def project(tokens, seg_row, vectors, wq, wk, wv, heads):
    length, features = tokens.shape
    width = heads * HEAD
    return kernel_call(
        project_body,
        (tokens, seg_row, vectors, wq, wk, wv),
        grid=(length // TILE,),
        in_specs=[
            pl.BlockSpec((TILE, features), lambda i: (i, 0)),
            pl.BlockSpec((1, TILE), lambda i: (0, i)),
            const(vectors.shape), const(wq.shape), const(wk.shape), const(wv.shape),
        ],
        out_specs=[
            pl.BlockSpec((TILE, features), lambda i: (i, 0)),
            pl.BlockSpec((heads, WIDE, TILE), lambda i: (0, 0, i)),
            pl.BlockSpec((width, TILE), lambda i: (0, i)),
            pl.BlockSpec((heads, HEAD + 16, TILE), lambda i: (0, 0, i)),
            pl.BlockSpec((heads, TILE, WIDE), lambda i: (0, i, 0)),
            pl.BlockSpec((heads, TILE, WIDE), lambda i: (0, i, 0)),
        ],
        out_shape=[
            shape_of(length, features),
            shape_of(heads, WIDE, length),
            shape_of(width, length),
            shape_of(heads, HEAD + 16, length),
            shape_of(heads, length, WIDE),
            shape_of(heads, length, WIDE),
        ],
        cost_estimate=cost(6e9, 14e6),
        name="project",
    )


def key_range(seg_ref, seg_all, i):
    first = seg_ref[0, i * TILE]
    last = seg_ref[0, i * TILE + TILE - 1]
    before = jnp.sum(jnp.where(seg_all < first, 1.0, 0.0)).astype(jnp.int32)
    until = jnp.sum(jnp.where(seg_all <= last, 1.0, 0.0)).astype(jnp.int32)
    return before // TILE, (until + TILE - 1) // TILE


def shifted(one_hot, pieces):
    row = lax.broadcasted_iota(jnp.int32, one_hot.shape, 0)
    value = one_hot
    for n, piece in enumerate(pieces):
        value = jnp.where(row == 8 + n, piece, value)
    return value.astype(BF16)


def forward_body(offset, segs_ref, seg_ref, qt_ref, kn_ref, vt_ref, out_ref, extra_ref, qa_ref, acc_ref):
    heads, _, tile = qt_ref.shape
    low, high = key_range(segs_ref, seg_ref[...], pl.program_id(0) + offset)
    acc_ref[...] = jnp.zeros_like(acc_ref)
    qa_ref[...] = qt_ref[...]

    def look(kb, tops):
        keys = pl.ds(pl.multiple_of(kb * TILE, TILE), TILE)
        return tuple(
            jnp.maximum(tops[h], jnp.max(nn(kn_ref[h, keys, :], qa_ref[h]).reshape(-1, 8, tile), axis=0))
            for h in range(heads)
        )

    tops = lax.fori_loop(low, high, look, (jnp.full((8, tile), -jnp.inf, F32),) * heads)
    tops = [jnp.max(top, axis=0, keepdims=True) for top in tops]
    one_hots = [qt_ref[h, HEAD:HEAD + 16, :].astype(F32) for h in range(heads)]
    for h in range(heads):
        qa_ref[h, HEAD:HEAD + 16, :] = shifted(one_hots[h], split(-tops[h], 3))

    def step(kb, carry):
        keys = pl.ds(pl.multiple_of(kb * TILE, TILE), TILE)
        for h in range(heads):
            powered = jnp.exp(nn(kn_ref[h, keys, :], qa_ref[h])).astype(BF16)
            acc_ref[h] += nn(vt_ref[h, :, keys], powered)
        return carry

    lax.fori_loop(low, high, step, 0)
    for h in range(heads):
        total = acc_ref[h, HEAD:HEAD + 1, :]
        out_ref[0, h * HEAD:(h + 1) * HEAD, :] = (acc_ref[h, :HEAD, :] / total).astype(BF16)
        extra_ref[h] = shifted(one_hots[h], split(-(tops[h] + jnp.log(total)), 3))


def attend_forward(part, seg_row, qt, kn, vt):
    heads, _, length = qt.shape
    width = heads * HEAD
    count = length // TILE // PARTS
    offset = part * count

    def body(*refs):
        forward_body(offset, *refs)

    return kernel_call(
        body,
        (seg_row, seg_row, qt, kn, vt),
        grid=(count,),
        in_specs=[
            pl.BlockSpec(memory_space=pltpu.SMEM),
            const((1, length)),
            pl.BlockSpec((heads, WIDE, TILE), lambda i: (0, 0, i + offset)),
            const(kn.shape), const(vt.shape),
        ],
        out_specs=[
            pl.BlockSpec((1, width, TILE), lambda i: (i, 0, 0)),
            pl.BlockSpec((heads, 16, TILE), lambda i: (0, 0, i)),
        ],
        out_shape=[
            shape_of(count, width, TILE),
            shape_of(heads, 16, count * TILE),
        ],
        scratch_shapes=[
            pltpu.VMEM((heads, WIDE, TILE), BF16),
            pltpu.VMEM((heads, HEAD + 16, TILE), F32),
        ],
        cost_estimate=cost(9e9, 5e6, 4e6),
        name="attend_forward",
    )


def backward_body(part, me_ref, segs_ref, seg_ref, qt_ref, extra_ref, kn_ref, kt_ref, vn_ref, out_ref,
                  g0_ref, g1_ref, g2_ref, g3_ref, *rest):
    heads, _, tile = qt_ref.shape
    width = heads * HEAD
    length = kt_ref.shape[1]
    if part == 0:
        dq_out, dk_ref, dv_ref, qa_ref, da_ref, dq_ref = rest[-6:]
    else:
        dq_in, dk_in, dv_in = rest[:3]
        grads_ref, qa_ref, da_ref, dq_ref, dk_ref, dv_ref = rest[-6:]
    i = pl.program_id(0)
    count = length // TILE // PARTS
    at_here = i + part * count
    low, high = key_range(segs_ref, seg_ref[...], at_here)

    @pl.when(i == 0)
    def _():
        if part == 0:
            dk_ref[...] = jnp.zeros_like(dk_ref)
            dv_ref[...] = jnp.zeros_like(dv_ref)
        else:
            dk_ref[...] = dk_in[...]
            dv_ref[...] = dv_in[...]
            grads_ref[:width, :count * TILE] = dq_in[...]
        qa_ref[...] = jnp.zeros_like(qa_ref)
        da_ref[...] = jnp.zeros_like(da_ref)

    source = i ^ me_ref[0]
    for n, g_ref in enumerate((g0_ref, g1_ref, g2_ref, g3_ref)):
        @pl.when(source == n)
        def _(g_ref=g_ref):
            for h in range(heads):
                da_ref[h, :HEAD, :] = g_ref[h * HEAD:(h + 1) * HEAD]

    dq_ref[...] = jnp.zeros_like(dq_ref)
    row = lax.broadcasted_iota(jnp.int32, (16, tile), 0)
    for h in range(heads):
        rows = slice(h * HEAD, (h + 1) * HEAD)
        qa_ref[h, :HEAD, :] = qt_ref[h, :HEAD, :]
        qa_ref[h, HEAD:HEAD + 16, :] = extra_ref[h]
        inner = jnp.sum(da_ref[h, :HEAD, :].astype(F32) * out_ref[0, rows].astype(F32), axis=0, keepdims=True)
        first, second = split(-inner, 2)
        value = jnp.where(row == 0, first, jnp.where(row == 1, second, 0.0))
        da_ref[h, HEAD:HEAD + 16, :] = value.astype(BF16)

    def step(kb, carry):
        keys = pl.ds(pl.multiple_of(kb * TILE, TILE), TILE)
        for h in range(heads):
            rows = slice(h * HEAD, (h + 1) * HEAD)
            probs = jnp.exp(nn(kn_ref[h, keys, :], qa_ref[h]))
            ds = (probs * nn(vn_ref[h, keys, :], da_ref[h])).astype(BF16)
            dv_ref[rows, keys] += nt(da_ref[h, :HEAD, :], probs.astype(BF16))
            dk_ref[rows, keys] += nt(qa_ref[h, :HEAD, :], ds)
            dq_ref[rows] += nn(kt_ref[rows, keys], ds)
        return carry

    lax.fori_loop(low, high, step, 0)
    dq = (dq_ref[...] * HEAD ** -0.5).astype(BF16)
    if part == 0:
        dq_out[...] = dq
    else:
        grads_ref[:width, pl.ds(pl.multiple_of(at_here * TILE, TILE), TILE)] = dq

        @pl.when(i == pl.num_programs(0) - 1)
        def _():
            grads_ref[width:2 * width] = dk_ref[...].astype(BF16)
            grads_ref[2 * width:] = dv_ref[...].astype(BF16)


def attend_backward(part, me, seg_row, qt, extra, kn, kt, vn, out, grad, earlier, after):
    heads, _, length = qt.shape
    width = heads * HEAD
    count = length // TILE // PARTS
    offset = part * count

    def body(*refs):
        backward_body(part, *refs)

    in_specs = [
        pl.BlockSpec(memory_space=pltpu.SMEM),
        const((1, length)),
        pl.BlockSpec((heads, WIDE, TILE), lambda i, m: (0, 0, i + offset)),
        pl.BlockSpec((heads, 16, TILE), lambda i, m: (0, 0, i)),
        const(kn.shape), const(kt.shape), const(vn.shape),
        pl.BlockSpec((1, width, TILE), lambda i, m: (i, 0, 0)),
        const(grad[0].shape), const(grad[1].shape), const(grad[2].shape), const(grad[3].shape),
    ] + [const(v.shape) for v in earlier] + [pl.BlockSpec(memory_space=pl.ANY)] * len(after)
    scratch = [
        pltpu.VMEM((heads, WIDE, TILE), BF16),
        pltpu.VMEM((heads, WIDE, TILE), BF16),
        pltpu.VMEM((width, TILE), F32),
    ]
    if part == 0:
        out_specs = [pl.BlockSpec((width, TILE), lambda i, m: (0, i)), const((width, length)), const((width, length))]
        out_shape = [shape_of(width, count * TILE), shape_of(width, length, dtype=F32), shape_of(width, length, dtype=F32)]
    else:
        out_specs = const((3 * width, length))
        out_shape = shape_of(3 * width, length)
        scratch += [pltpu.VMEM((width, length), F32), pltpu.VMEM((width, length), F32)]
    return kernel_call(
        body,
        (me, seg_row, seg_row, qt, extra, kn, kt, vn, out, *grad, *earlier, *after),
        free_in=(10, 11, 12) + tuple(range(13 + len(earlier), 13 + len(earlier) + len(after))),
        grid_spec=pltpu.PrefetchScalarGridSpec(
            num_scalar_prefetch=1, grid=(count,), in_specs=in_specs, out_specs=out_specs, scratch_shapes=scratch,
        ),
        out_shape=out_shape,
        cost_estimate=cost(16e9, 10e6, 4e6),
        name="attend_backward",
    )


def middle_body(me_ref, x_ref, m0_ref, m1_ref, m2_ref, m3_ref, w0_ref, w1_ref, w2_ref, w3_ref,
                vec_ref, residual_ref, own_ref, mixed_ref):
    total = x_ref[...].astype(F32) + vec_ref[2:3, :]
    pairs = ((m0_ref, w0_ref), (m1_ref, w1_ref), (m2_ref, w2_ref), (m3_ref, w3_ref))
    for n, (m_ref, w_ref) in enumerate(pairs):
        total = total + tn(m_ref[...], w_ref[...])
        mixed_ref[n] = m_ref[...]
    residual_ref[...] = total
    normed, _ = stats(total)
    own_ref[...] = (normed * vec_ref[3:4, :] + vec_ref[4:5, :]).astype(BF16)


def middle(part, me, tokens, mixed, weights, vectors):
    features = tokens.shape[1]
    width = weights[0].shape[0]
    return kernel_call(
        middle_body,
        (me, tokens, *mixed, *weights, vectors),
        free_in=(3, 4, 5),
        free_out=(1,),
        grid_spec=pltpu.PrefetchScalarGridSpec(
            num_scalar_prefetch=1,
            grid=(1,),
            in_specs=[pl.BlockSpec((TILE, features), lambda i, m: (4 * part + m[0], 0))]
            + [const(v.shape) for v in mixed] + [const(v.shape) for v in weights] + [const(vectors.shape)],
            out_specs=[const((TILE, features)), const((TILE, features)), const((4, width, TILE))],
        ),
        out_shape=[shape_of(TILE, features, dtype=F32), shape_of(TILE, features), shape_of(4, width, TILE)],
        cost_estimate=cost(2e9, 3e6),
        name="middle",
    )


def feed_body(me_ref, x0_ref, x1_ref, g_ref, inner_ref, vec_ref, outer_ref, *rest):
    act_ref, dh_ref, xs_ref, gs_ref, out0_ref, out1_ref, back0_ref, back1_ref, sum_ref = rest[-9:]
    i = pl.program_id(0)

    @pl.when(i == 0)
    def _():
        xs_ref[...] = x0_ref[...]

    @pl.when(i == 1)
    def _():
        xs_ref[...] = x1_ref[...]

    gs_ref[...] = g_ref[...]
    hidden = nn(xs_ref[...], inner_ref[...]) + vec_ref[7:8, :]
    half = 0.5 + 0.5 * lax.erf(hidden * 0.5 ** 0.5)
    act = (hidden * half).astype(BF16)
    act_ref[...] = act
    slope = half + hidden * (jnp.exp(-0.5 * hidden * hidden) * 0.3989422804014327)
    dh = (nt(g_ref[...], outer_ref[...]) * slope).astype(BF16)
    dh_ref[...] = dh
    sums = fold(dh.astype(F32))
    out = nn(act, outer_ref[...]).astype(BF16)
    back = nt(dh, inner_ref[...]).astype(BF16)

    @pl.when(i == 0)
    def _():
        sum_ref[...] = sums
        out0_ref[...] = out
        back0_ref[...] = back

    @pl.when(i == 1)
    def _():
        sum_ref[...] += sums
        out1_ref[...] = out
        back1_ref[...] = back


def feed(part, base, me, first, second, cot, inner, vectors, outer, kept, outs):
    length, features = cot.shape
    units = inner.shape[1]
    at = 4 * part + base
    rows = lambda n: pl.BlockSpec((TILE, n), lambda i, m: (at + i, 0))
    piece = const((TILE, features))
    half = pl.BlockSpec((TILE, features), lambda i, m: (part, 0))
    kept = (*kept, *outs)
    targets = list(range(4)) * (len(kept) >= 4) + [4, 5] * (len(outs) > 0)
    return kernel_call(
        feed_body,
        (me, first, second, cot, inner, vectors, outer, *kept),
        free_in=(1, 2),
        free_out=(7,),
        grid_spec=pltpu.PrefetchScalarGridSpec(
            num_scalar_prefetch=1,
            grid=(2,),
            in_specs=[
                piece, piece,
                pl.BlockSpec((TILE, features), lambda i, m: (4 * part + (m[0] ^ (base + i)), 0)),
                const(inner.shape), const(vectors.shape), const(outer.shape),
            ] + [pl.BlockSpec(memory_space=pl.ANY)] * len(kept),
            out_specs=[rows(units), rows(units), rows(features), rows(features), half, half, piece, piece,
                       const((8, units))],
        ),
        out_shape=[shape_of(length, units), shape_of(length, units), shape_of(length, features),
                   shape_of(length, features)] + [shape_of(PARTS * TILE, features)] * 2
        + [shape_of(TILE, features)] * 2 + [shape_of(8, units, dtype=F32)],
        input_output_aliases={7 + n: target for n, target in enumerate(targets)},
        cost_estimate=cost(5e9, 8e6, 1e6),
        name="feed",
    )


def back_body(me_ref, b0_ref, b1_ref, b2_ref, residual_ref, g_ref, vec_ref, w0_ref, w1_ref, w2_ref, w3_ref,
              grad_ref, low_ref, a0_ref, a1_ref, a2_ref, a3_ref, sum_ref):
    grad_mid = b0_ref[...].astype(F32) + b1_ref[...].astype(F32) + b2_ref[...].astype(F32)
    normed, scale = stats(residual_ref[...])
    upstream = g_ref[...].astype(F32)
    grad = upstream + norm_back(grad_mid, normed, scale, vec_ref[3:4, :])
    grad_ref[...] = grad
    low = grad.astype(BF16)
    low_ref[...] = low
    for w_ref, a_ref in ((w0_ref, a0_ref), (w1_ref, a1_ref), (w2_ref, a2_ref), (w3_ref, a3_ref)):
        a_ref[...] = nt(w_ref[...], low).astype(BF16)
    for n, value in enumerate((grad_mid * normed, grad_mid, grad, upstream)):
        sum_ref[8 * n:8 * n + 8] = fold(value)


def middle_back(part, me, sums, residual, cot, vectors, weights):
    features = cot.shape[1]
    piece = const((TILE, features))
    width = weights[0].shape[0]
    return kernel_call(
        back_body,
        (me, *sums, residual, cot, vectors, *weights),
        free_in=(2, 3),
        free_out=(3, 4, 5),
        grid_spec=pltpu.PrefetchScalarGridSpec(
            num_scalar_prefetch=1,
            grid=(1,),
            in_specs=[piece] * 4
            + [pl.BlockSpec((TILE, features), lambda i, m: (4 * part + m[0], 0)), const(vectors.shape)]
            + [const(v.shape) for v in weights],
            out_specs=[piece, piece] + [const((width, TILE))] * 4 + [const((32, features))],
        ),
        out_shape=[shape_of(TILE, features, dtype=F32), shape_of(TILE, features)]
        + [shape_of(width, TILE)] * 4 + [shape_of(32, features, dtype=F32)],
        cost_estimate=cost(2e9, 4e6),
        name="middle_back",
    )


def output_body(*refs):
    mixed, lows, outs = refs[:PARTS], refs[PARTS:2 * PARTS], refs[2 * PARTS:]
    for n in range(4):
        total = nn(mixed[0][n], lows[0][...])
        for p in range(1, PARTS):
            total = total + nn(mixed[p][n], lows[p][...])
        outs[n][...] = total.astype(BF16)


def output_grad(mixed, lows):
    width, features = mixed[0].shape[1], lows[0].shape[1]
    return kernel_call(
        output_body,
        (*mixed, *lows),
        free_out=(1, 3),
        out_shape=[shape_of(width, features)] * 4,
        cost_estimate=cost(2e9, 4e6),
        name="output_grad",
    )


def tail_body(me_ref, g_ref, wq_ref, wk_ref, wv_ref, *rest):
    o0_ref, o1_ref, sum_ref = rest[-3:]
    i, p = pl.program_id(0), pl.program_id(1)
    grads = g_ref[...]
    width = wq_ref.shape[0]
    value = tn(grads[:width], wq_ref[...]) + tn(grads[width:2 * width], wk_ref[...])
    value = (value + tn(grads[2 * width:], wv_ref[...])).astype(BF16)
    sums = nt(jnp.ones((8, grads.shape[1]), BF16), grads)

    @pl.when((i == 0) & (p == 0))
    def _():
        sum_ref[...] = jnp.zeros_like(sum_ref)

    sum_ref[...] += sums
    for step, o_ref in enumerate((o1_ref, o0_ref)):
        @pl.when(i == step)
        def _(o_ref=o_ref):
            o_ref[pl.ds(pl.multiple_of(p * TILE, TILE), TILE), :] = value


def tail(base, me, grads, wq, wk, wv, after):
    deep = grads.shape[0]
    features = wq.shape[1]
    share = const((PARTS * TILE, features))
    return kernel_call(
        tail_body,
        (me, grads, wq, wk, wv, *after),
        free_in=tuple(range(5, 5 + len(after))),
        free_out=(1,),
        grid_spec=pltpu.PrefetchScalarGridSpec(
            num_scalar_prefetch=1,
            grid=(2, PARTS),
            in_specs=[pl.BlockSpec((deep, TILE), lambda i, p, m: (0, 4 * p + (m[0] ^ (base + 1 - i)))),
                      const(wq.shape), const(wk.shape), const(wv.shape)]
            + [pl.BlockSpec(memory_space=pl.ANY)] * len(after),
            out_specs=[share] * 2 + [const((8, deep))],
        ),
        out_shape=[shape_of(PARTS * TILE, features)] * 2 + [shape_of(8, deep, dtype=F32)],
        cost_estimate=cost(2e9, 4e6),
        name="tail",
    )


def weights_body(xz_ref, g_ref, ai_ref, go_ref, keep_ref, send_ref):
    i = pl.program_id(0)
    count = pl.num_programs(0)
    mine = i // (count // 2) == xz_ref[0]
    rows = g_ref.shape[0]
    at = pl.ds(pl.multiple_of(i % (count // 2) * rows, rows), rows)
    for inside in (True, False):
        for to_ref, chosen in ((keep_ref, mine), (send_ref, jnp.logical_not(mine))):
            @pl.when(chosen & ((i < count * 3 // 4) == inside))
            def _(to_ref=to_ref, inside=inside):
                to_ref[at, :] = nn(g_ref[...], ai_ref[...]).astype(BF16) if inside else go_ref[...]


def weight_grads(xz, grads, attend_in, grad_output):
    deep, length = grads.shape
    width, features = grad_output.shape
    rows = width // 2
    half = const((2 * width, features))
    return kernel_call(
        weights_body,
        (xz, grads, attend_in, grad_output),
        free_in=(3,),
        free_out=(0, 1),
        grid_spec=pltpu.PrefetchScalarGridSpec(
            num_scalar_prefetch=1,
            grid=(8,),
            in_specs=[pl.BlockSpec((rows, length), lambda i, m: (jnp.minimum(i, 5), 0)), const(attend_in.shape),
                      pl.BlockSpec((rows, features), lambda i, m: (jnp.maximum(i - 6, 0), 0))],
            out_specs=[half, half],
        ),
        out_shape=[shape_of(2 * width, features)] * 2,
        cost_estimate=cost(2e9, 8e6),
        name="weight_grads",
    )


def quarter_body(xz_ref, one_ref, two_ref, *outs):
    for n, out_ref in enumerate(outs):
        @pl.when(pl.program_id(0) == n)
        def _(out_ref=out_ref):
            out_ref[...] = (one_ref[...].astype(F32) + two_ref[...].astype(F32)).astype(BF16)


def quarters(xz, one, two, count):
    rows, features = one.shape
    block = pl.BlockSpec((rows // count, features), lambda i, m: ((m[1] + i) % count, 0))
    return kernel_call(
        quarter_body,
        (xz, one, two),
        free_in=(1, 2),
        free_out=tuple(range(count)),
        grid_spec=pltpu.PrefetchScalarGridSpec(
            num_scalar_prefetch=1,
            grid=(count,),
            in_specs=[block, block],
            out_specs=[const((rows // count, features))] * count,
        ),
        out_shape=[shape_of(rows // count, features)] * count,
        cost_estimate=cost(1e6, 2e6),
        name="quarters",
    )


def whole_body(xz_ref, *refs):
    out_ref = refs[-1]
    for n, in_ref in enumerate(refs[:-1]):
        @pl.when(pl.program_id(0) == n)
        def _(in_ref=in_ref):
            out_ref[...] = in_ref[...]


def whole(xz, pieces):
    count = len(pieces)
    rows, features = pieces[0].shape
    return kernel_call(
        whole_body,
        (xz, *pieces),
        free_in=tuple(range(1, count + 1)),
        free_out=(0,),
        grid_spec=pltpu.PrefetchScalarGridSpec(
            num_scalar_prefetch=1,
            grid=(count,),
            in_specs=[const((rows, features))] * count,
            out_specs=pl.BlockSpec((rows, features), lambda i, m: ((m[1] + count - i) % count, 0)),
        ),
        out_shape=shape_of(rows * count, features),
        cost_estimate=cost(1e6, 2e6),
        name="whole",
    )


def ready_body(xz_ref, mine_ref, other_ref, *outs):
    width = outs[0].shape[0]
    for n, out_ref in enumerate(outs):
        rows = slice(n % 2 * width, (n % 2 + 1) * width)
        for to_ref, chosen in ((mine_ref, xz_ref[0] == n // 2), (other_ref, xz_ref[0] != n // 2)):
            @pl.when(chosen)
            def _(to_ref=to_ref, out_ref=out_ref, rows=rows):
                out_ref[...] = to_ref[rows].astype(F32)


def ready(xz, mine, other):
    rows, features = mine.shape
    width = rows // 2
    return kernel_call(
        ready_body,
        (xz, mine, other),
        free_in=(1, 2),
        grid_spec=pltpu.PrefetchScalarGridSpec(
            num_scalar_prefetch=1,
            grid=(1,),
            in_specs=[const(mine.shape), const(other.shape)],
            out_specs=[const((width, features))] * 4,
        ),
        out_shape=[shape_of(width, features, dtype=F32)] * 4,
        cost_estimate=cost(1e6, 4e6),
        name="ready",
    )


def final_body(me_ref, b0_ref, b1_ref, b2_ref, x_ref, *rest):
    grad_refs, (vec_ref, out_ref, sum_ref) = rest[:PARTS], rest[PARTS:]
    p = pl.program_id(0)
    grad_attend = b0_ref[...].astype(F32) + b1_ref[...].astype(F32) + b2_ref[...].astype(F32)
    normed, scale = stats(x_ref[...].astype(F32))
    back = norm_back(grad_attend, normed, scale, vec_ref[0:1, :])
    for n, grad_ref in enumerate(grad_refs):
        @pl.when(p == n)
        def _(grad_ref=grad_ref):
            out_ref[...] = (grad_ref[...] + back).astype(BF16)

    @pl.when(p == 0)
    def _():
        sum_ref[...] = jnp.zeros_like(sum_ref)

    sum_ref[:8] += fold(grad_attend * normed)
    sum_ref[8:] += fold(grad_attend)


def final(me, sums, tokens, grads, vectors):
    features = tokens.shape[1]
    rows = pl.BlockSpec((TILE, features), lambda p, m: (p, 0))
    return kernel_call(
        final_body,
        (me, *sums, tokens, *grads, vectors),
        free_in=(2, 3),
        free_out=(0,),
        grid_spec=pltpu.PrefetchScalarGridSpec(
            num_scalar_prefetch=1,
            grid=(PARTS,),
            in_specs=[rows] * 3 + [pl.BlockSpec((TILE, features), lambda p, m: (4 * p + m[0], 0))]
            + [const((TILE, features))] * PARTS + [const(vectors.shape)],
            out_specs=[rows, const((16, features))],
        ),
        out_shape=[shape_of(PARTS * TILE, features), shape_of(16, features, dtype=F32)],
        cost_estimate=cost(1e8, 5e6),
        name="final",
    )


def place_body(me_ref, p0_ref, p1_ref, p2_ref, p3_ref, out_ref):
    for step, p_ref in enumerate((p0_ref, p1_ref, p2_ref, p3_ref)):
        @pl.when(pl.program_id(0) == step)
        def _(p_ref=p_ref):
            at = pl.ds(pl.multiple_of(pl.program_id(1) * TILE, TILE), TILE)
            out_ref[...] = p_ref[at, :].astype(out_ref.dtype)


def place(me, shares, dtype):
    rows, features = shares[0].shape
    return kernel_call(
        place_body,
        (me, *shares),
        free_in=(1, 2, 3, 4),
        grid_spec=pltpu.PrefetchScalarGridSpec(
            num_scalar_prefetch=1,
            grid=(4, PARTS),
            in_specs=[const((rows, features))] * 4,
            out_specs=pl.BlockSpec((TILE, features), lambda i, p, m: (4 * p + (m[0] ^ i), 0)),
        ),
        out_shape=shape_of(4 * rows, features, dtype=dtype),
        cost_estimate=cost(1e6, 9e6),
        name="place",
    )


def fence_body(*refs):
    pass


def fence(value, *after, space=pltpu.HBM):
    anywhere = pl.BlockSpec(memory_space=pl.ANY)
    return pl.pallas_call(
        fence_body,
        in_specs=[anywhere] * (1 + len(after)),
        out_specs=anywhere,
        out_shape=space(value.shape, value.dtype),
        input_output_aliases={0: 0},
        name="fence",
    )(pltpu.with_memory_space_constraint(value, space), *after)


def other_core(value):
    return lax.ppermute(value, "core", SWAP)


def other_chip(value):
    return lax.ppermute(value, "y", SWAP)


def crosswise(value):
    return lax.ppermute(value, MP, [(n, n ^ 3) for n in range(4)])


def exchange(pieces):
    return [pieces[0], other_core(pieces[1]), other_chip(pieces[2]), crosswise(pieces[3])]


def gather_sum(pieces):
    near = other_core(pieces[1])
    far = (pieces[2].astype(F32) + other_core(pieces[3]).astype(F32)).astype(BF16)
    return [pieces[0], near, other_chip(far)], far


def spread(value):
    far = other_chip(value)
    return [value, other_core(value), far, other_core(far)]


def pick(values, at):
    return lax.dynamic_index_in_dim(values, at, 0, keepdims=False)


def turned(values, way):
    size = lax.axis_size("z")
    return lax.ppermute(values, "z", [(n, (n + way) % size) for n in range(size)])


def sum_weights(grads, attend_in, grad_output):
    size = lax.axis_size("z")
    x, z = lax.axis_index("x"), lax.axis_index("z")
    xz = jnp.stack([x, z]).astype(jnp.int32)
    keep, send = weight_grads(xz, grads, attend_in, grad_output)
    if size > 4:
        keep = lax.psum(keep + lax.ppermute(send, "x", SWAP), "z")
    else:
        parts = quarters(xz, keep, lax.ppermute(send, "x", SWAP), size)
        total = parts[0].astype(F32)
        for way in range(1, size):
            total = total + turned(parts[way], way).astype(F32)
        total = total.astype(BF16)
        keep = whole(xz, [turned(total, way) if way else total for way in range(size)])
    return ready(xz, keep, lax.ppermute(keep, "x", SWAP))


def sum_small(value):
    size = lax.axis_size("z")
    if size > 4:
        return lax.psum(value, DP)
    value = value + lax.ppermute(value, "x", SWAP)
    total = value
    for way in range(1, size):
        total = total + turned(value, way)
    return total


def local(
    tokens,
    segment_ids,
    gain_one,
    bias_one,
    query_weight,
    query_bias,
    key_weight,
    value_weight,
    value_bias,
    output_weight,
    output_bias,
    gain_two,
    bias_two,
    inner_weight,
    inner_bias,
    outer_weight,
    outer_bias,
    cotangent,
):
    _, length, features = tokens.shape
    width = query_weight.shape[1]
    heads = width // HEAD
    tokens = tokens.reshape(length, features)
    cot = cotangent.reshape(length, features)
    at = lax.axis_index(MP).astype(jnp.int32)
    me = at[None]
    apart = jnp.concatenate([query_bias, value_bias, jnp.zeros((features - 2 * width,), F32)])
    vectors = jnp.stack([gain_one, bias_one, output_bias, gain_two, bias_two, outer_bias, apart, inner_bias])
    wq, wk, wv = query_weight.T, key_weight.T, value_weight.T

    output_weights = exchange([output_weight] * 4)
    attend_in, qt, kt, vt, kn, vn = project(tokens, segment_ids, vectors, wq, wk, wv, heads)

    parts = range(PARTS)
    attended, extras, mixed, residuals, pieces = [], [], [], [], []
    for p in parts:
        out, extra = attend_forward(p, segment_ids, qt, kn, vt)
        attended.append(out)
        extras.append(extra)
        arrived = exchange([pick(out, at ^ n) for n in range(4)])
        residual, own, together = middle(p, me, tokens, arrived, output_weights, vectors)
        mixed.append(together)
        residuals.append(residual)
        pieces.append([own, other_core(own), other_chip(own)])

    outs, backs, sums, kept = [], {}, [], ()
    for base in (0, 2):
        held = ()
        for p in parts:
            if base:
                far = fence(pieces[p][2], backs[p, 0], space=pltpu.VMEM)
                pieces[p] = [None, None, far, other_core(far)]
            result = feed(p, base, me, pieces[p][base], pieces[p][base + 1], cot,
                          inner_weight, vectors, outer_weight, kept, held)
            kept, held = result[:4], result[4:6]
            backs[p, base], backs[p, base + 1] = result[6:8]
            sums.append(result[8])
        outs += held
    acts, dhs, xs, gs = kept

    gathered, far_sums = zip(*[gather_sum([backs[p, n] for n in range(4)]) for p in parts])
    grad_residuals, lows, grads_attended, inner_sums = [], [], [], []
    for p in parts:
        grad, low, a0, a1, a2, a3, vector = middle_back(
            p, me, gathered[p], residuals[p], cot, vectors, output_weights
        )
        grad_residuals.append(grad)
        lows.append(low)
        inner_sums.append(vector)
        grads_attended.append(exchange([a0, a1, a2, a3]))

    grad_outer = tn(fence(acts, *far_sums), gs).astype(BF16)
    grad_inner = tn(fence(xs, *far_sums), dhs).astype(BF16)
    feed_sum = lax.psum_scatter(jnp.concatenate([grad_outer, grad_inner]), DP, scatter_dimension=0, tiled=True)

    last = fence(outs[3], lows[-1])
    near = other_core(fence(outs[1], lows[-1]))
    far = (outs[2].astype(F32) + other_core(last).astype(F32)).astype(BF16)
    earlier = attend_backward(0, me, segment_ids, qt, extras[0], kn, kt, vn, attended[0], grads_attended[0], (),
                              (far, near))
    result = jnp.concatenate(residuals) + outs[0].astype(F32) + near.astype(F32)
    result = (result + other_chip(far).astype(F32) + outer_bias).astype(BF16)
    (one, two, three), _ = gather_sum(output_grad(mixed, lows))
    grad_output = (one.astype(F32) + two.astype(F32) + three.astype(F32)).astype(BF16)
    grads = attend_backward(1, me, segment_ids, qt, extras[1], kn, kt, vn, attended[1], grads_attended[1], earlier,
                            (result, grad_output))

    feed_sum = lax.all_gather(fence(feed_sum, grads), DP, axis=0, tiled=True).astype(F32)
    wide = sum_weights(grads, attend_in, grad_output)
    near, far = other_core(result), other_chip(result)
    back_far, back_across, sum_far = tail(2, me, grads, wq, wk, wv, (near, far))
    back_own, back_near, sum_near = tail(0, me, grads, wq, wk, wv, ())
    arrived, _ = gather_sum([back_own, back_near, back_far, back_across])
    share, outer_sums = final(me, arrived, tokens, grad_residuals, vectors)
    layer_out = place(me, [result, near, far, other_core(far)], BF16)
    input_grad = place(me, spread(share), F32)

    fold_rows = lambda v: jnp.sum(v.reshape(-1, 8, v.shape[-1]), axis=1)
    shared = jnp.concatenate([fold_rows(sum(inner_sums)), fold_rows(outer_sums), jnp.zeros((2, features), F32)])
    shared = shared + other_core(shared)
    shared = shared + other_chip(shared)
    row_sum = (sum_far + sum_near)[:1]
    apart = jnp.concatenate([
        jnp.sum(sum(sums), axis=0, keepdims=True),
        jnp.pad(row_sum, ((0, 0), (0, features - row_sum.shape[1]))),
        jnp.zeros((6, features), F32),
    ])
    small = sum_small(jnp.concatenate([shared, apart]))
    return (
        layer_out.reshape(1, length, features),
        input_grad.reshape(1, length, features),
        small[4],
        small[5],
        wide[0].T,
        small[9, :width],
        wide[1].T,
        wide[2].T,
        small[9, 2 * width:3 * width],
        wide[3],
        small[2],
        small[0],
        small[1],
        feed_sum[features:],
        small[8],
        feed_sum[:features],
        small[3],
    )


def solution(mesh):
    rows = mesh.shape["dp"]
    inner = Mesh(mesh.devices.reshape(rows // 2, 2, 2, 2), DP + MP)
    placed = (
        P(DP, None, None),
        P(DP, None),
        P(),
        P(),
        P(None, MP),
        P(MP),
        P(None, MP),
        P(None, MP),
        P(MP),
        P(MP, None),
        P(),
        P(),
        P(),
        P(None, MP),
        P(MP),
        P(MP, None),
        P(),
        P(DP, None, None),
    )
    return jax.shard_map(
        local,
        mesh=inner,
        in_specs=placed,
        out_specs=(
            P(DP, None, None),
            P(DP, None, None),
            P(),
            P(),
            P(None, MP),
            P(MP),
            P(None, MP),
            P(None, MP),
            P(MP),
            P(MP, None),
            P(),
            P(),
            P(),
            P(None, MP),
            P(MP),
            P(MP, None),
            P(),
        ),
        check_vma=False,
    )
```

time: 367 us -> 332 us (0.905)
  Pallas kernels: 137 us -> 171 us
  local copies, waits for them, and re-layouts: 41.7 us -> 15.3 us
  waiting for transfers between devices: 86.1 us -> 64.5 us
  starting transfers between devices: 55.9 us -> 47.2 us
  matrix products: 14.3 us -> 8.44 us
    ppermute x19 -> x15, waiting for transfers between devices: 66.1 us -> 29.9 us  [other_chip(): return lax.ppermute(value, 'y', SWAP)]
    pallas_call x22 -> x30, Pallas kernels: 137 us -> 171 us  [the longest x23 171 us: kernel_call(): pl.pallas_call(body, out_shape=shapes if many else shapes[0], compiler_pa...]
    unnamed x202 -> x50, local copies, waits for them, and re-layouts: 30 us -> 1.88 us
    ppermute x2, waiting for transfers between devices: 0.01 us -> 11.1 us  [the longest x1 11.1 us: sum_weights(): parts = quarters(xz, keep, lax.ppermute(send, 'x', SWAP), size)]
    another operation x1 -> x9, local copies, waits for them, and re-layouts: 0.08 us -> 5.47 us  [local(): jnp.stack([gain_one, bias_one, output_bias, gain_two, bias_two, outer_bia...]
    convert_element_type x5 -> x3, other arithmetic: 6.56 us -> 2.04 us  [the longest x1 1.57 us: local(): far = (outs[2].astype(F32) + other_core(last).astype(F32)).astype(BF16)]
    dot_general x1 -> x0, matrix products: 3.89 us -> none  [nn(): lax.dot_general(left, right, (((1,), (0,)), ((), ())), preferred_element_...]
    ppermute x32 -> x24, starting transfers between devices: 7.49 us -> 6.34 us  [other_core(): return lax.ppermute(value, 'core', SWAP)]
  transfers between devices with their start and end apart: 69 -> 58, of which waited for: 24 -> 12; matrix products, arithmetic and copies ran while one was open for 8% -> 6% of each run, Pallas kernels for 28% -> 42%
where the time goes in v3:
time: 332 us
  Pallas kernels  171 us (52%)
  waiting for transfers between devices  64.5 us (19%)
  starting transfers between devices  47.2 us (14%)
  local copies, waits for them, and re-layouts  15.3 us (5%)
  between operations  14.7 us (4%)
  other arithmetic  11 us (3%)
  matrix products  8.44 us (3%)
    pallas_call x23, Pallas kernels, kernel_call(): pl.pallas_call(body, out_shape=shapes if many else shapes[0], compiler_pa...  171 us
    ppermute x15, waiting for transfers between devices, other_chip(): return lax.ppermute(value, 'y', SWAP)  29.9 us
    ppermute x15, starting transfers between devices, other_chip(): return lax.ppermute(value, 'y', SWAP)  23.1 us
    ppermute x9, waiting for transfers between devices, turned(): lax.ppermute(values, 'z', [(n, (n + way) % size) for n in range(size)])  16.8 us
    ppermute x9, starting transfers between devices, turned(): lax.ppermute(values, 'z', [(n, (n + way) % size) for n in range(size)])  16.4 us
    ppermute x1, waiting for transfers between devices, sum_weights(): parts = quarters(xz, keep, lax.ppermute(send, 'x', SWAP), size)  11.1 us
    dot_general x2, matrix products, tn(): lax.dot_general(left, right, (((0,), (0,)), ((), ())), preferred_element_...  8.44 us
  transfers between devices with their start and end apart: 58, of which 12 were waited for; matrix products, arithmetic and copies ran while one was open for 6% of the time, Pallas kernels for 42%

profile of v3, /device:TPU:0, one launch (start us, length us, event | category | flops | bytes accessed | tf_op | source)
XLA Modules:
  0.0 331.7 jit_solution(9854944578330348460)
XLA Ops:
  14.2 10.4 %project.1 = (bf16[2048,768]{1,0:T(8,128)(2,1)}, bf16[3,128,2048]{2,1,0:T(8,128)(2,1)}, bf16[192,2048]{1,0:T(8,128)(2,1)}, bf16[3,80,2048]{2,1,0:T(8,128)(2,1)},...) custom-call(bf16[2048,768]{1,0:T(8,128)(2,1)} %bitcast.46, s32[1,2048]{1,0:T(1,128)S(1)} %copy-done, ...), custom_call_target="tpu_custom_call" | custom-call | flops 6000000000 | bytes 14000000 | tf_op jit(solution)/shard_map/project/pallas_call | solution.py:82
  24.6 19.5 %attend_forward.2 = (bf16[4,192,256]{2,1,0:T(8,128)(2,1)}, bf16[3,16,1024]{2,1,0:T(8,128)(2,1)}) custom-call(s32[1,2048]{1,0:T(1,128)S(1)} %copy-done, s32[1,2048]{1,0:T(1,128)S(1)} %copy-done, bf16[3,128,2048]{2,1,0:T(8,128)(2,1)} %get-tuple-element.108.refs_2_.refs_3_, bf16[3,2048,128]{2,1,0:T(8,128)(2,1)} %get-tuple-element.109.refs_3_.refs_5_, ...), custom_call_target="tpu_custom_call" | custom-call | flops 8999999488 | bytes 5000000 | tf_op jit(solution)/shard_map/attend_forward/pallas_call | solution.py:82
  51.0 23.4 %attend_forward.3 = (bf16[4,192,256]{2,1,0:T(8,128)(2,1)}, bf16[3,16,1024]{2,1,0:T(8,128)(2,1)}) custom-call(s32[1,2048]{1,0:T(1,128)S(1)} %copy-done, s32[1,2048]{1,0:T(1,128)S(1)} %copy-done, bf16[3,128,2048]{2,1,0:T(8,128)(2,1)} %get-tuple-element.108.refs_2_.refs_3_, bf16[3,2048,128]{2,1,0:T(8,128)(2,1)} %get-tuple-element.109.refs_3_.refs_5_, ...), custom_call_target="tpu_custom_call" | custom-call | flops 8999999488 | bytes 5000000 | tf_op jit(solution)/shard_map/attend_forward/pallas_call | solution.py:82
  91.7 6.5 %feed.4 = (bf16[2048,768]{1,0:T(8,128)(2,1)}, bf16[2048,768]{1,0:T(8,128)(2,1)}, bf16[2048,768]{1,0:T(8,128)(2,1)}, bf16[2048,768]{1,0:T(8,128)(2,1)}, bf16[512,...) custom-call(s32[1]{0:T(128)} %bitcast.me_ref.refs_0_, ...), custom_call_target="tpu_custom_call" | custom-call | flops 5000000000 | bytes 8000000 | tf_op jit(solution)/shard_map/feed/pallas_call | solution.py:82
  98.3 6.5 %feed.5 = (bf16[2048,768]{1,0:T(8,128)(2,1)}, bf16[2048,768]{1,0:T(8,128)(2,1)}, bf16[2048,768]{1,0:T(8,128)(2,1)}, bf16[2048,768]{1,0:T(8,128)(2,1)}, bf16[512,...) custom-call(s32[1]{0:T(128)} %bitcast.me_ref.refs_0_, ...), custom_call_target="tpu_custom_call", output_to_operand_aliasing={{0}: (7, {}), {1}: (8, {}), {2}: (9, {}), {3}: (10, {}), {4... | custom-call | flops 5000000000 | bytes 8000000 | tf_op jit(solution)/shard_map/feed/pallas_call | solution.py:82
  105.4 6.5 %feed.6 = (bf16[2048,768]{1,0:T(8,128)(2,1)}, bf16[2048,768]{1,0:T(8,128)(2,1)}, bf16[2048,768]{1,0:T(8,128)(2,1)}, bf16[2048,768]{1,0:T(8,128)(2,1)}, bf16[512,...) custom-call(s32[1]{0:T(128)} %bitcast.me_ref.refs_0_, ...), custom_call_target="tpu_custom_call", output_to_operand_aliasing={{0}: (7, {}), {1}: (8, {}), {2}: (9, {}), {3}: (10, {})} | custom-call | flops 5000000000 | bytes 8000000 | tf_op jit(solution)/shard_map/feed/pallas_call | solution.py:82
  112.0 6.7 %feed.7 = (bf16[2048,768]{1,0:T(8,128)(2,1)}, bf16[2048,768]{1,0:T(8,128)(2,1)}, bf16[2048,768]{1,0:T(8,128)(2,1)}, bf16[2048,768]{1,0:T(8,128)(2,1)}, bf16[512,...) custom-call(s32[1]{0:T(128)} %bitcast.me_ref.refs_0_, ...), custom_call_target="tpu_custom_call", output_to_operand_aliasing={{0}: (7, {}), {1}: (8, {}), {2}: (9, {}), {3}: (10, {}), {4... | custom-call | flops 5000000000 | bytes 8000000 | tf_op jit(solution)/shard_map/feed/pallas_call | solution.py:82
  123.1 5.7 %convolution_convert_fusion.1 = bf16[768,768]{1,0:T(8,128)(2,1)S(1)} fusion(bf16[2048,768]{1,0:T(8,128)(2,1)} %fence.11, bf16[2048,768]{1,0:T(8,128)(2,1)} %get-tuple-element.196), kind=kOutput, calls=%fused_computation.9 | convolution fusion | flops 2416508928 | bytes 7471104 | tf_op jit(solution)/shard_map/dot_general | solution.py:31
  151.0 7.4 %collective-permute-done.35 = bf16[192,768]{1,0:T(8,128)(2,1)} collective-permute-done((bf16[192,768]{1,0:T(8,128)(2,1)S(1)}, bf16[192,768]{1,0:T(8,128)(2,1)}, u32[]{:S(2)}, u32[]{:S(2)}) %collective-permute-start.35) | collective-permute-done | bytes 294944 | tf_op jit(solution)/shard_map/ppermute | solution.py:763
  165.6 19.6 %attend_backward.2 = (bf16[192,1024]{1,0:T(8,128)(2,1)}, f32[192,2048]{1,0:T(8,128)}, f32[192,2048]{1,0:T(8,128)}) custom-call(s32[1]{0:T(128)} %bitcast.me_ref.refs_0_, s32[1,2048]{1,0:T(1,128)S(1)} %copy-done.1, s32[1,2048]{1,0:T(1,128)S(1)} %copy-done.1, bf16[3,128,2048]{2,1,0:T(8,128)(2,1)} %get-tuple-element.108.refs_2_.refs_3_, ...), custom_call_target="tpu_custom_call" | custom-call | flops 16000000000 | bytes 10000000 | tf_op jit(solution)/shard_map/attend_backward/pallas_call | solution.py:82
  188.5 23.7 %attend_backward.3.g_ref.refs_1_ = bf16[576,2048]{1,0:T(8,128)(2,1)} custom-call(s32[1]{0:T(128)} %bitcast.me_ref.refs_0_, s32[1,2048]{1,0:T(1,128)S(1)} %copy-done.1, s32[1,2048]{1,0:T(1,128)S(1)} %copy-done.1, bf16[3,128,2048]{2,1,0:T(8,128)(2,1)} %get-tuple-element.108.refs_2_.refs_3_, bf16[3,16,1024]{2,1,0:T(8,128)(2,1)} %get-tuple-element.143.refs_4_, ...), custom_call_target="tpu_custom_call" | custom-call | flops 16000000000 | bytes 10000000 | tf_op jit(solution)/shard_map/attend_backward/pallas_call | solution.py:82
  212.2 4.9 %tail.3 = (bf16[512,768]{1,0:T(8,128)(2,1)}, bf16[512,768]{1,0:T(8,128)(2,1)S(1)}, f32[8,576]{1,0:T(8,128)}) custom-call(s32[1]{0:T(128)} %bitcast.me_ref.refs_0_, bf16[576,2048]{1,0:T(8,128)(2,1)} %attend_backward.3.g_ref.refs_1_, bf16[192,768]{1,0:T(8,128)(2,1)} %bitcast.57, bf16[192,768]{1,0:T(8,128)(2,1)} %bitcast.60, bf16[192,768]{1,0:T(8,128)(2,1)} %bitcast.63, ...), custom_call_target="tpu_custom_call" | custom-call | flops 2000000000 | bytes 4000000 | tf_op jit(solution)/shard_map/tail/pallas_call | solution.py:82
  217.3 7.4 %weight_grads.1 = (bf16[384,768]{1,0:T(8,128)(2,1)S(1)}, bf16[384,768]{1,0:T(8,128)(2,1)S(1)}) custom-call(s32[2]{0:T(128)S(1)} %pad_add_fusion.xz_ref, bf16[576,2048]{1,0:T(8,128)(2,1)} %attend_backward.3.g_ref.refs_1_, bf16[2048,768]{1,0:T(8,128)(2,1)} %get-tuple-element.184.ai_ref, bf16[192,768]{1,0:T(8,128)(2,1)S(1)} %add_convert_fusion.4.refs_17_.go_ref), custom_call_target="tpu_custom_call" | custom-call | flops 2000000000 | bytes 8000000 | tf_op jit(solution)/shard_map/weight_grads/pallas_call | solution.py:82
  224.8 4.9 %tail.2 = (bf16[512,768]{1,0:T(8,128)(2,1)}, bf16[512,768]{1,0:T(8,128)(2,1)S(1)}, f32[8,576]{1,0:T(8,128)}) custom-call(s32[1]{0:T(128)} %bitcast.me_ref.refs_0_, bf16[576,2048]{1,0:T(8,128)(2,1)} %attend_backward.3.g_ref.refs_1_, bf16[192,768]{1,0:T(8,128)(2,1)} %bitcast.58, bf16[192,768]{1,0:T(8,128)(2,1)} %bitcast.61, bf16[192,768]{1,0:T(8,128)(2,1)} %bitcast.64), custom_call_target="tpu_custom_call" | custom-call | flops 2000000000 | bytes 4000000 | tf_op jit(solution)/shard_map/tail/pallas_call | solution.py:82
  232.1 11.1 %collective-permute-done.48.two_ref = bf16[384,768]{1,0:T(8,128)(2,1)S(1)} collective-permute-done((bf16[384,768]{1,0:T(8,128)(2,1)S(1)}, bf16[384,768]{1,0:T(8,128)(2,1)S(1)}, u32[]{:S(2)}, u32[]{:S(2)}) %collective-permute-start.48) | collective-permute-done | bytes 589856 | tf_op jit(solution)/shard_map/ppermute | solution.py:802
  244.2 3.7 %collective-permute-start.51 = (bf16[96,768]{1,0:T(8,128)(2,1)S(1)}, bf16[96,768]{1,0:T(8,128)(2,1)S(1)}, u32[]{:S(2)}, u32[]{:S(2)}) collective-permute-start(bf16[96,768]{1,0:T(8,128)(2,1)S(1)} %get-tuple-element.190), channel_id=1, source_target_pairs={{0,24},{8,0},{16,8},{24,16},{1,25},{9,1},{17,9},{25,17},{2,26},{10... | collective-permute-start | bytes 442376 | tf_op jit(solution)/shard_map/ppermute | solution.py:791
  248.1 7.6 %collective-permute-done.49 = bf16[96,768]{1,0:T(8,128)(2,1)S(1)} collective-permute-done((bf16[96,768]{1,0:T(8,128)(2,1)S(1)}, bf16[96,768]{1,0:T(8,128)(2,1)S(1)}, u32[]{:S(2)}, u32[]{:S(2)}) %collective-permute-start.49) | collective-permute-done | bytes 147488 | tf_op jit(solution)/shard_map/ppermute | solution.py:791
  255.7 9.2 %collective-permute-done.50 = bf16[96,768]{1,0:T(8,128)(2,1)S(1)} collective-permute-done((bf16[96,768]{1,0:T(8,128)(2,1)S(1)}, bf16[96,768]{1,0:T(8,128)(2,1)S(1)}, u32[]{:S(2)}, u32[]{:S(2)}) %collective-permute-start.50) | collective-permute-done | bytes 147488 | tf_op jit(solution)/shard_map/ppermute | solution.py:791
  265.0 6.2 %collective-permute-start.52 = (bf16[96,768]{1,0:T(8,128)(2,1)S(1)}, bf16[96,768]{1,0:T(8,128)(2,1)S(1)}, u32[]{:S(2)}, u32[]{:S(2)}) collective-permute-start(bf16[96,768]{1,0:T(8,128)(2,1)S(1)} %add_convert_fusion.6.refs_0_), channel_id=1, source_target_pairs={{0,8},{8,16},{16,24},{24,0},{1,9},{9,17},{17,25},{25,1},{2,10},{10... | collective-permute-start | bytes 442376 | tf_op jit(solution)/shard_map/ppermute | solution.py:791
  273.7 3.9 %final.1 = (bf16[512,768]{1,0:T(8,128)(2,1)S(1)}, f32[16,768]{1,0:T(8,128)}) custom-call(s32[1]{0:T(128)} %bitcast.me_ref.refs_0_, bf16[512,768]{1,0:T(8,128)(2,1)} %get-tuple-element.168.b0_ref, bf16[512,768]{1,0:T(8,128)(2,1)S(1)} %collective-permute-done.36.b1_ref, bf16[512,768]{1,0:T(8,128)(2,1)S(1)} %collective-permute-done.38.b2_ref, ...), custom_call_target="tpu_custom_call" | custom-call | flops 100000000 | bytes 5000000 | tf_op jit(solution)/shard_map/final/pallas_call | solution.py:82
  278.5 4.7 %collective-permute-start.40 = (bf16[512,768]{1,0:T(8,128)(2,1)S(1)}, bf16[512,768]{1,0:T(8,128)(2,1)S(1)}, u32[]{:S(2)}, u32[]{:S(2)}) collective-permute-start(bf16[512,768]{1,0:T(8,128)(2,1)S(1)} %get-tuple-element.174.p0_ref), channel_id=1, source_target_pairs={{0,2},{2,0},{1,3},{3,1},{4,6},{6,4},{5,7},{7,5},{8,10},{10,8},{9,1... | collective-permute-start | bytes 2359304 | tf_op jit(solution)/shard_map/ppermute | solution.py:763
  285.4 16.4 %collective-permute-done.43 = f32[8,768]{1,0:T(8,128)S(1)} collective-permute-done((f32[8,768]{1,0:T(8,128)S(1)}, f32[8,768]{1,0:T(8,128)S(1)}, u32[]{:S(2)}, u32[]{:S(2)}) %collective-permute-start.43) | collective-permute-done | bytes 24608 | tf_op jit(solution)/shard_map/ppermute | solution.py:763
  316.6 4.1 %place.3 = f32[2048,768]{1,0:T(8,128)} custom-call(s32[1]{0:T(128)} %bitcast.me_ref.refs_0_, bf16[512,768]{1,0:T(8,128)(2,1)S(1)} %get-tuple-element.174.p0_ref, bf16[512,768]{1,0:T(8,128)(2,1)S(1)} %collective-permute-done.39.p1_ref, bf16[512,768]{1,0:T(8,128)(2,1)S(1)} %collective-permute-done.40.p2_ref, bf16[512,768]{1,0:T(8,128)(2,1)S(1)} %collective-permute-done.41.p3_ref), custom_call_target="tpu_custom_call" | custom-call | flops 1000000 | bytes 9000000 | tf_op jit(solution)/shard_map/place/pallas_call | solution.py:82
  320.7 4.2 %fusion.8 = (f32[768,768]{1,0:T(8,128)}, f32[768,768]{1,0:T(8,128)}) fusion(bf16[1536,768]{1,0:T(8,128)(2,1)} %all-gather.2.cloned.1.call-done), kind=kLoop, calls=%fused_computation.45 | loop fusion | bytes 9437184 | tf_op jit(solution)/shard_map/slice | solution.py:947
  (217 shorter events, 93.0 us)
Async XLA Ops:
  7.2 205.0 %reduce-scatter.2.cloned.1.call-start = ((), (), s32[]{:S(2)}) async-start(), calls=%async_computation.1 | async-start | bytes 2654208 | tf_op jit(solution)/shard_map/reduce_scatter | solution.py:896
  46.2 28.2 %collective-permute-start.3 = (bf16[192,768]{1,0:T(8,128)(2,1)S(1)}, bf16[192,768]{1,0:T(8,128)(2,1)S(1)}, u32[]{:S(2)}, u32[]{:S(2)}) collective-permute-start(bf16[192,768]{1,0:T(8,128)(2,1)S(1)} %copy-done.21), channel_id=1, source_target_pairs={{0,1},{1,0},{2,3},{3,2},{4,5},{5,4},{6,7},{7,6},{8,9},{9,8},{10,11... | collective-permute-start | bytes 884744 | tf_op jit(solution)/shard_map/ppermute | solution.py:759
  46.3 28.2 %collective-permute-start.4 = (bf16[192,768]{1,0:T(8,128)(2,1)S(1)}, bf16[192,768]{1,0:T(8,128)(2,1)S(1)}, u32[]{:S(2)}, u32[]{:S(2)}) collective-permute-start(bf16[192,768]{1,0:T(8,128)(2,1)S(1)} %copy-done.21), channel_id=1, source_target_pairs={{0,2},{2,0},{1,3},{3,1},{4,6},{6,4},{5,7},{7,5},{8,10},{10,8},{9,1... | collective-permute-start | bytes 884744 | tf_op jit(solution)/shard_map/ppermute | solution.py:763
  49.2 25.2 %collective-permute-start.5 = (bf16[192,768]{1,0:T(8,128)(2,1)S(1)}, bf16[192,768]{1,0:T(8,128)(2,1)S(1)}, u32[]{:S(2)}, u32[]{:S(2)}) collective-permute-start(bf16[192,768]{1,0:T(8,128)(2,1)S(1)} %copy-done.21), channel_id=1, source_target_pairs={{0,3},{1,2},{2,1},{3,0},{4,7},{5,6},{6,5},{7,4},{8,11},{9,10},{10,... | collective-permute-start | bytes 884744 | tf_op jit(solution)/shard_map/ppermute | solution.py:767
  49.2 25.2 %collective-permute-start.1 = (bf16[192,256]{1,0:T(8,128)(2,1)S(1)}, bf16[192,256]{1,0:T(8,128)(2,1)S(1)}, u32[]{:S(2)}, u32[]{:S(2)}) collective-permute-start(bf16[192,256]{1,0:T(8,128)(2,1)S(1)} %get-tuple-element.209), channel_id=1, source_target_pairs={{0,2},{2,0},{1,3},{3,1},{4,6},{6,4},{5,7},{7,5},{8,10},{10,8},{9,1... | collective-permute-start | bytes 294920 | tf_op jit(solution)/shard_map/ppermute | solution.py:763
  50.6 23.8 %collective-permute-start.2 = (bf16[192,256]{1,0:T(8,128)(2,1)S(1)}, bf16[192,256]{1,0:T(8,128)(2,1)S(1)}, u32[]{:S(2)}, u32[]{:S(2)}) collective-permute-start(bf16[192,256]{1,0:T(8,128)(2,1)S(1)} %get-tuple-element.208), channel_id=1, source_target_pairs={{0,3},{1,2},{2,1},{3,0},{4,7},{5,6},{6,5},{7,4},{8,11},{9,10},{10,... | collective-permute-start | bytes 294920 | tf_op jit(solution)/shard_map/ppermute | solution.py:767
  119.3 17.6 %collective-permute-start.11 = (bf16[256,768]{1,0:T(8,128)(2,1)S(1)}, bf16[256,768]{1,0:T(8,128)(2,1)S(1)}, u32[]{:S(2)}, u32[]{:S(2)}) collective-permute-start(bf16[256,768]{1,0:T(8,128)(2,1)S(1)} %get-tuple-element.126), channel_id=1, source_target_pairs={{0,1},{1,0},{2,3},{3,2},{4,5},{5,4},{6,7},{7,6},{8,9},{9,8},{10,11... | collective-permute-start | bytes 1179656 | tf_op jit(solution)/shard_map/ppermute | solution.py:759
  121.7 17.8 %collective-permute-start.17 = (bf16[256,768]{1,0:T(8,128)(2,1)S(1)}, bf16[256,768]{1,0:T(8,128)(2,1)S(1)}, u32[]{:S(2)}, u32[]{:S(2)}) collective-permute-start(bf16[256,768]{1,0:T(8,128)(2,1)S(1)} %add_convert_fusion.3.refs_2_), channel_id=1, source_target_pairs={{0,2},{2,0},{1,3},{3,1},{4,6},{6,4},{5,7},{7,5},{8,10},{10,8},{9,1... | collective-permute-start | bytes 1179656 | tf_op jit(solution)/shard_map/ppermute | solution.py:763
  133.2 187.5 %all-gather.2.cloned.1.call-start = ((), (), s32[]{:S(2)}) async-start(), calls=%async_computation.2 | async-start | bytes 2654208 | tf_op jit(solution)/shard_map/all_gather | solution.py:910
  159.6 28.9 %collective-permute-start.24 = (bf16[192,256]{1,0:T(8,128)(2,1)S(1)}, bf16[192,256]{1,0:T(8,128)(2,1)S(1)}, u32[]{:S(2)}, u32[]{:S(2)}) collective-permute-start(bf16[192,256]{1,0:T(8,128)(2,1)S(1)} %get-tuple-element.147), channel_id=1, source_target_pairs={{0,1},{1,0},{2,3},{3,2},{4,5},{5,4},{6,7},{7,6},{8,9},{9,8},{10,11... | collective-permute-start | bytes 294920 | tf_op jit(solution)/shard_map/ppermute | solution.py:759
  162.0 26.4 %collective-permute-start.25 = (bf16[192,256]{1,0:T(8,128)(2,1)S(1)}, bf16[192,256]{1,0:T(8,128)(2,1)S(1)}, u32[]{:S(2)}, u32[]{:S(2)}) collective-permute-start(bf16[192,256]{1,0:T(8,128)(2,1)S(1)} %get-tuple-element.148), channel_id=1, source_target_pairs={{0,2},{2,0},{1,3},{3,1},{4,6},{6,4},{5,7},{7,5},{8,10},{10,8},{9,1... | collective-permute-start | bytes 294920 | tf_op jit(solution)/shard_map/ppermute | solution.py:763
  163.4 25.0 %collective-permute-start.26 = (bf16[192,256]{1,0:T(8,128)(2,1)S(1)}, bf16[192,256]{1,0:T(8,128)(2,1)S(1)}, u32[]{:S(2)}, u32[]{:S(2)}) collective-permute-start(bf16[192,256]{1,0:T(8,128)(2,1)S(1)} %get-tuple-element.149), channel_id=1, source_target_pairs={{0,3},{1,2},{2,1},{3,0},{4,7},{5,6},{6,5},{7,4},{8,11},{9,10},{10,... | collective-permute-start | bytes 294920 | tf_op jit(solution)/shard_map/ppermute | solution.py:767
  164.0 22.3 %collective-permute-start.20 = (bf16[512,768]{1,0:T(8,128)(2,1)S(1)}, bf16[512,768]{1,0:T(8,128)(2,1)S(1)}, u32[]{:S(2)}, u32[]{:S(2)}) collective-permute-start(bf16[512,768]{1,0:T(8,128)(2,1)S(1)} %add_convert_fusion.1.refs_13_), channel_id=1, source_target_pairs={{0,2},{2,0},{1,3},{3,1},{4,6},{6,4},{5,7},{7,5},{8,10},{10,8},{9,1... | collective-permute-start | bytes 2359304 | tf_op jit(solution)/shard_map/ppermute | solution.py:763
  186.8 25.4 %collective-permute-start.21 = (bf16[512,768]{1,0:T(8,128)(2,1)S(1)}, bf16[512,768]{1,0:T(8,128)(2,1)S(1)}, u32[]{:S(2)}, u32[]{:S(2)}) collective-permute-start(bf16[512,768]{1,0:T(8,128)(2,1)S(1)} %fusion.3.p0_ref.refs_16_), channel_id=1, source_target_pairs={{0,1},{1,0},{2,3},{3,2},{4,5},{5,4},{6,7},{7,6},{8,9},{9,8},{10,11... | collective-permute-start | bytes 2359304 | tf_op jit(solution)/shard_map/ppermute | solution.py:759
  186.8 25.4 %collective-permute-start.22 = (bf16[512,768]{1,0:T(8,128)(2,1)S(1)}, bf16[512,768]{1,0:T(8,128)(2,1)S(1)}, u32[]{:S(2)}, u32[]{:S(2)}) collective-permute-start(bf16[512,768]{1,0:T(8,128)(2,1)S(1)} %fusion.3.p0_ref.refs_16_), channel_id=1, source_target_pairs={{0,2},{2,0},{1,3},{3,1},{4,6},{6,4},{5,7},{7,5},{8,10},{10,8},{9,1... | collective-permute-start | bytes 2359304 | tf_op jit(solution)/shard_map/ppermute | solution.py:763
  224.7 18.5 %collective-permute-start.48 = (bf16[384,768]{1,0:T(8,128)(2,1)S(1)}, bf16[384,768]{1,0:T(8,128)(2,1)S(1)}, u32[]{:S(2)}, u32[]{:S(2)}) collective-permute-start(bf16[384,768]{1,0:T(8,128)(2,1)S(1)} %get-tuple-element.186), channel_id=1, source_target_pairs={{0,4},{4,0},{1,5},{5,1},{2,6},{6,2},{3,7},{7,3},{8,12},{12,8},{9,1... | collective-permute-start | bytes 1769480 | tf_op jit(solution)/shard_map/ppermute | solution.py:802
  229.8 43.9 %collective-permute-start.36 = (bf16[512,768]{1,0:T(8,128)(2,1)S(1)}, bf16[512,768]{1,0:T(8,128)(2,1)S(1)}, u32[]{:S(2)}, u32[]{:S(2)}) collective-permute-start(bf16[512,768]{1,0:T(8,128)(2,1)S(1)} %get-tuple-element.169), channel_id=1, source_target_pairs={{0,1},{1,0},{2,3},{3,2},{4,5},{5,4},{6,7},{7,6},{8,9},{9,8},{10,11... | collective-permute-start | bytes 2359304 | tf_op jit(solution)/shard_map/ppermute | solution.py:759
  231.5 42.1 %collective-permute-start.38 = (bf16[512,768]{1,0:T(8,128)(2,1)S(1)}, bf16[512,768]{1,0:T(8,128)(2,1)S(1)}, u32[]{:S(2)}, u32[]{:S(2)}) collective-permute-start(bf16[512,768]{1,0:T(8,128)(2,1)S(1)} %add_convert_fusion), channel_id=1, source_target_pairs={{0,2},{2,0},{1,3},{3,1},{4,6},{6,4},{5,7},{7,5},{8,10},{10,8},{9,1... | collective-permute-start | bytes 2359304 | tf_op jit(solution)/shard_map/ppermute | solution.py:763
  244.1 20.8 %collective-permute-start.50 = (bf16[96,768]{1,0:T(8,128)(2,1)S(1)}, bf16[96,768]{1,0:T(8,128)(2,1)S(1)}, u32[]{:S(2)}, u32[]{:S(2)}) collective-permute-start(bf16[96,768]{1,0:T(8,128)(2,1)S(1)} %get-tuple-element.189), channel_id=1, source_target_pairs={{0,16},{8,24},{16,0},{24,8},{1,17},{9,25},{17,1},{25,9},{2,18},{10... | collective-permute-start | bytes 442376 | tf_op jit(solution)/shard_map/ppermute | solution.py:791
  244.2 20.7 %collective-permute-start.51 = (bf16[96,768]{1,0:T(8,128)(2,1)S(1)}, bf16[96,768]{1,0:T(8,128)(2,1)S(1)}, u32[]{:S(2)}, u32[]{:S(2)}) collective-permute-start(bf16[96,768]{1,0:T(8,128)(2,1)S(1)} %get-tuple-element.190), channel_id=1, source_target_pairs={{0,24},{8,0},{16,8},{24,16},{1,25},{9,1},{17,9},{25,17},{2,26},{10... | collective-permute-start | bytes 442376 | tf_op jit(solution)/shard_map/ppermute | solution.py:791
  265.0 18.2 %collective-permute-start.52 = (bf16[96,768]{1,0:T(8,128)(2,1)S(1)}, bf16[96,768]{1,0:T(8,128)(2,1)S(1)}, u32[]{:S(2)}, u32[]{:S(2)}) collective-permute-start(bf16[96,768]{1,0:T(8,128)(2,1)S(1)} %add_convert_fusion.6.refs_0_), channel_id=1, source_target_pairs={{0,8},{8,16},{16,24},{24,0},{1,9},{9,17},{17,25},{25,1},{2,10},{10... | collective-permute-start | bytes 442376 | tf_op jit(solution)/shard_map/ppermute | solution.py:791
  278.5 23.5 %collective-permute-start.40 = (bf16[512,768]{1,0:T(8,128)(2,1)S(1)}, bf16[512,768]{1,0:T(8,128)(2,1)S(1)}, u32[]{:S(2)}, u32[]{:S(2)}) collective-permute-start(bf16[512,768]{1,0:T(8,128)(2,1)S(1)} %get-tuple-element.174.p0_ref), channel_id=1, source_target_pairs={{0,2},{2,0},{1,3},{3,1},{4,6},{6,4},{5,7},{7,5},{8,10},{10,8},{9,1... | collective-permute-start | bytes 2359304 | tf_op jit(solution)/shard_map/ppermute | solution.py:763
  283.2 25.4 %collective-permute-start.23 = (bf16[512,768]{1,0:T(8,128)(2,1)S(1)}, bf16[512,768]{1,0:T(8,128)(2,1)S(1)}, u32[]{:S(2)}, u32[]{:S(2)}) collective-permute-start(bf16[512,768]{1,0:T(8,128)(2,1)S(1)} %collective-permute-done.22.p2_ref.rest_1_), channel_id=1, source_target_pairs={{0,1},{1,0},{2,3},{3,2},{4,5},{5,4},{6,7},{7,6},{8,9},{9,8},{10,11... | collective-permute-start | bytes 2359304 | tf_op jit(solution)/shard_map/ppermute | solution.py:759
  284.2 21.9 %collective-permute-start.55 = (bf16[384,768]{1,0:T(8,128)(2,1)S(1)}, bf16[384,768]{1,0:T(8,128)(2,1)S(1)}, u32[]{:S(2)}, u32[]{:S(2)}) collective-permute-start(bf16[384,768]{1,0:T(8,128)(2,1)S(1)} %whole.1.mine_ref), channel_id=1, source_target_pairs={{0,4},{4,0},{1,5},{5,1},{2,6},{6,2},{3,7},{7,3},{8,12},{12,8},{9,1... | collective-permute-start | bytes 1769480 | tf_op jit(solution)/shard_map/ppermute | solution.py:808
  (59 other events, 578.1 us)
Sparse Core Ops, SparseCore 0:
  133.3 67.3 reduce-scatter.1
  212.3 57.8 all-gather.1

commit v4 on v3

--- a/solution.py
+++ b/solution.py
@@ -67,8 +67,8 @@
     return jax.ShapeDtypeStruct(dims, dtype)
 
 
-def params():
-    return pltpu.CompilerParams(vmem_limit_bytes=40 << 20)
+def params(mib=40):
+    return pltpu.CompilerParams(vmem_limit_bytes=mib << 20)
 
 
 def kernel_call(body, values, free_in=(), free_out=(), **options):
@@ -157,6 +157,13 @@
     return before // TILE, (until + TILE - 1) // TILE
 
 
+def by_pairs(low, high, step, carry):
+    keys = lambda kb: pl.ds(pl.multiple_of(kb * TILE, TILE), TILE)
+    pairs = (high - low) // 2
+    carry = lax.fori_loop(0, pairs, lambda n, c: step([keys(low + 2 * n), keys(low + 2 * n + 1)], c), carry)
+    return lax.fori_loop(low + 2 * pairs, high, lambda kb, c: step([keys(kb)], c), carry)
+
+
 def shifted(one_hot, pieces):
     row = lax.broadcasted_iota(jnp.int32, one_hot.shape, 0)
     value = one_hot
@@ -165,40 +172,42 @@
     return value.astype(BF16)
 
 
-def forward_body(offset, segs_ref, seg_ref, qt_ref, kn_ref, vt_ref, out_ref, extra_ref, qa_ref, acc_ref):
+def forward_body(offset, me_ref, segs_ref, seg_ref, qt_ref, kn_ref, vt_ref,
+                 out_ref, extra_ref, o0_ref, o1_ref, o2_ref, o3_ref, acc_ref):
     heads, _, tile = qt_ref.shape
-    low, high = key_range(segs_ref, seg_ref[...], pl.program_id(0) + offset)
+    i = pl.program_id(0)
+    low, high = key_range(segs_ref, seg_ref[...], i + offset)
     acc_ref[...] = jnp.zeros_like(acc_ref)
-    qa_ref[...] = qt_ref[...]
-
-    def look(kb, tops):
-        keys = pl.ds(pl.multiple_of(kb * TILE, TILE), TILE)
-        return tuple(
-            jnp.maximum(tops[h], jnp.max(nn(kn_ref[h, keys, :], qa_ref[h]).reshape(-1, 8, tile), axis=0))
-            for h in range(heads)
-        )
-
-    tops = lax.fori_loop(low, high, look, (jnp.full((8, tile), -jnp.inf, F32),) * heads)
-    tops = [jnp.max(top, axis=0, keepdims=True) for top in tops]
-    one_hots = [qt_ref[h, HEAD:HEAD + 16, :].astype(F32) for h in range(heads)]
-    for h in range(heads):
-        qa_ref[h, HEAD:HEAD + 16, :] = shifted(one_hots[h], split(-tops[h], 3))
-
-    def step(kb, carry):
-        keys = pl.ds(pl.multiple_of(kb * TILE, TILE), TILE)
+
+    def step(keys, tops):
+        scores = [[nn(kn_ref[h, at, :], qt_ref[h]) for at in keys] for h in range(heads)]
+        new_tops = []
         for h in range(heads):
-            powered = jnp.exp(nn(kn_ref[h, keys, :], qa_ref[h])).astype(BF16)
-            acc_ref[h] += nn(vt_ref[h, :, keys], powered)
-        return carry
-
-    lax.fori_loop(low, high, step, 0)
+            top = tops[h]
+            for score in scores[h]:
+                top = jnp.maximum(top, jnp.max(score, axis=0, keepdims=True))
+            new_tops.append(top)
+        powered = [[jnp.exp(score - new_tops[h]).astype(BF16) for score in scores[h]] for h in range(heads)]
+        for h in range(heads):
+            total = acc_ref[h] * jnp.exp(tops[h] - new_tops[h])
+            for at, power in zip(keys, powered[h]):
+                total = total + nn(vt_ref[h, :, at], power)
+            acc_ref[h] = total
+        return tuple(new_tops)
+
+    tops = by_pairs(low, high, step, (jnp.full((1, tile), -jnp.inf, F32),) * heads)
     for h in range(heads):
         total = acc_ref[h, HEAD:HEAD + 1, :]
         out_ref[0, h * HEAD:(h + 1) * HEAD, :] = (acc_ref[h, :HEAD, :] / total).astype(BF16)
-        extra_ref[h] = shifted(one_hots[h], split(-(tops[h] + jnp.log(total)), 3))
-
-
-def attend_forward(part, seg_row, qt, kn, vt):
+        one_hot = qt_ref[h, HEAD:HEAD + 16, :].astype(F32)
+        extra_ref[h] = shifted(one_hot, split(-(tops[h] + jnp.log(total)), 3))
+    for n, o_ref in enumerate((o0_ref, o1_ref, o2_ref, o3_ref)):
+        @pl.when((i ^ me_ref[0]) == n)
+        def _(o_ref=o_ref):
+            o_ref[...] = out_ref[0]
+
+
+def attend_forward(part, me, seg_row, qt, kn, vt):
     heads, _, length = qt.shape
     width = heads * HEAD
     count = length // TILE // PARTS
@@ -209,26 +218,24 @@
 
     return kernel_call(
         body,
-        (seg_row, seg_row, qt, kn, vt),
-        grid=(count,),
-        in_specs=[
-            pl.BlockSpec(memory_space=pltpu.SMEM),
-            const((1, length)),
-            pl.BlockSpec((heads, WIDE, TILE), lambda i: (0, 0, i + offset)),
-            const(kn.shape), const(vt.shape),
-        ],
-        out_specs=[
-            pl.BlockSpec((1, width, TILE), lambda i: (i, 0, 0)),
-            pl.BlockSpec((heads, 16, TILE), lambda i: (0, 0, i)),
-        ],
-        out_shape=[
-            shape_of(count, width, TILE),
-            shape_of(heads, 16, count * TILE),
-        ],
-        scratch_shapes=[
-            pltpu.VMEM((heads, WIDE, TILE), BF16),
-            pltpu.VMEM((heads, HEAD + 16, TILE), F32),
-        ],
+        (me, seg_row, seg_row, qt, kn, vt),
+        free_out=(3, 4, 5),
+        grid_spec=pltpu.PrefetchScalarGridSpec(
+            num_scalar_prefetch=1,
+            grid=(count,),
+            in_specs=[
+                pl.BlockSpec(memory_space=pltpu.SMEM),
+                const((1, length)),
+                pl.BlockSpec((heads, WIDE, TILE), lambda i, m: (0, 0, i + offset)),
+                const(kn.shape), const(vt.shape),
+            ],
+            out_specs=[
+                pl.BlockSpec((1, width, TILE), lambda i, m: (i, 0, 0)),
+                pl.BlockSpec((heads, 16, TILE), lambda i, m: (0, 0, i)),
+            ] + [const((width, TILE))] * 4,
+            scratch_shapes=[pltpu.VMEM((heads, HEAD + 16, TILE), F32)],
+        ),
+        out_shape=[shape_of(count, width, TILE), shape_of(heads, 16, count * TILE)] + [shape_of(width, TILE)] * 4,
         cost_estimate=cost(9e9, 5e6, 4e6),
         name="attend_forward",
     )
@@ -279,18 +286,24 @@
         value = jnp.where(row == 0, first, jnp.where(row == 1, second, 0.0))
         da_ref[h, HEAD:HEAD + 16, :] = value.astype(BF16)
 
-    def step(kb, carry):
-        keys = pl.ds(pl.multiple_of(kb * TILE, TILE), TILE)
-        for h in range(heads):
-            rows = slice(h * HEAD, (h + 1) * HEAD)
-            probs = jnp.exp(nn(kn_ref[h, keys, :], qa_ref[h]))
-            ds = (probs * nn(vn_ref[h, keys, :], da_ref[h])).astype(BF16)
-            dv_ref[rows, keys] += nt(da_ref[h, :HEAD, :], probs.astype(BF16))
-            dk_ref[rows, keys] += nt(qa_ref[h, :HEAD, :], ds)
-            dq_ref[rows] += nn(kt_ref[rows, keys], ds)
+    def step(keys, carry):
+        every = range(heads)
+        rows = [slice(h * HEAD, (h + 1) * HEAD) for h in every]
+        scores = [[nn(kn_ref[h, at, :], qa_ref[h]) for at in keys] for h in every]
+        slopes = [[nn(vn_ref[h, at, :], da_ref[h]) for at in keys] for h in every]
+        probs = [[jnp.exp(score) for score in scores[h]] for h in every]
+        ds = [[(p * s).astype(BF16) for p, s in zip(probs[h], slopes[h])] for h in every]
+        probs = [[p.astype(BF16) for p in probs[h]] for h in every]
+        for h in every:
+            total = dq_ref[rows[h]]
+            for n, at in enumerate(keys):
+                dv_ref[rows[h], at] += nt(da_ref[h, :HEAD, :], probs[h][n])
+                dk_ref[rows[h], at] += nt(qa_ref[h, :HEAD, :], ds[h][n])
+                total = total + nn(kt_ref[rows[h], at], ds[h][n])
+            dq_ref[rows[h]] = total
         return carry
 
-    lax.fori_loop(low, high, step, 0)
+    by_pairs(low, high, step, 0)
     dq = (dq_ref[...] * HEAD ** -0.5).astype(BF16)
     if part == 0:
         dq_out[...] = dq
@@ -347,7 +360,8 @@
 
 
 def middle_body(me_ref, x_ref, m0_ref, m1_ref, m2_ref, m3_ref, w0_ref, w1_ref, w2_ref, w3_ref,
-                vec_ref, residual_ref, own_ref, mixed_ref):
+                vec_ref, *rest):
+    residual_ref, own_ref, mixed_ref = rest[-3:]
     total = x_ref[...].astype(F32) + vec_ref[2:3, :]
     pairs = ((m0_ref, w0_ref), (m1_ref, w1_ref), (m2_ref, w2_ref), (m3_ref, w3_ref))
     for n, (m_ref, w_ref) in enumerate(pairs):
@@ -358,19 +372,20 @@
     own_ref[...] = (normed * vec_ref[3:4, :] + vec_ref[4:5, :]).astype(BF16)
 
 
-def middle(part, me, tokens, mixed, weights, vectors):
+def middle(part, me, tokens, mixed, weights, vectors, after):
     features = tokens.shape[1]
     width = weights[0].shape[0]
     return kernel_call(
         middle_body,
-        (me, tokens, *mixed, *weights, vectors),
+        (me, tokens, *mixed, *weights, vectors, *after),
         free_in=(3, 4, 5),
         free_out=(1,),
         grid_spec=pltpu.PrefetchScalarGridSpec(
             num_scalar_prefetch=1,
             grid=(1,),
             in_specs=[pl.BlockSpec((TILE, features), lambda i, m: (4 * part + m[0], 0))]
-            + [const(v.shape) for v in mixed] + [const(v.shape) for v in weights] + [const(vectors.shape)],
+            + [const(v.shape) for v in mixed] + [const(v.shape) for v in weights] + [const(vectors.shape)]
+            + [pl.BlockSpec(memory_space=pl.ANY)] * len(after),
             out_specs=[const((TILE, features)), const((TILE, features)), const((4, width, TILE))],
         ),
         out_shape=[shape_of(TILE, features, dtype=F32), shape_of(TILE, features), shape_of(4, width, TILE)],
@@ -380,25 +395,25 @@
 
 
 def feed_body(me_ref, x0_ref, x1_ref, g_ref, inner_ref, vec_ref, outer_ref, *rest):
-    act_ref, dh_ref, xs_ref, gs_ref, out0_ref, out1_ref, back0_ref, back1_ref, sum_ref = rest[-9:]
+    left_ref, right_ref, out0_ref, out1_ref, back0_ref, back1_ref, sum_ref = rest[-7:]
     i = pl.program_id(0)
 
     @pl.when(i == 0)
     def _():
-        xs_ref[...] = x0_ref[...]
+        left_ref[1] = x0_ref[...]
 
     @pl.when(i == 1)
     def _():
-        xs_ref[...] = x1_ref[...]
-
-    gs_ref[...] = g_ref[...]
-    hidden = nn(xs_ref[...], inner_ref[...]) + vec_ref[7:8, :]
+        left_ref[1] = x1_ref[...]
+
+    right_ref[0] = g_ref[...]
+    hidden = nn(left_ref[1], inner_ref[...]) + vec_ref[7:8, :]
     half = 0.5 + 0.5 * lax.erf(hidden * 0.5 ** 0.5)
     act = (hidden * half).astype(BF16)
-    act_ref[...] = act
+    left_ref[0] = act
     slope = half + hidden * (jnp.exp(-0.5 * hidden * hidden) * 0.3989422804014327)
     dh = (nt(g_ref[...], outer_ref[...]) * slope).astype(BF16)
-    dh_ref[...] = dh
+    right_ref[1] = dh
     sums = fold(dh.astype(F32))
     out = nn(act, outer_ref[...]).astype(BF16)
     back = nt(dh, inner_ref[...]).astype(BF16)
@@ -420,16 +435,16 @@
     length, features = cot.shape
     units = inner.shape[1]
     at = 4 * part + base
-    rows = lambda n: pl.BlockSpec((TILE, n), lambda i, m: (at + i, 0))
+    rows = pl.BlockSpec((2, TILE, features), lambda i, m: (0, at + i, 0))
     piece = const((TILE, features))
     half = pl.BlockSpec((TILE, features), lambda i, m: (part, 0))
     kept = (*kept, *outs)
-    targets = list(range(4)) * (len(kept) >= 4) + [4, 5] * (len(outs) > 0)
+    targets = list(range(2)) * (len(kept) >= 2) + [2, 3] * (len(outs) > 0)
     return kernel_call(
         feed_body,
         (me, first, second, cot, inner, vectors, outer, *kept),
         free_in=(1, 2),
-        free_out=(7,),
+        free_out=(5,),
         grid_spec=pltpu.PrefetchScalarGridSpec(
             num_scalar_prefetch=1,
             grid=(2,),
@@ -438,11 +453,9 @@
                 pl.BlockSpec((TILE, features), lambda i, m: (4 * part + (m[0] ^ (base + i)), 0)),
                 const(inner.shape), const(vectors.shape), const(outer.shape),
             ] + [pl.BlockSpec(memory_space=pl.ANY)] * len(kept),
-            out_specs=[rows(units), rows(units), rows(features), rows(features), half, half, piece, piece,
-                       const((8, units))],
-        ),
-        out_shape=[shape_of(length, units), shape_of(length, units), shape_of(length, features),
-                   shape_of(length, features)] + [shape_of(PARTS * TILE, features)] * 2
+            out_specs=[rows, rows, half, half, piece, piece, const((8, units))],
+        ),
+        out_shape=[shape_of(2, length, features)] * 2 + [shape_of(PARTS * TILE, features)] * 2
         + [shape_of(TILE, features)] * 2 + [shape_of(8, units, dtype=F32)],
         input_output_aliases={7 + n: target for n, target in enumerate(targets)},
         cost_estimate=cost(5e9, 8e6, 1e6),
@@ -553,61 +566,62 @@
     )
 
 
-def weights_body(xz_ref, g_ref, ai_ref, go_ref, keep_ref, send_ref):
-    i = pl.program_id(0)
-    count = pl.num_programs(0)
-    mine = i // (count // 2) == xz_ref[0]
-    rows = g_ref.shape[0]
-    at = pl.ds(pl.multiple_of(i % (count // 2) * rows, rows), rows)
-    for inside in (True, False):
-        for to_ref, chosen in ((keep_ref, mine), (send_ref, jnp.logical_not(mine))):
-            @pl.when(chosen & ((i < count * 3 // 4) == inside))
-            def _(to_ref=to_ref, inside=inside):
-                to_ref[at, :] = nn(g_ref[...], ai_ref[...]).astype(BF16) if inside else go_ref[...]
-
-
-def weight_grads(xz, grads, attend_in, grad_output):
-    deep, length = grads.shape
+def halves_body(xz_ref, g_ref, go_ref, keep_ref, send_ref):
+    width = go_ref.shape[0]
+    for to_ref, half in ((keep_ref, xz_ref[0]), (send_ref, 1 - xz_ref[0])):
+        @pl.when(half == 0)
+        def _(to_ref=to_ref):
+            to_ref[...] = g_ref[:2 * width]
+
+        @pl.when(half == 1)
+        def _(to_ref=to_ref):
+            to_ref[:width] = g_ref[2 * width:]
+            to_ref[width:] = go_ref[...]
+
+
+def halves(xz, grad_weights, grad_output):
     width, features = grad_output.shape
-    rows = width // 2
     half = const((2 * width, features))
     return kernel_call(
-        weights_body,
-        (xz, grads, attend_in, grad_output),
-        free_in=(3,),
-        free_out=(0, 1),
+        halves_body,
+        (xz, grad_weights, grad_output),
+        free_in=(1, 2),
+        free_out=(1,),
         grid_spec=pltpu.PrefetchScalarGridSpec(
             num_scalar_prefetch=1,
-            grid=(8,),
-            in_specs=[pl.BlockSpec((rows, length), lambda i, m: (jnp.minimum(i, 5), 0)), const(attend_in.shape),
-                      pl.BlockSpec((rows, features), lambda i, m: (jnp.maximum(i - 6, 0), 0))],
+            grid=(1,),
+            in_specs=[const(grad_weights.shape), const(grad_output.shape)],
             out_specs=[half, half],
         ),
         out_shape=[shape_of(2 * width, features)] * 2,
-        cost_estimate=cost(2e9, 8e6),
-        name="weight_grads",
-    )
-
-
-def quarter_body(xz_ref, one_ref, two_ref, *outs):
-    for n, out_ref in enumerate(outs):
+        cost_estimate=cost(1e6, 4e6),
+        name="halves",
+    )
+
+
+def quarter_body(count, xz_ref, one_ref, two_ref, *rest):
+    for n, out_ref in enumerate(rest[-count:]):
         @pl.when(pl.program_id(0) == n)
         def _(out_ref=out_ref):
             out_ref[...] = (one_ref[...].astype(F32) + two_ref[...].astype(F32)).astype(BF16)
 
 
-def quarters(xz, one, two, count):
+def quarters(xz, one, two, count, after):
     rows, features = one.shape
+
+    def body(*refs):
+        quarter_body(count, *refs)
+
     block = pl.BlockSpec((rows // count, features), lambda i, m: ((m[1] + i) % count, 0))
     return kernel_call(
-        quarter_body,
-        (xz, one, two),
-        free_in=(1, 2),
+        body,
+        (xz, one, two, *after),
+        free_in=(2,) + tuple(range(3, 3 + len(after))),
         free_out=tuple(range(count)),
         grid_spec=pltpu.PrefetchScalarGridSpec(
             num_scalar_prefetch=1,
             grid=(count,),
-            in_specs=[block, block],
+            in_specs=[block, block] + [pl.BlockSpec(memory_space=pl.ANY)] * len(after),
             out_specs=[const((rows // count, features))] * count,
         ),
         out_shape=[shape_of(rows // count, features)] * count,
@@ -644,7 +658,8 @@
     )
 
 
-def ready_body(xz_ref, mine_ref, other_ref, *outs):
+def ready_body(xz_ref, mine_ref, other_ref, *rest):
+    outs = rest[-4:]
     width = outs[0].shape[0]
     for n, out_ref in enumerate(outs):
         rows = slice(n % 2 * width, (n % 2 + 1) * width)
@@ -654,17 +669,17 @@
                 out_ref[...] = to_ref[rows].astype(F32)
 
 
-def ready(xz, mine, other):
+def ready(xz, mine, other, after):
     rows, features = mine.shape
     width = rows // 2
     return kernel_call(
         ready_body,
-        (xz, mine, other),
-        free_in=(1, 2),
+        (xz, mine, other, *after),
+        free_in=(1, 2) + tuple(range(3, 3 + len(after))),
         grid_spec=pltpu.PrefetchScalarGridSpec(
             num_scalar_prefetch=1,
             grid=(1,),
-            in_specs=[const(mine.shape), const(other.shape)],
+            in_specs=[const(mine.shape), const(other.shape)] + [pl.BlockSpec(memory_space=pl.ANY)] * len(after),
             out_specs=[const((width, features))] * 4,
         ),
         out_shape=[shape_of(width, features, dtype=F32)] * 4,
@@ -674,7 +689,7 @@
 
 
 def final_body(me_ref, b0_ref, b1_ref, b2_ref, x_ref, *rest):
-    grad_refs, (vec_ref, out_ref, sum_ref) = rest[:PARTS], rest[PARTS:]
+    grad_refs, vec_ref, (out_ref, sum_ref) = rest[:PARTS], rest[PARTS], rest[-2:]
     p = pl.program_id(0)
     grad_attend = b0_ref[...].astype(F32) + b1_ref[...].astype(F32) + b2_ref[...].astype(F32)
     normed, scale = stats(x_ref[...].astype(F32))
@@ -692,19 +707,20 @@
     sum_ref[8:] += fold(grad_attend)
 
 
-def final(me, sums, tokens, grads, vectors):
+def final(me, sums, tokens, grads, vectors, after):
     features = tokens.shape[1]
     rows = pl.BlockSpec((TILE, features), lambda p, m: (p, 0))
     return kernel_call(
         final_body,
-        (me, *sums, tokens, *grads, vectors),
-        free_in=(2, 3),
+        (me, *sums, tokens, *grads, vectors, *after),
+        free_in=(2, 3) + tuple(range(6 + PARTS, 6 + PARTS + len(after))),
         free_out=(0,),
         grid_spec=pltpu.PrefetchScalarGridSpec(
             num_scalar_prefetch=1,
             grid=(PARTS,),
             in_specs=[rows] * 3 + [pl.BlockSpec((TILE, features), lambda p, m: (4 * p + m[0], 0))]
-            + [const((TILE, features))] * PARTS + [const(vectors.shape)],
+            + [const((TILE, features))] * PARTS + [const(vectors.shape)]
+            + [pl.BlockSpec(memory_space=pl.ANY)] * len(after),
             out_specs=[rows, const((16, features))],
         ),
         out_shape=[shape_of(PARTS * TILE, features), shape_of(16, features, dtype=F32)],
@@ -791,21 +807,28 @@
     return lax.ppermute(values, "z", [(n, (n + way) % size) for n in range(size)])
 
 
-def sum_weights(grads, attend_in, grad_output):
+def sum_first(xz, keep, send, after):
     size = lax.axis_size("z")
-    x, z = lax.axis_index("x"), lax.axis_index("z")
-    xz = jnp.stack([x, z]).astype(jnp.int32)
-    keep, send = weight_grads(xz, grads, attend_in, grad_output)
+    got = lax.ppermute(send, "x", SWAP)
     if size > 4:
-        keep = lax.psum(keep + lax.ppermute(send, "x", SWAP), "z")
+        return [lax.psum(keep + got, "z")]
+    return quarters(xz, keep, got, size, after)
+
+
+def sum_second(parts):
+    total = parts[0].astype(F32)
+    for way in range(1, len(parts)):
+        total = total + turned(parts[way], way).astype(F32)
+    return total.astype(BF16)
+
+
+def sum_third(xz, total):
+    size = lax.axis_size("z")
+    if size > 4:
+        keep = total
     else:
-        parts = quarters(xz, keep, lax.ppermute(send, "x", SWAP), size)
-        total = parts[0].astype(F32)
-        for way in range(1, size):
-            total = total + turned(parts[way], way).astype(F32)
-        total = total.astype(BF16)
         keep = whole(xz, [turned(total, way) if way else total for way in range(size)])
-    return ready(xz, keep, lax.ppermute(keep, "x", SWAP))
+    return keep, lax.ppermute(keep, "x", SWAP)
 
 
 def sum_small(value):
@@ -847,20 +870,23 @@
     at = lax.axis_index(MP).astype(jnp.int32)
     me = at[None]
     apart = jnp.concatenate([query_bias, value_bias, jnp.zeros((features - 2 * width,), F32)])
-    vectors = jnp.stack([gain_one, bias_one, output_bias, gain_two, bias_two, outer_bias, apart, inner_bias])
+    vectors = jnp.concatenate([gain_one, bias_one, output_bias, gain_two, bias_two, outer_bias, apart, inner_bias])
+    vectors = vectors.reshape(8, features)
     wq, wk, wv = query_weight.T, key_weight.T, value_weight.T
 
     output_weights = exchange([output_weight] * 4)
     attend_in, qt, kt, vt, kn, vn = project(tokens, segment_ids, vectors, wq, wk, wv, heads)
 
     parts = range(PARTS)
-    attended, extras, mixed, residuals, pieces = [], [], [], [], []
+    attended, extras, fours = [], [], []
     for p in parts:
-        out, extra = attend_forward(p, segment_ids, qt, kn, vt)
+        out, extra, *four = attend_forward(p, me, segment_ids, qt, kn, vt)
         attended.append(out)
         extras.append(extra)
-        arrived = exchange([pick(out, at ^ n) for n in range(4)])
-        residual, own, together = middle(p, me, tokens, arrived, output_weights, vectors)
+        fours.append(exchange(four))
+    mixed, residuals, pieces = [], [], []
+    for p in parts:
+        residual, own, together = middle(p, me, tokens, fours[p], output_weights, vectors, extras[p + 1:])
         mixed.append(together)
         residuals.append(residual)
         pieces.append([own, other_core(own), other_chip(own)])
@@ -874,11 +900,11 @@
                 pieces[p] = [None, None, far, other_core(far)]
             result = feed(p, base, me, pieces[p][base], pieces[p][base + 1], cot,
                           inner_weight, vectors, outer_weight, kept, held)
-            kept, held = result[:4], result[4:6]
-            backs[p, base], backs[p, base + 1] = result[6:8]
-            sums.append(result[8])
+            kept, held = result[:2], result[2:4]
+            backs[p, base], backs[p, base + 1] = result[4:6]
+            sums.append(result[6])
         outs += held
-    acts, dhs, xs, gs = kept
+    left, right = kept
 
     gathered, far_sums = zip(*[gather_sum([backs[p, n] for n in range(4)]) for p in parts])
     grad_residuals, lows, grads_attended, inner_sums = [], [], [], []
@@ -891,30 +917,39 @@
         inner_sums.append(vector)
         grads_attended.append(exchange([a0, a1, a2, a3]))
 
-    grad_outer = tn(fence(acts, *far_sums), gs).astype(BF16)
-    grad_inner = tn(fence(xs, *far_sums), dhs).astype(BF16)
-    feed_sum = lax.psum_scatter(jnp.concatenate([grad_outer, grad_inner]), DP, scatter_dimension=0, tiled=True)
-
-    last = fence(outs[3], lows[-1])
-    near = other_core(fence(outs[1], lows[-1]))
-    far = (outs[2].astype(F32) + other_core(last).astype(F32)).astype(BF16)
+    grad_feed = lax.dot_general(fence(left, *far_sums), right, (((1,), (1,)), ((0,), (0,))), preferred_element_type=F32)
+    grad_feed = grad_feed.astype(BF16).reshape(2 * features, features)
+    feed_sum = lax.psum_scatter(grad_feed, DP, scatter_dimension=0, tiled=True)
+
+    near = other_core(fence(outs[1], *far_sums))
+    far = (outs[2].astype(F32) + other_core(fence(outs[3], *far_sums)).astype(F32)).astype(BF16)
+    far = fence(far, lows[-1], space=pltpu.VMEM)
+    part = output_grad(mixed, lows)
     earlier = attend_backward(0, me, segment_ids, qt, extras[0], kn, kt, vn, attended[0], grads_attended[0], (),
-                              (far, near))
+                              (far, near, part[0]))
     result = jnp.concatenate(residuals) + outs[0].astype(F32) + near.astype(F32)
     result = (result + other_chip(far).astype(F32) + outer_bias).astype(BF16)
-    (one, two, three), _ = gather_sum(output_grad(mixed, lows))
-    grad_output = (one.astype(F32) + two.astype(F32) + three.astype(F32)).astype(BF16)
+    part_far = fence(part[2], earlier[0])
+    part_far = (part_far.astype(F32) + other_core(part[3]).astype(F32)).astype(BF16)
+    part_near = other_core(part[1])
     grads = attend_backward(1, me, segment_ids, qt, extras[1], kn, kt, vn, attended[1], grads_attended[1], earlier,
-                            (result, grad_output))
-
-    feed_sum = lax.all_gather(fence(feed_sum, grads), DP, axis=0, tiled=True).astype(F32)
-    wide = sum_weights(grads, attend_in, grad_output)
+                            (result, part_far, part_near))
+
+    xz = jnp.stack([lax.axis_index("x"), lax.axis_index("z")]).astype(jnp.int32)
+    grad_output = fence(part[0], grads).astype(F32) + part_near.astype(F32) + other_chip(part_far).astype(F32)
+    keep, send = halves(xz, nn(grads, attend_in).astype(BF16), grad_output.astype(BF16))
     near, far = other_core(result), other_chip(result)
-    back_far, back_across, sum_far = tail(2, me, grads, wq, wk, wv, (near, far))
-    back_own, back_near, sum_near = tail(0, me, grads, wq, wk, wv, ())
-    arrived, _ = gather_sum([back_own, back_near, back_far, back_across])
-    share, outer_sums = final(me, arrived, tokens, grad_residuals, vectors)
+    back_far, back_across, sum_far = tail(2, me, grads, wq, wk, wv, (near, far, send))
+    back_far = (back_far.astype(F32) + other_core(back_across).astype(F32)).astype(BF16)
+    quarter = sum_first(xz, keep, send, (back_far,))
+    back_own, back_near, sum_near = tail(0, me, grads, wq, wk, wv, quarter[-1:])
     layer_out = place(me, [result, near, far, other_core(far)], BF16)
+    feed_sum = lax.all_gather(fence(feed_sum, layer_out), DP, axis=0, tiled=True).astype(F32)
+    total = fence(sum_second(quarter), layer_out, back_own, space=pltpu.VMEM)
+    arrived = [back_own, other_core(back_near), other_chip(back_far)]
+    share, outer_sums = final(me, arrived, tokens, grad_residuals, vectors, (total,))
+    mine, other = sum_third(xz, total)
+    wide = ready(xz, mine, other, ())
     input_grad = place(me, spread(share), F32)
 
     fold_rows = lambda v: jnp.sum(v.reshape(-1, 8, v.shape[-1]), axis=1)

time: 332 us -> 314 us (0.946)
  Pallas kernels: 171 us -> 135 us
  starting transfers between devices: 47.2 us -> 55.2 us
  waiting for transfers between devices: 64.5 us -> 71.3 us
  matrix products: 8.44 us -> 14.7 us
  local copies, waits for them, and re-layouts: 15.3 us -> 10.2 us
    pallas_call x23, Pallas kernels: 171 us -> 134 us  [kernel_call(): pl.pallas_call(body, out_shape=shapes if many else shapes[0], compiler_pa...]
    ppermute x9, starting transfers between devices: 16.4 us -> 25.4 us  [turned(): lax.ppermute(values, 'z', [(n, (n + way) % size) for n in range(size)])]
    dot_general x2, matrix products: 8.44 us -> 14.7 us  [the longest x1 10.1 us: local(): lax.dot_general(fence(left, *far_sums), right, (((1,), (1,)), ((0,), (0,)...]
    another operation x9 -> x0, local copies, waits for them, and re-layouts: 5.47 us -> none  [local(): jnp.stack([gain_one, bias_one, output_bias, gain_two, bias_two, outer_bia...]
    ppermute x15, starting transfers between devices: 23.1 us -> 18.6 us  [other_chip(): return lax.ppermute(value, 'y', SWAP)]
    ppermute x2, waiting for transfers between devices: 11.1 us -> 15.1 us  [the longest x1 15.1 us: sum_first(): got = lax.ppermute(send, 'x', SWAP)]
  transfers between devices with their start and end apart: 58 -> 58, of which waited for: 12 -> 17; matrix products, arithmetic and copies ran while one was open for 6% -> 9% of each run, Pallas kernels for 42% -> 34%
where the time goes in v4:
time: 314 us; the launch traced here: 312 us
  Pallas kernels  135 us (43%)
  waiting for transfers between devices  71.3 us (23%)
  starting transfers between devices  55.2 us (18%)
  matrix products  14.7 us (5%)
  between operations  14.5 us (5%)
  other arithmetic  12.1 us (4%)
  local copies, waits for them, and re-layouts  10.2 us (3%)
    pallas_call x23, Pallas kernels, kernel_call(): pl.pallas_call(body, out_shape=shapes if many else shapes[0], compiler_pa...  134 us
    ppermute x15, waiting for transfers between devices, other_chip(): return lax.ppermute(value, 'y', SWAP)  29.6 us
    ppermute x9, starting transfers between devices, turned(): lax.ppermute(values, 'z', [(n, (n + way) % size) for n in range(size)])  25.4 us
    ppermute x9, waiting for transfers between devices, turned(): lax.ppermute(values, 'z', [(n, (n + way) % size) for n in range(size)])  19.1 us
    ppermute x15, starting transfers between devices, other_chip(): return lax.ppermute(value, 'y', SWAP)  18.6 us
    ppermute x1, waiting for transfers between devices, sum_first(): got = lax.ppermute(send, 'x', SWAP)  15.1 us
    dot_general x1, matrix products, local(): lax.dot_general(fence(left, *far_sums), right, (((1,), (1,)), ((0,), (0,)...  10.1 us
  transfers between devices with their start and end apart: 58, of which 17 were waited for; matrix products, arithmetic and copies ran while one was open for 9% of the time, Pallas kernels for 34%

profile of v4, /device:TPU:0, one launch (start us, length us, event | category | flops | bytes accessed | tf_op | source)
XLA Modules:
  0.0 312.5 jit_solution(13059860345617512112)
XLA Ops:
  9.4 10.4 %project.1 = (bf16[2048,768]{1,0:T(8,128)(2,1)}, bf16[3,128,2048]{2,1,0:T(8,128)(2,1)}, bf16[192,2048]{1,0:T(8,128)(2,1)}, bf16[3,80,2048]{2,1,0:T(8,128)(2,1)},...) custom-call(bf16[2048,768]{1,0:T(8,128)(2,1)} %bitcast.32, s32[1,2048]{1,0:T(1,128)S(1)} %copy-done.3, ...), custom_call_target="tpu_custom_call" | custom-call | flops 6000000000 | bytes 14000000 | tf_op jit(solution)/shard_map/project/pallas_call | solution.py:82
  19.8 9.9 %attend_forward.2 = (bf16[4,192,256]{2,1,0:T(8,128)(2,1)}, bf16[3,16,1024]{2,1,0:T(8,128)(2,1)}, bf16[192,256]{1,0:T(8,128)(2,1)}, bf16[192,256]{1,0:T(8,128)(2,...) custom-call(s32[1]{0:T(128)} %bitcast.refs_0_.me_ref, s32[1,2048]{1,0:T(1,128)S(1)} %copy-done.3, ...), custom_call_target="tpu_custom_call" | custom-call | flops 8999999488 | bytes 5000000 | tf_op jit(solution)/shard_map/attend_forward/pallas_call | solution.py:82
  35.1 11.7 %attend_forward.3 = (bf16[4,192,256]{2,1,0:T(8,128)(2,1)}, bf16[3,16,1024]{2,1,0:T(8,128)(2,1)}, bf16[192,256]{1,0:T(8,128)(2,1)}, bf16[192,256]{1,0:T(8,128)(2,...) custom-call(s32[1]{0:T(128)} %bitcast.refs_0_.me_ref, s32[1,2048]{1,0:T(1,128)S(1)} %copy-done.3, ...), custom_call_target="tpu_custom_call" | custom-call | flops 8999999488 | bytes 5000000 | tf_op jit(solution)/shard_map/attend_forward/pallas_call | solution.py:82
  67.0 6.5 %feed.4 = (bf16[2,2048,768]{2,1,0:T(8,128)(2,1)}, bf16[2,2048,768]{2,1,0:T(8,128)(2,1)}, bf16[512,768]{1,0:T(8,128)(2,1)}, bf16[512,768]{1,0:T(8,128)(2,1)}, bf1...) custom-call(s32[1]{0:T(128)} %bitcast.refs_0_.me_ref, ...), custom_call_target="tpu_custom_call" | custom-call | flops 5000000000 | bytes 8000000 | tf_op jit(solution)/shard_map/feed/pallas_call | solution.py:82
  73.5 6.5 %feed.5 = (bf16[2,2048,768]{2,1,0:T(8,128)(2,1)}, bf16[2,2048,768]{2,1,0:T(8,128)(2,1)}, bf16[512,768]{1,0:T(8,128)(2,1)}, bf16[512,768]{1,0:T(8,128)(2,1)}, bf1...) custom-call(s32[1]{0:T(128)} %bitcast.refs_0_.me_ref, ...), custom_call_target="tpu_custom_call", output_to_operand_aliasing={{0}: (7, {}), {1}: (8, {}), {2}: (9, {}), {3}: (10, {})} | custom-call | flops 5000000000 | bytes 8000000 | tf_op jit(solution)/shard_map/feed/pallas_call | solution.py:82
  80.6 6.5 %feed.6 = (bf16[2,2048,768]{2,1,0:T(8,128)(2,1)}, bf16[2,2048,768]{2,1,0:T(8,128)(2,1)}, bf16[512,768]{1,0:T(8,128)(2,1)}, bf16[512,768]{1,0:T(8,128)(2,1)}, bf1...) custom-call(s32[1]{0:T(128)} %bitcast.refs_0_.me_ref, ...), custom_call_target="tpu_custom_call", output_to_operand_aliasing={{0}: (7, {}), {1}: (8, {})} | custom-call | flops 5000000000 | bytes 8000000 | tf_op jit(solution)/shard_map/feed/pallas_call | solution.py:82
  87.1 6.5 %feed.7 = (bf16[2,2048,768]{2,1,0:T(8,128)(2,1)}, bf16[2,2048,768]{2,1,0:T(8,128)(2,1)}, bf16[512,768]{1,0:T(8,128)(2,1)}, bf16[512,768]{1,0:T(8,128)(2,1)}, bf1...) custom-call(s32[1]{0:T(128)} %bitcast.refs_0_.me_ref, ...), custom_call_target="tpu_custom_call", output_to_operand_aliasing={{0}: (7, {}), {1}: (8, {}), {2}: (9, {}), {3}: (10, {})} | custom-call | flops 5000000000 | bytes 8000000 | tf_op jit(solution)/shard_map/feed/pallas_call | solution.py:82
  100.4 10.1 %convolution_convert_fusion = bf16[2,768,768]{2,1,0:T(8,128)(2,1)} fusion(bf16[2,2048,768]{2,1,0:T(8,128)(2,1)} %fence.18, bf16[2,2048,768]{2,1,0:T(8,128)(2,1)} %get-tuple-element.198), kind=kOutput, calls=%fused_computation | convolution fusion | flops 4833017856 | bytes 14942208 | tf_op jit(solution)/shard_map/dot_general | solution.py:920
  111.1 6.3 %collective-permute-done.29.b2_ref = bf16[256,768]{1,0:T(8,128)(2,1)} collective-permute-done((bf16[256,768]{1,0:T(8,128)(2,1)}, bf16[256,768]{1,0:T(8,128)(2,1)}, u32[]{:S(2)}, u32[]{:S(2)}) %collective-permute-start.29) | collective-permute-done | bytes 393248 | tf_op jit(solution)/shard_map/ppermute | solution.py:779
  117.4 3.9 %middle_back.3 = (f32[256,768]{1,0:T(8,128)}, bf16[256,768]{1,0:T(8,128)(2,1)}, bf16[192,256]{1,0:T(8,128)(2,1)}, bf16[192,256]{1,0:T(8,128)(2,1)S(1)}, bf16[192...) custom-call(s32[1]{0:T(128)} %bitcast.refs_0_.me_ref, ...), custom_call_target="tpu_custom_call" | custom-call | flops 2000000000 | bytes 4000000 | tf_op jit(solution)/shard_map/middle_back/pallas_call | solution.py:82
  135.6 14.5 %attend_backward.2 = (bf16[192,1024]{1,0:T(8,128)(2,1)}, f32[192,2048]{1,0:T(8,128)}, f32[192,2048]{1,0:T(8,128)}) custom-call(s32[1]{0:T(128)} %bitcast.refs_0_.me_ref, s32[1,2048]{1,0:T(1,128)S(1)} %copy-done.4, s32[1,2048]{1,0:T(1,128)S(1)} %copy-done.4, bf16[3,128,2048]{2,1,0:T(8,128)(2,1)} %get-tuple-element.108.refs_3_, ...), custom_call_target="tpu_custom_call" | custom-call | flops 16000000000 | bytes 10000000 | tf_op jit(solution)/shard_map/attend_backward/pallas_call | solution.py:82
  151.3 3.9 %collective-permute-done.21 = bf16[512,768]{1,0:T(8,128)(2,1)} collective-permute-done((bf16[512,768]{1,0:T(8,128)(2,1)S(1)}, bf16[512,768]{1,0:T(8,128)(2,1)}, u32[]{:S(2)}, u32[]{:S(2)}) %collective-permute-start.21) | collective-permute-done | bytes 786464 | tf_op jit(solution)/shard_map/ppermute | solution.py:779
  159.6 17.7 %attend_backward.3.refs_1_.g_ref = bf16[576,2048]{1,0:T(8,128)(2,1)} custom-call(s32[1]{0:T(128)} %bitcast.refs_0_.me_ref, s32[1,2048]{1,0:T(1,128)S(1)} %copy-done.4, s32[1,2048]{1,0:T(1,128)S(1)} %copy-done.4, bf16[3,128,2048]{2,1,0:T(8,128)(2,1)} %get-tuple-element.108.refs_3_, bf16[3,16,1024]{2,1,0:T(8,128)(2,1)} %get-tuple-element.115.rest_0_.refs_4_, ...), custom_call_target="tpu_custom_call" | custom-call | flops 16000000000 | bytes 10000000 | tf_op jit(solution)/shard_map/attend_backward/pallas_call | solution.py:82
  180.8 4.6 %convolution_convert_fusion.1.g_ref = bf16[576,768]{1,0:T(8,128)(2,1)S(1)} fusion(bf16[576,2048]{1,0:T(8,128)(2,1)} %attend_backward.3.refs_1_.g_ref, bf16[2048,768]{1,0:T(8,128)(2,1)} %get-tuple-element.170), kind=kOutput, calls=%fused_computation.8 | convolution fusion | flops 1812381696 | bytes 6389760 | tf_op jit(solution)/shard_map/dot_general | solution.py:23
  190.1 4.9 %tail.2 = (bf16[512,768]{1,0:T(8,128)(2,1)}, bf16[512,768]{1,0:T(8,128)(2,1)S(1)}, f32[8,576]{1,0:T(8,128)}) custom-call(s32[1]{0:T(128)} %bitcast.refs_0_.me_ref, bf16[576,2048]{1,0:T(8,128)(2,1)} %attend_backward.3.refs_1_.g_ref, bf16[192,768]{1,0:T(8,128)(2,1)} %bitcast.43, bf16[192,768]{1,0:T(8,128)(2,1)} %bitcast.46, bf16[192,768]{1,0:T(8,128)(2,1)} %bitcast.49, ...), custom_call_target="tpu_custom_call" | custom-call | flops 2000000000 | bytes 4000000 | tf_op jit(solution)/shard_map/tail/pallas_call | solution.py:82
  198.8 15.1 %collective-permute-done.36.refs_2_ = bf16[384,768]{1,0:T(8,128)(2,1)S(1)} collective-permute-done((bf16[384,768]{1,0:T(8,128)(2,1)S(1)}, bf16[384,768]{1,0:T(8,128)(2,1)S(1)}, u32[]{:S(2)}, u32[]{:S(2)}) %collective-permute-start.36) | collective-permute-done | bytes 589856 | tf_op jit(solution)/shard_map/ppermute | solution.py:812
  216.6 5.2 %tail.3 = (bf16[512,768]{1,0:T(8,128)(2,1)}, bf16[512,768]{1,0:T(8,128)(2,1)}, f32[8,576]{1,0:T(8,128)}) custom-call(s32[1]{0:T(128)} %bitcast.refs_0_.me_ref, bf16[576,2048]{1,0:T(8,128)(2,1)} %attend_backward.3.refs_1_.g_ref, bf16[192,768]{1,0:T(8,128)(2,1)} %bitcast.44, bf16[192,768]{1,0:T(8,128)(2,1)} %bitcast.47, bf16[192,768]{1,0:T(8,128)(2,1)} %bitcast.50, ...), custom_call_target="tpu_custom_call" | custom-call | flops 2000000000 | bytes 4000000 | tf_op jit(solution)/shard_map/tail/pallas_call | solution.py:82
  222.1 4.7 %collective-permute-start.40 = (bf16[96,768]{1,0:T(8,128)(2,1)S(1)}, bf16[96,768]{1,0:T(8,128)(2,1)S(1)}, u32[]{:S(2)}, u32[]{:S(2)}) collective-permute-start(bf16[96,768]{1,0:T(8,128)(2,1)S(1)} %get-tuple-element.181), channel_id=1, source_target_pairs={{0,8},{8,16},{16,24},{24,0},{1,9},{9,17},{17,25},{25,1},{2,10},{10... | collective-permute-start | bytes 442376 | tf_op jit(solution)/shard_map/ppermute | solution.py:807
  234.8 11.3 %collective-permute-done.41 = bf16[96,768]{1,0:T(8,128)(2,1)S(1)} collective-permute-done((bf16[96,768]{1,0:T(8,128)(2,1)S(1)}, bf16[96,768]{1,0:T(8,128)(2,1)S(1)}, u32[]{:S(2)}, u32[]{:S(2)}) %collective-permute-start.41) | collective-permute-done | bytes 147488 | tf_op jit(solution)/shard_map/ppermute | solution.py:807
  246.5 10.5 %collective-permute-start.52 = (bf16[96,768]{1,0:T(8,128)(2,1)S(1)}, bf16[96,768]{1,0:T(8,128)(2,1)S(1)}, u32[]{:S(2)}, u32[]{:S(2)}) collective-permute-start(bf16[96,768]{1,0:T(8,128)(2,1)S(1)} %fence.17.rest_3_.refs_0_), channel_id=1, source_target_pairs={{0,8},{8,16},{16,24},{24,0},{1,9},{9,17},{17,25},{25,1},{2,10},{10... | collective-permute-start | bytes 442376 | tf_op jit(solution)/shard_map/ppermute | solution.py:807
  259.5 3.8 %final.1 = (bf16[512,768]{1,0:T(8,128)(2,1)S(1)}, f32[16,768]{1,0:T(8,128)}) custom-call(s32[1]{0:T(128)} %bitcast.refs_0_.me_ref, bf16[512,768]{1,0:T(8,128)(2,1)} %get-tuple-element.176.refs_2_.b0_ref, bf16[512,768]{1,0:T(8,128)(2,1)S(1)} %collective-permute-done.38.b1_ref, bf16[512,768]{1,0:T(8,128)(2,1)S(1)} %collective-permute-done.39.b2_ref, ...), custom_call_target="tpu_custom_call" | custom-call | flops 100000000 | bytes 5000000 | tf_op jit(solution)/shard_map/final/pallas_call | solution.py:82
  272.6 12.2 %collective-permute-done.47 = f32[8,768]{1,0:T(8,128)S(1)} collective-permute-done((f32[8,768]{1,0:T(8,128)S(1)}, f32[8,768]{1,0:T(8,128)S(1)}, u32[]{:S(2)}, u32[]{:S(2)}) %collective-permute-start.47) | collective-permute-done | bytes 24608 | tf_op jit(solution)/shard_map/ppermute | solution.py:779
  297.4 4.1 %place.3 = f32[2048,768]{1,0:T(8,128)} custom-call(s32[1]{0:T(128)} %bitcast.refs_0_.me_ref, bf16[512,768]{1,0:T(8,128)(2,1)S(1)} %get-tuple-element.183.p0_ref, bf16[512,768]{1,0:T(8,128)(2,1)S(1)} %collective-permute-done.43.p1_ref, bf16[512,768]{1,0:T(8,128)(2,1)S(1)} %collective-permute-done.44.p2_ref, bf16[512,768]{1,0:T(8,128)(2,1)S(1)} %collective-permute-done.45.p3_ref), custom_call_target="tpu_custom_call" | custom-call | flops 1000000 | bytes 9000000 | tf_op jit(solution)/shard_map/place/pallas_call | solution.py:82
  301.5 4.2 %fusion.8 = (f32[768,768]{1,0:T(8,128)}, f32[768,768]{1,0:T(8,128)}) fusion(bf16[1536,768]{1,0:T(8,128)(2,1)} %all-gather.2.cloned.1.call-done), kind=kLoop, calls=%fused_computation.35 | loop fusion | bytes 9437184 | tf_op jit(solution)/shard_map/slice | solution.py:982
  (195 shorter events, 103.0 us)
Async XLA Ops:
  7.2 182.9 %reduce-scatter.2.cloned.1.call-start = ((), (), s32[]{:S(2)}) async-start(), calls=%async_computation.1 | async-start | bytes 2654208 | tf_op jit(solution)/shard_map/reduce_scatter | solution.py:922
  30.3 20.3 %collective-permute-start.3 = (bf16[192,768]{1,0:T(8,128)(2,1)S(1)}, bf16[192,768]{1,0:T(8,128)(2,1)S(1)}, u32[]{:S(2)}, u32[]{:S(2)}) collective-permute-start(bf16[192,768]{1,0:T(8,128)(2,1)S(1)} %copy-done.14), channel_id=1, source_target_pairs={{0,1},{1,0},{2,3},{3,2},{4,5},{5,4},{6,7},{7,6},{8,9},{9,8},{10,11... | collective-permute-start | bytes 884744 | tf_op jit(solution)/shard_map/ppermute | solution.py:775
  30.4 20.2 %collective-permute-start.4 = (bf16[192,768]{1,0:T(8,128)(2,1)S(1)}, bf16[192,768]{1,0:T(8,128)(2,1)S(1)}, u32[]{:S(2)}, u32[]{:S(2)}) collective-permute-start(bf16[192,768]{1,0:T(8,128)(2,1)S(1)} %copy-done.14), channel_id=1, source_target_pairs={{0,2},{2,0},{1,3},{3,1},{4,6},{6,4},{5,7},{7,5},{8,10},{10,8},{9,1... | collective-permute-start | bytes 884744 | tf_op jit(solution)/shard_map/ppermute | solution.py:779
  94.3 27.1 %collective-permute-start.19 = (bf16[256,768]{1,0:T(8,128)(2,1)S(1)}, bf16[256,768]{1,0:T(8,128)(2,1)S(1)}, u32[]{:S(2)}, u32[]{:S(2)}) collective-permute-start(bf16[256,768]{1,0:T(8,128)(2,1)S(1)} %get-tuple-element.144), channel_id=1, source_target_pairs={{0,1},{1,0},{2,3},{3,2},{4,5},{5,4},{6,7},{7,6},{8,9},{9,8},{10,11... | collective-permute-start | bytes 1179656 | tf_op jit(solution)/shard_map/ppermute | solution.py:775
  97.5 24.2 %collective-permute-start.20 = (bf16[256,768]{1,0:T(8,128)(2,1)}, bf16[256,768]{1,0:T(8,128)(2,1)S(1)}, u32[]{:S(2)}, u32[]{:S(2)}) collective-permute-start(bf16[256,768]{1,0:T(8,128)(2,1)} %add_convert_fusion.2.refs_2_), channel_id=1, source_target_pairs={{0,2},{2,0},{1,3},{3,1},{4,6},{6,4},{5,7},{7,5},{8,10},{10,8},{9,1... | collective-permute-start | bytes 1179656 | tf_op jit(solution)/shard_map/ppermute | solution.py:779
  98.7 18.7 %collective-permute-start.29 = (bf16[256,768]{1,0:T(8,128)(2,1)}, bf16[256,768]{1,0:T(8,128)(2,1)}, u32[]{:S(2)}, u32[]{:S(2)}) collective-permute-start(bf16[256,768]{1,0:T(8,128)(2,1)} %add_convert_fusion.3.refs_1_), channel_id=1, source_target_pairs={{0,2},{2,0},{1,3},{3,1},{4,6},{6,4},{5,7},{7,5},{8,10},{10,8},{9,1... | collective-permute-start | bytes 1179656 | tf_op jit(solution)/shard_map/ppermute | solution.py:779
  100.4 29.3 %collective-permute-start.18 = (bf16[512,768]{1,0:T(8,128)(2,1)}, bf16[512,768]{1,0:T(8,128)(2,1)}, u32[]{:S(2)}, u32[]{:S(2)}) collective-permute-start(bf16[512,768]{1,0:T(8,128)(2,1)} %fence.13), channel_id=1, source_target_pairs={{0,1},{1,0},{2,3},{3,2},{4,5},{5,4},{6,7},{7,6},{8,9},{9,8},{10,11... | collective-permute-start | bytes 2359304 | tf_op jit(solution)/shard_map/ppermute | solution.py:775
  110.5 191.0 %all-gather.2.cloned.1.call-start = ((), (), s32[]{:S(2)}) async-start(), calls=%async_computation.2 | async-start | bytes 2654208 | tf_op jit(solution)/shard_map/all_gather | solution.py:947
  110.6 22.4 %collective-permute-start.17 = (bf16[512,768]{1,0:T(8,128)(2,1)}, bf16[512,768]{1,0:T(8,128)(2,1)S(1)}, u32[]{:S(2)}, u32[]{:S(2)}) collective-permute-start(bf16[512,768]{1,0:T(8,128)(2,1)} %fence.12), channel_id=1, source_target_pairs={{0,1},{1,0},{2,3},{3,2},{4,5},{5,4},{6,7},{7,6},{8,9},{9,8},{10,11... | collective-permute-start | bytes 2359304 | tf_op jit(solution)/shard_map/ppermute | solution.py:775
  129.7 20.5 %collective-permute-start.33 = (bf16[192,768]{1,0:T(8,128)(2,1)S(1)}, bf16[192,768]{1,0:T(8,128)(2,1)}, u32[]{:S(2)}, u32[]{:S(2)}) collective-permute-start(bf16[192,768]{1,0:T(8,128)(2,1)S(1)} %get-tuple-element.168), channel_id=1, source_target_pairs={{0,1},{1,0},{2,3},{3,2},{4,5},{5,4},{6,7},{7,6},{8,9},{9,8},{10,11... | collective-permute-start | bytes 884744 | tf_op jit(solution)/shard_map/ppermute | solution.py:775
  131.4 28.2 %collective-permute-start.34 = (bf16[192,768]{1,0:T(8,128)(2,1)S(1)}, bf16[192,768]{1,0:T(8,128)(2,1)S(1)}, u32[]{:S(2)}, u32[]{:S(2)}) collective-permute-start(bf16[192,768]{1,0:T(8,128)(2,1)S(1)} %get-tuple-element.169), channel_id=1, source_target_pairs={{0,1},{1,0},{2,3},{3,2},{4,5},{5,4},{6,7},{7,6},{8,9},{9,8},{10,11... | collective-permute-start | bytes 884744 | tf_op jit(solution)/shard_map/ppermute | solution.py:775
  131.7 26.1 %collective-permute-start.25 = (bf16[192,256]{1,0:T(8,128)(2,1)S(1)}, bf16[192,256]{1,0:T(8,128)(2,1)S(1)}, u32[]{:S(2)}, u32[]{:S(2)}) collective-permute-start(bf16[192,256]{1,0:T(8,128)(2,1)S(1)} %get-tuple-element.150), channel_id=1, source_target_pairs={{0,1},{1,0},{2,3},{3,2},{4,5},{5,4},{6,7},{7,6},{8,9},{9,8},{10,11... | collective-permute-start | bytes 294920 | tf_op jit(solution)/shard_map/ppermute | solution.py:775
  132.6 26.9 %collective-permute-start.26 = (bf16[192,256]{1,0:T(8,128)(2,1)S(1)}, bf16[192,256]{1,0:T(8,128)(2,1)S(1)}, u32[]{:S(2)}, u32[]{:S(2)}) collective-permute-start(bf16[192,256]{1,0:T(8,128)(2,1)S(1)} %get-tuple-element.151), channel_id=1, source_target_pairs={{0,2},{2,0},{1,3},{3,1},{4,6},{6,4},{5,7},{7,5},{8,10},{10,8},{9,1... | collective-permute-start | bytes 294920 | tf_op jit(solution)/shard_map/ppermute | solution.py:779
  132.9 22.3 %collective-permute-start.21 = (bf16[512,768]{1,0:T(8,128)(2,1)S(1)}, bf16[512,768]{1,0:T(8,128)(2,1)}, u32[]{:S(2)}, u32[]{:S(2)}) collective-permute-start(bf16[512,768]{1,0:T(8,128)(2,1)S(1)} %fence.14.refs_13_), channel_id=1, source_target_pairs={{0,2},{2,0},{1,3},{3,1},{4,6},{6,4},{5,7},{7,5},{8,10},{10,8},{9,1... | collective-permute-start | bytes 2359304 | tf_op jit(solution)/shard_map/ppermute | solution.py:779
  155.2 24.4 %collective-permute-start.35 = (bf16[192,768]{1,0:T(8,128)(2,1)S(1)}, bf16[192,768]{1,0:T(8,128)(2,1)}, u32[]{:S(2)}, u32[]{:S(2)}) collective-permute-start(bf16[192,768]{1,0:T(8,128)(2,1)S(1)} %add_convert_fusion.5.refs_17_), channel_id=1, source_target_pairs={{0,2},{2,0},{1,3},{3,1},{4,6},{6,4},{5,7},{7,5},{8,10},{10,8},{9,1... | collective-permute-start | bytes 884744 | tf_op jit(solution)/shard_map/ppermute | solution.py:779
  157.7 21.9 %collective-permute-start.23 = (bf16[512,768]{1,0:T(8,128)(2,1)S(1)}, bf16[512,768]{1,0:T(8,128)(2,1)S(1)}, u32[]{:S(2)}, u32[]{:S(2)}) collective-permute-start(bf16[512,768]{1,0:T(8,128)(2,1)S(1)} %fusion.3.p0_ref.refs_16_), channel_id=1, source_target_pairs={{0,2},{2,0},{1,3},{3,1},{4,6},{6,4},{5,7},{7,5},{8,10},{10,8},{9,1... | collective-permute-start | bytes 2359304 | tf_op jit(solution)/shard_map/ppermute | solution.py:779
  159.6 27.3 %collective-permute-start.22 = (bf16[512,768]{1,0:T(8,128)(2,1)S(1)}, bf16[512,768]{1,0:T(8,128)(2,1)S(1)}, u32[]{:S(2)}, u32[]{:S(2)}) collective-permute-start(bf16[512,768]{1,0:T(8,128)(2,1)S(1)} %fusion.3.p0_ref.refs_16_), channel_id=1, source_target_pairs={{0,1},{1,0},{2,3},{3,2},{4,5},{5,4},{6,7},{7,6},{8,9},{9,8},{10,11... | collective-permute-start | bytes 2359304 | tf_op jit(solution)/shard_map/ppermute | solution.py:775
  221.7 37.8 %collective-permute-start.38 = (bf16[512,768]{1,0:T(8,128)(2,1)}, bf16[512,768]{1,0:T(8,128)(2,1)S(1)}, u32[]{:S(2)}, u32[]{:S(2)}) collective-permute-start(bf16[512,768]{1,0:T(8,128)(2,1)} %get-tuple-element.177), channel_id=1, source_target_pairs={{0,1},{1,0},{2,3},{3,2},{4,5},{5,4},{6,7},{7,6},{8,9},{9,8},{10,11... | collective-permute-start | bytes 2359304 | tf_op jit(solution)/shard_map/ppermute | solution.py:775
  221.7 37.8 %collective-permute-start.39 = (bf16[512,768]{1,0:T(8,128)(2,1)S(1)}, bf16[512,768]{1,0:T(8,128)(2,1)S(1)}, u32[]{:S(2)}, u32[]{:S(2)}) collective-permute-start(bf16[512,768]{1,0:T(8,128)(2,1)S(1)} %add_convert_fusion.refs_3_), channel_id=1, source_target_pairs={{0,2},{2,0},{1,3},{3,1},{4,6},{6,4},{5,7},{7,5},{8,10},{10,8},{9,1... | collective-permute-start | bytes 2359304 | tf_op jit(solution)/shard_map/ppermute | solution.py:779
  226.8 19.2 %collective-permute-start.41 = (bf16[96,768]{1,0:T(8,128)(2,1)S(1)}, bf16[96,768]{1,0:T(8,128)(2,1)S(1)}, u32[]{:S(2)}, u32[]{:S(2)}) collective-permute-start(bf16[96,768]{1,0:T(8,128)(2,1)S(1)} %get-tuple-element.182), channel_id=1, source_target_pairs={{0,16},{8,24},{16,0},{24,8},{1,17},{9,25},{17,1},{25,9},{2,18},{10... | collective-permute-start | bytes 442376 | tf_op jit(solution)/shard_map/ppermute | solution.py:807
  227.9 18.6 %collective-permute-start.42 = (bf16[96,768]{1,0:T(8,128)(2,1)S(1)}, bf16[96,768]{1,0:T(8,128)(2,1)S(1)}, u32[]{:S(2)}, u32[]{:S(2)}) collective-permute-start(bf16[96,768]{1,0:T(8,128)(2,1)S(1)} %get-tuple-element.175.rest_0_), channel_id=1, source_target_pairs={{0,24},{8,0},{16,8},{24,16},{1,25},{9,1},{17,9},{25,17},{2,26},{10... | collective-permute-start | bytes 442376 | tf_op jit(solution)/shard_map/ppermute | solution.py:807
  246.5 19.1 %collective-permute-start.52 = (bf16[96,768]{1,0:T(8,128)(2,1)S(1)}, bf16[96,768]{1,0:T(8,128)(2,1)S(1)}, u32[]{:S(2)}, u32[]{:S(2)}) collective-permute-start(bf16[96,768]{1,0:T(8,128)(2,1)S(1)} %fence.17.rest_3_.refs_0_), channel_id=1, source_target_pairs={{0,8},{8,16},{16,24},{24,0},{1,9},{9,17},{17,25},{25,1},{2,10},{10... | collective-permute-start | bytes 442376 | tf_op jit(solution)/shard_map/ppermute | solution.py:807
  264.3 21.8 %collective-permute-start.44 = (bf16[512,768]{1,0:T(8,128)(2,1)S(1)}, bf16[512,768]{1,0:T(8,128)(2,1)S(1)}, u32[]{:S(2)}, u32[]{:S(2)}) collective-permute-start(bf16[512,768]{1,0:T(8,128)(2,1)S(1)} %get-tuple-element.183.p0_ref), channel_id=1, source_target_pairs={{0,2},{2,0},{1,3},{3,1},{4,6},{6,4},{5,7},{7,5},{8,10},{10,8},{9,1... | collective-permute-start | bytes 2359304 | tf_op jit(solution)/shard_map/ppermute | solution.py:779
  268.9 22.7 %collective-permute-start.55 = (bf16[384,768]{1,0:T(8,128)(2,1)S(1)}, bf16[384,768]{1,0:T(8,128)(2,1)S(1)}, u32[]{:S(2)}, u32[]{:S(2)}) collective-permute-start(bf16[384,768]{1,0:T(8,128)(2,1)S(1)} %whole.1.mine_ref), channel_id=1, source_target_pairs={{0,4},{4,0},{1,5},{5,1},{2,6},{6,2},{3,7},{7,3},{8,12},{12,8},{9,1... | collective-permute-start | bytes 1769480 | tf_op jit(solution)/shard_map/ppermute | solution.py:831
  (52 other events, 435.1 us)
Sparse Core Ops, SparseCore 0:
  110.6 70.1 reduce-scatter.1
  190.3 67.6 all-gather.1

commit v5 on v4

--- a/solution.py
+++ b/solution.py
@@ -32,9 +32,10 @@
 
 
 def stats(values):
-    center = values - jnp.mean(values, axis=-1, keepdims=True)
+    mean = jnp.mean(values, axis=-1, keepdims=True)
+    center = values - mean
     scale = lax.rsqrt(jnp.mean(center * center, axis=-1, keepdims=True) + 1e-05)
-    return center * scale, scale
+    return center * scale, scale, mean
 
 
 def norm_back(grad_out, normed, scale, gain):
@@ -89,11 +90,13 @@
 
 
 def project_body(x_ref, seg_ref, vec_ref, wq_ref, wk_ref, wv_ref,
-                 ai_ref, qt_ref, kt_ref, vt_ref, kn_ref, vn_ref):
+                 ai_ref, qt_ref, kt_ref, vt_ref, kn_ref, vn_ref, stat_ref):
     heads = kn_ref.shape[0]
     width = heads * HEAD
     tile = x_ref.shape[0]
-    normed, _ = stats(x_ref[...].astype(F32))
+    normed, scale, mean = stats(x_ref[...].astype(F32))
+    lane = lax.broadcasted_iota(jnp.int32, stat_ref.shape, 1)
+    stat_ref[...] = jnp.where(lane == 0, mean, scale)
     ai = (normed * vec_ref[0:1, :] + vec_ref[1:2, :]).astype(BF16)
     ai_ref[...] = ai
     column = vec_ref[...].T[:2 * width, 6:7]
@@ -135,6 +138,7 @@
             pl.BlockSpec((heads, HEAD + 16, TILE), lambda i: (0, 0, i)),
             pl.BlockSpec((heads, TILE, WIDE), lambda i: (0, i, 0)),
             pl.BlockSpec((heads, TILE, WIDE), lambda i: (0, i, 0)),
+            pl.BlockSpec((TILE, WIDE), lambda i: (i, 0)),
         ],
         out_shape=[
             shape_of(length, features),
@@ -143,6 +147,7 @@
             shape_of(heads, HEAD + 16, length),
             shape_of(heads, length, WIDE),
             shape_of(heads, length, WIDE),
+            shape_of(length, WIDE, dtype=F32),
         ],
         cost_estimate=cost(6e9, 14e6),
         name="project",
@@ -368,7 +373,7 @@
         total = total + tn(m_ref[...], w_ref[...])
         mixed_ref[n] = m_ref[...]
     residual_ref[...] = total
-    normed, _ = stats(total)
+    normed, _, _ = stats(total)
     own_ref[...] = (normed * vec_ref[3:4, :] + vec_ref[4:5, :]).astype(BF16)
 
 
@@ -466,7 +471,7 @@
 def back_body(me_ref, b0_ref, b1_ref, b2_ref, residual_ref, g_ref, vec_ref, w0_ref, w1_ref, w2_ref, w3_ref,
               grad_ref, low_ref, a0_ref, a1_ref, a2_ref, a3_ref, sum_ref):
     grad_mid = b0_ref[...].astype(F32) + b1_ref[...].astype(F32) + b2_ref[...].astype(F32)
-    normed, scale = stats(residual_ref[...])
+    normed, scale, _ = stats(residual_ref[...])
     upstream = g_ref[...].astype(F32)
     grad = upstream + norm_back(grad_mid, normed, scale, vec_ref[3:4, :])
     grad_ref[...] = grad
@@ -523,47 +528,91 @@
     )
 
 
-def tail_body(me_ref, g_ref, wq_ref, wk_ref, wv_ref, *rest):
-    o0_ref, o1_ref, sum_ref = rest[-3:]
+def tail_body(me_ref, g_ref, wq_ref, wk_ref, wv_ref, x_ref, stat_ref, *rest):
+    early = rest[:PARTS]
+    o0_ref, o1_ref, o2_ref, o3_ref, row_ref, vec_ref, sum_ref = rest[-7:]
     i, p = pl.program_id(0), pl.program_id(1)
     grads = g_ref[...]
     width = wq_ref.shape[0]
     value = tn(grads[:width], wq_ref[...]) + tn(grads[width:2 * width], wk_ref[...])
-    value = (value + tn(grads[2 * width:], wv_ref[...])).astype(BF16)
-    sums = nt(jnp.ones((8, grads.shape[1]), BF16), grads)
+    value = value + tn(grads[2 * width:], wv_ref[...])
 
     @pl.when((i == 0) & (p == 0))
     def _():
+        row_ref[...] = jnp.zeros_like(row_ref)
         sum_ref[...] = jnp.zeros_like(sum_ref)
 
-    sum_ref[...] += sums
-    for step, o_ref in enumerate((o1_ref, o0_ref)):
+    row_ref[...] += nt(jnp.ones((8, grads.shape[1]), BF16), grads)
+    normed = (x_ref[...].astype(F32) - stat_ref[:, 0:1]) * stat_ref[:, 1:2]
+    sum_ref[:8] += fold(value * normed)
+    sum_ref[8:] += fold(value)
+    value = value.astype(BF16)
+    for step, o_ref in enumerate((o3_ref, o2_ref, o1_ref, o0_ref)):
         @pl.when(i == step)
         def _(o_ref=o_ref):
             o_ref[pl.ds(pl.multiple_of(p * TILE, TILE), TILE), :] = value
 
-
-def tail(base, me, grads, wq, wk, wv, after):
+    @pl.when((i == 3) & (p == PARTS - 1))
+    def _():
+        row = lax.broadcasted_iota(jnp.int32, vec_ref.shape, 0)
+        vectors = jnp.zeros(vec_ref.shape, F32)
+        before = early[0][...]
+        for ref in early[1:]:
+            before = before + ref[...]
+        parts = [before[8 * n:8 * n + 8] for n in range(4)] + [sum_ref[:8], sum_ref[8:]]
+        for n, part in enumerate(parts):
+            vectors = jnp.where(row == n, jnp.sum(part, axis=0, keepdims=True), vectors)
+        vec_ref[...] = vectors
+        o3_ref[PARTS * TILE:] = paired(vectors)
+
+
+def tail(me, grads, wq, wk, wv, tokens, stat, early, after):
     deep = grads.shape[0]
     features = wq.shape[1]
     share = const((PARTS * TILE, features))
+    more = const((PARTS * TILE + 16, features))
+    at = lambda i, p, m: 4 * p + (m[0] ^ (3 - i))
     return kernel_call(
         tail_body,
-        (me, grads, wq, wk, wv, *after),
-        free_in=tuple(range(5, 5 + len(after))),
-        free_out=(1,),
+        (me, grads, wq, wk, wv, tokens, stat, *early, *after),
+        free_in=tuple(range(7 + PARTS, 7 + PARTS + len(after))),
+        free_out=(1, 3),
         grid_spec=pltpu.PrefetchScalarGridSpec(
             num_scalar_prefetch=1,
-            grid=(2, PARTS),
-            in_specs=[pl.BlockSpec((deep, TILE), lambda i, p, m: (0, 4 * p + (m[0] ^ (base + 1 - i)))),
-                      const(wq.shape), const(wk.shape), const(wv.shape)]
-            + [pl.BlockSpec(memory_space=pl.ANY)] * len(after),
-            out_specs=[share] * 2 + [const((8, deep))],
-        ),
-        out_shape=[shape_of(PARTS * TILE, features)] * 2 + [shape_of(8, deep, dtype=F32)],
-        cost_estimate=cost(2e9, 4e6),
+            grid=(4, PARTS),
+            in_specs=[pl.BlockSpec((deep, TILE), lambda i, p, m: (0, at(i, p, m))),
+                      const(wq.shape), const(wk.shape), const(wv.shape),
+                      pl.BlockSpec((TILE, features), lambda i, p, m: (at(i, p, m), 0)),
+                      pl.BlockSpec((TILE, WIDE), lambda i, p, m: (at(i, p, m), 0))]
+            + [const(v.shape) for v in early] + [pl.BlockSpec(memory_space=pl.ANY)] * len(after),
+            out_specs=[share, share, share, more, const((8, deep)), const((8, features))],
+            scratch_shapes=[pltpu.VMEM((16, features), F32)],
+        ),
+        out_shape=[shape_of(PARTS * TILE, features)] * 3 + [shape_of(PARTS * TILE + 16, features)]
+        + [shape_of(8, deep, dtype=F32), shape_of(8, features, dtype=F32)],
+        cost_estimate=cost(4e9, 10e6),
         name="tail",
     )
+
+
+def chip_body(one_ref, two_ref, vec_ref, out_ref):
+    rows = one_ref.shape[0]
+    out_ref[:rows] = (one_ref[...].astype(F32) + two_ref[:rows].astype(F32)).astype(BF16)
+    out_ref[rows:] = paired(vec_ref[...] + joined(two_ref[rows:]))
+
+
+def chip_sum(one, two, vectors):
+    return kernel_call(
+        chip_body,
+        (one, two, vectors),
+        free_in=(1,),
+        free_out=(0,),
+        grid=(1,),
+        in_specs=[const(one.shape), const(two.shape), const(vectors.shape)],
+        out_specs=[const(two.shape)],
+        out_shape=[shape_of(*two.shape)],
+        name="chip_sum",
+    )[0]
 
 
 def halves_body(xz_ref, g_ref, go_ref, keep_ref, send_ref):
@@ -617,7 +666,6 @@
         body,
         (xz, one, two, *after),
         free_in=(2,) + tuple(range(3, 3 + len(after))),
-        free_out=tuple(range(count)),
         grid_spec=pltpu.PrefetchScalarGridSpec(
             num_scalar_prefetch=1,
             grid=(count,),
@@ -630,48 +678,91 @@
     )
 
 
-def whole_body(xz_ref, *refs):
+def paired(value):
+    return jnp.concatenate(split(value, 2), axis=0).astype(BF16)
+
+
+def joined(both):
+    both = both.astype(F32)
+    half = both.shape[0] // 2
+    return both[:half] + both[half:]
+
+
+def second_body(total_ref, one_ref, two_ref, apart_ref, out_ref):
+    rows = total_ref.shape[0]
+    out_ref[:rows] = total_ref[...]
+    shared = joined(one_ref[...]) + joined(two_ref[...])
+    out_ref[rows:] = paired(jnp.concatenate([shared, apart_ref[...]], axis=0))
+
+
+def second(total, one, two, apart):
+    rows, features = total.shape
+    last = pl.BlockSpec((16, features), lambda i: (one.shape[0] // 16 - 1, 0))
+    return kernel_call(
+        second_body,
+        (total, one, two, apart),
+        free_in=(0, 1, 2),
+        free_out=(0,),
+        grid=(1,),
+        in_specs=[const(total.shape), last, last, const(apart.shape)],
+        out_specs=[const((rows + 32, features))],
+        out_shape=[shape_of(rows + 32, features)],
+        name="second",
+    )[0]
+
+
+def third_body(count, xz_ref, *refs):
     out_ref = refs[-1]
-    for n, in_ref in enumerate(refs[:-1]):
-        @pl.when(pl.program_id(0) == n)
-        def _(in_ref=in_ref):
-            out_ref[...] = in_ref[...]
-
-
-def whole(xz, pieces):
+    step = out_ref.shape[0] - (refs[0].shape[0] * count - out_ref.shape[0]) // (count - 1)
+    rows = step // count
+    sums = None
+    for n, ref in enumerate(refs[:count]):
+        place_at = lax.rem(xz_ref[1] + count - n, count)
+        out_ref[pl.ds(pl.multiple_of(place_at * rows, rows), rows), :] = ref[:rows]
+        value = joined(ref[rows:])
+        sums = value if sums is None else sums + value
+    out_ref[step:] = paired(sums)
+
+
+def third(xz, pieces, extra):
     count = len(pieces)
     rows, features = pieces[0].shape
-    return kernel_call(
-        whole_body,
+    total = (rows - extra) * count + extra
+
+    def body(*refs):
+        third_body(count, *refs)
+
+    return kernel_call(
+        body,
         (xz, *pieces),
         free_in=tuple(range(1, count + 1)),
-        free_out=(0,),
         grid_spec=pltpu.PrefetchScalarGridSpec(
             num_scalar_prefetch=1,
-            grid=(count,),
+            grid=(1,),
             in_specs=[const((rows, features))] * count,
-            out_specs=pl.BlockSpec((rows, features), lambda i, m: ((m[1] + count - i) % count, 0)),
-        ),
-        out_shape=shape_of(rows * count, features),
-        cost_estimate=cost(1e6, 2e6),
-        name="whole",
-    )
+            out_specs=[const((total, features))],
+        ),
+        out_shape=[shape_of(total, features)],
+        name="third",
+    )[0]
 
 
 def ready_body(xz_ref, mine_ref, other_ref, *rest):
-    outs = rest[-4:]
+    outs = rest[-5:]
+    small_ref = outs[4]
     width = outs[0].shape[0]
-    for n, out_ref in enumerate(outs):
+    for n, out_ref in enumerate(outs[:4]):
         rows = slice(n % 2 * width, (n % 2 + 1) * width)
         for to_ref, chosen in ((mine_ref, xz_ref[0] == n // 2), (other_ref, xz_ref[0] != n // 2)):
             @pl.when(chosen)
             def _(to_ref=to_ref, out_ref=out_ref, rows=rows):
                 out_ref[...] = to_ref[rows].astype(F32)
 
-
-def ready(xz, mine, other, after):
+    small_ref[...] = joined(mine_ref[2 * width:]) + joined(other_ref[2 * width:])
+
+
+def ready(xz, mine, other, width, count, after):
     rows, features = mine.shape
-    width = rows // 2
     return kernel_call(
         ready_body,
         (xz, mine, other, *after),
@@ -680,31 +771,24 @@
             num_scalar_prefetch=1,
             grid=(1,),
             in_specs=[const(mine.shape), const(other.shape)] + [pl.BlockSpec(memory_space=pl.ANY)] * len(after),
-            out_specs=[const((width, features))] * 4,
-        ),
-        out_shape=[shape_of(width, features, dtype=F32)] * 4,
+            out_specs=[const((width, features))] * 4 + [const((count, features))],
+        ),
+        out_shape=[shape_of(width, features, dtype=F32)] * 4 + [shape_of(count, features, dtype=F32)],
         cost_estimate=cost(1e6, 4e6),
         name="ready",
     )
 
 
 def final_body(me_ref, b0_ref, b1_ref, b2_ref, x_ref, *rest):
-    grad_refs, vec_ref, (out_ref, sum_ref) = rest[:PARTS], rest[PARTS], rest[-2:]
+    grad_refs, vec_ref, out_ref = rest[:PARTS], rest[PARTS], rest[-1]
     p = pl.program_id(0)
     grad_attend = b0_ref[...].astype(F32) + b1_ref[...].astype(F32) + b2_ref[...].astype(F32)
-    normed, scale = stats(x_ref[...].astype(F32))
+    normed, scale, _ = stats(x_ref[...].astype(F32))
     back = norm_back(grad_attend, normed, scale, vec_ref[0:1, :])
     for n, grad_ref in enumerate(grad_refs):
         @pl.when(p == n)
         def _(grad_ref=grad_ref):
             out_ref[...] = (grad_ref[...] + back).astype(BF16)
-
-    @pl.when(p == 0)
-    def _():
-        sum_ref[...] = jnp.zeros_like(sum_ref)
-
-    sum_ref[:8] += fold(grad_attend * normed)
-    sum_ref[8:] += fold(grad_attend)
 
 
 def final(me, sums, tokens, grads, vectors, after):
@@ -721,15 +805,16 @@
             in_specs=[rows] * 3 + [pl.BlockSpec((TILE, features), lambda p, m: (4 * p + m[0], 0))]
             + [const((TILE, features))] * PARTS + [const(vectors.shape)]
             + [pl.BlockSpec(memory_space=pl.ANY)] * len(after),
-            out_specs=[rows, const((16, features))],
-        ),
-        out_shape=[shape_of(PARTS * TILE, features), shape_of(16, features, dtype=F32)],
+            out_specs=[rows],
+        ),
+        out_shape=[shape_of(PARTS * TILE, features)],
         cost_estimate=cost(1e8, 5e6),
         name="final",
-    )
-
-
-def place_body(me_ref, p0_ref, p1_ref, p2_ref, p3_ref, out_ref):
+    )[0]
+
+
+def place_body(me_ref, p0_ref, p1_ref, p2_ref, p3_ref, *rest):
+    out_ref = rest[-1]
     for step, p_ref in enumerate((p0_ref, p1_ref, p2_ref, p3_ref)):
         @pl.when(pl.program_id(0) == step)
         def _(p_ref=p_ref):
@@ -737,16 +822,16 @@
             out_ref[...] = p_ref[at, :].astype(out_ref.dtype)
 
 
-def place(me, shares, dtype):
+def place(me, shares, dtype, after):
     rows, features = shares[0].shape
     return kernel_call(
         place_body,
-        (me, *shares),
-        free_in=(1, 2, 3, 4),
+        (me, *shares, *after),
+        free_in=tuple(range(1, 5 + len(after))),
         grid_spec=pltpu.PrefetchScalarGridSpec(
             num_scalar_prefetch=1,
             grid=(4, PARTS),
-            in_specs=[const((rows, features))] * 4,
+            in_specs=[const((rows, features))] * 4 + [pl.BlockSpec(memory_space=pl.ANY)] * len(after),
             out_specs=pl.BlockSpec((TILE, features), lambda i, p, m: (4 * p + (m[0] ^ i), 0)),
         ),
         out_shape=shape_of(4 * rows, features, dtype=dtype),
@@ -807,9 +892,8 @@
     return lax.ppermute(values, "z", [(n, (n + way) % size) for n in range(size)])
 
 
-def sum_first(xz, keep, send, after):
+def sum_first(xz, keep, got, after):
     size = lax.axis_size("z")
-    got = lax.ppermute(send, "x", SWAP)
     if size > 4:
         return [lax.psum(keep + got, "z")]
     return quarters(xz, keep, got, size, after)
@@ -822,24 +906,11 @@
     return total.astype(BF16)
 
 
-def sum_third(xz, total):
+def gather_z(value):
     size = lax.axis_size("z")
     if size > 4:
-        keep = total
-    else:
-        keep = whole(xz, [turned(total, way) if way else total for way in range(size)])
-    return keep, lax.ppermute(keep, "x", SWAP)
-
-
-def sum_small(value):
-    size = lax.axis_size("z")
-    if size > 4:
-        return lax.psum(value, DP)
-    value = value + lax.ppermute(value, "x", SWAP)
-    total = value
-    for way in range(1, size):
-        total = total + turned(value, way)
-    return total
+        return [lax.all_gather(value, "z", axis=0, tiled=True)]
+    return [turned(value, way) if way else value for way in range(size)]
 
 
 def local(
@@ -875,7 +946,7 @@
     wq, wk, wv = query_weight.T, key_weight.T, value_weight.T
 
     output_weights = exchange([output_weight] * 4)
-    attend_in, qt, kt, vt, kn, vn = project(tokens, segment_ids, vectors, wq, wk, wv, heads)
+    attend_in, qt, kt, vt, kn, vn, stat = project(tokens, segment_ids, vectors, wq, wk, wv, heads)
 
     parts = range(PARTS)
     attended, extras, fours = [], [], []
@@ -936,33 +1007,38 @@
                             (result, part_far, part_near))
 
     xz = jnp.stack([lax.axis_index("x"), lax.axis_index("z")]).astype(jnp.int32)
-    grad_output = fence(part[0], grads).astype(F32) + part_near.astype(F32) + other_chip(part_far).astype(F32)
+    near, far = other_core(result), other_chip(result)
+    part_across = other_chip(part_far)
+    back_own, back_near, back_far, back_across, row_sum, summed = tail(
+        me, grads, wq, wk, wv, tokens, stat, inner_sums, (near, far, part_across)
+    )
+    grads = fence(grads, row_sum)
+    feed_sum = lax.all_gather(fence(feed_sum, row_sum), DP, axis=0, tiled=True)
+    feed_sum = (feed_sum[:features].astype(F32), feed_sum[features:].astype(F32))
+    grad_output = fence(part[0], row_sum).astype(F32) + part_near.astype(F32) + part_across.astype(F32)
     keep, send = halves(xz, nn(grads, attend_in).astype(BF16), grad_output.astype(BF16))
-    near, far = other_core(result), other_chip(result)
-    back_far, back_across, sum_far = tail(2, me, grads, wq, wk, wv, (near, far, send))
-    back_far = (back_far.astype(F32) + other_core(back_across).astype(F32)).astype(BF16)
-    quarter = sum_first(xz, keep, send, (back_far,))
-    back_own, back_near, sum_near = tail(0, me, grads, wq, wk, wv, quarter[-1:])
-    layer_out = place(me, [result, near, far, other_core(far)], BF16)
-    feed_sum = lax.all_gather(fence(feed_sum, layer_out), DP, axis=0, tiled=True).astype(F32)
-    total = fence(sum_second(quarter), layer_out, back_own, space=pltpu.VMEM)
-    arrived = [back_own, other_core(back_near), other_chip(back_far)]
-    share, outer_sums = final(me, arrived, tokens, grad_residuals, vectors, (total,))
-    mine, other = sum_third(xz, total)
-    wide = ready(xz, mine, other, ())
-    input_grad = place(me, spread(share), F32)
-
-    fold_rows = lambda v: jnp.sum(v.reshape(-1, 8, v.shape[-1]), axis=1)
-    shared = jnp.concatenate([fold_rows(sum(inner_sums)), fold_rows(outer_sums), jnp.zeros((2, features), F32)])
-    shared = shared + other_core(shared)
-    shared = shared + other_chip(shared)
-    row_sum = (sum_far + sum_near)[:1]
+    back_far = chip_sum(back_far, other_core(back_across), summed)
+    back_there = other_chip(back_far)
+    got = lax.ppermute(send, "x", SWAP)
+    quarter = sum_first(xz, keep, got, (back_far,))
+    layer_out = place(me, [result, near, far, other_core(far)], BF16, quarter[-1:])
+    row_sum = row_sum[:1]
     apart = jnp.concatenate([
         jnp.sum(sum(sums), axis=0, keepdims=True),
         jnp.pad(row_sum, ((0, 0), (0, features - row_sum.shape[1]))),
         jnp.zeros((6, features), F32),
     ])
-    small = sum_small(jnp.concatenate([shared, apart]))
+    total = sum_second(quarter)
+    if len(quarter) > 1:
+        held = second(total, back_far, back_there, apart)
+        mine = third(xz, gather_z(held), 32)
+    else:
+        small = jnp.concatenate([joined(back_far[-16:]) + joined(back_there[-16:]), apart])
+        held = mine = jnp.concatenate([total, paired(lax.psum(small, "z"))])
+    share = final(me, [back_own, other_core(back_near), back_there], tokens, grad_residuals, vectors, (layer_out, held))
+    near, far = other_core(share), fence(other_chip(share), mine, space=pltpu.VMEM)
+    input_grad = place(me, [share, near, far, other_core(far)], F32, (mine,))
+    *wide, small = ready(xz, mine, lax.ppermute(mine, "x", SWAP), width, 16, feed_sum)
     return (
         layer_out.reshape(1, length, features),
         input_grad.reshape(1, length, features),
@@ -977,9 +1053,9 @@
         small[2],
         small[0],
         small[1],
-        feed_sum[features:],
+        feed_sum[1],
         small[8],
-        feed_sum[:features],
+        feed_sum[0],
         small[3],
     )
 

time: 314 us -> 301 us (0.959)
  starting transfers between devices: 55.2 us -> 46.7 us
  waiting for transfers between devices: 71.3 us -> 64.1 us
    ppermute x15 -> x14, waiting for transfers between devices: 29.6 us -> 13.1 us  [other_chip(): return lax.ppermute(value, 'y', SWAP)]
    ppermute x9 -> x6, starting transfers between devices: 25.4 us -> 17.7 us  [turned(): lax.ppermute(values, 'z', [(n, (n + way) % size) for n in range(size)])]
    ppermute x3 -> x2, waiting for transfers between devices: 17.6 us -> 23.7 us  [the longest x1 14.5 us: local(): got = lax.ppermute(send, 'x', SWAP)]
    ppermute x9 -> x6, waiting for transfers between devices: 19.1 us -> 24.6 us  [turned(): lax.ppermute(values, 'z', [(n, (n + way) % size) for n in range(size)])]
    unnamed x36 -> x54, local copies, waits for them, and re-layouts: 3.16 us -> 7.75 us
    slice x1, local copies, waits for them, and re-layouts: 4.17 us -> 0.73 us  [local(): row_sum = row_sum[:1]]
    pallas_call x23 -> x24, Pallas kernels: 134 us -> 137 us  [kernel_call(): pl.pallas_call(body, out_shape=shapes if many else shapes[0], compiler_pa...]
    ppermute x15 -> x14, starting transfers between devices: 18.6 us -> 18 us  [other_chip(): return lax.ppermute(value, 'y', SWAP)]
  transfers between devices with their start and end apart: 58 -> 52, of which waited for: 17 -> 15; matrix products, arithmetic and copies ran while one was open for 9% -> 8% of each run, Pallas kernels for 34% -> 37%
where the time goes in v5:
time: 301 us; the launch traced here: 299 us
  Pallas kernels  137 us (46%)
  waiting for transfers between devices  64.1 us (21%)
  starting transfers between devices  46.7 us (16%)
  matrix products  14.7 us (5%)
  between operations  14.5 us (5%)
  local copies, waits for them, and re-layouts  13.1 us (4%)
  other arithmetic  9.63 us (3%)
    pallas_call x24, Pallas kernels, kernel_call(): pl.pallas_call(body, out_shape=shapes if many else shapes[0], compiler_pa...  137 us
    ppermute x6, waiting for transfers between devices, turned(): lax.ppermute(values, 'z', [(n, (n + way) % size) for n in range(size)])  24.6 us
    ppermute x14, starting transfers between devices, other_chip(): return lax.ppermute(value, 'y', SWAP)  18 us
    ppermute x6, starting transfers between devices, turned(): lax.ppermute(values, 'z', [(n, (n + way) % size) for n in range(size)])  17.7 us
    ppermute x1, waiting for transfers between devices, local(): got = lax.ppermute(send, 'x', SWAP)  14.5 us
    ppermute x14, waiting for transfers between devices, other_chip(): return lax.ppermute(value, 'y', SWAP)  13.1 us
    dot_general x1, matrix products, local(): lax.dot_general(fence(left, *far_sums), right, (((1,), (1,)), ((0,), (0,)...  10.1 us
    ppermute x1, waiting for transfers between devices, local(): lax.ppermute(mine, 'x', SWAP)  9.2 us
  transfers between devices with their start and end apart: 52, of which 15 were waited for; matrix products, arithmetic and copies ran while one was open for 8% of the time, Pallas kernels for 37%

profile of v5, /device:TPU:0, one launch (start us, length us, event | category | flops | bytes accessed | tf_op | source)
XLA Modules:
  0.0 299.5 jit_solution(6317433970105411699)
XLA Ops:
  9.5 10.6 %project.1 = (bf16[2048,768]{1,0:T(8,128)(2,1)}, bf16[3,128,2048]{2,1,0:T(8,128)(2,1)}, bf16[192,2048]{1,0:T(8,128)(2,1)}, bf16[3,80,2048]{2,1,0:T(8,128)(2,1)},...) custom-call(bf16[2048,768]{1,0:T(8,128)(2,1)} %bitcast.28, ...), custom_call_target="tpu_custom_call" | custom-call | flops 6000000000 | bytes 14000000 | tf_op jit(solution)/shard_map/project/pallas_call | solution.py:83
  20.0 9.9 %attend_forward.2 = (bf16[4,192,256]{2,1,0:T(8,128)(2,1)}, bf16[3,16,1024]{2,1,0:T(8,128)(2,1)}, bf16[192,256]{1,0:T(8,128)(2,1)}, bf16[192,256]{1,0:T(8,128)(2,...) custom-call(s32[1]{0:T(128)} %bitcast.refs_0_.me_ref, s32[1,2048]{1,0:T(1,128)S(1)} %copy-done.12, ...), custom_call_target="tpu_custom_call" | custom-call | flops 8999999488 | bytes 5000000 | tf_op jit(solution)/shard_map/attend_forward/pallas_call | solution.py:83
  35.3 10.7 %attend_forward.3 = (bf16[4,192,256]{2,1,0:T(8,128)(2,1)}, bf16[3,16,1024]{2,1,0:T(8,128)(2,1)}, bf16[192,256]{1,0:T(8,128)(2,1)}, bf16[192,256]{1,0:T(8,128)(2,...) custom-call(s32[1]{0:T(128)} %bitcast.refs_0_.me_ref, s32[1,2048]{1,0:T(1,128)S(1)} %copy-done.13, ...), custom_call_target="tpu_custom_call" | custom-call | flops 8999999488 | bytes 5000000 | tf_op jit(solution)/shard_map/attend_forward/pallas_call | solution.py:83
  46.0 3.8 %collective-permute-done.1.m2_ref = bf16[192,256]{1,0:T(8,128)(2,1)S(1)} collective-permute-done((bf16[192,256]{1,0:T(8,128)(2,1)S(1)}, bf16[192,256]{1,0:T(8,128)(2,1)S(1)}, u32[]{:S(2)}, u32[]{:S(2)}) %collective-permute-start.1) | collective-permute-done | bytes 98336 | tf_op jit(solution)/shard_map/ppermute | solution.py:864
  67.1 6.5 %feed.4 = (bf16[2,2048,768]{2,1,0:T(8,128)(2,1)}, bf16[2,2048,768]{2,1,0:T(8,128)(2,1)}, bf16[512,768]{1,0:T(8,128)(2,1)}, bf16[512,768]{1,0:T(8,128)(2,1)}, bf1...) custom-call(s32[1]{0:T(128)} %bitcast.refs_0_.me_ref, ...), custom_call_target="tpu_custom_call" | custom-call | flops 5000000000 | bytes 8000000 | tf_op jit(solution)/shard_map/feed/pallas_call | solution.py:83
  73.7 6.5 %feed.5 = (bf16[2,2048,768]{2,1,0:T(8,128)(2,1)}, bf16[2,2048,768]{2,1,0:T(8,128)(2,1)}, bf16[512,768]{1,0:T(8,128)(2,1)}, bf16[512,768]{1,0:T(8,128)(2,1)}, bf1...) custom-call(s32[1]{0:T(128)} %bitcast.refs_0_.me_ref, ...), custom_call_target="tpu_custom_call", output_to_operand_aliasing={{0}: (7, {}), {1}: (8, {}), {2}: (9, {}), {3}: (10, {})} | custom-call | flops 5000000000 | bytes 8000000 | tf_op jit(solution)/shard_map/feed/pallas_call | solution.py:83
  80.8 6.5 %feed.6 = (bf16[2,2048,768]{2,1,0:T(8,128)(2,1)}, bf16[2,2048,768]{2,1,0:T(8,128)(2,1)}, bf16[512,768]{1,0:T(8,128)(2,1)}, bf16[512,768]{1,0:T(8,128)(2,1)}, bf1...) custom-call(s32[1]{0:T(128)} %bitcast.refs_0_.me_ref, ...), custom_call_target="tpu_custom_call", output_to_operand_aliasing={{0}: (7, {}), {1}: (8, {})} | custom-call | flops 5000000000 | bytes 8000000 | tf_op jit(solution)/shard_map/feed/pallas_call | solution.py:83
  87.4 6.5 %feed.7 = (bf16[2,2048,768]{2,1,0:T(8,128)(2,1)}, bf16[2,2048,768]{2,1,0:T(8,128)(2,1)}, bf16[512,768]{1,0:T(8,128)(2,1)}, bf16[512,768]{1,0:T(8,128)(2,1)}, bf1...) custom-call(s32[1]{0:T(128)} %bitcast.refs_0_.me_ref, ...), custom_call_target="tpu_custom_call", output_to_operand_aliasing={{0}: (7, {}), {1}: (8, {}), {2}: (9, {}), {3}: (10, {})} | custom-call | flops 5000000000 | bytes 8000000 | tf_op jit(solution)/shard_map/feed/pallas_call | solution.py:83
  99.0 10.1 %convolution_convert_fusion = bf16[2,768,768]{2,1,0:T(8,128)(2,1)} fusion(bf16[2,2048,768]{2,1,0:T(8,128)(2,1)} %fence.20, bf16[2,2048,768]{2,1,0:T(8,128)(2,1)} %get-tuple-element.193), kind=kOutput, calls=%fused_computation | convolution fusion | flops 4833017856 | bytes 14942208 | tf_op jit(solution)/shard_map/dot_general | solution.py:991
  109.8 3.7 %middle_back.3 = (f32[256,768]{1,0:T(8,128)}, bf16[256,768]{1,0:T(8,128)(2,1)}, bf16[192,256]{1,0:T(8,128)(2,1)}, bf16[192,256]{1,0:T(8,128)(2,1)S(1)}, bf16[192...) custom-call(s32[1]{0:T(128)} %bitcast.refs_0_.me_ref, ...), custom_call_target="tpu_custom_call" | custom-call | flops 2000000000 | bytes 4000000 | tf_op jit(solution)/shard_map/middle_back/pallas_call | solution.py:83
  115.4 3.7 %middle_back.2 = (f32[256,768]{1,0:T(8,128)}, bf16[256,768]{1,0:T(8,128)(2,1)}, bf16[192,256]{1,0:T(8,128)(2,1)}, bf16[192,256]{1,0:T(8,128)(2,1)S(1)}, bf16[192...) custom-call(s32[1]{0:T(128)} %bitcast.refs_0_.me_ref, ...), custom_call_target="tpu_custom_call" | custom-call | flops 2000000000 | bytes 4000000 | tf_op jit(solution)/shard_map/middle_back/pallas_call | solution.py:83
  126.2 14.6 %attend_backward.2 = (bf16[192,1024]{1,0:T(8,128)(2,1)}, f32[192,2048]{1,0:T(8,128)}, f32[192,2048]{1,0:T(8,128)}) custom-call(s32[1]{0:T(128)} %bitcast.refs_0_.me_ref, s32[1,2048]{1,0:T(1,128)S(1)} %copy-done.13, s32[1,2048]{1,0:T(1,128)S(1)} %copy-done.13, bf16[3,128,2048]{2,1,0:T(8,128)(2,1)} %get-tuple-element.108.refs_3_, ...), custom_call_target="tpu_custom_call" | custom-call | flops 16000000000 | bytes 10000000 | tf_op jit(solution)/shard_map/attend_backward/pallas_call | solution.py:83
  142.1 4.6 %collective-permute-done.21 = bf16[512,768]{1,0:T(8,128)(2,1)} collective-permute-done((bf16[512,768]{1,0:T(8,128)(2,1)S(1)}, bf16[512,768]{1,0:T(8,128)(2,1)}, u32[]{:S(2)}, u32[]{:S(2)}) %collective-permute-start.21) | collective-permute-done | bytes 786464 | tf_op jit(solution)/shard_map/ppermute | solution.py:864
  152.6 16.3 %attend_backward.3.g_ref.refs_0_ = bf16[576,2048]{1,0:T(8,128)(2,1)} custom-call(s32[1]{0:T(128)} %bitcast.refs_0_.me_ref, s32[1,2048]{1,0:T(1,128)S(1)} %copy-done.13, s32[1,2048]{1,0:T(1,128)S(1)} %copy-done.13, bf16[3,128,2048]{2,1,0:T(8,128)(2,1)} %get-tuple-element.108.refs_3_, bf16[3,16,1024]{2,1,0:T(8,128)(2,1)} %get-tuple-element.115.rest_0_.refs_4_, ...), custom_call_target="tpu_custom_call" | custom-call | flops 16000000000 | bytes 10000000 | tf_op jit(solution)/shard_map/attend_backward/pallas_call | solution.py:83
  171.1 10.6 %tail.1 = (bf16[512,768]{1,0:T(8,128)(2,1)}, bf16[512,768]{1,0:T(8,128)(2,1)S(1)}, bf16[512,768]{1,0:T(8,128)(2,1)}, bf16[528,768]{1,0:T(8,128)(2,1)S(1)}, f32[8,576]{1,0:T(8,128)}, /*index=5*/f32[8,768]{1,0:T(8,128)}) custom-call(s32[1]{0:T(128)} %bitcast.refs_0_.me_ref, bf16[576,2048]{1,0:T(8,128)(2,1)} %attend_backward.3.g_ref.refs_0_, ...), custom_call_target="tpu_custom_call" | custom-call | flops 4000000000 | bytes 10000000 | tf_op jit(solution)/shard_map/tail/pallas_call | solution.py:83
  184.2 4.6 %convolution_convert_fusion.1.g_ref = bf16[576,768]{1,0:T(8,128)(2,1)S(1)} fusion(bf16[576,2048]{1,0:T(8,128)(2,1)} %fence.17, bf16[2048,768]{1,0:T(8,128)(2,1)} %get-tuple-element.174), kind=kOutput, calls=%fused_computation.7 | convolution fusion | flops 1812381696 | bytes 6389760 | tf_op jit(solution)/shard_map/dot_general | solution.py:23
  194.5 14.5 %collective-permute-done.36.refs_2_ = bf16[384,768]{1,0:T(8,128)(2,1)S(1)} collective-permute-done((bf16[384,768]{1,0:T(8,128)(2,1)S(1)}, bf16[384,768]{1,0:T(8,128)(2,1)S(1)}, u32[]{:S(2)}, u32[]{:S(2)}) %collective-permute-start.36) | collective-permute-done | bytes 589856 | tf_op jit(solution)/shard_map/ppermute | solution.py:1022
  212.4 3.5 %collective-permute-start.40 = (bf16[96,768]{1,0:T(8,128)(2,1)}, bf16[96,768]{1,0:T(8,128)(2,1)S(1)}, u32[]{:S(2)}, u32[]{:S(2)}) collective-permute-start(bf16[96,768]{1,0:T(8,128)(2,1)} %get-tuple-element.186), channel_id=1, source_target_pairs={{0,8},{8,16},{16,24},{24,0},{1,9},{9,17},{17,25},{25,1},{2,10},{10... | collective-permute-start | bytes 442376 | tf_op jit(solution)/shard_map/ppermute | solution.py:892
  223.5 9.8 %collective-permute-done.41 = bf16[96,768]{1,0:T(8,128)(2,1)S(1)} collective-permute-done((bf16[96,768]{1,0:T(8,128)(2,1)}, bf16[96,768]{1,0:T(8,128)(2,1)S(1)}, u32[]{:S(2)}, u32[]{:S(2)}) %collective-permute-start.41) | collective-permute-done | bytes 147488 | tf_op jit(solution)/shard_map/ppermute | solution.py:892
  242.6 8.3 %collective-permute-start.45 = (bf16[128,768]{1,0:T(8,128)(2,1)S(1)}, bf16[128,768]{1,0:T(8,128)(2,1)S(1)}, u32[]{:S(2)}, u32[]{:S(2)}) collective-permute-start(bf16[128,768]{1,0:T(8,128)(2,1)S(1)} %second.1.rest_4_.refs_1_), channel_id=1, source_target_pairs={{0,8},{8,16},{16,24},{24,0},{1,9},{9,17},{17,25},{25,1},{2,10},{10... | collective-permute-start | bytes 589832 | tf_op jit(solution)/shard_map/ppermute | solution.py:892
  254.1 5.3 %collective-permute-done.45.refs_2_ = bf16[128,768]{1,0:T(8,128)(2,1)S(1)} collective-permute-done((bf16[128,768]{1,0:T(8,128)(2,1)S(1)}, bf16[128,768]{1,0:T(8,128)(2,1)S(1)}, u32[]{:S(2)}, u32[]{:S(2)}) %collective-permute-start.45) | collective-permute-done | bytes 196640 | tf_op jit(solution)/shard_map/ppermute | solution.py:892
  259.5 6.9 %collective-permute-done.46.refs_3_ = bf16[128,768]{1,0:T(8,128)(2,1)S(1)} collective-permute-done((bf16[128,768]{1,0:T(8,128)(2,1)S(1)}, bf16[128,768]{1,0:T(8,128)(2,1)S(1)}, u32[]{:S(2)}, u32[]{:S(2)}) %collective-permute-start.46) | collective-permute-done | bytes 196640 | tf_op jit(solution)/shard_map/ppermute | solution.py:892
  271.1 4.1 %place.3 = f32[2048,768]{1,0:T(8,128)} custom-call(s32[1]{0:T(128)} %bitcast.refs_0_.me_ref, bf16[512,768]{1,0:T(8,128)(2,1)S(1)} %final.1.p0_ref, bf16[512,768]{1,0:T(8,128)(2,1)S(1)} %collective-permute-done.43.p1_ref, bf16[512,768]{1,0:T(8,128)(2,1)S(1)} %fence.19.p2_ref, bf16[512,768]{1,0:T(8,128)(2,1)S(1)} %collective-permute-done.48.p3_ref, ...), custom_call_target="tpu_custom_call" | custom-call | flops 1000000 | bytes 9000000 | tf_op jit(solution)/shard_map/place/pallas_call | solution.py:83
  277.2 9.2 %collective-permute-done.49.other_ref = bf16[416,768]{1,0:T(8,128)(2,1)} collective-permute-done((bf16[416,768]{1,0:T(8,128)(2,1)}, bf16[416,768]{1,0:T(8,128)(2,1)}, u32[]{:S(2)}, u32[]{:S(2)}) %collective-permute-start.49) | collective-permute-done | bytes 639008 | tf_op jit(solution)/shard_map/ppermute | solution.py:1041
  (193 shorter events, 94.2 us)
Async XLA Ops:
  7.2 176.4 %reduce-scatter.2.cloned.1.call-start = ((), (), s32[]{:S(2)}) async-start(), calls=%async_computation.1 | async-start | bytes 2654208 | tf_op jit(solution)/shard_map/reduce_scatter | solution.py:993
  30.5 20.2 %collective-permute-start.3 = (bf16[192,768]{1,0:T(8,128)(2,1)S(1)}, bf16[192,768]{1,0:T(8,128)(2,1)S(1)}, u32[]{:S(2)}, u32[]{:S(2)}) collective-permute-start(bf16[192,768]{1,0:T(8,128)(2,1)S(1)} %copy-done.23), channel_id=1, source_target_pairs={{0,1},{1,0},{2,3},{3,2},{4,5},{5,4},{6,7},{7,6},{8,9},{9,8},{10,11... | collective-permute-start | bytes 884744 | tf_op jit(solution)/shard_map/ppermute | solution.py:860
  30.6 20.2 %collective-permute-start.4 = (bf16[192,768]{1,0:T(8,128)(2,1)S(1)}, bf16[192,768]{1,0:T(8,128)(2,1)S(1)}, u32[]{:S(2)}, u32[]{:S(2)}) collective-permute-start(bf16[192,768]{1,0:T(8,128)(2,1)S(1)} %copy-done.23), channel_id=1, source_target_pairs={{0,2},{2,0},{1,3},{3,1},{4,6},{6,4},{5,7},{7,5},{8,10},{10,8},{9,1... | collective-permute-start | bytes 884744 | tf_op jit(solution)/shard_map/ppermute | solution.py:864
  33.5 17.3 %collective-permute-start.5 = (bf16[192,768]{1,0:T(8,128)(2,1)S(1)}, bf16[192,768]{1,0:T(8,128)(2,1)S(1)}, u32[]{:S(2)}, u32[]{:S(2)}) collective-permute-start(bf16[192,768]{1,0:T(8,128)(2,1)S(1)} %copy-done.23), channel_id=1, source_target_pairs={{0,3},{1,2},{2,1},{3,0},{4,7},{5,6},{6,5},{7,4},{8,11},{9,10},{10,... | collective-permute-start | bytes 884744 | tf_op jit(solution)/shard_map/ppermute | solution.py:868
  94.5 19.0 %collective-permute-start.19 = (bf16[256,768]{1,0:T(8,128)(2,1)S(1)}, bf16[256,768]{1,0:T(8,128)(2,1)S(1)}, u32[]{:S(2)}, u32[]{:S(2)}) collective-permute-start(bf16[256,768]{1,0:T(8,128)(2,1)S(1)} %get-tuple-element.144), channel_id=1, source_target_pairs={{0,1},{1,0},{2,3},{3,2},{4,5},{5,4},{6,7},{7,6},{8,9},{9,8},{10,11... | collective-permute-start | bytes 1179656 | tf_op jit(solution)/shard_map/ppermute | solution.py:860
  97.6 17.0 %collective-permute-start.20 = (bf16[256,768]{1,0:T(8,128)(2,1)}, bf16[256,768]{1,0:T(8,128)(2,1)S(1)}, u32[]{:S(2)}, u32[]{:S(2)}) collective-permute-start(bf16[256,768]{1,0:T(8,128)(2,1)} %add_convert_fusion.1.refs_2_), channel_id=1, source_target_pairs={{0,2},{2,0},{1,3},{3,1},{4,6},{6,4},{5,7},{7,5},{8,10},{10,8},{9,1... | collective-permute-start | bytes 1179656 | tf_op jit(solution)/shard_map/ppermute | solution.py:864
  99.0 22.9 %collective-permute-start.18 = (bf16[512,768]{1,0:T(8,128)(2,1)}, bf16[512,768]{1,0:T(8,128)(2,1)}, u32[]{:S(2)}, u32[]{:S(2)}) collective-permute-start(bf16[512,768]{1,0:T(8,128)(2,1)} %fence.14), channel_id=1, source_target_pairs={{0,1},{1,0},{2,3},{3,2},{4,5},{5,4},{6,7},{7,6},{8,9},{9,8},{10,11... | collective-permute-start | bytes 2359304 | tf_op jit(solution)/shard_map/ppermute | solution.py:860
  109.1 166.0 %all-gather.2.cloned.1.call-start = ((), (), s32[]{:S(2)}) async-start(), calls=%async_computation.2 | async-start | bytes 2654208 | tf_op jit(solution)/shard_map/all_gather | solution.py:1016
  121.9 18.9 %collective-permute-start.33 = (bf16[192,768]{1,0:T(8,128)(2,1)S(1)}, bf16[192,768]{1,0:T(8,128)(2,1)}, u32[]{:S(2)}, u32[]{:S(2)}) collective-permute-start(bf16[192,768]{1,0:T(8,128)(2,1)S(1)} %get-tuple-element.168), channel_id=1, source_target_pairs={{0,1},{1,0},{2,3},{3,2},{4,5},{5,4},{6,7},{7,6},{8,9},{9,8},{10,11... | collective-permute-start | bytes 884744 | tf_op jit(solution)/shard_map/ppermute | solution.py:860
  123.6 28.1 %collective-permute-start.34 = (bf16[192,768]{1,0:T(8,128)(2,1)S(1)}, bf16[192,768]{1,0:T(8,128)(2,1)S(1)}, u32[]{:S(2)}, u32[]{:S(2)}) collective-permute-start(bf16[192,768]{1,0:T(8,128)(2,1)S(1)} %get-tuple-element.169), channel_id=1, source_target_pairs={{0,1},{1,0},{2,3},{3,2},{4,5},{5,4},{6,7},{7,6},{8,9},{9,8},{10,11... | collective-permute-start | bytes 884744 | tf_op jit(solution)/shard_map/ppermute | solution.py:860
  123.8 26.2 %collective-permute-start.25 = (bf16[192,256]{1,0:T(8,128)(2,1)S(1)}, bf16[192,256]{1,0:T(8,128)(2,1)S(1)}, u32[]{:S(2)}, u32[]{:S(2)}) collective-permute-start(bf16[192,256]{1,0:T(8,128)(2,1)S(1)} %get-tuple-element.150), channel_id=1, source_target_pairs={{0,1},{1,0},{2,3},{3,2},{4,5},{5,4},{6,7},{7,6},{8,9},{9,8},{10,11... | collective-permute-start | bytes 294920 | tf_op jit(solution)/shard_map/ppermute | solution.py:860
  124.2 26.5 %collective-permute-start.26 = (bf16[192,256]{1,0:T(8,128)(2,1)S(1)}, bf16[192,256]{1,0:T(8,128)(2,1)}, u32[]{:S(2)}, u32[]{:S(2)}) collective-permute-start(bf16[192,256]{1,0:T(8,128)(2,1)S(1)} %get-tuple-element.151), channel_id=1, source_target_pairs={{0,2},{2,0},{1,3},{3,1},{4,6},{6,4},{5,7},{7,5},{8,10},{10,8},{9,1... | collective-permute-start | bytes 294920 | tf_op jit(solution)/shard_map/ppermute | solution.py:864
  125.2 21.6 %collective-permute-start.21 = (bf16[512,768]{1,0:T(8,128)(2,1)S(1)}, bf16[512,768]{1,0:T(8,128)(2,1)}, u32[]{:S(2)}, u32[]{:S(2)}) collective-permute-start(bf16[512,768]{1,0:T(8,128)(2,1)S(1)} %fence.15.refs_13_), channel_id=1, source_target_pairs={{0,2},{2,0},{1,3},{3,1},{4,6},{6,4},{5,7},{7,5},{8,10},{10,8},{9,1... | collective-permute-start | bytes 2359304 | tf_op jit(solution)/shard_map/ppermute | solution.py:864
  146.8 22.2 %collective-permute-start.35 = (bf16[192,768]{1,0:T(8,128)(2,1)S(1)}, bf16[192,768]{1,0:T(8,128)(2,1)S(1)}, u32[]{:S(2)}, u32[]{:S(2)}) collective-permute-start(bf16[192,768]{1,0:T(8,128)(2,1)S(1)} %add_convert_fusion.4.refs_17_), channel_id=1, source_target_pairs={{0,2},{2,0},{1,3},{3,1},{4,6},{6,4},{5,7},{7,5},{8,10},{10,8},{9,1... | collective-permute-start | bytes 884744 | tf_op jit(solution)/shard_map/ppermute | solution.py:864
  150.7 18.3 %collective-permute-start.22 = (bf16[512,768]{1,0:T(8,128)(2,1)S(1)}, bf16[512,768]{1,0:T(8,128)(2,1)S(1)}, u32[]{:S(2)}, u32[]{:S(2)}) collective-permute-start(bf16[512,768]{1,0:T(8,128)(2,1)S(1)} %fusion.3.refs_16_.p0_ref), channel_id=1, source_target_pairs={{0,1},{1,0},{2,3},{3,2},{4,5},{5,4},{6,7},{7,6},{8,9},{9,8},{10,11... | collective-permute-start | bytes 2359304 | tf_op jit(solution)/shard_map/ppermute | solution.py:860
  150.7 20.5 %collective-permute-start.23 = (bf16[512,768]{1,0:T(8,128)(2,1)S(1)}, bf16[512,768]{1,0:T(8,128)(2,1)S(1)}, u32[]{:S(2)}, u32[]{:S(2)}) collective-permute-start(bf16[512,768]{1,0:T(8,128)(2,1)S(1)} %fusion.3.refs_16_.p0_ref), channel_id=1, source_target_pairs={{0,2},{2,0},{1,3},{3,1},{4,6},{6,4},{5,7},{7,5},{8,10},{10,8},{9,1... | collective-permute-start | bytes 2359304 | tf_op jit(solution)/shard_map/ppermute | solution.py:864
  183.7 32.8 %collective-permute-start.24 = (bf16[512,768]{1,0:T(8,128)(2,1)S(1)}, bf16[512,768]{1,0:T(8,128)(2,1)S(1)}, u32[]{:S(2)}, u32[]{:S(2)}) collective-permute-start(bf16[512,768]{1,0:T(8,128)(2,1)S(1)} %collective-permute-done.23.rest_3_.p2_ref), channel_id=1, source_target_pairs={{0,1},{1,0},{2,3},{3,2},{4,5},{5,4},{6,7},{7,6},{8,9},{9,8},{10,11... | collective-permute-start | bytes 2359304 | tf_op jit(solution)/shard_map/ppermute | solution.py:860
  190.5 18.5 %collective-permute-start.36 = (bf16[384,768]{1,0:T(8,128)(2,1)S(1)}, bf16[384,768]{1,0:T(8,128)(2,1)S(1)}, u32[]{:S(2)}, u32[]{:S(2)}) collective-permute-start(bf16[384,768]{1,0:T(8,128)(2,1)S(1)} %get-tuple-element.176), channel_id=1, source_target_pairs={{0,4},{4,0},{1,5},{5,1},{2,6},{6,2},{3,7},{7,3},{8,12},{12,8},{9,1... | collective-permute-start | bytes 1769480 | tf_op jit(solution)/shard_map/ppermute | solution.py:1022
  192.5 43.3 %collective-permute-start.39 = (bf16[528,768]{1,0:T(8,128)(2,1)S(1)}, bf16[528,768]{1,0:T(8,128)(2,1)S(1)}, u32[]{:S(2)}, u32[]{:S(2)}) collective-permute-start(bf16[528,768]{1,0:T(8,128)(2,1)S(1)} %chip_sum.1.refs_3_.one_ref), channel_id=1, source_target_pairs={{0,2},{2,0},{1,3},{3,1},{4,6},{6,4},{5,7},{7,5},{8,10},{10,8},{9,1... | collective-permute-start | bytes 2433032 | tf_op jit(solution)/shard_map/ppermute | solution.py:864
  193.6 43.0 %collective-permute-start.38 = (bf16[512,768]{1,0:T(8,128)(2,1)S(1)}, bf16[512,768]{1,0:T(8,128)(2,1)S(1)}, u32[]{:S(2)}, u32[]{:S(2)}) collective-permute-start(bf16[512,768]{1,0:T(8,128)(2,1)S(1)} %copy-done.9), channel_id=1, source_target_pairs={{0,1},{1,0},{2,3},{3,2},{4,5},{5,4},{6,7},{7,6},{8,9},{9,8},{10,11... | collective-permute-start | bytes 2359304 | tf_op jit(solution)/shard_map/ppermute | solution.py:860
  215.8 17.5 %collective-permute-start.41 = (bf16[96,768]{1,0:T(8,128)(2,1)}, bf16[96,768]{1,0:T(8,128)(2,1)S(1)}, u32[]{:S(2)}, u32[]{:S(2)}) collective-permute-start(bf16[96,768]{1,0:T(8,128)(2,1)} %get-tuple-element.187), channel_id=1, source_target_pairs={{0,16},{8,24},{16,0},{24,8},{1,17},{9,25},{17,1},{25,9},{2,18},{10... | collective-permute-start | bytes 442376 | tf_op jit(solution)/shard_map/ppermute | solution.py:892
  216.5 19.2 %collective-permute-start.42 = (bf16[96,768]{1,0:T(8,128)(2,1)}, bf16[96,768]{1,0:T(8,128)(2,1)S(1)}, u32[]{:S(2)}, u32[]{:S(2)}) collective-permute-start(bf16[96,768]{1,0:T(8,128)(2,1)} %get-tuple-element.180.rest_0_), channel_id=1, source_target_pairs={{0,24},{8,0},{16,8},{24,16},{1,25},{9,1},{17,9},{25,17},{2,26},{10... | collective-permute-start | bytes 442376 | tf_op jit(solution)/shard_map/ppermute | solution.py:892
  241.6 26.2 %collective-permute-start.44 = (bf16[512,768]{1,0:T(8,128)(2,1)S(1)}, bf16[512,768]{1,0:T(8,128)(2,1)S(1)}, u32[]{:S(2)}, u32[]{:S(2)}) collective-permute-start(bf16[512,768]{1,0:T(8,128)(2,1)S(1)} %final.1.p0_ref), channel_id=1, source_target_pairs={{0,2},{2,0},{1,3},{3,1},{4,6},{6,4},{5,7},{7,5},{8,10},{10,8},{9,1... | collective-permute-start | bytes 2359304 | tf_op jit(solution)/shard_map/ppermute | solution.py:864
  267.8 18.6 %collective-permute-start.49 = (bf16[416,768]{1,0:T(8,128)(2,1)}, bf16[416,768]{1,0:T(8,128)(2,1)}, u32[]{:S(2)}, u32[]{:S(2)}) collective-permute-start(bf16[416,768]{1,0:T(8,128)(2,1)} %third.1.refs_1_.rest_0_.mine_ref), channel_id=1, source_target_pairs={{0,4},{4,0},{1,5},{5,1},{2,6},{6,2},{3,7},{7,3},{8,12},{12,8},{9,1... | collective-permute-start | bytes 1916936 | tf_op jit(solution)/shard_map/ppermute | solution.py:1041
  (55 other events, 445.9 us)
Sparse Core Ops, SparseCore 0:
  109.3 69.7 reduce-scatter.1
  183.7 64.7 all-gather.1

commit v6 on v5

--- a/solution.py
+++ b/solution.py
@@ -354,7 +354,7 @@
     return kernel_call(
         body,
         (me, seg_row, seg_row, qt, extra, kn, kt, vn, out, *grad, *earlier, *after),
-        free_in=(10, 11, 12) + tuple(range(13 + len(earlier), 13 + len(earlier) + len(after))),
+        free_in=(10, 11, 12) + tuple(range(13 + len(earlier), 13 + len(earlier) + 2)),
         grid_spec=pltpu.PrefetchScalarGridSpec(
             num_scalar_prefetch=1, grid=(count,), in_specs=in_specs, out_specs=out_specs, scratch_shapes=scratch,
         ),
@@ -529,8 +529,8 @@
 
 
 def tail_body(me_ref, g_ref, wq_ref, wk_ref, wv_ref, x_ref, stat_ref, *rest):
-    early = rest[:PARTS]
-    o0_ref, o1_ref, o2_ref, o3_ref, row_ref, vec_ref, sum_ref = rest[-7:]
+    early, units = rest[:PARTS], rest[PARTS:3 * PARTS]
+    o0_ref, o1_ref, o2_ref, o3_ref, apart_ref, vec_ref, sum_ref, row_ref = rest[-8:]
     i, p = pl.program_id(0), pl.program_id(1)
     grads = g_ref[...]
     width = wq_ref.shape[0]
@@ -563,10 +563,16 @@
         for n, part in enumerate(parts):
             vectors = jnp.where(row == n, jnp.sum(part, axis=0, keepdims=True), vectors)
         vec_ref[...] = vectors
+        inside = units[0][...]
+        for ref in units[1:]:
+            inside = inside + ref[...]
+        apart_ref[0:1] = jnp.sum(inside, axis=0, keepdims=True)
+        apart_ref[1:] = jnp.zeros((7, apart_ref.shape[1]), F32)
+        apart_ref[1:2, :row_ref.shape[1]] = row_ref[0:1]
         o3_ref[PARTS * TILE:] = paired(vectors)
 
 
-def tail(me, grads, wq, wk, wv, tokens, stat, early, after):
+def tail(me, grads, wq, wk, wv, tokens, stat, early, units, after):
     deep = grads.shape[0]
     features = wq.shape[1]
     share = const((PARTS * TILE, features))
@@ -574,8 +580,8 @@
     at = lambda i, p, m: 4 * p + (m[0] ^ (3 - i))
     return kernel_call(
         tail_body,
-        (me, grads, wq, wk, wv, tokens, stat, *early, *after),
-        free_in=tuple(range(7 + PARTS, 7 + PARTS + len(after))),
+        (me, grads, wq, wk, wv, tokens, stat, *early, *units, *after),
+        free_in=tuple(range(7 + 3 * PARTS, 9 + 3 * PARTS)),
         free_out=(1, 3),
         grid_spec=pltpu.PrefetchScalarGridSpec(
             num_scalar_prefetch=1,
@@ -584,31 +590,33 @@
                       const(wq.shape), const(wk.shape), const(wv.shape),
                       pl.BlockSpec((TILE, features), lambda i, p, m: (at(i, p, m), 0)),
                       pl.BlockSpec((TILE, WIDE), lambda i, p, m: (at(i, p, m), 0))]
-            + [const(v.shape) for v in early] + [pl.BlockSpec(memory_space=pl.ANY)] * len(after),
-            out_specs=[share, share, share, more, const((8, deep)), const((8, features))],
-            scratch_shapes=[pltpu.VMEM((16, features), F32)],
+            + [const(v.shape) for v in (*early, *units)] + [pl.BlockSpec(memory_space=pl.ANY)] * len(after),
+            out_specs=[share, share, share, more, const((8, features)), const((8, features))],
+            scratch_shapes=[pltpu.VMEM((16, features), F32), pltpu.VMEM((8, deep), F32)],
         ),
         out_shape=[shape_of(PARTS * TILE, features)] * 3 + [shape_of(PARTS * TILE + 16, features)]
-        + [shape_of(8, deep, dtype=F32), shape_of(8, features, dtype=F32)],
+        + [shape_of(8, features, dtype=F32)] * 2,
         cost_estimate=cost(4e9, 10e6),
         name="tail",
     )
 
 
-def chip_body(one_ref, two_ref, vec_ref, out_ref):
+def chip_body(one_ref, two_ref, vec_ref, *rest):
+    out_ref = rest[-1]
     rows = one_ref.shape[0]
     out_ref[:rows] = (one_ref[...].astype(F32) + two_ref[:rows].astype(F32)).astype(BF16)
     out_ref[rows:] = paired(vec_ref[...] + joined(two_ref[rows:]))
 
 
-def chip_sum(one, two, vectors):
+def chip_sum(one, two, vectors, after):
     return kernel_call(
         chip_body,
-        (one, two, vectors),
-        free_in=(1,),
+        (one, two, vectors, *after),
+        free_in=(1,) + tuple(range(3, 3 + len(after))),
         free_out=(0,),
         grid=(1,),
-        in_specs=[const(one.shape), const(two.shape), const(vectors.shape)],
+        in_specs=[const(one.shape), const(two.shape), const(vectors.shape)]
+        + [pl.BlockSpec(memory_space=pl.ANY)] * len(after),
         out_specs=[const(two.shape)],
         out_shape=[shape_of(*two.shape)],
         name="chip_sum",
@@ -635,7 +643,6 @@
         halves_body,
         (xz, grad_weights, grad_output),
         free_in=(1, 2),
-        free_out=(1,),
         grid_spec=pltpu.PrefetchScalarGridSpec(
             num_scalar_prefetch=1,
             grid=(1,),
@@ -649,10 +656,10 @@
 
 
 def quarter_body(count, xz_ref, one_ref, two_ref, *rest):
+    rows = one_ref.shape[0] // count
     for n, out_ref in enumerate(rest[-count:]):
-        @pl.when(pl.program_id(0) == n)
-        def _(out_ref=out_ref):
-            out_ref[...] = (one_ref[...].astype(F32) + two_ref[...].astype(F32)).astype(BF16)
+        at = pl.ds(pl.multiple_of(lax.rem(xz_ref[1] + n, count) * rows, rows), rows)
+        out_ref[...] = (one_ref[at, :].astype(F32) + two_ref[at, :].astype(F32)).astype(BF16)
 
 
 def quarters(xz, one, two, count, after):
@@ -661,15 +668,14 @@
     def body(*refs):
         quarter_body(count, *refs)
 
-    block = pl.BlockSpec((rows // count, features), lambda i, m: ((m[1] + i) % count, 0))
     return kernel_call(
         body,
         (xz, one, two, *after),
-        free_in=(2,) + tuple(range(3, 3 + len(after))),
+        free_in=(2,),
         grid_spec=pltpu.PrefetchScalarGridSpec(
             num_scalar_prefetch=1,
-            grid=(count,),
-            in_specs=[block, block] + [pl.BlockSpec(memory_space=pl.ANY)] * len(after),
+            grid=(1,),
+            in_specs=[const(one.shape), const(two.shape)] + [pl.BlockSpec(memory_space=pl.ANY)] * len(after),
             out_specs=[const((rows // count, features))] * count,
         ),
         out_shape=[shape_of(rows // count, features)] * count,
@@ -688,23 +694,32 @@
     return both[:half] + both[half:]
 
 
-def second_body(total_ref, one_ref, two_ref, apart_ref, out_ref):
-    rows = total_ref.shape[0]
-    out_ref[:rows] = total_ref[...]
+def second_body(count, *refs):
+    one_ref, two_ref, apart_ref, out_ref = refs[count], refs[count + 1], refs[count + 2], refs[-1]
+    rows = refs[0].shape[0]
+    total = refs[0][...].astype(F32)
+    for ref in refs[1:count]:
+        total = total + ref[...].astype(F32)
+    out_ref[:rows] = total.astype(BF16)
     shared = joined(one_ref[...]) + joined(two_ref[...])
     out_ref[rows:] = paired(jnp.concatenate([shared, apart_ref[...]], axis=0))
 
 
-def second(total, one, two, apart):
-    rows, features = total.shape
+def second(parts, one, two, apart, after):
+    count = len(parts)
+    rows, features = parts[0].shape
     last = pl.BlockSpec((16, features), lambda i: (one.shape[0] // 16 - 1, 0))
-    return kernel_call(
-        second_body,
-        (total, one, two, apart),
-        free_in=(0, 1, 2),
-        free_out=(0,),
+
+    def body(*refs):
+        second_body(count, *refs)
+
+    return kernel_call(
+        body,
+        (*parts, one, two, apart, *after),
+        free_in=tuple(range(1, count + 2)) + tuple(range(count + 3, count + 3 + len(after))),
         grid=(1,),
-        in_specs=[const(total.shape), last, last, const(apart.shape)],
+        in_specs=[const((rows, features))] * count + [last, last, const(apart.shape)]
+        + [pl.BlockSpec(memory_space=pl.ANY)] * len(after),
         out_specs=[const((rows + 32, features))],
         out_shape=[shape_of(rows + 32, features)],
         name="second",
@@ -724,7 +739,7 @@
     out_ref[step:] = paired(sums)
 
 
-def third(xz, pieces, extra):
+def third(xz, pieces, extra, after):
     count = len(pieces)
     rows, features = pieces[0].shape
     total = (rows - extra) * count + extra
@@ -734,12 +749,12 @@
 
     return kernel_call(
         body,
-        (xz, *pieces),
+        (xz, *pieces, *after),
         free_in=tuple(range(1, count + 1)),
         grid_spec=pltpu.PrefetchScalarGridSpec(
             num_scalar_prefetch=1,
             grid=(1,),
-            in_specs=[const((rows, features))] * count,
+            in_specs=[const((rows, features))] * count + [pl.BlockSpec(memory_space=pl.ANY)] * len(after),
             out_specs=[const((total, features))],
         ),
         out_shape=[shape_of(total, features)],
@@ -748,8 +763,7 @@
 
 
 def ready_body(xz_ref, mine_ref, other_ref, *rest):
-    outs = rest[-5:]
-    small_ref = outs[4]
+    outs = rest[-16:]
     width = outs[0].shape[0]
     for n, out_ref in enumerate(outs[:4]):
         rows = slice(n % 2 * width, (n % 2 + 1) * width)
@@ -758,22 +772,27 @@
             def _(to_ref=to_ref, out_ref=out_ref, rows=rows):
                 out_ref[...] = to_ref[rows].astype(F32)
 
-    small_ref[...] = joined(mine_ref[2 * width:]) + joined(other_ref[2 * width:])
-
-
-def ready(xz, mine, other, width, count, after):
+    small = joined(mine_ref[2 * width:]) + joined(other_ref[2 * width:])
+    for n, out_ref in enumerate(outs[4:13]):
+        out_ref[...] = small[n]
+    for n, out_ref in enumerate(outs[13:]):
+        out_ref[...] = small[9, n * width:(n + 1) * width]
+
+
+def ready(xz, mine, other, width, after):
     rows, features = mine.shape
+    sizes = [(features,)] * 9 + [(width,)] * 3
     return kernel_call(
         ready_body,
         (xz, mine, other, *after),
-        free_in=(1, 2) + tuple(range(3, 3 + len(after))),
+        free_in=(2,),
         grid_spec=pltpu.PrefetchScalarGridSpec(
             num_scalar_prefetch=1,
             grid=(1,),
             in_specs=[const(mine.shape), const(other.shape)] + [pl.BlockSpec(memory_space=pl.ANY)] * len(after),
-            out_specs=[const((width, features))] * 4 + [const((count, features))],
-        ),
-        out_shape=[shape_of(width, features, dtype=F32)] * 4 + [shape_of(count, features, dtype=F32)],
+            out_specs=[const((width, features))] * 4 + [const(size) for size in sizes],
+        ),
+        out_shape=[shape_of(width, features, dtype=F32)] * 4 + [shape_of(*size, dtype=F32) for size in sizes],
         cost_estimate=cost(1e6, 4e6),
         name="ready",
     )
@@ -827,7 +846,7 @@
     return kernel_call(
         place_body,
         (me, *shares, *after),
-        free_in=tuple(range(1, 5 + len(after))),
+        free_in=(1, 2, 3, 4),
         grid_spec=pltpu.PrefetchScalarGridSpec(
             num_scalar_prefetch=1,
             grid=(4, PARTS),
@@ -897,13 +916,6 @@
     if size > 4:
         return [lax.psum(keep + got, "z")]
     return quarters(xz, keep, got, size, after)
-
-
-def sum_second(parts):
-    total = parts[0].astype(F32)
-    for way in range(1, len(parts)):
-        total = total + turned(parts[way], way).astype(F32)
-    return total.astype(BF16)
 
 
 def gather_z(value):
@@ -1004,59 +1016,58 @@
     part_far = (part_far.astype(F32) + other_core(part[3]).astype(F32)).astype(BF16)
     part_near = other_core(part[1])
     grads = attend_backward(1, me, segment_ids, qt, extras[1], kn, kt, vn, attended[1], grads_attended[1], earlier,
-                            (result, part_far, part_near))
+                            (part_near, part_far, result))
 
     xz = jnp.stack([lax.axis_index("x"), lax.axis_index("z")]).astype(jnp.int32)
     near, far = other_core(result), other_chip(result)
     part_across = other_chip(part_far)
-    back_own, back_near, back_far, back_across, row_sum, summed = tail(
-        me, grads, wq, wk, wv, tokens, stat, inner_sums, (near, far, part_across)
-    )
-    grads = fence(grads, row_sum)
-    feed_sum = lax.all_gather(fence(feed_sum, row_sum), DP, axis=0, tiled=True)
+    grad_output = fence(part[0], grads).astype(F32) + part_near.astype(F32) + part_across.astype(F32)
+    keep, send = halves(xz, nn(grads, attend_in).astype(BF16), grad_output.astype(BF16))
+    near, far = other_core(result), other_chip(result)
+    got = lax.ppermute(send, "x", SWAP)
+    back_own, back_near, back_far, back_across, apart, summed = tail(
+        me, grads, wq, wk, wv, tokens, stat, inner_sums, sums, (near, far, send)
+    )
+    feed_sum = lax.all_gather(fence(feed_sum, send), DP, axis=0, tiled=True)
     feed_sum = (feed_sum[:features].astype(F32), feed_sum[features:].astype(F32))
-    grad_output = fence(part[0], row_sum).astype(F32) + part_near.astype(F32) + part_across.astype(F32)
-    keep, send = halves(xz, nn(grads, attend_in).astype(BF16), grad_output.astype(BF16))
-    back_far = chip_sum(back_far, other_core(back_across), summed)
+    quarter = sum_first(xz, keep, got, (apart,))
+    back_across = other_core(fence(back_across, quarter[-1], space=pltpu.VMEM))
+    back_far = chip_sum(back_far, back_across, summed, ())
     back_there = other_chip(back_far)
-    got = lax.ppermute(send, "x", SWAP)
-    quarter = sum_first(xz, keep, got, (back_far,))
-    layer_out = place(me, [result, near, far, other_core(far)], BF16, quarter[-1:])
-    row_sum = row_sum[:1]
-    apart = jnp.concatenate([
-        jnp.sum(sum(sums), axis=0, keepdims=True),
-        jnp.pad(row_sum, ((0, 0), (0, features - row_sum.shape[1]))),
-        jnp.zeros((6, features), F32),
-    ])
-    total = sum_second(quarter)
+    share = final(me, [back_own, other_core(back_near), back_there], tokens, grad_residuals, vectors, ())
     if len(quarter) > 1:
-        held = second(total, back_far, back_there, apart)
-        mine = third(xz, gather_z(held), 32)
+        turns = [quarter[0]] + [turned(part, n + 1) for n, part in enumerate(quarter[1:])]
+        held = second(turns, back_far, back_there, apart, (share,))
+        layer_out = place(me, [result, near, far, other_core(far)], BF16, (held,))
+        mine = third(xz, gather_z(held), 32, (layer_out,))
     else:
         small = jnp.concatenate([joined(back_far[-16:]) + joined(back_there[-16:]), apart])
-        held = mine = jnp.concatenate([total, paired(lax.psum(small, "z"))])
-    share = final(me, [back_own, other_core(back_near), back_there], tokens, grad_residuals, vectors, (layer_out, held))
+        layer_out = place(me, [result, near, far, other_core(far)], BF16, ())
+        mine = jnp.concatenate([quarter[0], paired(lax.psum(small, "z"))])
+    share = fence(share, held if len(quarter) > 1 else mine, space=pltpu.VMEM)
     near, far = other_core(share), fence(other_chip(share), mine, space=pltpu.VMEM)
     input_grad = place(me, [share, near, far, other_core(far)], F32, (mine,))
-    *wide, small = ready(xz, mine, lax.ppermute(mine, "x", SWAP), width, 16, feed_sum)
+    *wide, two_gain, two_bias, output_sum, outer_bias, one_gain, one_bias, _, _, inner_bias, query, _, value = ready(
+        xz, mine, lax.ppermute(mine, "x", SWAP), width, feed_sum
+    )
     return (
         layer_out.reshape(1, length, features),
         input_grad.reshape(1, length, features),
-        small[4],
-        small[5],
+        one_gain,
+        one_bias,
         wide[0].T,
-        small[9, :width],
+        query,
         wide[1].T,
         wide[2].T,
-        small[9, 2 * width:3 * width],
+        value,
         wide[3],
-        small[2],
-        small[0],
-        small[1],
+        output_sum,
+        two_gain,
+        two_bias,
         feed_sum[1],
-        small[8],
+        inner_bias,
         feed_sum[0],
-        small[3],
+        outer_bias,
     )
 
 

time: 301 us -> 287 us (0.953)
  waiting for transfers between devices: 64.1 us -> 53.5 us
  local copies, waits for them, and re-layouts: 13.1 us -> 3.14 us
  other arithmetic: 9.63 us -> 13.8 us
  Pallas kernels: 137 us -> 141 us
    ppermute x6, waiting for transfers between devices: 24.6 us -> 6.58 us  [turned(): lax.ppermute(values, 'z', [(n, (n + way) % size) for n in range(size)])]
    ppermute x14, waiting for transfers between devices: 13.1 us -> 26 us  [other_chip(): return lax.ppermute(value, 'y', SWAP)]
    ppermute x1, waiting for transfers between devices: 14.5 us -> 5.78 us  [local(): got = lax.ppermute(send, 'x', SWAP)]
    unnamed x54 -> x36, local copies, waits for them, and re-layouts: 7.75 us -> 1.63 us
    pallas_call x24, Pallas kernels: 137 us -> 141 us  [kernel_call(): pl.pallas_call(body, out_shape=shapes if many else shapes[0], compiler_pa...]
    reduce_scatter x1, waiting for transfers between devices: 0.01 us -> 3.82 us  [local(): feed_sum = lax.psum_scatter(grad_feed, DP, scatter_dimension=0, tiled=True)]
    ppermute x1, waiting for transfers between devices: 9.2 us -> 5.4 us  [local(): lax.ppermute(mine, 'x', SWAP)]
    slice x3 -> x0, local copies, waits for them, and re-layouts: 3.76 us -> none  [the longest x1 1.75 us: local(): small[3]]
  transfers between devices with their start and end apart: 52 -> 52, of which waited for: 15 -> 13; matrix products, arithmetic and copies ran while one was open for 8% -> 10% of each run, Pallas kernels for 37% -> 40%
where the time goes in v6:
time: 287 us; the launch traced here: 284 us
  Pallas kernels  141 us (49%)
  waiting for transfers between devices  53.5 us (19%)
  starting transfers between devices  43.9 us (15%)
  matrix products  14.8 us (5%)
  between operations  14.5 us (5%)
  other arithmetic  13.8 us (5%)
  local copies, waits for them, and re-layouts  3.14 us (1%)
    pallas_call x24, Pallas kernels, kernel_call(): pl.pallas_call(body, out_shape=shapes if many else shapes[0], compiler_pa...  141 us
    ppermute x14, waiting for transfers between devices, other_chip(): return lax.ppermute(value, 'y', SWAP)  26 us
    ppermute x14, starting transfers between devices, other_chip(): return lax.ppermute(value, 'y', SWAP)  18.8 us
    ppermute x6, starting transfers between devices, turned(): lax.ppermute(values, 'z', [(n, (n + way) % size) for n in range(size)])  16.5 us
    dot_general x1, matrix products, local(): lax.dot_general(fence(left, *far_sums), right, (((1,), (1,)), ((0,), (0,)...  10.1 us
    ppermute x6, waiting for transfers between devices, turned(): lax.ppermute(values, 'z', [(n, (n + way) % size) for n in range(size)])  6.58 us
    ppermute x1, waiting for transfers between devices, local(): got = lax.ppermute(send, 'x', SWAP)  5.78 us
  transfers between devices with their start and end apart: 52, of which 13 were waited for; matrix products, arithmetic and copies ran while one was open for 10% of the time, Pallas kernels for 40%

profile of v6, /device:TPU:0, one launch (start us, length us, event | category | flops | bytes accessed | tf_op | source)
XLA Modules:
  0.0 284.1 jit_solution(3311209125129979797)
XLA Ops:
  9.4 10.6 %project.1 = (bf16[2048,768]{1,0:T(8,128)(2,1)}, bf16[3,128,2048]{2,1,0:T(8,128)(2,1)}, bf16[192,2048]{1,0:T(8,128)(2,1)}, bf16[3,80,2048]{2,1,0:T(8,128)(2,1)},...) custom-call(bf16[2048,768]{1,0:T(8,128)(2,1)} %bitcast.26, ...), custom_call_target="tpu_custom_call" | custom-call | flops 6000000000 | bytes 14000000 | tf_op jit(solution)/shard_map/project/pallas_call | solution.py:83
  20.0 9.2 %attend_forward.2 = (bf16[4,192,256]{2,1,0:T(8,128)(2,1)}, bf16[3,16,1024]{2,1,0:T(8,128)(2,1)}, bf16[192,256]{1,0:T(8,128)(2,1)}, bf16[192,256]{1,0:T(8,128)(2,...) custom-call(s32[1]{0:T(128)} %bitcast.refs_0_.me_ref, s32[1,2048]{1,0:T(1,128)S(1)} %copy-done.5, ...), custom_call_target="tpu_custom_call" | custom-call | flops 8999999488 | bytes 5000000 | tf_op jit(solution)/shard_map/attend_forward/pallas_call | solution.py:83
  34.6 11.7 %attend_forward.3 = (bf16[4,192,256]{2,1,0:T(8,128)(2,1)}, bf16[3,16,1024]{2,1,0:T(8,128)(2,1)}, bf16[192,256]{1,0:T(8,128)(2,1)}, bf16[192,256]{1,0:T(8,128)(2,...) custom-call(s32[1]{0:T(128)} %bitcast.refs_0_.me_ref, s32[1,2048]{1,0:T(1,128)S(1)} %copy-done.5, ...), custom_call_target="tpu_custom_call" | custom-call | flops 8999999488 | bytes 5000000 | tf_op jit(solution)/shard_map/attend_forward/pallas_call | solution.py:83
  66.4 6.5 %feed.4 = (bf16[2,2048,768]{2,1,0:T(8,128)(2,1)}, bf16[2,2048,768]{2,1,0:T(8,128)(2,1)}, bf16[512,768]{1,0:T(8,128)(2,1)}, bf16[512,768]{1,0:T(8,128)(2,1)}, bf1...) custom-call(s32[1]{0:T(128)} %bitcast.refs_0_.me_ref, ...), custom_call_target="tpu_custom_call" | custom-call | flops 5000000000 | bytes 8000000 | tf_op jit(solution)/shard_map/feed/pallas_call | solution.py:83
  73.0 6.5 %feed.5 = (bf16[2,2048,768]{2,1,0:T(8,128)(2,1)}, bf16[2,2048,768]{2,1,0:T(8,128)(2,1)}, bf16[512,768]{1,0:T(8,128)(2,1)}, bf16[512,768]{1,0:T(8,128)(2,1)}, bf1...) custom-call(s32[1]{0:T(128)} %bitcast.refs_0_.me_ref, ...), custom_call_target="tpu_custom_call", output_to_operand_aliasing={{0}: (7, {}), {1}: (8, {}), {2}: (9, {}), {3}: (10, {})} | custom-call | flops 5000000000 | bytes 8000000 | tf_op jit(solution)/shard_map/feed/pallas_call | solution.py:83
  80.1 6.5 %feed.6 = (bf16[2,2048,768]{2,1,0:T(8,128)(2,1)}, bf16[2,2048,768]{2,1,0:T(8,128)(2,1)}, bf16[512,768]{1,0:T(8,128)(2,1)}, bf16[512,768]{1,0:T(8,128)(2,1)}, bf1...) custom-call(s32[1]{0:T(128)} %bitcast.refs_0_.me_ref, ...), custom_call_target="tpu_custom_call", output_to_operand_aliasing={{0}: (7, {}), {1}: (8, {})} | custom-call | flops 5000000000 | bytes 8000000 | tf_op jit(solution)/shard_map/feed/pallas_call | solution.py:83
  86.6 6.5 %feed.7 = (bf16[2,2048,768]{2,1,0:T(8,128)(2,1)}, bf16[2,2048,768]{2,1,0:T(8,128)(2,1)}, bf16[512,768]{1,0:T(8,128)(2,1)}, bf16[512,768]{1,0:T(8,128)(2,1)}, bf1...) custom-call(s32[1]{0:T(128)} %bitcast.refs_0_.me_ref, ...), custom_call_target="tpu_custom_call", output_to_operand_aliasing={{0}: (7, {}), {1}: (8, {}), {2}: (9, {}), {3}: (10, {})} | custom-call | flops 5000000000 | bytes 8000000 | tf_op jit(solution)/shard_map/feed/pallas_call | solution.py:83
  100.1 10.1 %convolution_convert_fusion = bf16[2,768,768]{2,1,0:T(8,128)(2,1)} fusion(bf16[2,2048,768]{2,1,0:T(8,128)(2,1)} %fence.22, bf16[2,2048,768]{2,1,0:T(8,128)(2,1)} %get-tuple-element.201), kind=kOutput, calls=%fused_computation | convolution fusion | flops 4833017856 | bytes 14942208 | tf_op jit(solution)/shard_map/dot_general | solution.py:1003
  110.8 3.7 %middle_back.3 = (f32[256,768]{1,0:T(8,128)}, bf16[256,768]{1,0:T(8,128)(2,1)}, bf16[192,256]{1,0:T(8,128)(2,1)}, bf16[192,256]{1,0:T(8,128)(2,1)}, bf16[192,256...) custom-call(s32[1]{0:T(128)} %bitcast.refs_0_.me_ref, ...), custom_call_target="tpu_custom_call" | custom-call | flops 2000000000 | bytes 4000000 | tf_op jit(solution)/shard_map/middle_back/pallas_call | solution.py:83
  116.4 3.6 %middle_back.2 = (f32[256,768]{1,0:T(8,128)}, bf16[256,768]{1,0:T(8,128)(2,1)}, bf16[192,256]{1,0:T(8,128)(2,1)}, bf16[192,256]{1,0:T(8,128)(2,1)}, bf16[192,256...) custom-call(s32[1]{0:T(128)} %bitcast.refs_0_.me_ref, ...), custom_call_target="tpu_custom_call" | custom-call | flops 2000000000 | bytes 4000000 | tf_op jit(solution)/shard_map/middle_back/pallas_call | solution.py:83
  127.2 13.5 %attend_backward.2 = (bf16[192,1024]{1,0:T(8,128)(2,1)}, f32[192,2048]{1,0:T(8,128)}, f32[192,2048]{1,0:T(8,128)}) custom-call(s32[1]{0:T(128)} %bitcast.refs_0_.me_ref, s32[1,2048]{1,0:T(1,128)S(1)} %copy-done.6, s32[1,2048]{1,0:T(1,128)S(1)} %copy-done.6, bf16[3,128,2048]{2,1,0:T(8,128)(2,1)} %get-tuple-element.116.refs_3_, ...), custom_call_target="tpu_custom_call" | custom-call | flops 16000000000 | bytes 10000000 | tf_op jit(solution)/shard_map/attend_backward/pallas_call | solution.py:83
  142.3 5.5 %collective-permute-done.21 = bf16[512,768]{1,0:T(8,128)(2,1)} collective-permute-done((bf16[512,768]{1,0:T(8,128)(2,1)S(1)}, bf16[512,768]{1,0:T(8,128)(2,1)}, u32[]{:S(2)}, u32[]{:S(2)}) %collective-permute-start.21) | collective-permute-done | bytes 786464 | tf_op jit(solution)/shard_map/ppermute | solution.py:883
  152.2 17.9 %attend_backward.3.refs_1_.g_ref = bf16[576,2048]{1,0:T(8,128)(2,1)} custom-call(s32[1]{0:T(128)} %bitcast.refs_0_.me_ref, s32[1,2048]{1,0:T(1,128)S(1)} %copy-done.6, s32[1,2048]{1,0:T(1,128)S(1)} %copy-done.6, bf16[3,128,2048]{2,1,0:T(8,128)(2,1)} %get-tuple-element.116.refs_3_, bf16[3,16,1024]{2,1,0:T(8,128)(2,1)} %get-tuple-element.123.rest_0_.refs_4_, ...), custom_call_target="tpu_custom_call" | custom-call | flops 16000000000 | bytes 10000000 | tf_op jit(solution)/shard_map/attend_backward/pallas_call | solution.py:83
  170.2 4.7 %convolution_convert_fusion.1.g_ref = bf16[576,768]{1,0:T(8,128)(2,1)S(1)} fusion(bf16[576,2048]{1,0:T(8,128)(2,1)} %attend_backward.3.refs_1_.g_ref, bf16[2048,768]{1,0:T(8,128)(2,1)} %get-tuple-element.178), kind=kOutput, calls=%fused_computation.7 | convolution fusion | flops 1812381696 | bytes 6389760 | tf_op jit(solution)/shard_map/dot_general | solution.py:23
  177.6 3.8 %reduce-scatter.2.cloned.1.call-done.refs_0_ = bf16[192,768]{1,0:T(8,128)(2,1)} async-done(((bf16[1536,768]{1,0:T(8,128)(2,1)}), bf16[192,768]{1,0:T(8,128)(2,1)}) %reduce-scatter.2.cloned.1.call-update) | async-done | bytes 294928 | tf_op jit(solution)/shard_map/reduce_scatter | solution.py:1005
  182.2 11.0 %tail.1 = (bf16[512,768]{1,0:T(8,128)(2,1)}, bf16[512,768]{1,0:T(8,128)(2,1)S(1)}, bf16[512,768]{1,0:T(8,128)(2,1)}, bf16[528,768]{1,0:T(8,128)(2,1)S(1)}, f32[8,768]{1,0:T(8,128)}, /*index=5*/f32[8,768]{1,0:T(8,128)}) custom-call(s32[1]{0:T(128)} %bitcast.refs_0_.me_ref, bf16[576,2048]{1,0:T(8,128)(2,1)} %attend_backward.3.refs_1_.g_ref, ...), custom_call_target="tpu_custom_call" | custom-call | flops 4000000000 | bytes 10000000 | tf_op jit(solution)/shard_map/tail/pallas_call | solution.py:83
  193.2 5.8 %collective-permute-done.36.refs_2_ = bf16[384,768]{1,0:T(8,128)(2,1)S(1)} collective-permute-done((bf16[384,768]{1,0:T(8,128)(2,1)}, bf16[384,768]{1,0:T(8,128)(2,1)S(1)}, u32[]{:S(2)}, u32[]{:S(2)}) %collective-permute-start.36) | collective-permute-done | bytes 589856 | tf_op jit(solution)/shard_map/ppermute | solution.py:1027
  210.5 14.8 %collective-permute-done.41.b2_ref.refs_5_ = bf16[528,768]{1,0:T(8,128)(2,1)S(1)} collective-permute-done((bf16[528,768]{1,0:T(8,128)(2,1)S(1)}, bf16[528,768]{1,0:T(8,128)(2,1)S(1)}, u32[]{:S(2)}, u32[]{:S(2)}) %collective-permute-start.41) | collective-permute-done | bytes 811040 | tf_op jit(solution)/shard_map/ppermute | solution.py:883
  231.6 10.3 %collective-permute-start.45 = (bf16[128,768]{1,0:T(8,128)(2,1)}, bf16[128,768]{1,0:T(8,128)(2,1)S(1)}, u32[]{:S(2)}, u32[]{:S(2)}) collective-permute-start(bf16[128,768]{1,0:T(8,128)(2,1)} %second.1.rest_0_.refs_1_), channel_id=1, source_target_pairs={{0,8},{8,16},{16,24},{24,0},{1,9},{9,17},{17,25},{25,1},{2,10},{10... | collective-permute-start | bytes 589832 | tf_op jit(solution)/shard_map/ppermute | solution.py:911
  244.3 4.7 %place.2.refs_5_ = bf16[2048,768]{1,0:T(8,128)(2,1)} custom-call(s32[1]{0:T(128)} %bitcast.refs_0_.me_ref, bf16[512,768]{1,0:T(8,128)(2,1)S(1)} %copy-done.2, bf16[512,768]{1,0:T(8,128)(2,1)S(1)} %copy-done.4, bf16[512,768]{1,0:T(8,128)(2,1)} %collective-permute-done.23.rest_7_.p2_ref, bf16[512,768]{1,0:T(8,128)(2,1)} %collective-permute-done.24.p3_ref, ...), custom_call_target="tpu_custom_call" | custom-call | flops 1000000 | bytes 9000000 | tf_op jit(solution)/shard_map/place/pallas_call | solution.py:83
  249.0 6.6 %collective-permute-done.46.refs_3_ = bf16[128,768]{1,0:T(8,128)(2,1)S(1)} collective-permute-done((bf16[128,768]{1,0:T(8,128)(2,1)}, bf16[128,768]{1,0:T(8,128)(2,1)S(1)}, u32[]{:S(2)}, u32[]{:S(2)}) %collective-permute-start.46) | collective-permute-done | bytes 196640 | tf_op jit(solution)/shard_map/ppermute | solution.py:911
  259.3 5.2 %place.3 = f32[2048,768]{1,0:T(8,128)} custom-call(s32[1]{0:T(128)} %bitcast.refs_0_.me_ref, bf16[512,768]{1,0:T(8,128)(2,1)S(1)} %fence.20.p0_ref, bf16[512,768]{1,0:T(8,128)(2,1)} %collective-permute-done.43.p1_ref, bf16[512,768]{1,0:T(8,128)(2,1)S(1)} %fence.21.p2_ref, bf16[512,768]{1,0:T(8,128)(2,1)S(1)} %collective-permute-done.48.p3_ref, ...), custom_call_target="tpu_custom_call" | custom-call | flops 1000000 | bytes 9000000 | tf_op jit(solution)/shard_map/place/pallas_call | solution.py:83
  264.4 4.2 %slice_convert_fusion = (f32[768,768]{1,0:T(8,128)}, f32[768,768]{1,0:T(8,128)}) fusion(bf16[1536,768]{1,0:T(8,128)(2,1)} %all-gather.2.cloned.1.call-done), kind=kLoop, calls=%fused_computation.8 | loop fusion | flops 1179648 | bytes 7077888 | tf_op jit(solution)/shard_map/convert_element_type | solution.py:1032
  268.6 5.4 %collective-permute-done.49.other_ref = bf16[416,768]{1,0:T(8,128)(2,1)S(1)} collective-permute-done((bf16[416,768]{1,0:T(8,128)(2,1)}, bf16[416,768]{1,0:T(8,128)(2,1)S(1)}, u32[]{:S(2)}, u32[]{:S(2)}) %collective-permute-start.49) | collective-permute-done | bytes 639008 | tf_op jit(solution)/shard_map/ppermute | solution.py:1051
  (167 shorter events, 81.6 us)
Async XLA Ops:
  7.2 174.2 %reduce-scatter.2.cloned.1.call-start = ((), (), s32[]{:S(2)}) async-start(), calls=%async_computation.1 | async-start | bytes 2654208 | tf_op jit(solution)/shard_map/reduce_scatter | solution.py:1005
  29.8 20.3 %collective-permute-start.3 = (bf16[192,768]{1,0:T(8,128)(2,1)S(1)}, bf16[192,768]{1,0:T(8,128)(2,1)S(1)}, u32[]{:S(2)}, u32[]{:S(2)}) collective-permute-start(bf16[192,768]{1,0:T(8,128)(2,1)S(1)} %copy-done.12), channel_id=1, source_target_pairs={{0,1},{1,0},{2,3},{3,2},{4,5},{5,4},{6,7},{7,6},{8,9},{9,8},{10,11... | collective-permute-start | bytes 884744 | tf_op jit(solution)/shard_map/ppermute | solution.py:879
  29.9 20.2 %collective-permute-start.4 = (bf16[192,768]{1,0:T(8,128)(2,1)S(1)}, bf16[192,768]{1,0:T(8,128)(2,1)S(1)}, u32[]{:S(2)}, u32[]{:S(2)}) collective-permute-start(bf16[192,768]{1,0:T(8,128)(2,1)S(1)} %copy-done.12), channel_id=1, source_target_pairs={{0,2},{2,0},{1,3},{3,1},{4,6},{6,4},{5,7},{7,5},{8,10},{10,8},{9,1... | collective-permute-start | bytes 884744 | tf_op jit(solution)/shard_map/ppermute | solution.py:883
  32.8 17.3 %collective-permute-start.5 = (bf16[192,768]{1,0:T(8,128)(2,1)S(1)}, bf16[192,768]{1,0:T(8,128)(2,1)S(1)}, u32[]{:S(2)}, u32[]{:S(2)}) collective-permute-start(bf16[192,768]{1,0:T(8,128)(2,1)S(1)} %copy-done.12), channel_id=1, source_target_pairs={{0,3},{1,2},{2,1},{3,0},{4,7},{5,6},{6,5},{7,4},{8,11},{9,10},{10,... | collective-permute-start | bytes 884744 | tf_op jit(solution)/shard_map/ppermute | solution.py:887
  93.8 20.7 %collective-permute-start.19 = (bf16[256,768]{1,0:T(8,128)(2,1)S(1)}, bf16[256,768]{1,0:T(8,128)(2,1)S(1)}, u32[]{:S(2)}, u32[]{:S(2)}) collective-permute-start(bf16[256,768]{1,0:T(8,128)(2,1)S(1)} %get-tuple-element.152), channel_id=1, source_target_pairs={{0,1},{1,0},{2,3},{3,2},{4,5},{5,4},{6,7},{7,6},{8,9},{9,8},{10,11... | collective-permute-start | bytes 1179656 | tf_op jit(solution)/shard_map/ppermute | solution.py:879
  98.4 17.5 %collective-permute-start.20 = (bf16[256,768]{1,0:T(8,128)(2,1)}, bf16[256,768]{1,0:T(8,128)(2,1)S(1)}, u32[]{:S(2)}, u32[]{:S(2)}) collective-permute-start(bf16[256,768]{1,0:T(8,128)(2,1)} %add_convert_fusion.1.refs_2_), channel_id=1, source_target_pairs={{0,2},{2,0},{1,3},{3,1},{4,6},{6,4},{5,7},{7,5},{8,10},{10,8},{9,1... | collective-permute-start | bytes 1179656 | tf_op jit(solution)/shard_map/ppermute | solution.py:883
  100.1 22.8 %collective-permute-start.18 = (bf16[512,768]{1,0:T(8,128)(2,1)}, bf16[512,768]{1,0:T(8,128)(2,1)}, u32[]{:S(2)}, u32[]{:S(2)}) collective-permute-start(bf16[512,768]{1,0:T(8,128)(2,1)} %fence.15), channel_id=1, source_target_pairs={{0,1},{1,0},{2,3},{3,2},{4,5},{5,4},{6,7},{7,6},{8,9},{9,8},{10,11... | collective-permute-start | bytes 2359304 | tf_op jit(solution)/shard_map/ppermute | solution.py:879
  110.2 154.2 %all-gather.2.cloned.1.call-start = ((), (), s32[]{:S(2)}) async-start(), calls=%async_computation.2 | async-start | bytes 2654208 | tf_op jit(solution)/shard_map/all_gather | solution.py:1031
  122.9 17.8 %collective-permute-start.34 = (bf16[192,768]{1,0:T(8,128)(2,1)S(1)}, bf16[192,768]{1,0:T(8,128)(2,1)}, u32[]{:S(2)}, u32[]{:S(2)}) collective-permute-start(bf16[192,768]{1,0:T(8,128)(2,1)S(1)} %get-tuple-element.177), channel_id=1, source_target_pairs={{0,1},{1,0},{2,3},{3,2},{4,5},{5,4},{6,7},{7,6},{8,9},{9,8},{10,11... | collective-permute-start | bytes 884744 | tf_op jit(solution)/shard_map/ppermute | solution.py:879
  124.6 27.6 %collective-permute-start.33 = (bf16[192,768]{1,0:T(8,128)(2,1)S(1)}, bf16[192,768]{1,0:T(8,128)(2,1)S(1)}, u32[]{:S(2)}, u32[]{:S(2)}) collective-permute-start(bf16[192,768]{1,0:T(8,128)(2,1)S(1)} %get-tuple-element.175), channel_id=1, source_target_pairs={{0,1},{1,0},{2,3},{3,2},{4,5},{5,4},{6,7},{7,6},{8,9},{9,8},{10,11... | collective-permute-start | bytes 884744 | tf_op jit(solution)/shard_map/ppermute | solution.py:879
  124.8 26.5 %collective-permute-start.25 = (bf16[192,256]{1,0:T(8,128)(2,1)}, bf16[192,256]{1,0:T(8,128)(2,1)}, u32[]{:S(2)}, u32[]{:S(2)}) collective-permute-start(bf16[192,256]{1,0:T(8,128)(2,1)} %get-tuple-element.158), channel_id=1, source_target_pairs={{0,1},{1,0},{2,3},{3,2},{4,5},{5,4},{6,7},{7,6},{8,9},{9,8},{10,11... | collective-permute-start | bytes 294920 | tf_op jit(solution)/shard_map/ppermute | solution.py:879
  125.2 26.2 %collective-permute-start.26 = (bf16[192,256]{1,0:T(8,128)(2,1)S(1)}, bf16[192,256]{1,0:T(8,128)(2,1)}, u32[]{:S(2)}, u32[]{:S(2)}) collective-permute-start(bf16[192,256]{1,0:T(8,128)(2,1)S(1)} %get-tuple-element.159), channel_id=1, source_target_pairs={{0,2},{2,0},{1,3},{3,1},{4,6},{6,4},{5,7},{7,5},{8,10},{10,8},{9,1... | collective-permute-start | bytes 294920 | tf_op jit(solution)/shard_map/ppermute | solution.py:883
  126.4 21.3 %collective-permute-start.21 = (bf16[512,768]{1,0:T(8,128)(2,1)S(1)}, bf16[512,768]{1,0:T(8,128)(2,1)}, u32[]{:S(2)}, u32[]{:S(2)}) collective-permute-start(bf16[512,768]{1,0:T(8,128)(2,1)S(1)} %fence.16.refs_13_), channel_id=1, source_target_pairs={{0,2},{2,0},{1,3},{3,1},{4,6},{6,4},{5,7},{7,5},{8,10},{10,8},{9,1... | collective-permute-start | bytes 2359304 | tf_op jit(solution)/shard_map/ppermute | solution.py:883
  147.8 27.1 %collective-permute-start.35 = (bf16[192,768]{1,0:T(8,128)(2,1)S(1)}, bf16[192,768]{1,0:T(8,128)(2,1)}, u32[]{:S(2)}, u32[]{:S(2)}) collective-permute-start(bf16[192,768]{1,0:T(8,128)(2,1)S(1)} %add_convert_fusion.4.refs_17_), channel_id=1, source_target_pairs={{0,2},{2,0},{1,3},{3,1},{4,6},{6,4},{5,7},{7,5},{8,10},{10,8},{9,1... | collective-permute-start | bytes 884744 | tf_op jit(solution)/shard_map/ppermute | solution.py:883
  151.3 30.9 %collective-permute-start.22 = (bf16[512,768]{1,0:T(8,128)(2,1)S(1)}, bf16[512,768]{1,0:T(8,128)(2,1)S(1)}, u32[]{:S(2)}, u32[]{:S(2)}) collective-permute-start(bf16[512,768]{1,0:T(8,128)(2,1)S(1)} %fusion.3.refs_18_.p0_ref), channel_id=1, source_target_pairs={{0,1},{1,0},{2,3},{3,2},{4,5},{5,4},{6,7},{7,6},{8,9},{9,8},{10,11... | collective-permute-start | bytes 2359304 | tf_op jit(solution)/shard_map/ppermute | solution.py:879
  151.4 30.8 %collective-permute-start.23 = (bf16[512,768]{1,0:T(8,128)(2,1)S(1)}, bf16[512,768]{1,0:T(8,128)(2,1)}, u32[]{:S(2)}, u32[]{:S(2)}) collective-permute-start(bf16[512,768]{1,0:T(8,128)(2,1)S(1)} %fusion.3.refs_18_.p0_ref), channel_id=1, source_target_pairs={{0,2},{2,0},{1,3},{3,1},{4,6},{6,4},{5,7},{7,5},{8,10},{10,8},{9,1... | collective-permute-start | bytes 2359304 | tf_op jit(solution)/shard_map/ppermute | solution.py:883
  181.4 17.5 %collective-permute-start.36 = (bf16[384,768]{1,0:T(8,128)(2,1)}, bf16[384,768]{1,0:T(8,128)(2,1)S(1)}, u32[]{:S(2)}, u32[]{:S(2)}) collective-permute-start(bf16[384,768]{1,0:T(8,128)(2,1)} %get-tuple-element.180.rest_8_.refs_1_), channel_id=1, source_target_pairs={{0,4},{4,0},{1,5},{5,1},{2,6},{6,2},{3,7},{7,3},{8,12},{12,8},{9,1... | collective-permute-start | bytes 1769480 | tf_op jit(solution)/shard_map/ppermute | solution.py:1027
  205.2 20.2 %collective-permute-start.41 = (bf16[528,768]{1,0:T(8,128)(2,1)S(1)}, bf16[528,768]{1,0:T(8,128)(2,1)S(1)}, u32[]{:S(2)}, u32[]{:S(2)}) collective-permute-start(bf16[528,768]{1,0:T(8,128)(2,1)S(1)} %chip_sum.1.refs_4_), channel_id=1, source_target_pairs={{0,2},{2,0},{1,3},{3,1},{4,6},{6,4},{5,7},{7,5},{8,10},{10,8},{9,1... | collective-permute-start | bytes 2433032 | tf_op jit(solution)/shard_map/ppermute | solution.py:883
  206.6 21.7 %collective-permute-start.37 = (bf16[96,768]{1,0:T(8,128)(2,1)S(1)}, bf16[96,768]{1,0:T(8,128)(2,1)S(1)}, u32[]{:S(2)}, u32[]{:S(2)}) collective-permute-start(bf16[96,768]{1,0:T(8,128)(2,1)S(1)} %copy-done.17), channel_id=1, source_target_pairs={{0,8},{8,16},{16,24},{24,0},{1,9},{9,17},{17,25},{25,1},{2,10},{10... | collective-permute-start | bytes 442376 | tf_op jit(solution)/shard_map/ppermute | solution.py:911
  207.0 21.4 %collective-permute-start.38 = (bf16[96,768]{1,0:T(8,128)(2,1)S(1)}, bf16[96,768]{1,0:T(8,128)(2,1)S(1)}, u32[]{:S(2)}, u32[]{:S(2)}) collective-permute-start(bf16[96,768]{1,0:T(8,128)(2,1)S(1)} %copy-done.16), channel_id=1, source_target_pairs={{0,16},{8,24},{16,0},{24,8},{1,17},{9,25},{17,1},{25,9},{2,18},{10... | collective-permute-start | bytes 442376 | tf_op jit(solution)/shard_map/ppermute | solution.py:911
  207.1 21.3 %collective-permute-start.39 = (bf16[96,768]{1,0:T(8,128)(2,1)S(1)}, bf16[96,768]{1,0:T(8,128)(2,1)S(1)}, u32[]{:S(2)}, u32[]{:S(2)}) collective-permute-start(bf16[96,768]{1,0:T(8,128)(2,1)S(1)} %copy-done.10), channel_id=1, source_target_pairs={{0,24},{8,0},{16,8},{24,16},{1,25},{9,1},{17,9},{25,17},{2,26},{10... | collective-permute-start | bytes 442376 | tf_op jit(solution)/shard_map/ppermute | solution.py:911
  210.5 33.7 %collective-permute-start.24 = (bf16[512,768]{1,0:T(8,128)(2,1)}, bf16[512,768]{1,0:T(8,128)(2,1)}, u32[]{:S(2)}, u32[]{:S(2)}) collective-permute-start(bf16[512,768]{1,0:T(8,128)(2,1)} %collective-permute-done.23.rest_7_.p2_ref), channel_id=1, source_target_pairs={{0,1},{1,0},{2,3},{3,2},{4,5},{5,4},{6,7},{7,6},{8,9},{9,8},{10,11... | collective-permute-start | bytes 2359304 | tf_op jit(solution)/shard_map/ppermute | solution.py:879
  230.2 26.8 %collective-permute-start.44 = (bf16[512,768]{1,0:T(8,128)(2,1)S(1)}, bf16[512,768]{1,0:T(8,128)(2,1)S(1)}, u32[]{:S(2)}, u32[]{:S(2)}) collective-permute-start(bf16[512,768]{1,0:T(8,128)(2,1)S(1)} %fence.20.p0_ref), channel_id=1, source_target_pairs={{0,2},{2,0},{1,3},{3,1},{4,6},{6,4},{5,7},{7,5},{8,10},{10,8},{9,1... | collective-permute-start | bytes 2359304 | tf_op jit(solution)/shard_map/ppermute | solution.py:883
  231.6 17.3 %collective-permute-start.45 = (bf16[128,768]{1,0:T(8,128)(2,1)}, bf16[128,768]{1,0:T(8,128)(2,1)S(1)}, u32[]{:S(2)}, u32[]{:S(2)}) collective-permute-start(bf16[128,768]{1,0:T(8,128)(2,1)} %second.1.rest_0_.refs_1_), channel_id=1, source_target_pairs={{0,8},{8,16},{16,24},{24,0},{1,9},{9,17},{17,25},{25,1},{2,10},{10... | collective-permute-start | bytes 589832 | tf_op jit(solution)/shard_map/ppermute | solution.py:911
  (46 other events, 424.6 us)
Sparse Core Ops, SparseCore 0:
  110.3 71.0 reduce-scatter.1
  183.6 70.2 all-gather.1

commit v7 on v6

--- a/solution.py
+++ b/solution.py
@@ -399,71 +399,77 @@
     )
 
 
-def feed_body(me_ref, x0_ref, x1_ref, g_ref, inner_ref, vec_ref, outer_ref, *rest):
-    left_ref, right_ref, out0_ref, out1_ref, back0_ref, back1_ref, sum_ref = rest[-7:]
+def feed_body(me_ref, *refs):
+    count = 2 * PARTS
+    x_refs = refs[:count]
+    g_ref, inner_ref, vec_ref, outer_ref = refs[count:count + 4]
+    before = refs[count + 4:-(count + 8)]
+    out_refs, back_refs = refs[-(count + 8):-(count + 6)], refs[-(count + 6):-6]
+    sum_ref, grad_ref, x_all, g_all, act_all, dh_all = refs[-6:]
     i = pl.program_id(0)
-
-    @pl.when(i == 0)
-    def _():
-        left_ref[1] = x0_ref[...]
-
-    @pl.when(i == 1)
-    def _():
-        left_ref[1] = x1_ref[...]
-
-    right_ref[0] = g_ref[...]
-    hidden = nn(left_ref[1], inner_ref[...]) + vec_ref[7:8, :]
+    at = pl.ds(pl.multiple_of(i * TILE, TILE), TILE)
+    for n, x_ref in enumerate(x_refs):
+        @pl.when(i == n)
+        def _(n=n, x_ref=x_ref):
+            x_all[n * TILE:(n + 1) * TILE] = x_ref[...]
+
+    g_all[at] = g_ref[...]
+    hidden = nn(x_all[at], inner_ref[...]) + vec_ref[7:8, :]
     half = 0.5 + 0.5 * lax.erf(hidden * 0.5 ** 0.5)
     act = (hidden * half).astype(BF16)
-    left_ref[0] = act
+    act_all[at] = act
     slope = half + hidden * (jnp.exp(-0.5 * hidden * hidden) * 0.3989422804014327)
     dh = (nt(g_ref[...], outer_ref[...]) * slope).astype(BF16)
-    right_ref[1] = dh
+    dh_all[at] = dh
     sums = fold(dh.astype(F32))
     out = nn(act, outer_ref[...]).astype(BF16)
     back = nt(dh, inner_ref[...]).astype(BF16)
 
     @pl.when(i == 0)
     def _():
-        sum_ref[...] = sums
-        out0_ref[...] = out
-        back0_ref[...] = back
-
-    @pl.when(i == 1)
+        sum_ref[...] = jnp.zeros_like(sum_ref)
+
+    sum_ref[...] += sums
+    for n in range(count):
+        @pl.when(i == n)
+        def _(n=n):
+            out_refs[n % 2][n // 2 * TILE:(n // 2 + 1) * TILE] = out
+            back_refs[n][...] = back
+
+    @pl.when(i == count - 1)
     def _():
-        sum_ref[...] += sums
-        out1_ref[...] = out
-        back1_ref[...] = back
-
-
-def feed(part, base, me, first, second, cot, inner, vectors, outer, kept, outs):
-    length, features = cot.shape
+        for n, (left, right) in enumerate(((act_all, g_all), (x_all, dh_all))):
+            grad = tn(left[...], right[...])
+            for ref in before:
+                grad = grad + ref[n].astype(F32)
+            grad_ref[n] = grad.astype(BF16)
+
+
+def feed(base, me, pieces, cot, inner, vectors, outer, before):
+    features = cot.shape[1]
     units = inner.shape[1]
-    at = 4 * part + base
-    rows = pl.BlockSpec((2, TILE, features), lambda i, m: (0, at + i, 0))
+    count = 2 * PARTS
     piece = const((TILE, features))
-    half = pl.BlockSpec((TILE, features), lambda i, m: (part, 0))
-    kept = (*kept, *outs)
-    targets = list(range(2)) * (len(kept) >= 2) + [2, 3] * (len(outs) > 0)
+    scratch = lambda n: pltpu.VMEM((count * TILE, n), BF16)
     return kernel_call(
         feed_body,
-        (me, first, second, cot, inner, vectors, outer, *kept),
-        free_in=(1, 2),
-        free_out=(5,),
+        (me, *pieces, cot, inner, vectors, outer, *before),
+        free_in=tuple(range(1, count + 1)),
+        free_out=(3, 5),
         grid_spec=pltpu.PrefetchScalarGridSpec(
             num_scalar_prefetch=1,
-            grid=(2,),
-            in_specs=[
-                piece, piece,
-                pl.BlockSpec((TILE, features), lambda i, m: (4 * part + (m[0] ^ (base + i)), 0)),
-                const(inner.shape), const(vectors.shape), const(outer.shape),
-            ] + [pl.BlockSpec(memory_space=pl.ANY)] * len(kept),
-            out_specs=[rows, rows, half, half, piece, piece, const((8, units))],
-        ),
-        out_shape=[shape_of(2, length, features)] * 2 + [shape_of(PARTS * TILE, features)] * 2
-        + [shape_of(TILE, features)] * 2 + [shape_of(8, units, dtype=F32)],
-        input_output_aliases={7 + n: target for n, target in enumerate(targets)},
-        cost_estimate=cost(5e9, 8e6, 1e6),
+            grid=(count,),
+            in_specs=[piece] * count
+            + [pl.BlockSpec((TILE, features), lambda i, m: (4 * (i // 2) + (m[0] ^ (base + i % 2)), 0)),
+               const(inner.shape), const(vectors.shape), const(outer.shape)]
+            + [const(v.shape) for v in before],
+            out_specs=[const((PARTS * TILE, features))] * 2 + [piece] * count
+            + [const((8, units)), const((2, units, features))],
+            scratch_shapes=[scratch(features), scratch(features), scratch(units), scratch(units)],
+        ),
+        out_shape=[shape_of(PARTS * TILE, features)] * 2 + [shape_of(TILE, features)] * count
+        + [shape_of(8, units, dtype=F32), shape_of(2, units, features)],
+        cost_estimate=cost(15e9, 12e6, 2e6),
         name="feed",
     )
 
@@ -529,7 +535,7 @@
 
 
 def tail_body(me_ref, g_ref, wq_ref, wk_ref, wv_ref, x_ref, stat_ref, *rest):
-    early, units = rest[:PARTS], rest[PARTS:3 * PARTS]
+    early, units = rest[:PARTS], rest[PARTS:PARTS + 2]
     o0_ref, o1_ref, o2_ref, o3_ref, apart_ref, vec_ref, sum_ref, row_ref = rest[-8:]
     i, p = pl.program_id(0), pl.program_id(1)
     grads = g_ref[...]
@@ -581,7 +587,6 @@
     return kernel_call(
         tail_body,
         (me, grads, wq, wk, wv, tokens, stat, *early, *units, *after),
-        free_in=tuple(range(7 + 3 * PARTS, 9 + 3 * PARTS)),
         free_out=(1, 3),
         grid_spec=pltpu.PrefetchScalarGridSpec(
             num_scalar_prefetch=1,
@@ -623,7 +628,8 @@
     )[0]
 
 
-def halves_body(xz_ref, g_ref, go_ref, keep_ref, send_ref):
+def halves_body(xz_ref, g_ref, go_ref, *rest):
+    keep_ref, send_ref = rest[-2:]
     width = go_ref.shape[0]
     for to_ref, half in ((keep_ref, xz_ref[0]), (send_ref, 1 - xz_ref[0])):
         @pl.when(half == 0)
@@ -636,17 +642,18 @@
             to_ref[width:] = go_ref[...]
 
 
-def halves(xz, grad_weights, grad_output):
+def halves(xz, grad_weights, grad_output, after):
     width, features = grad_output.shape
     half = const((2 * width, features))
     return kernel_call(
         halves_body,
-        (xz, grad_weights, grad_output),
-        free_in=(1, 2),
+        (xz, grad_weights, grad_output, *after),
+        free_in=(1, 2, 3),
         grid_spec=pltpu.PrefetchScalarGridSpec(
             num_scalar_prefetch=1,
             grid=(1,),
-            in_specs=[const(grad_weights.shape), const(grad_output.shape)],
+            in_specs=[const(grad_weights.shape), const(grad_output.shape)]
+            + [pl.BlockSpec(memory_space=pl.ANY)] * len(after),
             out_specs=[half, half],
         ),
         out_shape=[shape_of(2 * width, features)] * 2,
@@ -671,7 +678,7 @@
     return kernel_call(
         body,
         (xz, one, two, *after),
-        free_in=(2,),
+        free_in=(2, 3, 4),
         grid_spec=pltpu.PrefetchScalarGridSpec(
             num_scalar_prefetch=1,
             grid=(1,),
@@ -974,20 +981,20 @@
         residuals.append(residual)
         pieces.append([own, other_core(own), other_chip(own)])
 
-    outs, backs, sums, kept = [], {}, [], ()
+    outs, backs, sums, before = [], {}, [], ()
     for base in (0, 2):
-        held = ()
         for p in parts:
             if base:
-                far = fence(pieces[p][2], backs[p, 0], space=pltpu.VMEM)
+                far = fence(pieces[p][2], backs[0, 0], space=pltpu.VMEM)
                 pieces[p] = [None, None, far, other_core(far)]
-            result = feed(p, base, me, pieces[p][base], pieces[p][base + 1], cot,
-                          inner_weight, vectors, outer_weight, kept, held)
-            kept, held = result[:2], result[2:4]
-            backs[p, base], backs[p, base + 1] = result[4:6]
-            sums.append(result[6])
-        outs += held
-    left, right = kept
+        result = feed(base, me, [pieces[p][base + n] for p in parts for n in (0, 1)], cot,
+                      inner_weight, vectors, outer_weight, before)
+        outs += result[:2]
+        for p in parts:
+            backs[p, base], backs[p, base + 1] = result[2 + 2 * p:4 + 2 * p]
+        sums.append(result[2 + 2 * PARTS])
+        before = result[3 + 2 * PARTS:]
+    feed_sum = lax.psum_scatter(before[0].reshape(-1, features), DP, scatter_dimension=0, tiled=True)
 
     gathered, far_sums = zip(*[gather_sum([backs[p, n] for n in range(4)]) for p in parts])
     grad_residuals, lows, grads_attended, inner_sums = [], [], [], []
@@ -1000,37 +1007,33 @@
         inner_sums.append(vector)
         grads_attended.append(exchange([a0, a1, a2, a3]))
 
-    grad_feed = lax.dot_general(fence(left, *far_sums), right, (((1,), (1,)), ((0,), (0,))), preferred_element_type=F32)
-    grad_feed = grad_feed.astype(BF16).reshape(2 * features, features)
-    feed_sum = lax.psum_scatter(grad_feed, DP, scatter_dimension=0, tiled=True)
-
     near = other_core(fence(outs[1], *far_sums))
     far = (outs[2].astype(F32) + other_core(fence(outs[3], *far_sums)).astype(F32)).astype(BF16)
     far = fence(far, lows[-1], space=pltpu.VMEM)
     part = output_grad(mixed, lows)
     earlier = attend_backward(0, me, segment_ids, qt, extras[0], kn, kt, vn, attended[0], grads_attended[0], (),
                               (far, near, part[0]))
-    result = jnp.concatenate(residuals) + outs[0].astype(F32) + near.astype(F32)
-    result = (result + other_chip(far).astype(F32) + outer_bias).astype(BF16)
     part_far = fence(part[2], earlier[0])
     part_far = (part_far.astype(F32) + other_core(part[3]).astype(F32)).astype(BF16)
     part_near = other_core(part[1])
     grads = attend_backward(1, me, segment_ids, qt, extras[1], kn, kt, vn, attended[1], grads_attended[1], earlier,
-                            (part_near, part_far, result))
+                            (part_near, part_far))
 
     xz = jnp.stack([lax.axis_index("x"), lax.axis_index("z")]).astype(jnp.int32)
-    near, far = other_core(result), other_chip(result)
     part_across = other_chip(part_far)
     grad_output = fence(part[0], grads).astype(F32) + part_near.astype(F32) + part_across.astype(F32)
-    keep, send = halves(xz, nn(grads, attend_in).astype(BF16), grad_output.astype(BF16))
+    there = other_chip(far)
+    keep, send = halves(xz, nn(grads, attend_in).astype(BF16), grad_output.astype(BF16), (there,))
+    result = jnp.concatenate(residuals) + fence(outs[0], send).astype(F32) + near.astype(F32)
+    result = (result + there.astype(F32) + outer_bias).astype(BF16)
     near, far = other_core(result), other_chip(result)
     got = lax.ppermute(send, "x", SWAP)
     back_own, back_near, back_far, back_across, apart, summed = tail(
-        me, grads, wq, wk, wv, tokens, stat, inner_sums, sums, (near, far, send)
+        me, grads, wq, wk, wv, tokens, stat, inner_sums, sums, (send,)
     )
     feed_sum = lax.all_gather(fence(feed_sum, send), DP, axis=0, tiled=True)
     feed_sum = (feed_sum[:features].astype(F32), feed_sum[features:].astype(F32))
-    quarter = sum_first(xz, keep, got, (apart,))
+    quarter = sum_first(xz, keep, got, (near, far, apart))
     back_across = other_core(fence(back_across, quarter[-1], space=pltpu.VMEM))
     back_far = chip_sum(back_far, back_across, summed, ())
     back_there = other_chip(back_far)

time: 287 us -> 292 us (1.017)
  waiting for transfers between devices: 53.5 us -> 71.2 us
  matrix products: 14.8 us -> 4.63 us
  Pallas kernels: 141 us -> 132 us
  local copies, waits for them, and re-layouts: 3.14 us -> 9.47 us
    ppermute x14, waiting for transfers between devices: 26 us -> 39 us  [other_chip(): return lax.ppermute(value, 'y', SWAP)]
    dot_general x1 -> x0, matrix products: 10.1 us -> none  [local(): lax.dot_general(fence(left, *far_sums), right, (((1,), (1,)), ((0,), (0,)...]
    pallas_call x24 -> x22, Pallas kernels: 141 us -> 132 us  [kernel_call(): pl.pallas_call(body, out_shape=shapes if many else shapes[0], compiler_pa...]
    ppermute x6, waiting for transfers between devices: 6.58 us -> 13.3 us  [turned(): lax.ppermute(values, 'z', [(n, (n + way) % size) for n in range(size)])]
    unnamed x36 -> x50, local copies, waits for them, and re-layouts: 1.63 us -> 7.96 us
    ppermute x14, starting transfers between devices: 18.8 us -> 14.3 us  [other_chip(): return lax.ppermute(value, 'y', SWAP)]
    reduce_scatter x1, waiting for transfers between devices: 3.82 us -> 0.05 us  [local(): lax.psum_scatter(before[0].reshape(-1, features), DP, scatter_dimension=0...]
  transfers between devices with their start and end apart: 52 -> 52, of which waited for: 13 -> 17; matrix products, arithmetic and copies ran while one was open for 10% -> 6% of each run, Pallas kernels for 40% -> 33%
where the time goes in v7:
time: 292 us; the launch traced here: 291 us
  Pallas kernels  132 us (45%)
  waiting for transfers between devices  71.2 us (24%)
  starting transfers between devices  46.5 us (16%)
  between operations  14.4 us (5%)
  other arithmetic  13.1 us (4%)
  local copies, waits for them, and re-layouts  9.47 us (3%)
  matrix products  4.63 us (2%)
    pallas_call x22, Pallas kernels, kernel_call(): pl.pallas_call(body, out_shape=shapes if many else shapes[0], compiler_pa...  132 us
    ppermute x14, waiting for transfers between devices, other_chip(): return lax.ppermute(value, 'y', SWAP)  39 us
    ppermute x6, starting transfers between devices, turned(): lax.ppermute(values, 'z', [(n, (n + way) % size) for n in range(size)])  17.8 us
    ppermute x14, starting transfers between devices, other_chip(): return lax.ppermute(value, 'y', SWAP)  14.3 us
    ppermute x6, waiting for transfers between devices, turned(): lax.ppermute(values, 'z', [(n, (n + way) % size) for n in range(size)])  13.3 us
    unnamed x50, local copies, waits for them, and re-layouts  7.96 us
    ppermute x1, waiting for transfers between devices, local(): got = lax.ppermute(send, 'x', SWAP)  6.48 us
  transfers between devices with their start and end apart: 52, of which 17 were waited for; matrix products, arithmetic and copies ran while one was open for 6% of the time, Pallas kernels for 33%

profile of v7, /device:TPU:0, one launch (start us, length us, event | category | flops | bytes accessed | tf_op | source)
XLA Modules:
  0.0 291.4 jit_solution(11733203881662805883)
XLA Ops:
  9.5 10.6 %project.1 = (bf16[2048,768]{1,0:T(8,128)(2,1)}, bf16[3,128,2048]{2,1,0:T(8,128)(2,1)}, bf16[192,2048]{1,0:T(8,128)(2,1)}, bf16[3,80,2048]{2,1,0:T(8,128)(2,1)},...) custom-call(bf16[2048,768]{1,0:T(8,128)(2,1)} %bitcast.18, ...), custom_call_target="tpu_custom_call" | custom-call | flops 6000000000 | bytes 14000000 | tf_op jit(solution)/shard_map/project/pallas_call | solution.py:83
  20.0 9.7 %attend_forward.2 = (bf16[4,192,256]{2,1,0:T(8,128)(2,1)}, bf16[3,16,1024]{2,1,0:T(8,128)(2,1)}, bf16[192,256]{1,0:T(8,128)(2,1)}, bf16[192,256]{1,0:T(8,128)(2,...) custom-call(s32[1]{0:T(128)} %bitcast.refs_0_.me_ref, s32[1,2048]{1,0:T(1,128)S(1)} %copy-done.8, ...), custom_call_target="tpu_custom_call" | custom-call | flops 8999999488 | bytes 5000000 | tf_op jit(solution)/shard_map/attend_forward/pallas_call | solution.py:83
  35.1 7.6 %attend_forward.3 = (bf16[4,192,256]{2,1,0:T(8,128)(2,1)}, bf16[3,16,1024]{2,1,0:T(8,128)(2,1)}, bf16[192,256]{1,0:T(8,128)(2,1)}, bf16[192,256]{1,0:T(8,128)(2,...) custom-call(s32[1]{0:T(128)} %bitcast.refs_0_.me_ref, s32[1,2048]{1,0:T(1,128)S(1)} %copy-done.8, ...), custom_call_target="tpu_custom_call" | custom-call | flops 8999999488 | bytes 5000000 | tf_op jit(solution)/shard_map/attend_forward/pallas_call | solution.py:83
  42.7 6.5 %collective-permute-done.1.m2_ref = bf16[192,256]{1,0:T(8,128)(2,1)S(1)} collective-permute-done((bf16[192,256]{1,0:T(8,128)(2,1)S(1)}, bf16[192,256]{1,0:T(8,128)(2,1)S(1)}, u32[]{:S(2)}, u32[]{:S(2)}) %collective-permute-start.1) | collective-permute-done | bytes 98336 | tf_op jit(solution)/shard_map/ppermute | solution.py:890
  62.5 13.0 %feed.2 = (bf16[512,768]{1,0:T(8,128)(2,1)}, bf16[512,768]{1,0:T(8,128)(2,1)}, bf16[256,768]{1,0:T(8,128)(2,1)}, bf16[256,768]{1,0:T(8,128)(2,1)S(1)}, bf16[256,...) custom-call(s32[1]{0:T(128)} %bitcast.refs_0_.me_ref, ...), custom_call_target="tpu_custom_call" | custom-call | flops 15000000512 | bytes 12000000 | tf_op jit(solution)/shard_map/feed/pallas_call | solution.py:83
  75.6 4.6 %collective-permute-done.14.refs_0_ = bf16[256,768]{1,0:T(8,128)(2,1)S(1)} collective-permute-done((bf16[256,768]{1,0:T(8,128)(2,1)S(1)}, bf16[256,768]{1,0:T(8,128)(2,1)S(1)}, u32[]{:S(2)}, u32[]{:S(2)}) %collective-permute-start.14) | collective-permute-done | bytes 393248 | tf_op jit(solution)/shard_map/ppermute | solution.py:890
  81.9 13.7 %feed.3 = (bf16[512,768]{1,0:T(8,128)(2,1)}, bf16[512,768]{1,0:T(8,128)(2,1)}, bf16[256,768]{1,0:T(8,128)(2,1)}, bf16[256,768]{1,0:T(8,128)(2,1)S(1)}, bf16[256,...) custom-call(s32[1]{0:T(128)} %bitcast.refs_0_.me_ref, ...), custom_call_target="tpu_custom_call" | custom-call | flops 15000000512 | bytes 12000000 | tf_op jit(solution)/shard_map/feed/pallas_call | solution.py:83
  104.4 7.0 %collective-permute-done.23.b2_ref = bf16[256,768]{1,0:T(8,128)(2,1)S(1)} collective-permute-done((bf16[256,768]{1,0:T(8,128)(2,1)}, bf16[256,768]{1,0:T(8,128)(2,1)S(1)}, u32[]{:S(2)}, u32[]{:S(2)}) %collective-permute-start.23) | collective-permute-done | bytes 393248 | tf_op jit(solution)/shard_map/ppermute | solution.py:890
  111.4 3.8 %middle_back.3 = (f32[256,768]{1,0:T(8,128)}, bf16[256,768]{1,0:T(8,128)(2,1)}, bf16[192,256]{1,0:T(8,128)(2,1)}, bf16[192,256]{1,0:T(8,128)(2,1)}, bf16[192,256...) custom-call(s32[1]{0:T(128)} %bitcast.refs_0_.me_ref, ...), custom_call_target="tpu_custom_call" | custom-call | flops 2000000000 | bytes 4000000 | tf_op jit(solution)/shard_map/middle_back/pallas_call | solution.py:83
  131.4 14.3 %attend_backward.2 = (bf16[192,1024]{1,0:T(8,128)(2,1)}, f32[192,2048]{1,0:T(8,128)}, f32[192,2048]{1,0:T(8,128)}) custom-call(s32[1]{0:T(128)} %bitcast.refs_0_.me_ref, s32[1,2048]{1,0:T(1,128)S(1)} %copy-done.9, s32[1,2048]{1,0:T(1,128)S(1)} %copy-done.9, bf16[3,128,2048]{2,1,0:T(8,128)(2,1)} %get-tuple-element.104.refs_3_, ...), custom_call_target="tpu_custom_call" | custom-call | flops 16000000000 | bytes 10000000 | tf_op jit(solution)/shard_map/attend_backward/pallas_call | solution.py:83
  149.0 12.1 %attend_backward.3.refs_1_.g_ref = bf16[576,2048]{1,0:T(8,128)(2,1)} custom-call(s32[1]{0:T(128)} %bitcast.refs_0_.me_ref, s32[1,2048]{1,0:T(1,128)S(1)} %copy-done.9, s32[1,2048]{1,0:T(1,128)S(1)} %copy-done.9, bf16[3,128,2048]{2,1,0:T(8,128)(2,1)} %get-tuple-element.104.refs_3_, bf16[3,16,1024]{2,1,0:T(8,128)(2,1)} %get-tuple-element.111.rest_0_.refs_4_, ...), custom_call_target="tpu_custom_call" | custom-call | flops 16000000000 | bytes 10000000 | tf_op jit(solution)/shard_map/attend_backward/pallas_call | solution.py:83
  161.1 4.6 %convolution_convert_fusion.g_ref = bf16[576,768]{1,0:T(8,128)(2,1)S(1)} fusion(bf16[576,2048]{1,0:T(8,128)(2,1)} %attend_backward.3.refs_1_.g_ref, bf16[2048,768]{1,0:T(8,128)(2,1)} %get-tuple-element.157), kind=kOutput, calls=%fused_computation.6 | convolution fusion | flops 1812381696 | bytes 6389760 | tf_op jit(solution)/shard_map/dot_general | solution.py:23
  165.7 6.4 %collective-permute-done.31 = bf16[192,768]{1,0:T(8,128)(2,1)} collective-permute-done((bf16[192,768]{1,0:T(8,128)(2,1)S(1)}, bf16[192,768]{1,0:T(8,128)(2,1)}, u32[]{:S(2)}, u32[]{:S(2)}) %collective-permute-start.31) | collective-permute-done | bytes 294944 | tf_op jit(solution)/shard_map/ppermute | solution.py:890
  178.3 3.7 %collective-permute-start.36 = (bf16[384,768]{1,0:T(8,128)(2,1)S(1)}, bf16[384,768]{1,0:T(8,128)(2,1)S(1)}, u32[]{:S(2)}, u32[]{:S(2)}) collective-permute-start(bf16[384,768]{1,0:T(8,128)(2,1)S(1)} %copy-done.13), channel_id=1, source_target_pairs={{0,4},{4,0},{1,5},{5,1},{2,6},{6,2},{3,7},{7,3},{8,12},{12,8},{9,1... | collective-permute-start | bytes 1769480 | tf_op jit(solution)/shard_map/ppermute | solution.py:1030
  182.0 10.7 %tail.1 = (bf16[512,768]{1,0:T(8,128)(2,1)}, bf16[512,768]{1,0:T(8,128)(2,1)S(1)}, bf16[512,768]{1,0:T(8,128)(2,1)}, bf16[528,768]{1,0:T(8,128)(2,1)S(1)}, f32[8,768]{1,0:T(8,128)}, /*index=5*/f32[8,768]{1,0:T(8,128)}) custom-call(s32[1]{0:T(128)} %bitcast.refs_0_.me_ref, bf16[576,2048]{1,0:T(8,128)(2,1)} %attend_backward.3.refs_1_.g_ref, ...), custom_call_target="tpu_custom_call" | custom-call | flops 4000000000 | bytes 10000000 | tf_op jit(solution)/shard_map/tail/pallas_call | solution.py:83
  192.7 6.5 %collective-permute-done.36.refs_2_ = bf16[384,768]{1,0:T(8,128)(2,1)S(1)} collective-permute-done((bf16[384,768]{1,0:T(8,128)(2,1)S(1)}, bf16[384,768]{1,0:T(8,128)(2,1)S(1)}, u32[]{:S(2)}, u32[]{:S(2)}) %collective-permute-start.36) | collective-permute-done | bytes 589856 | tf_op jit(solution)/shard_map/ppermute | solution.py:1030
  207.9 4.3 %collective-permute-start.37 = (bf16[96,768]{1,0:T(8,128)(2,1)S(1)}, bf16[96,768]{1,0:T(8,128)(2,1)S(1)}, u32[]{:S(2)}, u32[]{:S(2)}) collective-permute-start(bf16[96,768]{1,0:T(8,128)(2,1)S(1)} %copy-done.24), channel_id=1, source_target_pairs={{0,8},{8,16},{16,24},{24,0},{1,9},{9,17},{17,25},{25,1},{2,10},{10... | collective-permute-start | bytes 442376 | tf_op jit(solution)/shard_map/ppermute | solution.py:918
  214.7 11.8 %collective-permute-done.41.b2_ref.refs_5_ = bf16[528,768]{1,0:T(8,128)(2,1)S(1)} collective-permute-done((bf16[528,768]{1,0:T(8,128)(2,1)S(1)}, bf16[528,768]{1,0:T(8,128)(2,1)S(1)}, u32[]{:S(2)}, u32[]{:S(2)}) %collective-permute-start.41) | collective-permute-done | bytes 811040 | tf_op jit(solution)/shard_map/ppermute | solution.py:890
  234.5 10.1 %collective-permute-start.47 = (bf16[128,768]{1,0:T(8,128)(2,1)S(1)}, bf16[128,768]{1,0:T(8,128)(2,1)S(1)}, u32[]{:S(2)}, u32[]{:S(2)}) collective-permute-start(bf16[128,768]{1,0:T(8,128)(2,1)S(1)} %copy-done), channel_id=1, source_target_pairs={{0,24},{8,0},{16,8},{24,16},{1,25},{9,1},{17,9},{25,17},{2,26},{10... | collective-permute-start | bytes 589832 | tf_op jit(solution)/shard_map/ppermute | solution.py:918
  247.9 4.4 %place.2.refs_5_ = bf16[2048,768]{1,0:T(8,128)(2,1)} custom-call(s32[1]{0:T(128)} %bitcast.refs_0_.me_ref, bf16[512,768]{1,0:T(8,128)(2,1)S(1)} %copy-done.5, bf16[512,768]{1,0:T(8,128)(2,1)S(1)} %copy-done.3, bf16[512,768]{1,0:T(8,128)(2,1)S(1)} %collective-permute-done.34.refs_4_.p2_ref, bf16[512,768]{1,0:T(8,128)(2,1)} %collective-permute-done.35.p3_ref, ...), custom_call_target="tpu_custom_call" | custom-call | flops 1000000 | bytes 9000000 | tf_op jit(solution)/shard_map/place/pallas_call | solution.py:83
  252.3 10.8 %collective-permute-done.46.refs_3_ = bf16[128,768]{1,0:T(8,128)(2,1)S(1)} collective-permute-done((bf16[128,768]{1,0:T(8,128)(2,1)S(1)}, bf16[128,768]{1,0:T(8,128)(2,1)S(1)}, u32[]{:S(2)}, u32[]{:S(2)}) %collective-permute-start.46) | collective-permute-done | bytes 196640 | tf_op jit(solution)/shard_map/ppermute | solution.py:918
  266.9 5.2 %place.3 = f32[2048,768]{1,0:T(8,128)} custom-call(s32[1]{0:T(128)} %bitcast.refs_0_.me_ref, bf16[512,768]{1,0:T(8,128)(2,1)S(1)} %fence.21.p0_ref, bf16[512,768]{1,0:T(8,128)(2,1)} %collective-permute-done.43.p1_ref, bf16[512,768]{1,0:T(8,128)(2,1)S(1)} %fence.22.p2_ref, bf16[512,768]{1,0:T(8,128)(2,1)S(1)} %collective-permute-done.48.p3_ref, ...), custom_call_target="tpu_custom_call" | custom-call | flops 1000000 | bytes 9000000 | tf_op jit(solution)/shard_map/place/pallas_call | solution.py:83
  272.1 4.2 %slice_convert_fusion = (f32[768,768]{1,0:T(8,128)}, f32[768,768]{1,0:T(8,128)}) fusion(bf16[1536,768]{1,0:T(8,128)(2,1)} %all-gather.2.cloned.1.call-done), kind=kLoop, calls=%fused_computation.7 | loop fusion | flops 1179648 | bytes 7077888 | tf_op jit(solution)/shard_map/convert_element_type | solution.py:1035
  276.3 5.0 %collective-permute-done.49.other_ref = bf16[416,768]{1,0:T(8,128)(2,1)S(1)} collective-permute-done((bf16[416,768]{1,0:T(8,128)(2,1)S(1)}, bf16[416,768]{1,0:T(8,128)(2,1)S(1)}, u32[]{:S(2)}, u32[]{:S(2)}) %collective-permute-start.49) | collective-permute-done | bytes 639008 | tf_op jit(solution)/shard_map/ppermute | solution.py:1054
  (178 shorter events, 86.7 us)
Async XLA Ops:
  7.2 167.7 %reduce-scatter.2.cloned.1.call-start = ((), (), s32[]{:S(2)}) async-start(), calls=%async_computation.1 | async-start | bytes 2654208 | tf_op jit(solution)/shard_map/reduce_scatter | solution.py:997
  30.3 21.9 %collective-permute-start.5 = (bf16[192,768]{1,0:T(8,128)(2,1)S(1)}, bf16[192,768]{1,0:T(8,128)(2,1)S(1)}, u32[]{:S(2)}, u32[]{:S(2)}) collective-permute-start(bf16[192,768]{1,0:T(8,128)(2,1)S(1)} %copy-done.19), channel_id=1, source_target_pairs={{0,3},{1,2},{2,1},{3,0},{4,7},{5,6},{6,5},{7,4},{8,11},{9,10},{10,... | collective-permute-start | bytes 884744 | tf_op jit(solution)/shard_map/ppermute | solution.py:894
  32.9 19.3 %collective-permute-start.4 = (bf16[192,768]{1,0:T(8,128)(2,1)S(1)}, bf16[192,768]{1,0:T(8,128)(2,1)S(1)}, u32[]{:S(2)}, u32[]{:S(2)}) collective-permute-start(bf16[192,768]{1,0:T(8,128)(2,1)S(1)} %copy-done.19), channel_id=1, source_target_pairs={{0,2},{2,0},{1,3},{3,1},{4,6},{6,4},{5,7},{7,5},{8,10},{10,8},{9,1... | collective-permute-start | bytes 884744 | tf_op jit(solution)/shard_map/ppermute | solution.py:890
  33.0 19.3 %collective-permute-start.3 = (bf16[192,768]{1,0:T(8,128)(2,1)S(1)}, bf16[192,768]{1,0:T(8,128)(2,1)S(1)}, u32[]{:S(2)}, u32[]{:S(2)}) collective-permute-start(bf16[192,768]{1,0:T(8,128)(2,1)S(1)} %copy-done.19), channel_id=1, source_target_pairs={{0,1},{1,0},{2,3},{3,2},{4,5},{5,4},{6,7},{7,6},{8,9},{9,8},{10,11... | collective-permute-start | bytes 884744 | tf_op jit(solution)/shard_map/ppermute | solution.py:886
  102.6 23.4 %collective-permute-start.27 = (bf16[512,768]{1,0:T(8,128)(2,1)}, bf16[512,768]{1,0:T(8,128)(2,1)}, u32[]{:S(2)}, u32[]{:S(2)}) collective-permute-start(bf16[512,768]{1,0:T(8,128)(2,1)} %fence.14), channel_id=1, source_target_pairs={{0,1},{1,0},{2,3},{3,2},{4,5},{5,4},{6,7},{7,6},{8,9},{9,8},{10,11... | collective-permute-start | bytes 2359304 | tf_op jit(solution)/shard_map/ppermute | solution.py:886
  104.2 167.9 %all-gather.2.cloned.1.call-start = ((), (), s32[]{:S(2)}) async-start(), calls=%async_computation.2 | async-start | bytes 2654208 | tf_op jit(solution)/shard_map/all_gather | solution.py:1034
  104.3 27.0 %collective-permute-start.28 = (bf16[512,768]{1,0:T(8,128)(2,1)}, bf16[512,768]{1,0:T(8,128)(2,1)S(1)}, u32[]{:S(2)}, u32[]{:S(2)}) collective-permute-start(bf16[512,768]{1,0:T(8,128)(2,1)} %fence.16), channel_id=1, source_target_pairs={{0,1},{1,0},{2,3},{3,2},{4,5},{5,4},{6,7},{7,6},{8,9},{9,8},{10,11... | collective-permute-start | bytes 2359304 | tf_op jit(solution)/shard_map/ppermute | solution.py:886
  126.0 21.3 %collective-permute-start.18 = (bf16[192,256]{1,0:T(8,128)(2,1)S(1)}, bf16[192,256]{1,0:T(8,128)(2,1)}, u32[]{:S(2)}, u32[]{:S(2)}) collective-permute-start(bf16[192,256]{1,0:T(8,128)(2,1)S(1)} %get-tuple-element.131), channel_id=1, source_target_pairs={{0,1},{1,0},{2,3},{3,2},{4,5},{5,4},{6,7},{7,6},{8,9},{9,8},{10,11... | collective-permute-start | bytes 294920 | tf_op jit(solution)/shard_map/ppermute | solution.py:886
  129.1 19.9 %collective-permute-start.19 = (bf16[192,256]{1,0:T(8,128)(2,1)S(1)}, bf16[192,256]{1,0:T(8,128)(2,1)}, u32[]{:S(2)}, u32[]{:S(2)}) collective-permute-start(bf16[192,256]{1,0:T(8,128)(2,1)S(1)} %get-tuple-element.132), channel_id=1, source_target_pairs={{0,2},{2,0},{1,3},{3,1},{4,6},{6,4},{5,7},{7,5},{8,10},{10,8},{9,1... | collective-permute-start | bytes 294920 | tf_op jit(solution)/shard_map/ppermute | solution.py:890
  129.6 19.4 %collective-permute-start.20 = (bf16[192,256]{1,0:T(8,128)(2,1)S(1)}, bf16[192,256]{1,0:T(8,128)(2,1)}, u32[]{:S(2)}, u32[]{:S(2)}) collective-permute-start(bf16[192,256]{1,0:T(8,128)(2,1)S(1)} %get-tuple-element.133), channel_id=1, source_target_pairs={{0,3},{1,2},{2,1},{3,0},{4,7},{5,6},{6,5},{7,4},{8,11},{9,10},{10,... | collective-permute-start | bytes 294920 | tf_op jit(solution)/shard_map/ppermute | solution.py:894
  130.5 18.5 %collective-permute-start.29 = (bf16[192,768]{1,0:T(8,128)(2,1)S(1)}, bf16[192,768]{1,0:T(8,128)(2,1)S(1)}, u32[]{:S(2)}, u32[]{:S(2)}) collective-permute-start(bf16[192,768]{1,0:T(8,128)(2,1)S(1)} %get-tuple-element.154), channel_id=1, source_target_pairs={{0,1},{1,0},{2,3},{3,2},{4,5},{5,4},{6,7},{7,6},{8,9},{9,8},{10,11... | collective-permute-start | bytes 884744 | tf_op jit(solution)/shard_map/ppermute | solution.py:886
  145.7 27.5 %collective-permute-start.32 = (bf16[512,768]{1,0:T(8,128)(2,1)S(1)}, bf16[512,768]{1,0:T(8,128)(2,1)S(1)}, u32[]{:S(2)}, u32[]{:S(2)}) collective-permute-start(bf16[512,768]{1,0:T(8,128)(2,1)S(1)} %fence.15.refs_13_), channel_id=1, source_target_pairs={{0,2},{2,0},{1,3},{3,1},{4,6},{6,4},{5,7},{7,5},{8,10},{10,8},{9,1... | collective-permute-start | bytes 2359304 | tf_op jit(solution)/shard_map/ppermute | solution.py:890
  147.3 24.8 %collective-permute-start.31 = (bf16[192,768]{1,0:T(8,128)(2,1)S(1)}, bf16[192,768]{1,0:T(8,128)(2,1)}, u32[]{:S(2)}, u32[]{:S(2)}) collective-permute-start(bf16[192,768]{1,0:T(8,128)(2,1)S(1)} %add_convert_fusion.4.refs_17_), channel_id=1, source_target_pairs={{0,2},{2,0},{1,3},{3,1},{4,6},{6,4},{5,7},{7,5},{8,10},{10,8},{9,1... | collective-permute-start | bytes 884744 | tf_op jit(solution)/shard_map/ppermute | solution.py:890
  177.8 21.4 %collective-permute-start.34 = (bf16[512,768]{1,0:T(8,128)(2,1)S(1)}, bf16[512,768]{1,0:T(8,128)(2,1)S(1)}, u32[]{:S(2)}, u32[]{:S(2)}) collective-permute-start(bf16[512,768]{1,0:T(8,128)(2,1)S(1)} %fusion.3.p0_ref), channel_id=1, source_target_pairs={{0,2},{2,0},{1,3},{3,1},{4,6},{6,4},{5,7},{7,5},{8,10},{10,8},{9,1... | collective-permute-start | bytes 2359304 | tf_op jit(solution)/shard_map/ppermute | solution.py:890
  178.3 20.8 %collective-permute-start.33 = (bf16[512,768]{1,0:T(8,128)(2,1)S(1)}, bf16[512,768]{1,0:T(8,128)(2,1)S(1)}, u32[]{:S(2)}, u32[]{:S(2)}) collective-permute-start(bf16[512,768]{1,0:T(8,128)(2,1)S(1)} %fusion.3.p0_ref), channel_id=1, source_target_pairs={{0,1},{1,0},{2,3},{3,2},{4,5},{5,4},{6,7},{7,6},{8,9},{9,8},{10,11... | collective-permute-start | bytes 2359304 | tf_op jit(solution)/shard_map/ppermute | solution.py:886
  178.3 20.8 %collective-permute-start.36 = (bf16[384,768]{1,0:T(8,128)(2,1)S(1)}, bf16[384,768]{1,0:T(8,128)(2,1)S(1)}, u32[]{:S(2)}, u32[]{:S(2)}) collective-permute-start(bf16[384,768]{1,0:T(8,128)(2,1)S(1)} %copy-done.13), channel_id=1, source_target_pairs={{0,4},{4,0},{1,5},{5,1},{2,6},{6,2},{3,7},{7,3},{8,12},{12,8},{9,1... | collective-permute-start | bytes 1769480 | tf_op jit(solution)/shard_map/ppermute | solution.py:1030
  206.3 20.2 %collective-permute-start.41 = (bf16[528,768]{1,0:T(8,128)(2,1)S(1)}, bf16[528,768]{1,0:T(8,128)(2,1)S(1)}, u32[]{:S(2)}, u32[]{:S(2)}) collective-permute-start(bf16[528,768]{1,0:T(8,128)(2,1)S(1)} %chip_sum.1.refs_4_), channel_id=1, source_target_pairs={{0,2},{2,0},{1,3},{3,1},{4,6},{6,4},{5,7},{7,5},{8,10},{10,8},{9,1... | collective-permute-start | bytes 2433032 | tf_op jit(solution)/shard_map/ppermute | solution.py:890
  207.9 21.5 %collective-permute-start.37 = (bf16[96,768]{1,0:T(8,128)(2,1)S(1)}, bf16[96,768]{1,0:T(8,128)(2,1)S(1)}, u32[]{:S(2)}, u32[]{:S(2)}) collective-permute-start(bf16[96,768]{1,0:T(8,128)(2,1)S(1)} %copy-done.24), channel_id=1, source_target_pairs={{0,8},{8,16},{16,24},{24,0},{1,9},{9,17},{17,25},{25,1},{2,10},{10... | collective-permute-start | bytes 442376 | tf_op jit(solution)/shard_map/ppermute | solution.py:918
  212.2 18.5 %collective-permute-start.38 = (bf16[96,768]{1,0:T(8,128)(2,1)S(1)}, bf16[96,768]{1,0:T(8,128)(2,1)S(1)}, u32[]{:S(2)}, u32[]{:S(2)}) collective-permute-start(bf16[96,768]{1,0:T(8,128)(2,1)S(1)} %copy-done.23), channel_id=1, source_target_pairs={{0,16},{8,24},{16,0},{24,8},{1,17},{9,25},{17,1},{25,9},{2,18},{10... | collective-permute-start | bytes 442376 | tf_op jit(solution)/shard_map/ppermute | solution.py:918
  212.2 19.7 %collective-permute-start.39 = (bf16[96,768]{1,0:T(8,128)(2,1)S(1)}, bf16[96,768]{1,0:T(8,128)(2,1)S(1)}, u32[]{:S(2)}, u32[]{:S(2)}) collective-permute-start(bf16[96,768]{1,0:T(8,128)(2,1)S(1)} %copy-done.17), channel_id=1, source_target_pairs={{0,24},{8,0},{16,8},{24,16},{1,25},{9,1},{17,9},{25,17},{2,26},{10... | collective-permute-start | bytes 442376 | tf_op jit(solution)/shard_map/ppermute | solution.py:918
  214.7 30.9 %collective-permute-start.35 = (bf16[512,768]{1,0:T(8,128)(2,1)S(1)}, bf16[512,768]{1,0:T(8,128)(2,1)}, u32[]{:S(2)}, u32[]{:S(2)}) collective-permute-start(bf16[512,768]{1,0:T(8,128)(2,1)S(1)} %collective-permute-done.34.refs_4_.p2_ref), channel_id=1, source_target_pairs={{0,1},{1,0},{2,3},{3,2},{4,5},{5,4},{6,7},{7,6},{8,9},{9,8},{10,11... | collective-permute-start | bytes 2359304 | tf_op jit(solution)/shard_map/ppermute | solution.py:886
  233.6 30.9 %collective-permute-start.44 = (bf16[512,768]{1,0:T(8,128)(2,1)S(1)}, bf16[512,768]{1,0:T(8,128)(2,1)S(1)}, u32[]{:S(2)}, u32[]{:S(2)}) collective-permute-start(bf16[512,768]{1,0:T(8,128)(2,1)S(1)} %fence.21.p0_ref), channel_id=1, source_target_pairs={{0,2},{2,0},{1,3},{3,1},{4,6},{6,4},{5,7},{7,5},{8,10},{10,8},{9,1... | collective-permute-start | bytes 2359304 | tf_op jit(solution)/shard_map/ppermute | solution.py:890
  244.6 18.4 %collective-permute-start.46 = (bf16[128,768]{1,0:T(8,128)(2,1)S(1)}, bf16[128,768]{1,0:T(8,128)(2,1)S(1)}, u32[]{:S(2)}, u32[]{:S(2)}) collective-permute-start(bf16[128,768]{1,0:T(8,128)(2,1)S(1)} %copy-done), channel_id=1, source_target_pairs={{0,16},{8,24},{16,0},{24,8},{1,17},{9,25},{17,1},{25,9},{2,18},{10... | collective-permute-start | bytes 589832 | tf_op jit(solution)/shard_map/ppermute | solution.py:918
  245.6 21.3 %collective-permute-start.43 = (bf16[512,768]{1,0:T(8,128)(2,1)S(1)}, bf16[512,768]{1,0:T(8,128)(2,1)}, u32[]{:S(2)}, u32[]{:S(2)}) collective-permute-start(bf16[512,768]{1,0:T(8,128)(2,1)S(1)} %fence.21.p0_ref), channel_id=1, source_target_pairs={{0,1},{1,0},{2,3},{3,2},{4,5},{5,4},{6,7},{7,6},{8,9},{9,8},{10,11... | collective-permute-start | bytes 2359304 | tf_op jit(solution)/shard_map/ppermute | solution.py:886
  (53 other events, 402.8 us)
Sparse Core Ops, SparseCore 0:
  104.3 70.4 reduce-scatter.1
  177.1 65.0 all-gather.1

commit v8 on v7

--- a/solution.py
+++ b/solution.py
@@ -177,8 +177,8 @@
     return value.astype(BF16)
 
 
-def forward_body(offset, me_ref, segs_ref, seg_ref, qt_ref, kn_ref, vt_ref,
-                 out_ref, extra_ref, o0_ref, o1_ref, o2_ref, o3_ref, acc_ref):
+def forward_body(offset, me_ref, segs_ref, seg_ref, qt_ref, kn_ref, vt_ref, *rest):
+    out_ref, extra_ref, o0_ref, o1_ref, o2_ref, o3_ref, acc_ref = rest[-7:]
     heads, _, tile = qt_ref.shape
     i = pl.program_id(0)
     low, high = key_range(segs_ref, seg_ref[...], i + offset)
@@ -212,7 +212,7 @@
             o_ref[...] = out_ref[0]
 
 
-def attend_forward(part, me, seg_row, qt, kn, vt):
+def attend_forward(part, me, seg_row, qt, kn, vt, after):
     heads, _, length = qt.shape
     width = heads * HEAD
     count = length // TILE // PARTS
@@ -223,7 +223,8 @@
 
     return kernel_call(
         body,
-        (me, seg_row, seg_row, qt, kn, vt),
+        (me, seg_row, seg_row, qt, kn, vt, *after),
+        free_in=tuple(range(6, 6 + len(after))),
         free_out=(3, 4, 5),
         grid_spec=pltpu.PrefetchScalarGridSpec(
             num_scalar_prefetch=1,
@@ -233,7 +234,7 @@
                 const((1, length)),
                 pl.BlockSpec((heads, WIDE, TILE), lambda i, m: (0, 0, i + offset)),
                 const(kn.shape), const(vt.shape),
-            ],
+            ] + [pl.BlockSpec(memory_space=pl.ANY)] * len(after),
             out_specs=[
                 pl.BlockSpec((1, width, TILE), lambda i, m: (i, 0, 0)),
                 pl.BlockSpec((heads, 16, TILE), lambda i, m: (0, 0, i)),
@@ -354,7 +355,7 @@
     return kernel_call(
         body,
         (me, seg_row, seg_row, qt, extra, kn, kt, vn, out, *grad, *earlier, *after),
-        free_in=(10, 11, 12) + tuple(range(13 + len(earlier), 13 + len(earlier) + 2)),
+        free_in=(10, 11, 12) + tuple(range(13 + len(earlier), 15 + len(earlier))),
         grid_spec=pltpu.PrefetchScalarGridSpec(
             num_scalar_prefetch=1, grid=(count,), in_specs=in_specs, out_specs=out_specs, scratch_shapes=scratch,
         ),
@@ -399,12 +400,21 @@
     )
 
 
-def feed_body(me_ref, *refs):
+def feed_piece(x, g, inner_ref, vec_ref, outer_ref):
+    hidden = nn(x, inner_ref[...]) + vec_ref[7:8, :]
+    half = 0.5 + 0.5 * lax.erf(hidden * 0.5 ** 0.5)
+    act = (hidden * half).astype(BF16)
+    slope = half + hidden * (jnp.exp(-0.5 * hidden * hidden) * 0.3989422804014327)
+    dh = (nt(g, outer_ref[...]) * slope).astype(BF16)
+    out = nn(act, outer_ref[...]).astype(BF16)
+    return act, dh, out, nt(dh, inner_ref[...]).astype(BF16)
+
+
+def near_body(me_ref, *refs):
     count = 2 * PARTS
     x_refs = refs[:count]
     g_ref, inner_ref, vec_ref, outer_ref = refs[count:count + 4]
-    before = refs[count + 4:-(count + 8)]
-    out_refs, back_refs = refs[-(count + 8):-(count + 6)], refs[-(count + 6):-6]
+    out_refs, back_refs = refs[count + 4:count + 6], refs[count + 6:-6]
     sum_ref, grad_ref, x_all, g_all, act_all, dh_all = refs[-6:]
     i = pl.program_id(0)
     at = pl.ds(pl.multiple_of(i * TILE, TILE), TILE)
@@ -414,16 +424,10 @@
             x_all[n * TILE:(n + 1) * TILE] = x_ref[...]
 
     g_all[at] = g_ref[...]
-    hidden = nn(x_all[at], inner_ref[...]) + vec_ref[7:8, :]
-    half = 0.5 + 0.5 * lax.erf(hidden * 0.5 ** 0.5)
-    act = (hidden * half).astype(BF16)
+    act, dh, out, back = feed_piece(x_all[at], g_ref[...], inner_ref, vec_ref, outer_ref)
     act_all[at] = act
-    slope = half + hidden * (jnp.exp(-0.5 * hidden * hidden) * 0.3989422804014327)
-    dh = (nt(g_ref[...], outer_ref[...]) * slope).astype(BF16)
     dh_all[at] = dh
     sums = fold(dh.astype(F32))
-    out = nn(act, outer_ref[...]).astype(BF16)
-    back = nt(dh, inner_ref[...]).astype(BF16)
 
     @pl.when(i == 0)
     def _():
@@ -438,31 +442,27 @@
 
     @pl.when(i == count - 1)
     def _():
-        for n, (left, right) in enumerate(((act_all, g_all), (x_all, dh_all))):
-            grad = tn(left[...], right[...])
-            for ref in before:
-                grad = grad + ref[n].astype(F32)
-            grad_ref[n] = grad.astype(BF16)
-
-
-def feed(base, me, pieces, cot, inner, vectors, outer, before):
+        grad_ref[0] = tn(act_all[...], g_all[...]).astype(BF16)
+        grad_ref[1] = tn(x_all[...], dh_all[...]).astype(BF16)
+
+
+def feed_near(me, pieces, cot, inner, vectors, outer):
     features = cot.shape[1]
     units = inner.shape[1]
     count = 2 * PARTS
     piece = const((TILE, features))
     scratch = lambda n: pltpu.VMEM((count * TILE, n), BF16)
     return kernel_call(
-        feed_body,
-        (me, *pieces, cot, inner, vectors, outer, *before),
+        near_body,
+        (me, *pieces, cot, inner, vectors, outer),
         free_in=tuple(range(1, count + 1)),
         free_out=(3, 5),
         grid_spec=pltpu.PrefetchScalarGridSpec(
             num_scalar_prefetch=1,
             grid=(count,),
             in_specs=[piece] * count
-            + [pl.BlockSpec((TILE, features), lambda i, m: (4 * (i // 2) + (m[0] ^ (base + i % 2)), 0)),
-               const(inner.shape), const(vectors.shape), const(outer.shape)]
-            + [const(v.shape) for v in before],
+            + [pl.BlockSpec((TILE, features), lambda i, m: (4 * (i // 2) + (m[0] ^ (i % 2)), 0)),
+               const(inner.shape), const(vectors.shape), const(outer.shape)],
             out_specs=[const((PARTS * TILE, features))] * 2 + [piece] * count
             + [const((8, units)), const((2, units, features))],
             scratch_shapes=[scratch(features), scratch(features), scratch(units), scratch(units)],
@@ -470,8 +470,79 @@
         out_shape=[shape_of(PARTS * TILE, features)] * 2 + [shape_of(TILE, features)] * count
         + [shape_of(8, units, dtype=F32), shape_of(2, units, features)],
         cost_estimate=cost(15e9, 12e6, 2e6),
-        name="feed",
-    )
+        name="feed_near",
+    )
+
+
+def far_body(me_ref, x0_ref, x1_ref, g_ref, inner_ref, vec_ref, outer_ref, *rest):
+    left_ref, right_ref, out0_ref, out1_ref, back0_ref, back1_ref, sum_ref = rest[-7:]
+    i = pl.program_id(0)
+    for n, x_ref in enumerate((x0_ref, x1_ref)):
+        @pl.when(i == n)
+        def _(x_ref=x_ref):
+            left_ref[1] = x_ref[...]
+
+    right_ref[0] = g_ref[...]
+    act, dh, out, back = feed_piece(left_ref[1], g_ref[...], inner_ref, vec_ref, outer_ref)
+    left_ref[0] = act
+    right_ref[1] = dh
+    sums = fold(dh.astype(F32))
+    for n, (out_ref, back_ref) in enumerate(((out0_ref, back0_ref), (out1_ref, back1_ref))):
+        @pl.when(i == n)
+        def _(n=n, out_ref=out_ref, back_ref=back_ref):
+            sum_ref[...] = sum_ref[...] + sums if n else sums
+            out_ref[...] = out
+            back_ref[...] = back
+
+
+def feed_far(part, me, first, second, cot, inner, vectors, outer, kept):
+    features = cot.shape[1]
+    units = inner.shape[1]
+    rows = pl.BlockSpec((2, TILE, features), lambda i, m: (0, 2 * part + i, 0))
+    piece = const((TILE, features))
+    half = pl.BlockSpec((TILE, features), lambda i, m: (part, 0))
+    return kernel_call(
+        far_body,
+        (me, first, second, cot, inner, vectors, outer, *kept),
+        free_in=(1, 2),
+        free_out=(5,),
+        grid_spec=pltpu.PrefetchScalarGridSpec(
+            num_scalar_prefetch=1,
+            grid=(2,),
+            in_specs=[
+                piece, piece,
+                pl.BlockSpec((TILE, features), lambda i, m: (4 * part + (m[0] ^ (2 + i)), 0)),
+                const(inner.shape), const(vectors.shape), const(outer.shape),
+            ] + [pl.BlockSpec(memory_space=pl.ANY)] * len(kept),
+            out_specs=[rows, rows, half, half, piece, piece, const((8, units))],
+        ),
+        out_shape=[shape_of(2, 2 * PARTS * TILE, features)] * 2 + [shape_of(PARTS * TILE, features)] * 2
+        + [shape_of(TILE, features)] * 2 + [shape_of(8, units, dtype=F32)],
+        input_output_aliases={7 + n: n for n in range(len(kept))},
+        cost_estimate=cost(5e9, 8e6, 1e6),
+        name="feed_far",
+    )
+
+
+def feed_grad_body(left_ref, right_ref, before_ref, *rest):
+    rest[-1][0] = (tn(left_ref[0], right_ref[0]) + before_ref[0].astype(F32)).astype(BF16)
+
+
+def feed_grad(left, right, before, after):
+    _, rows, features = left.shape
+    both = pl.BlockSpec((1, rows, features), lambda i: (i, 0, 0))
+    square = pl.BlockSpec((1, features, features), lambda i: (i, 0, 0))
+    return kernel_call(
+        feed_grad_body,
+        (left, right, before, *after),
+        free_in=tuple(range(3, 3 + len(after))),
+        grid=(2,),
+        in_specs=[both, both, square] + [pl.BlockSpec(memory_space=pl.ANY)] * len(after),
+        out_specs=[square],
+        out_shape=[shape_of(*before.shape)],
+        cost_estimate=cost(5e9, 10e6),
+        name="feed_grad",
+    )[0]
 
 
 def back_body(me_ref, b0_ref, b1_ref, b2_ref, residual_ref, g_ref, vec_ref, w0_ref, w1_ref, w2_ref, w3_ref,
@@ -535,7 +606,7 @@
 
 
 def tail_body(me_ref, g_ref, wq_ref, wk_ref, wv_ref, x_ref, stat_ref, *rest):
-    early, units = rest[:PARTS], rest[PARTS:PARTS + 2]
+    early, units = rest[:PARTS], rest[PARTS:2 * PARTS + 1]
     o0_ref, o1_ref, o2_ref, o3_ref, apart_ref, vec_ref, sum_ref, row_ref = rest[-8:]
     i, p = pl.program_id(0), pl.program_id(1)
     grads = g_ref[...]
@@ -964,13 +1035,13 @@
     vectors = vectors.reshape(8, features)
     wq, wk, wv = query_weight.T, key_weight.T, value_weight.T
 
-    output_weights = exchange([output_weight] * 4)
+    output_weights = spread(output_weight)
     attend_in, qt, kt, vt, kn, vn, stat = project(tokens, segment_ids, vectors, wq, wk, wv, heads)
 
     parts = range(PARTS)
     attended, extras, fours = [], [], []
     for p in parts:
-        out, extra, *four = attend_forward(p, me, segment_ids, qt, kn, vt)
+        out, extra, *four = attend_forward(p, me, segment_ids, qt, kn, vt, output_weights[1:3] if p == 0 else ())
         attended.append(out)
         extras.append(extra)
         fours.append(exchange(four))
@@ -981,22 +1052,23 @@
         residuals.append(residual)
         pieces.append([own, other_core(own), other_chip(own)])
 
-    outs, backs, sums, before = [], {}, [], ()
-    for base in (0, 2):
-        for p in parts:
-            if base:
-                far = fence(pieces[p][2], backs[0, 0], space=pltpu.VMEM)
-                pieces[p] = [None, None, far, other_core(far)]
-        result = feed(base, me, [pieces[p][base + n] for p in parts for n in (0, 1)], cot,
-                      inner_weight, vectors, outer_weight, before)
-        outs += result[:2]
-        for p in parts:
-            backs[p, base], backs[p, base + 1] = result[2 + 2 * p:4 + 2 * p]
-        sums.append(result[2 + 2 * PARTS])
-        before = result[3 + 2 * PARTS:]
-    feed_sum = lax.psum_scatter(before[0].reshape(-1, features), DP, scatter_dimension=0, tiled=True)
-
+    backs = {}
+    *outs, b00, b01, b10, b11, near_sum, near_grad = feed_near(
+        me, [pieces[p][n] for p in parts for n in (0, 1)], cot, inner_weight, vectors, outer_weight
+    )
+    backs[0, 0], backs[0, 1], backs[1, 0], backs[1, 1] = b00, b01, b10, b11
+    sums, kept = [near_sum], ()
+    for p in parts:
+        far = fence(pieces[p][2], b00, space=pltpu.VMEM)
+        *kept, backs[p, 2], backs[p, 3], far_sum = feed_far(
+            p, me, far, other_core(far), cot, inner_weight, vectors, outer_weight, kept
+        )
+        sums.append(far_sum)
+    left, right, *far_outs = kept
+    outs += far_outs
     gathered, far_sums = zip(*[gather_sum([backs[p, n] for n in range(4)]) for p in parts])
+    feed_sum = feed_grad(left, right, near_grad, far_sums).reshape(-1, features)
+    feed_sum = lax.psum_scatter(feed_sum, DP, scatter_dimension=0, tiled=True)
     grad_residuals, lows, grads_attended, inner_sums = [], [], [], []
     for p in parts:
         grad, low, a0, a1, a2, a3, vector = middle_back(
@@ -1013,17 +1085,17 @@
     part = output_grad(mixed, lows)
     earlier = attend_backward(0, me, segment_ids, qt, extras[0], kn, kt, vn, attended[0], grads_attended[0], (),
                               (far, near, part[0]))
+    there = other_chip(far)
     part_far = fence(part[2], earlier[0])
     part_far = (part_far.astype(F32) + other_core(part[3]).astype(F32)).astype(BF16)
     part_near = other_core(part[1])
     grads = attend_backward(1, me, segment_ids, qt, extras[1], kn, kt, vn, attended[1], grads_attended[1], earlier,
-                            (part_near, part_far))
+                            (part_near, part_far, there))
 
     xz = jnp.stack([lax.axis_index("x"), lax.axis_index("z")]).astype(jnp.int32)
     part_across = other_chip(part_far)
     grad_output = fence(part[0], grads).astype(F32) + part_near.astype(F32) + part_across.astype(F32)
-    there = other_chip(far)
-    keep, send = halves(xz, nn(grads, attend_in).astype(BF16), grad_output.astype(BF16), (there,))
+    keep, send = halves(xz, nn(grads, attend_in).astype(BF16), grad_output.astype(BF16), ())
     result = jnp.concatenate(residuals) + fence(outs[0], send).astype(F32) + near.astype(F32)
     result = (result + there.astype(F32) + outer_bias).astype(BF16)
     near, far = other_core(result), other_chip(result)

time: 292 us -> 289 us (0.990)
  Pallas kernels: 132 us -> 140 us
  waiting for transfers between devices: 71.2 us -> 66.9 us
  starting transfers between devices: 46.5 us -> 42.5 us
    ppermute x14, waiting for transfers between devices: 39 us -> 26.8 us  [other_chip(): return lax.ppermute(value, 'y', SWAP)]
    pallas_call x22 -> x24, Pallas kernels: 132 us -> 140 us  [kernel_call(): pl.pallas_call(body, out_shape=shapes if many else shapes[0], compiler_pa...]
    reduce_scatter x1, waiting for transfers between devices: 0.05 us -> 7.03 us  [local(): feed_sum = lax.psum_scatter(feed_sum, DP, scatter_dimension=0, tiled=True)]
    unnamed x50 -> x52, local copies, waits for them, and re-layouts: 7.96 us -> 6.24 us
  transfers between devices with their start and end apart: 52 -> 52, of which waited for: 17 -> 12; matrix products, arithmetic and copies ran while one was open for 6% -> 6% of each run, Pallas kernels for 33% -> 42%
where the time goes in v8:
time: 289 us; the launch traced here: 288 us
  Pallas kernels  140 us (48%)
  waiting for transfers between devices  66.9 us (23%)
  starting transfers between devices  42.5 us (15%)
  between operations  14.5 us (5%)
  other arithmetic  11.8 us (4%)
  local copies, waits for them, and re-layouts  7.75 us (3%)
  matrix products  4.59 us (2%)
    pallas_call x24, Pallas kernels, kernel_call(): pl.pallas_call(body, out_shape=shapes if many else shapes[0], compiler_pa...  140 us
    ppermute x14, waiting for transfers between devices, other_chip(): return lax.ppermute(value, 'y', SWAP)  26.8 us
    ppermute x6, starting transfers between devices, turned(): lax.ppermute(values, 'z', [(n, (n + way) % size) for n in range(size)])  16.9 us
    ppermute x14, starting transfers between devices, other_chip(): return lax.ppermute(value, 'y', SWAP)  14.3 us
    ppermute x6, waiting for transfers between devices, turned(): lax.ppermute(values, 'z', [(n, (n + way) % size) for n in range(size)])  11.7 us
    ppermute x1, waiting for transfers between devices, local(): got = lax.ppermute(send, 'x', SWAP)  7.43 us
    reduce_scatter x1, waiting for transfers between devices, local(): feed_sum = lax.psum_scatter(feed_sum, DP, scatter_dimension=0, tiled=True)  7.03 us
    unnamed x52, local copies, waits for them, and re-layouts  6.24 us
  transfers between devices with their start and end apart: 52, of which 12 were waited for; matrix products, arithmetic and copies ran while one was open for 6% of the time, Pallas kernels for 42%

profile of v8, /device:TPU:0, one launch (start us, length us, event | category | flops | bytes accessed | tf_op | source)
XLA Modules:
  0.0 287.6 jit_solution(14678142759272380873)
XLA Ops:
  12.5 10.6 %project.1 = (bf16[2048,768]{1,0:T(8,128)(2,1)}, bf16[3,128,2048]{2,1,0:T(8,128)(2,1)}, bf16[192,2048]{1,0:T(8,128)(2,1)}, bf16[3,80,2048]{2,1,0:T(8,128)(2,1)},...) custom-call(bf16[2048,768]{1,0:T(8,128)(2,1)} %bitcast.18, ...), custom_call_target="tpu_custom_call" | custom-call | flops 6000000000 | bytes 14000000 | tf_op jit(solution)/shard_map/project/pallas_call | solution.py:83
  23.1 9.8 %attend_forward.2 = (bf16[4,192,256]{2,1,0:T(8,128)(2,1)}, bf16[3,16,1024]{2,1,0:T(8,128)(2,1)}, bf16[192,256]{1,0:T(8,128)(2,1)}, bf16[192,256]{1,0:T(8,128)(2,...) custom-call(s32[1]{0:T(128)} %bitcast.refs_0_.me_ref, s32[1,2048]{1,0:T(1,128)S(1)} %copy-done.13, ...), custom_call_target="tpu_custom_call" | custom-call | flops 8999999488 | bytes 5000000 | tf_op jit(solution)/shard_map/attend_forward/pallas_call | solution.py:83
  35.7 8.4 %attend_forward.3 = (bf16[4,192,256]{2,1,0:T(8,128)(2,1)}, bf16[3,16,1024]{2,1,0:T(8,128)(2,1)}, bf16[192,256]{1,0:T(8,128)(2,1)}, bf16[192,256]{1,0:T(8,128)(2,...) custom-call(s32[1]{0:T(128)} %bitcast.refs_0_.me_ref, s32[1,2048]{1,0:T(1,128)S(1)} %copy-done.13, ...), custom_call_target="tpu_custom_call" | custom-call | flops 8999999488 | bytes 5000000 | tf_op jit(solution)/shard_map/attend_forward/pallas_call | solution.py:83
  56.2 13.0 %feed_near.1 = (bf16[512,768]{1,0:T(8,128)(2,1)}, bf16[512,768]{1,0:T(8,128)(2,1)}, bf16[256,768]{1,0:T(8,128)(2,1)}, bf16[256,768]{1,0:T(8,128)(2,1)S(1)}, bf16...) custom-call(s32[1]{0:T(128)} %bitcast.refs_0_.me_ref, ...), custom_call_target="tpu_custom_call" | custom-call | flops 15000000512 | bytes 12000000 | tf_op jit(solution)/shard_map/feed_near/pallas_call | solution.py:83
  69.3 4.6 %collective-permute-done.12.refs_0_ = bf16[256,768]{1,0:T(8,128)(2,1)S(1)} collective-permute-done((bf16[256,768]{1,0:T(8,128)(2,1)S(1)}, bf16[256,768]{1,0:T(8,128)(2,1)S(1)}, u32[]{:S(2)}, u32[]{:S(2)}) %collective-permute-start.12) | collective-permute-done | bytes 393248 | tf_op jit(solution)/shard_map/ppermute | solution.py:961
  73.8 6.5 %feed_far.2 = (bf16[2,1024,768]{2,1,0:T(8,128)(2,1)}, bf16[2,1024,768]{2,1,0:T(8,128)(2,1)}, bf16[512,768]{1,0:T(8,128)(2,1)}, bf16[512,768]{1,0:T(8,128)(2,1)},...) custom-call(s32[1]{0:T(128)} %bitcast.refs_0_.me_ref, ...), custom_call_target="tpu_custom_call" | custom-call | flops 5000000000 | bytes 8000000 | tf_op jit(solution)/shard_map/feed_far/pallas_call | solution.py:83
  80.4 6.7 %feed_far.3 = (bf16[2,1024,768]{2,1,0:T(8,128)(2,1)}, bf16[2,1024,768]{2,1,0:T(8,128)(2,1)}, bf16[512,768]{1,0:T(8,128)(2,1)}, bf16[512,768]{1,0:T(8,128)(2,1)},...) custom-call(s32[1]{0:T(128)} %bitcast.refs_0_.me_ref, ...), custom_call_target="tpu_custom_call", output_to_operand_aliasing={{0}: (7, {}), {1}: (8, {}), {2}: (9, {}), {3}: (10, {})} | custom-call | flops 5000000000 | bytes 8000000 | tf_op jit(solution)/shard_map/feed_far/pallas_call | solution.py:83
  96.1 6.1 %feed_grad.1 = bf16[2,768,768]{2,1,0:T(8,128)(2,1)} custom-call(bf16[2,1024,768]{2,1,0:T(8,128)(2,1)} %get-tuple-element.187.left_ref, bf16[2,1024,768]{2,1,0:T(8,128)(2,1)} %get-tuple-element.188.right_ref, bf16[2,768,768]{2,1,0:T(8,128)(2,1)} %get-tuple-element.189.before_ref, bf16[256,768]{1,0:T(8,128)(2,1)S(1)} %copy-done.3, bf16[256,768]{1,0:T(8,128)(2,1)S(1)} %copy-done.1), custom_call_target="tpu_custom_call" | custom-call | flops 5000000000 | bytes 10000000 | tf_op jit(solution)/shard_map/feed_grad/pallas_call | solution.py:83
  102.9 7.1 %collective-permute-done.23.b2_ref = bf16[256,768]{1,0:T(8,128)(2,1)S(1)} collective-permute-done((bf16[256,768]{1,0:T(8,128)(2,1)S(1)}, bf16[256,768]{1,0:T(8,128)(2,1)S(1)}, u32[]{:S(2)}, u32[]{:S(2)}) %collective-permute-start.23) | collective-permute-done | bytes 393248 | tf_op jit(solution)/shard_map/ppermute | solution.py:961
  110.0 3.7 %middle_back.3 = (f32[256,768]{1,0:T(8,128)}, bf16[256,768]{1,0:T(8,128)(2,1)}, bf16[192,256]{1,0:T(8,128)(2,1)}, bf16[192,256]{1,0:T(8,128)(2,1)}, bf16[192,256...) custom-call(s32[1]{0:T(128)} %bitcast.refs_0_.me_ref, ...), custom_call_target="tpu_custom_call" | custom-call | flops 2000000000 | bytes 4000000 | tf_op jit(solution)/shard_map/middle_back/pallas_call | solution.py:83
  115.5 3.6 %middle_back.2 = (f32[256,768]{1,0:T(8,128)}, bf16[256,768]{1,0:T(8,128)(2,1)}, bf16[192,256]{1,0:T(8,128)(2,1)}, bf16[192,256]{1,0:T(8,128)(2,1)S(1)}, bf16[192...) custom-call(s32[1]{0:T(128)} %bitcast.refs_0_.me_ref, ...), custom_call_target="tpu_custom_call" | custom-call | flops 2000000000 | bytes 4000000 | tf_op jit(solution)/shard_map/middle_back/pallas_call | solution.py:83
  126.3 14.4 %attend_backward.2 = (bf16[192,1024]{1,0:T(8,128)(2,1)}, f32[192,2048]{1,0:T(8,128)}, f32[192,2048]{1,0:T(8,128)}) custom-call(s32[1]{0:T(128)} %bitcast.refs_0_.me_ref, s32[1,2048]{1,0:T(1,128)S(1)} %copy-done.14, s32[1,2048]{1,0:T(1,128)S(1)} %copy-done.14, bf16[3,128,2048]{2,1,0:T(8,128)(2,1)} %get-tuple-element.110.refs_3_, ...), custom_call_target="tpu_custom_call" | custom-call | flops 16000000000 | bytes 10000000 | tf_op jit(solution)/shard_map/attend_backward/pallas_call | solution.py:83
  146.7 13.1 %attend_backward.3.refs_1_.g_ref = bf16[576,2048]{1,0:T(8,128)(2,1)} custom-call(s32[1]{0:T(128)} %bitcast.refs_0_.me_ref, s32[1,2048]{1,0:T(1,128)S(1)} %copy-done.14, s32[1,2048]{1,0:T(1,128)S(1)} %copy-done.14, bf16[3,128,2048]{2,1,0:T(8,128)(2,1)} %get-tuple-element.110.refs_3_, bf16[3,16,1024]{2,1,0:T(8,128)(2,1)} %get-tuple-element.117.rest_0_.refs_4_, ...), custom_call_target="tpu_custom_call" | custom-call | flops 16000000000 | bytes 10000000 | tf_op jit(solution)/shard_map/attend_backward/pallas_call | solution.py:83
  160.9 4.6 %convolution_convert_fusion.g_ref = bf16[576,768]{1,0:T(8,128)(2,1)S(1)} fusion(bf16[576,2048]{1,0:T(8,128)(2,1)} %attend_backward.3.refs_1_.g_ref, bf16[2048,768]{1,0:T(8,128)(2,1)} %get-tuple-element.166), kind=kOutput, calls=%fused_computation.6 | convolution fusion | flops 1812381696 | bytes 6389760 | tf_op jit(solution)/shard_map/dot_general | solution.py:23
  167.2 7.0 %reduce-scatter.2.cloned.1.call-done.refs_0_ = bf16[192,768]{1,0:T(8,128)(2,1)} async-done(((bf16[1536,768]{1,0:T(8,128)(2,1)}), bf16[192,768]{1,0:T(8,128)(2,1)}) %reduce-scatter.2.cloned.1.call-update) | async-done | bytes 294928 | tf_op jit(solution)/shard_map/reduce_scatter | solution.py:1071
  178.4 10.7 %tail.1 = (bf16[512,768]{1,0:T(8,128)(2,1)}, bf16[512,768]{1,0:T(8,128)(2,1)S(1)}, bf16[512,768]{1,0:T(8,128)(2,1)}, bf16[528,768]{1,0:T(8,128)(2,1)S(1)}, f32[8,768]{1,0:T(8,128)}, /*index=5*/f32[8,768]{1,0:T(8,128)}) custom-call(s32[1]{0:T(128)} %bitcast.refs_0_.me_ref, bf16[576,2048]{1,0:T(8,128)(2,1)} %attend_backward.3.refs_1_.g_ref, ...), custom_call_target="tpu_custom_call" | custom-call | flops 4000000000 | bytes 10000000 | tf_op jit(solution)/shard_map/tail/pallas_call | solution.py:83
  189.2 7.4 %collective-permute-done.36.refs_2_ = bf16[384,768]{1,0:T(8,128)(2,1)S(1)} collective-permute-done((bf16[384,768]{1,0:T(8,128)(2,1)S(1)}, bf16[384,768]{1,0:T(8,128)(2,1)S(1)}, u32[]{:S(2)}, u32[]{:S(2)}) %collective-permute-start.36) | collective-permute-done | bytes 589856 | tf_op jit(solution)/shard_map/ppermute | solution.py:1102
  208.7 15.2 %collective-permute-done.41.b2_ref.refs_5_ = bf16[528,768]{1,0:T(8,128)(2,1)S(1)} collective-permute-done((bf16[528,768]{1,0:T(8,128)(2,1)S(1)}, bf16[528,768]{1,0:T(8,128)(2,1)S(1)}, u32[]{:S(2)}, u32[]{:S(2)}) %collective-permute-start.41) | collective-permute-done | bytes 811040 | tf_op jit(solution)/shard_map/ppermute | solution.py:961
  229.2 10.9 %collective-permute-start.47 = (bf16[128,768]{1,0:T(8,128)(2,1)}, bf16[128,768]{1,0:T(8,128)(2,1)S(1)}, u32[]{:S(2)}, u32[]{:S(2)}) collective-permute-start(bf16[128,768]{1,0:T(8,128)(2,1)} %second.1.rest_0_.refs_1_), channel_id=1, source_target_pairs={{0,24},{8,0},{16,8},{24,16},{1,25},{9,1},{17,9},{25,17},{2,26},{10... | collective-permute-start | bytes 589832 | tf_op jit(solution)/shard_map/ppermute | solution.py:989
  243.0 4.4 %place.2.refs_5_ = bf16[2048,768]{1,0:T(8,128)(2,1)} custom-call(s32[1]{0:T(128)} %bitcast.refs_0_.me_ref, bf16[512,768]{1,0:T(8,128)(2,1)S(1)} %copy-done.8, bf16[512,768]{1,0:T(8,128)(2,1)S(1)} %copy-done.6, bf16[512,768]{1,0:T(8,128)(2,1)S(1)} %collective-permute-done.34.refs_4_.p2_ref, bf16[512,768]{1,0:T(8,128)(2,1)} %collective-permute-done.35.p3_ref, ...), custom_call_target="tpu_custom_call" | custom-call | flops 1000000 | bytes 9000000 | tf_op jit(solution)/shard_map/place/pallas_call | solution.py:83
  247.3 11.7 %collective-permute-done.46.refs_3_ = bf16[128,768]{1,0:T(8,128)(2,1)S(1)} collective-permute-done((bf16[128,768]{1,0:T(8,128)(2,1)}, bf16[128,768]{1,0:T(8,128)(2,1)S(1)}, u32[]{:S(2)}, u32[]{:S(2)}) %collective-permute-start.46) | collective-permute-done | bytes 196640 | tf_op jit(solution)/shard_map/ppermute | solution.py:989
  262.8 5.2 %place.3 = f32[2048,768]{1,0:T(8,128)} custom-call(s32[1]{0:T(128)} %bitcast.refs_0_.me_ref, bf16[512,768]{1,0:T(8,128)(2,1)S(1)} %fence.21.p0_ref, bf16[512,768]{1,0:T(8,128)(2,1)} %collective-permute-done.43.p1_ref, bf16[512,768]{1,0:T(8,128)(2,1)S(1)} %fence.22.p2_ref, bf16[512,768]{1,0:T(8,128)(2,1)S(1)} %collective-permute-done.48.p3_ref, ...), custom_call_target="tpu_custom_call" | custom-call | flops 1000000 | bytes 9000000 | tf_op jit(solution)/shard_map/place/pallas_call | solution.py:83
  268.0 4.2 %slice_convert_fusion = (f32[768,768]{1,0:T(8,128)}, f32[768,768]{1,0:T(8,128)}) fusion(bf16[1536,768]{1,0:T(8,128)(2,1)} %all-gather.2.cloned.1.call-done), kind=kLoop, calls=%fused_computation.7 | loop fusion | flops 1179648 | bytes 7077888 | tf_op jit(solution)/shard_map/convert_element_type | solution.py:1107
  272.1 5.4 %collective-permute-done.49.other_ref = bf16[416,768]{1,0:T(8,128)(2,1)S(1)} collective-permute-done((bf16[416,768]{1,0:T(8,128)(2,1)}, bf16[416,768]{1,0:T(8,128)(2,1)S(1)}, u32[]{:S(2)}, u32[]{:S(2)}) %collective-permute-start.49) | collective-permute-done | bytes 639008 | tf_op jit(solution)/shard_map/ppermute | solution.py:1126
  (182 shorter events, 79.0 us)
Async XLA Ops:
  7.2 167.0 %reduce-scatter.2.cloned.1.call-start = ((), (), s32[]{:S(2)}) async-start(), calls=%async_computation.1 | async-start | bytes 2654208 | tf_op jit(solution)/shard_map/reduce_scatter | solution.py:1071
  54.4 19.4 %collective-permute-start.12 = (bf16[256,768]{1,0:T(8,128)(2,1)S(1)}, bf16[256,768]{1,0:T(8,128)(2,1)S(1)}, u32[]{:S(2)}, u32[]{:S(2)}) collective-permute-start(bf16[256,768]{1,0:T(8,128)(2,1)S(1)} %get-tuple-element.125.refs_2_), channel_id=1, source_target_pairs={{0,2},{2,0},{1,3},{3,1},{4,6},{6,4},{5,7},{7,5},{8,10},{10,8},{9,1... | collective-permute-start | bytes 1179656 | tf_op jit(solution)/shard_map/ppermute | solution.py:961
  87.8 25.9 %collective-permute-start.11 = (bf16[256,768]{1,0:T(8,128)(2,1)S(1)}, bf16[256,768]{1,0:T(8,128)(2,1)S(1)}, u32[]{:S(2)}, u32[]{:S(2)}) collective-permute-start(bf16[256,768]{1,0:T(8,128)(2,1)S(1)} %get-tuple-element.131), channel_id=1, source_target_pairs={{0,1},{1,0},{2,3},{3,2},{4,5},{5,4},{6,7},{7,6},{8,9},{9,8},{10,11... | collective-permute-start | bytes 1179656 | tf_op jit(solution)/shard_map/ppermute | solution.py:957
  90.1 24.0 %collective-permute-start.17 = (bf16[256,768]{1,0:T(8,128)(2,1)S(1)}, bf16[256,768]{1,0:T(8,128)(2,1)S(1)}, u32[]{:S(2)}, u32[]{:S(2)}) collective-permute-start(bf16[256,768]{1,0:T(8,128)(2,1)S(1)} %add_convert_fusion.2.refs_2_.rest_1_), channel_id=1, source_target_pairs={{0,2},{2,0},{1,3},{3,1},{4,6},{6,4},{5,7},{7,5},{8,10},{10,8},{9,1... | collective-permute-start | bytes 1179656 | tf_op jit(solution)/shard_map/ppermute | solution.py:961
  94.1 27.8 %collective-permute-start.27 = (bf16[512,768]{1,0:T(8,128)(2,1)}, bf16[512,768]{1,0:T(8,128)(2,1)}, u32[]{:S(2)}, u32[]{:S(2)}) collective-permute-start(bf16[512,768]{1,0:T(8,128)(2,1)} %fence.14), channel_id=1, source_target_pairs={{0,1},{1,0},{2,3},{3,2},{4,5},{5,4},{6,7},{7,6},{8,9},{9,8},{10,11... | collective-permute-start | bytes 2359304 | tf_op jit(solution)/shard_map/ppermute | solution.py:957
  102.3 165.7 %all-gather.2.cloned.1.call-start = ((), (), s32[]{:S(2)}) async-start(), calls=%async_computation.2 | async-start | bytes 2654208 | tf_op jit(solution)/shard_map/all_gather | solution.py:1106
  102.3 22.3 %collective-permute-start.28 = (bf16[512,768]{1,0:T(8,128)(2,1)}, bf16[512,768]{1,0:T(8,128)(2,1)S(1)}, u32[]{:S(2)}, u32[]{:S(2)}) collective-permute-start(bf16[512,768]{1,0:T(8,128)(2,1)} %fence.16), channel_id=1, source_target_pairs={{0,1},{1,0},{2,3},{3,2},{4,5},{5,4},{6,7},{7,6},{8,9},{9,8},{10,11... | collective-permute-start | bytes 2359304 | tf_op jit(solution)/shard_map/ppermute | solution.py:957
  121.9 19.9 %collective-permute-start.18 = (bf16[192,256]{1,0:T(8,128)(2,1)S(1)}, bf16[192,256]{1,0:T(8,128)(2,1)S(1)}, u32[]{:S(2)}, u32[]{:S(2)}) collective-permute-start(bf16[192,256]{1,0:T(8,128)(2,1)S(1)} %get-tuple-element.140), channel_id=1, source_target_pairs={{0,1},{1,0},{2,3},{3,2},{4,5},{5,4},{6,7},{7,6},{8,9},{9,8},{10,11... | collective-permute-start | bytes 294920 | tf_op jit(solution)/shard_map/ppermute | solution.py:957
  123.7 19.6 %collective-permute-start.19 = (bf16[192,256]{1,0:T(8,128)(2,1)S(1)}, bf16[192,256]{1,0:T(8,128)(2,1)S(1)}, u32[]{:S(2)}, u32[]{:S(2)}) collective-permute-start(bf16[192,256]{1,0:T(8,128)(2,1)S(1)} %get-tuple-element.141), channel_id=1, source_target_pairs={{0,2},{2,0},{1,3},{3,1},{4,6},{6,4},{5,7},{7,5},{8,10},{10,8},{9,1... | collective-permute-start | bytes 294920 | tf_op jit(solution)/shard_map/ppermute | solution.py:961
  124.1 22.7 %collective-permute-start.29 = (bf16[192,768]{1,0:T(8,128)(2,1)S(1)}, bf16[192,768]{1,0:T(8,128)(2,1)S(1)}, u32[]{:S(2)}, u32[]{:S(2)}) collective-permute-start(bf16[192,768]{1,0:T(8,128)(2,1)S(1)} %get-tuple-element.163), channel_id=1, source_target_pairs={{0,1},{1,0},{2,3},{3,2},{4,5},{5,4},{6,7},{7,6},{8,9},{9,8},{10,11... | collective-permute-start | bytes 884744 | tf_op jit(solution)/shard_map/ppermute | solution.py:957
  124.6 22.2 %collective-permute-start.31 = (bf16[512,768]{1,0:T(8,128)(2,1)S(1)}, bf16[512,768]{1,0:T(8,128)(2,1)}, u32[]{:S(2)}, u32[]{:S(2)}) collective-permute-start(bf16[512,768]{1,0:T(8,128)(2,1)S(1)} %fence.15.refs_13_), channel_id=1, source_target_pairs={{0,2},{2,0},{1,3},{3,1},{4,6},{6,4},{5,7},{7,5},{8,10},{10,8},{9,1... | collective-permute-start | bytes 2359304 | tf_op jit(solution)/shard_map/ppermute | solution.py:961
  141.9 18.0 %collective-permute-start.32 = (bf16[192,768]{1,0:T(8,128)(2,1)S(1)}, bf16[192,768]{1,0:T(8,128)(2,1)S(1)}, u32[]{:S(2)}, u32[]{:S(2)}) collective-permute-start(bf16[192,768]{1,0:T(8,128)(2,1)S(1)} %add_convert_fusion.4.refs_17_), channel_id=1, source_target_pairs={{0,2},{2,0},{1,3},{3,1},{4,6},{6,4},{5,7},{7,5},{8,10},{10,8},{9,1... | collective-permute-start | bytes 884744 | tf_op jit(solution)/shard_map/ppermute | solution.py:961
  176.1 20.5 %collective-permute-start.34 = (bf16[512,768]{1,0:T(8,128)(2,1)S(1)}, bf16[512,768]{1,0:T(8,128)(2,1)S(1)}, u32[]{:S(2)}, u32[]{:S(2)}) collective-permute-start(bf16[512,768]{1,0:T(8,128)(2,1)S(1)} %fusion.3.p0_ref), channel_id=1, source_target_pairs={{0,2},{2,0},{1,3},{3,1},{4,6},{6,4},{5,7},{7,5},{8,10},{10,8},{9,1... | collective-permute-start | bytes 2359304 | tf_op jit(solution)/shard_map/ppermute | solution.py:961
  177.7 18.9 %collective-permute-start.33 = (bf16[512,768]{1,0:T(8,128)(2,1)S(1)}, bf16[512,768]{1,0:T(8,128)(2,1)S(1)}, u32[]{:S(2)}, u32[]{:S(2)}) collective-permute-start(bf16[512,768]{1,0:T(8,128)(2,1)S(1)} %fusion.3.p0_ref), channel_id=1, source_target_pairs={{0,1},{1,0},{2,3},{3,2},{4,5},{5,4},{6,7},{7,6},{8,9},{9,8},{10,11... | collective-permute-start | bytes 2359304 | tf_op jit(solution)/shard_map/ppermute | solution.py:957
  177.7 18.9 %collective-permute-start.36 = (bf16[384,768]{1,0:T(8,128)(2,1)S(1)}, bf16[384,768]{1,0:T(8,128)(2,1)S(1)}, u32[]{:S(2)}, u32[]{:S(2)}) collective-permute-start(bf16[384,768]{1,0:T(8,128)(2,1)S(1)} %copy-done.15), channel_id=1, source_target_pairs={{0,4},{4,0},{1,5},{5,1},{2,6},{6,2},{3,7},{7,3},{8,12},{12,8},{9,1... | collective-permute-start | bytes 1769480 | tf_op jit(solution)/shard_map/ppermute | solution.py:1102
  203.7 20.2 %collective-permute-start.41 = (bf16[528,768]{1,0:T(8,128)(2,1)S(1)}, bf16[528,768]{1,0:T(8,128)(2,1)S(1)}, u32[]{:S(2)}, u32[]{:S(2)}) collective-permute-start(bf16[528,768]{1,0:T(8,128)(2,1)S(1)} %chip_sum.1.refs_4_), channel_id=1, source_target_pairs={{0,2},{2,0},{1,3},{3,1},{4,6},{6,4},{5,7},{7,5},{8,10},{10,8},{9,1... | collective-permute-start | bytes 2433032 | tf_op jit(solution)/shard_map/ppermute | solution.py:961
  204.3 22.6 %collective-permute-start.37 = (bf16[96,768]{1,0:T(8,128)(2,1)S(1)}, bf16[96,768]{1,0:T(8,128)(2,1)S(1)}, u32[]{:S(2)}, u32[]{:S(2)}) collective-permute-start(bf16[96,768]{1,0:T(8,128)(2,1)S(1)} %copy-done.25), channel_id=1, source_target_pairs={{0,8},{8,16},{16,24},{24,0},{1,9},{9,17},{17,25},{25,1},{2,10},{10... | collective-permute-start | bytes 442376 | tf_op jit(solution)/shard_map/ppermute | solution.py:989
  205.4 21.5 %collective-permute-start.38 = (bf16[96,768]{1,0:T(8,128)(2,1)S(1)}, bf16[96,768]{1,0:T(8,128)(2,1)S(1)}, u32[]{:S(2)}, u32[]{:S(2)}) collective-permute-start(bf16[96,768]{1,0:T(8,128)(2,1)S(1)} %copy-done.24), channel_id=1, source_target_pairs={{0,16},{8,24},{16,0},{24,8},{1,17},{9,25},{17,1},{25,9},{2,18},{10... | collective-permute-start | bytes 442376 | tf_op jit(solution)/shard_map/ppermute | solution.py:989
  207.8 19.1 %collective-permute-start.39 = (bf16[96,768]{1,0:T(8,128)(2,1)S(1)}, bf16[96,768]{1,0:T(8,128)(2,1)S(1)}, u32[]{:S(2)}, u32[]{:S(2)}) collective-permute-start(bf16[96,768]{1,0:T(8,128)(2,1)S(1)} %copy-done.21), channel_id=1, source_target_pairs={{0,24},{8,0},{16,8},{24,16},{1,25},{9,1},{17,9},{25,17},{2,26},{10... | collective-permute-start | bytes 442376 | tf_op jit(solution)/shard_map/ppermute | solution.py:989
  208.7 33.1 %collective-permute-start.35 = (bf16[512,768]{1,0:T(8,128)(2,1)S(1)}, bf16[512,768]{1,0:T(8,128)(2,1)}, u32[]{:S(2)}, u32[]{:S(2)}) collective-permute-start(bf16[512,768]{1,0:T(8,128)(2,1)S(1)} %collective-permute-done.34.refs_4_.p2_ref), channel_id=1, source_target_pairs={{0,1},{1,0},{2,3},{3,2},{4,5},{5,4},{6,7},{7,6},{8,9},{9,8},{10,11... | collective-permute-start | bytes 2359304 | tf_op jit(solution)/shard_map/ppermute | solution.py:957
  228.7 31.8 %collective-permute-start.44 = (bf16[512,768]{1,0:T(8,128)(2,1)S(1)}, bf16[512,768]{1,0:T(8,128)(2,1)S(1)}, u32[]{:S(2)}, u32[]{:S(2)}) collective-permute-start(bf16[512,768]{1,0:T(8,128)(2,1)S(1)} %fence.21.p0_ref), channel_id=1, source_target_pairs={{0,2},{2,0},{1,3},{3,1},{4,6},{6,4},{5,7},{7,5},{8,10},{10,8},{9,1... | collective-permute-start | bytes 2359304 | tf_op jit(solution)/shard_map/ppermute | solution.py:961
  229.2 18.1 %collective-permute-start.47 = (bf16[128,768]{1,0:T(8,128)(2,1)}, bf16[128,768]{1,0:T(8,128)(2,1)S(1)}, u32[]{:S(2)}, u32[]{:S(2)}) collective-permute-start(bf16[128,768]{1,0:T(8,128)(2,1)} %second.1.rest_0_.refs_1_), channel_id=1, source_target_pairs={{0,24},{8,0},{16,8},{24,16},{1,25},{9,1},{17,9},{25,17},{2,26},{10... | collective-permute-start | bytes 589832 | tf_op jit(solution)/shard_map/ppermute | solution.py:989
  240.1 19.0 %collective-permute-start.46 = (bf16[128,768]{1,0:T(8,128)(2,1)}, bf16[128,768]{1,0:T(8,128)(2,1)S(1)}, u32[]{:S(2)}, u32[]{:S(2)}) collective-permute-start(bf16[128,768]{1,0:T(8,128)(2,1)} %second.1.rest_0_.refs_1_), channel_id=1, source_target_pairs={{0,16},{8,24},{16,0},{24,8},{1,17},{9,25},{17,1},{25,9},{2,18},{10... | collective-permute-start | bytes 589832 | tf_op jit(solution)/shard_map/ppermute | solution.py:989
  241.8 20.1 %collective-permute-start.43 = (bf16[512,768]{1,0:T(8,128)(2,1)S(1)}, bf16[512,768]{1,0:T(8,128)(2,1)}, u32[]{:S(2)}, u32[]{:S(2)}) collective-permute-start(bf16[512,768]{1,0:T(8,128)(2,1)S(1)} %fence.21.p0_ref), channel_id=1, source_target_pairs={{0,1},{1,0},{2,3},{3,2},{4,5},{5,4},{6,7},{7,6},{8,9},{9,8},{10,11... | collective-permute-start | bytes 2359304 | tf_op jit(solution)/shard_map/ppermute | solution.py:957
  (54 other events, 433.2 us)
Sparse Core Ops, SparseCore 0:
  102.4 71.8 reduce-scatter.1
  176.4 64.2 all-gather.1

commit v9 on v8

--- a/solution.py
+++ b/solution.py
@@ -643,9 +643,8 @@
         inside = units[0][...]
         for ref in units[1:]:
             inside = inside + ref[...]
-        apart_ref[0:1] = jnp.sum(inside, axis=0, keepdims=True)
-        apart_ref[1:] = jnp.zeros((7, apart_ref.shape[1]), F32)
-        apart_ref[1:2, :row_ref.shape[1]] = row_ref[0:1]
+        apart_ref[...] = jnp.where(row == 6, jnp.sum(inside, axis=0, keepdims=True), 0.0)
+        apart_ref[7:8, :row_ref.shape[1]] = row_ref[0:1]
         o3_ref[PARTS * TILE:] = paired(vectors)
 
 
@@ -779,8 +778,7 @@
     for ref in refs[1:count]:
         total = total + ref[...].astype(F32)
     out_ref[:rows] = total.astype(BF16)
-    shared = joined(one_ref[...]) + joined(two_ref[...])
-    out_ref[rows:] = paired(jnp.concatenate([shared, apart_ref[...]], axis=0))
+    out_ref[rows:] = paired(joined(one_ref[...]) + joined(two_ref[...]) + apart_ref[...])
 
 
 def second(parts, one, two, apart, after):
@@ -798,8 +796,8 @@
         grid=(1,),
         in_specs=[const((rows, features))] * count + [last, last, const(apart.shape)]
         + [pl.BlockSpec(memory_space=pl.ANY)] * len(after),
-        out_specs=[const((rows + 32, features))],
-        out_shape=[shape_of(rows + 32, features)],
+        out_specs=[const((rows + 16, features))],
+        out_shape=[shape_of(rows + 16, features)],
         name="second",
     )[0]
 
@@ -841,7 +839,7 @@
 
 
 def ready_body(xz_ref, mine_ref, other_ref, *rest):
-    outs = rest[-16:]
+    outs = rest[-14:]
     width = outs[0].shape[0]
     for n, out_ref in enumerate(outs[:4]):
         rows = slice(n % 2 * width, (n % 2 + 1) * width)
@@ -851,15 +849,15 @@
                 out_ref[...] = to_ref[rows].astype(F32)
 
     small = joined(mine_ref[2 * width:]) + joined(other_ref[2 * width:])
-    for n, out_ref in enumerate(outs[4:13]):
+    for n, out_ref in enumerate(outs[4:11]):
         out_ref[...] = small[n]
-    for n, out_ref in enumerate(outs[13:]):
-        out_ref[...] = small[9, n * width:(n + 1) * width]
+    for n, out_ref in enumerate(outs[11:]):
+        out_ref[...] = small[7, n * width:(n + 1) * width]
 
 
 def ready(xz, mine, other, width, after):
     rows, features = mine.shape
-    sizes = [(features,)] * 9 + [(width,)] * 3
+    sizes = [(features,)] * 7 + [(width,)] * 3
     return kernel_call(
         ready_body,
         (xz, mine, other, *after),
@@ -1057,16 +1055,21 @@
         me, [pieces[p][n] for p in parts for n in (0, 1)], cot, inner_weight, vectors, outer_weight
     )
     backs[0, 0], backs[0, 1], backs[1, 0], backs[1, 1] = b00, b01, b10, b11
-    sums, kept = [near_sum], ()
+    sums, kept, gathered, far_sums = [near_sum], (), [], [b00]
     for p in parts:
-        far = fence(pieces[p][2], b00, space=pltpu.VMEM)
+        far = fence(pieces[p][2], far_sums[-1], space=pltpu.VMEM)
         *kept, backs[p, 2], backs[p, 3], far_sum = feed_far(
             p, me, far, other_core(far), cot, inner_weight, vectors, outer_weight, kept
         )
         sums.append(far_sum)
+        if p:
+            backs[p, 3] = fence(backs[p, 3], gathered[-1][2], space=pltpu.VMEM)
+        summed, far_sum = gather_sum([backs[p, n] for n in range(4)])
+        gathered.append(summed)
+        far_sums.append(far_sum)
+    far_sums = far_sums[1:]
     left, right, *far_outs = kept
     outs += far_outs
-    gathered, far_sums = zip(*[gather_sum([backs[p, n] for n in range(4)]) for p in parts])
     feed_sum = feed_grad(left, right, near_grad, far_sums).reshape(-1, features)
     feed_sum = lax.psum_scatter(feed_sum, DP, scatter_dimension=0, tiled=True)
     grad_residuals, lows, grads_attended, inner_sums = [], [], [], []
@@ -1103,9 +1106,9 @@
     back_own, back_near, back_far, back_across, apart, summed = tail(
         me, grads, wq, wk, wv, tokens, stat, inner_sums, sums, (send,)
     )
-    feed_sum = lax.all_gather(fence(feed_sum, send), DP, axis=0, tiled=True)
+    quarter = sum_first(xz, keep, got, (near, far, apart))
+    feed_sum = lax.all_gather(fence(feed_sum, quarter[-1]), DP, axis=0, tiled=True)
     feed_sum = (feed_sum[:features].astype(F32), feed_sum[features:].astype(F32))
-    quarter = sum_first(xz, keep, got, (near, far, apart))
     back_across = other_core(fence(back_across, quarter[-1], space=pltpu.VMEM))
     back_far = chip_sum(back_far, back_across, summed, ())
     back_there = other_chip(back_far)
@@ -1114,15 +1117,15 @@
         turns = [quarter[0]] + [turned(part, n + 1) for n, part in enumerate(quarter[1:])]
         held = second(turns, back_far, back_there, apart, (share,))
         layer_out = place(me, [result, near, far, other_core(far)], BF16, (held,))
-        mine = third(xz, gather_z(held), 32, (layer_out,))
+        mine = third(xz, gather_z(held), 16, (layer_out,))
     else:
-        small = jnp.concatenate([joined(back_far[-16:]) + joined(back_there[-16:]), apart])
+        small = joined(back_far[-16:]) + joined(back_there[-16:]) + apart
         layer_out = place(me, [result, near, far, other_core(far)], BF16, ())
         mine = jnp.concatenate([quarter[0], paired(lax.psum(small, "z"))])
     share = fence(share, held if len(quarter) > 1 else mine, space=pltpu.VMEM)
     near, far = other_core(share), fence(other_chip(share), mine, space=pltpu.VMEM)
     input_grad = place(me, [share, near, far, other_core(far)], F32, (mine,))
-    *wide, two_gain, two_bias, output_sum, outer_bias, one_gain, one_bias, _, _, inner_bias, query, _, value = ready(
+    *wide, two_gain, two_bias, output_sum, outer_bias, one_gain, one_bias, inner_bias, query, _, value = ready(
         xz, mine, lax.ppermute(mine, "x", SWAP), width, feed_sum
     )
     return (

time: 289 us -> 302 us (1.045)
  waiting for transfers between devices: 66.9 us -> 80.8 us
  starting transfers between devices: 42.5 us -> 35.5 us
  Pallas kernels: 140 us -> 145 us
    ppermute x6, waiting for transfers between devices: 11.7 us -> 26.3 us  [turned(): lax.ppermute(values, 'z', [(n, (n + way) % size) for n in range(size)])]
    reduce_scatter x1, waiting for transfers between devices: 7.03 us -> 0.01 us  [local(): feed_sum = lax.psum_scatter(feed_sum, DP, scatter_dimension=0, tiled=True)]
    pallas_call x24, Pallas kernels: 140 us -> 145 us  [kernel_call(): pl.pallas_call(body, out_shape=shapes if many else shapes[0], compiler_pa...]
    ppermute x24, waiting for transfers between devices: 4 us -> 8.64 us  [other_core(): return lax.ppermute(value, 'core', SWAP)]
    ppermute x14, waiting for transfers between devices: 26.8 us -> 31.3 us  [other_chip(): return lax.ppermute(value, 'y', SWAP)]
    ppermute x14, starting transfers between devices: 14.3 us -> 10.5 us  [other_chip(): return lax.ppermute(value, 'y', SWAP)]
    ppermute x6, starting transfers between devices: 16.9 us -> 13.2 us  [turned(): lax.ppermute(values, 'z', [(n, (n + way) % size) for n in range(size)])]
    unnamed x52 -> x44, local copies, waits for them, and re-layouts: 6.24 us -> 5.75 us
  transfers between devices with their start and end apart: 52 -> 52, of which waited for: 12 -> 17; matrix products, arithmetic and copies ran while one was open for 6% -> 6% of each run, Pallas kernels for 42% -> 42%
where the time goes in v9:
time: 302 us; the launch traced here: 300 us
  Pallas kernels  145 us (48%)
  waiting for transfers between devices  80.8 us (27%)
  starting transfers between devices  35.5 us (12%)
  between operations  14.4 us (5%)
  other arithmetic  12.3 us (4%)
  local copies, waits for them, and re-layouts  7.25 us (2%)
  matrix products  4.8 us (2%)
    pallas_call x24, Pallas kernels, kernel_call(): pl.pallas_call(body, out_shape=shapes if many else shapes[0], compiler_pa...  145 us
    ppermute x14, waiting for transfers between devices, other_chip(): return lax.ppermute(value, 'y', SWAP)  31.3 us
    ppermute x6, waiting for transfers between devices, turned(): lax.ppermute(values, 'z', [(n, (n + way) % size) for n in range(size)])  26.3 us
    ppermute x6, starting transfers between devices, turned(): lax.ppermute(values, 'z', [(n, (n + way) % size) for n in range(size)])  13.2 us
    ppermute x14, starting transfers between devices, other_chip(): return lax.ppermute(value, 'y', SWAP)  10.5 us
    ppermute x24, waiting for transfers between devices, other_core(): return lax.ppermute(value, 'core', SWAP)  8.64 us
    ppermute x24, starting transfers between devices, other_core(): return lax.ppermute(value, 'core', SWAP)  7.71 us
  transfers between devices with their start and end apart: 52, of which 17 were waited for; matrix products, arithmetic and copies ran while one was open for 6% of the time, Pallas kernels for 42%

profile of v9, /device:TPU:0, one launch (start us, length us, event | category | flops | bytes accessed | tf_op | source)
XLA Modules:
  0.0 300.0 jit_solution(16032712578293404009)
XLA Ops:
  12.5 10.6 %project.1 = (bf16[2048,768]{1,0:T(8,128)(2,1)}, bf16[3,128,2048]{2,1,0:T(8,128)(2,1)}, bf16[192,2048]{1,0:T(8,128)(2,1)}, bf16[3,80,2048]{2,1,0:T(8,128)(2,1)},...) custom-call(bf16[2048,768]{1,0:T(8,128)(2,1)} %bitcast.18, ...), custom_call_target="tpu_custom_call" | custom-call | flops 6000000000 | bytes 14000000 | tf_op jit(solution)/shard_map/project/pallas_call | solution.py:83
  23.1 10.1 %attend_forward.2 = (bf16[4,192,256]{2,1,0:T(8,128)(2,1)}, bf16[3,16,1024]{2,1,0:T(8,128)(2,1)}, bf16[192,256]{1,0:T(8,128)(2,1)}, bf16[192,256]{1,0:T(8,128)(2,...) custom-call(s32[1]{0:T(128)} %bitcast.refs_0_.me_ref, s32[1,2048]{1,0:T(1,128)S(1)} %copy-done.11, ...), custom_call_target="tpu_custom_call" | custom-call | flops 8999999488 | bytes 5000000 | tf_op jit(solution)/shard_map/attend_forward/pallas_call | solution.py:83
  35.9 10.7 %attend_forward.3 = (bf16[4,192,256]{2,1,0:T(8,128)(2,1)}, bf16[3,16,1024]{2,1,0:T(8,128)(2,1)}, bf16[192,256]{1,0:T(8,128)(2,1)}, bf16[192,256]{1,0:T(8,128)(2,...) custom-call(s32[1]{0:T(128)} %bitcast.refs_0_.me_ref, s32[1,2048]{1,0:T(1,128)S(1)} %copy-done.11, ...), custom_call_target="tpu_custom_call" | custom-call | flops 8999999488 | bytes 5000000 | tf_op jit(solution)/shard_map/attend_forward/pallas_call | solution.py:83
  58.1 13.0 %feed_near.1 = (bf16[512,768]{1,0:T(8,128)(2,1)}, bf16[512,768]{1,0:T(8,128)(2,1)}, bf16[256,768]{1,0:T(8,128)(2,1)}, bf16[256,768]{1,0:T(8,128)(2,1)S(1)}, bf16...) custom-call(s32[1]{0:T(128)} %bitcast.refs_0_.me_ref, ...), custom_call_target="tpu_custom_call" | custom-call | flops 15000000512 | bytes 12000000 | tf_op jit(solution)/shard_map/feed_near/pallas_call | solution.py:83
  72.9 6.5 %feed_far.2 = (bf16[2,1024,768]{2,1,0:T(8,128)(2,1)}, bf16[2,1024,768]{2,1,0:T(8,128)(2,1)}, bf16[512,768]{1,0:T(8,128)(2,1)}, bf16[512,768]{1,0:T(8,128)(2,1)},...) custom-call(s32[1]{0:T(128)} %bitcast.refs_0_.me_ref, ...), custom_call_target="tpu_custom_call" | custom-call | flops 5000000000 | bytes 8000000 | tf_op jit(solution)/shard_map/feed_far/pallas_call | solution.py:83
  83.0 8.0 %collective-permute-done.12.refs_0_ = bf16[256,768]{1,0:T(8,128)(2,1)S(1)} collective-permute-done((bf16[256,768]{1,0:T(8,128)(2,1)S(1)}, bf16[256,768]{1,0:T(8,128)(2,1)S(1)}, u32[]{:S(2)}, u32[]{:S(2)}) %collective-permute-start.12) | collective-permute-done | bytes 393248 | tf_op jit(solution)/shard_map/ppermute | solution.py:959
  92.7 6.5 %feed_far.3 = (bf16[2,1024,768]{2,1,0:T(8,128)(2,1)}, bf16[2,1024,768]{2,1,0:T(8,128)(2,1)}, bf16[512,768]{1,0:T(8,128)(2,1)}, bf16[512,768]{1,0:T(8,128)(2,1)},...) custom-call(s32[1]{0:T(128)} %bitcast.refs_0_.me_ref, ...), custom_call_target="tpu_custom_call", output_to_operand_aliasing={{0}: (7, {}), {1}: (8, {}), {2}: (9, {}), {3}: (10, {})} | custom-call | flops 5000000000 | bytes 8000000 | tf_op jit(solution)/shard_map/feed_far/pallas_call | solution.py:83
  105.1 3.7 %middle_back.3 = (f32[256,768]{1,0:T(8,128)}, bf16[256,768]{1,0:T(8,128)(2,1)}, bf16[192,256]{1,0:T(8,128)(2,1)}, bf16[192,256]{1,0:T(8,128)(2,1)S(1)}, bf16[192...) custom-call(s32[1]{0:T(128)} %bitcast.refs_0_.me_ref, ...), custom_call_target="tpu_custom_call" | custom-call | flops 2000000000 | bytes 4000000 | tf_op jit(solution)/shard_map/middle_back/pallas_call | solution.py:83
  111.3 6.1 %feed_grad.1 = bf16[2,768,768]{2,1,0:T(8,128)(2,1)} custom-call(bf16[2,1024,768]{2,1,0:T(8,128)(2,1)} %get-tuple-element.187.left_ref, bf16[2,1024,768]{2,1,0:T(8,128)(2,1)} %get-tuple-element.188.right_ref, bf16[2,768,768]{2,1,0:T(8,128)(2,1)} %get-tuple-element.189.before_ref, bf16[256,768]{1,0:T(8,128)(2,1)S(1)} %copy-done, ...), custom_call_target="tpu_custom_call" | custom-call | flops 5000000000 | bytes 10000000 | tf_op jit(solution)/shard_map/feed_grad/pallas_call | solution.py:83
  121.8 3.6 %middle_back.2 = (f32[256,768]{1,0:T(8,128)}, bf16[256,768]{1,0:T(8,128)(2,1)}, bf16[192,256]{1,0:T(8,128)(2,1)}, bf16[192,256]{1,0:T(8,128)(2,1)S(1)}, bf16[192...) custom-call(s32[1]{0:T(128)} %bitcast.refs_0_.me_ref, ...), custom_call_target="tpu_custom_call" | custom-call | flops 2000000000 | bytes 4000000 | tf_op jit(solution)/shard_map/middle_back/pallas_call | solution.py:83
  132.7 14.3 %attend_backward.2 = (bf16[192,1024]{1,0:T(8,128)(2,1)}, f32[192,2048]{1,0:T(8,128)}, f32[192,2048]{1,0:T(8,128)}) custom-call(s32[1]{0:T(128)} %bitcast.refs_0_.me_ref, s32[1,2048]{1,0:T(1,128)S(1)} %copy-done.11, s32[1,2048]{1,0:T(1,128)S(1)} %copy-done.11, bf16[3,128,2048]{2,1,0:T(8,128)(2,1)} %get-tuple-element.110.refs_3_, ...), custom_call_target="tpu_custom_call" | custom-call | flops 16000000000 | bytes 10000000 | tf_op jit(solution)/shard_map/attend_backward/pallas_call | solution.py:83
  149.9 4.0 %collective-permute-done.22.refs_12_ = bf16[192,256]{1,0:T(8,128)(2,1)S(1)} collective-permute-done((bf16[192,256]{1,0:T(8,128)(2,1)S(1)}, bf16[192,256]{1,0:T(8,128)(2,1)S(1)}, u32[]{:S(2)}, u32[]{:S(2)}) %collective-permute-start.22) | collective-permute-done | bytes 98336 | tf_op jit(solution)/shard_map/ppermute | solution.py:963
  153.9 16.3 %attend_backward.3.refs_1_.g_ref = bf16[576,2048]{1,0:T(8,128)(2,1)} custom-call(s32[1]{0:T(128)} %bitcast.refs_0_.me_ref, s32[1,2048]{1,0:T(1,128)S(1)} %copy-done.11, s32[1,2048]{1,0:T(1,128)S(1)} %copy-done.11, bf16[3,128,2048]{2,1,0:T(8,128)(2,1)} %get-tuple-element.110.refs_3_, bf16[3,16,1024]{2,1,0:T(8,128)(2,1)} %get-tuple-element.117.rest_0_.refs_4_, ...), custom_call_target="tpu_custom_call" | custom-call | flops 16000000000 | bytes 10000000 | tf_op jit(solution)/shard_map/attend_backward/pallas_call | solution.py:83
  171.3 4.8 %convolution_convert_fusion.g_ref = bf16[576,768]{1,0:T(8,128)(2,1)S(1)} fusion(bf16[576,2048]{1,0:T(8,128)(2,1)} %attend_backward.3.refs_1_.g_ref, bf16[2048,768]{1,0:T(8,128)(2,1)} %get-tuple-element.166), kind=kOutput, calls=%fused_computation.6 | convolution fusion | flops 1812381696 | bytes 6389760 | tf_op jit(solution)/shard_map/dot_general | solution.py:23
  182.2 10.7 %tail.1 = (bf16[512,768]{1,0:T(8,128)(2,1)}, bf16[512,768]{1,0:T(8,128)(2,1)S(1)}, bf16[512,768]{1,0:T(8,128)(2,1)}, bf16[528,768]{1,0:T(8,128)(2,1)S(1)}, f32[8,768]{1,0:T(8,128)}, /*index=5*/f32[8,768]{1,0:T(8,128)}) custom-call(s32[1]{0:T(128)} %bitcast.refs_0_.me_ref, bf16[576,2048]{1,0:T(8,128)(2,1)} %attend_backward.3.refs_1_.g_ref, ...), custom_call_target="tpu_custom_call" | custom-call | flops 4000000000 | bytes 10000000 | tf_op jit(solution)/shard_map/tail/pallas_call | solution.py:83
  192.9 4.5 %collective-permute-done.36.refs_2_ = bf16[384,768]{1,0:T(8,128)(2,1)S(1)} collective-permute-done((bf16[384,768]{1,0:T(8,128)(2,1)S(1)}, bf16[384,768]{1,0:T(8,128)(2,1)S(1)}, u32[]{:S(2)}, u32[]{:S(2)}) %collective-permute-start.36) | collective-permute-done | bytes 589856 | tf_op jit(solution)/shard_map/ppermute | solution.py:1105
  208.2 4.9 %collective-permute-start.38 = (bf16[96,768]{1,0:T(8,128)(2,1)S(1)}, bf16[96,768]{1,0:T(8,128)(2,1)S(1)}, u32[]{:S(2)}, u32[]{:S(2)}) collective-permute-start(bf16[96,768]{1,0:T(8,128)(2,1)S(1)} %copy-done.20), channel_id=1, source_target_pairs={{0,16},{8,24},{16,0},{24,8},{1,17},{9,25},{17,1},{25,9},{2,18},{10... | collective-permute-start | bytes 442376 | tf_op jit(solution)/shard_map/ppermute | solution.py:987
  213.2 14.2 %collective-permute-done.41.b2_ref.refs_5_ = bf16[528,768]{1,0:T(8,128)(2,1)S(1)} collective-permute-done((bf16[528,768]{1,0:T(8,128)(2,1)S(1)}, bf16[528,768]{1,0:T(8,128)(2,1)S(1)}, u32[]{:S(2)}, u32[]{:S(2)}) %collective-permute-start.41) | collective-permute-done | bytes 811040 | tf_op jit(solution)/shard_map/ppermute | solution.py:959
  232.5 4.9 %collective-permute-start.47 = (bf16[112,768]{1,0:T(8,128)(2,1)}, bf16[112,768]{1,0:T(8,128)(2,1)S(1)}, u32[]{:S(2)}, u32[]{:S(2)}) collective-permute-start(bf16[112,768]{1,0:T(8,128)(2,1)} %second.1.rest_0_.refs_1_), channel_id=1, source_target_pairs={{0,24},{8,0},{16,8},{24,16},{1,25},{9,1},{17,9},{25,17},{2,26},{10... | collective-permute-start | bytes 516104 | tf_op jit(solution)/shard_map/ppermute | solution.py:987
  241.3 4.4 %place.2.refs_5_ = bf16[2048,768]{1,0:T(8,128)(2,1)} custom-call(s32[1]{0:T(128)} %bitcast.refs_0_.me_ref, bf16[512,768]{1,0:T(8,128)(2,1)S(1)} %copy-done.4, bf16[512,768]{1,0:T(8,128)(2,1)S(1)} %copy-done.2, bf16[512,768]{1,0:T(8,128)(2,1)S(1)} %collective-permute-done.34.refs_4_.p2_ref, bf16[512,768]{1,0:T(8,128)(2,1)} %collective-permute-done.35.p3_ref, ...), custom_call_target="tpu_custom_call" | custom-call | flops 1000000 | bytes 9000000 | tf_op jit(solution)/shard_map/place/pallas_call | solution.py:83
  247.0 25.1 %collective-permute-done.46.refs_3_ = bf16[112,768]{1,0:T(8,128)(2,1)S(1)} collective-permute-done((bf16[112,768]{1,0:T(8,128)(2,1)}, bf16[112,768]{1,0:T(8,128)(2,1)S(1)}, u32[]{:S(2)}, u32[]{:S(2)}) %collective-permute-start.46) | collective-permute-done | bytes 172064 | tf_op jit(solution)/shard_map/ppermute | solution.py:987
  275.8 5.2 %place.3 = f32[2048,768]{1,0:T(8,128)} custom-call(s32[1]{0:T(128)} %bitcast.refs_0_.me_ref, bf16[512,768]{1,0:T(8,128)(2,1)S(1)} %fence.23.p0_ref, bf16[512,768]{1,0:T(8,128)(2,1)} %collective-permute-done.43.p1_ref, bf16[512,768]{1,0:T(8,128)(2,1)S(1)} %fence.24.p2_ref, bf16[512,768]{1,0:T(8,128)(2,1)S(1)} %collective-permute-done.48.p3_ref, ...), custom_call_target="tpu_custom_call" | custom-call | flops 1000000 | bytes 9000000 | tf_op jit(solution)/shard_map/place/pallas_call | solution.py:83
  280.9 4.2 %slice_convert_fusion = (f32[768,768]{1,0:T(8,128)}, f32[768,768]{1,0:T(8,128)}) fusion(bf16[1536,768]{1,0:T(8,128)(2,1)} %all-gather.2.cloned.1.call-done), kind=kLoop, calls=%fused_computation.7 | loop fusion | flops 1179648 | bytes 7077888 | tf_op jit(solution)/shard_map/convert_element_type | solution.py:1111
  285.1 4.9 %collective-permute-done.49.other_ref = bf16[400,768]{1,0:T(8,128)(2,1)S(1)} collective-permute-done((bf16[400,768]{1,0:T(8,128)(2,1)}, bf16[400,768]{1,0:T(8,128)(2,1)S(1)}, u32[]{:S(2)}, u32[]{:S(2)}) %collective-permute-start.49) | collective-permute-done | bytes 614432 | tf_op jit(solution)/shard_map/ppermute | solution.py:1129
  (175 shorter events, 84.7 us)
Async XLA Ops:
  7.2 196.3 %reduce-scatter.2.cloned.1.call-start = ((), (), s32[]{:S(2)}) async-start(), calls=%async_computation.1 | async-start | bytes 2654208 | tf_op jit(solution)/shard_map/reduce_scatter | solution.py:1074
  7.2 15.8 %collective-permute-start.1 = (bf16[192,768]{1,0:T(8,128)(2,1)}, bf16[192,768]{1,0:T(8,128)(2,1)S(1)}, u32[]{:S(2)}, u32[]{:S(2)}) collective-permute-start(bf16[192,768]{1,0:T(8,128)(2,1)} %w0_ref.7), channel_id=1, source_target_pairs={{0,2},{2,0},{1,3},{3,1},{4,6},{6,4},{5,7},{7,5},{8,10},{10,8},{9,1... | collective-permute-start | bytes 884744 | tf_op jit(solution)/shard_map/ppermute | solution.py:959
  108.8 21.3 %collective-permute-start.24 = (bf16[192,256]{1,0:T(8,128)(2,1)S(1)}, bf16[192,256]{1,0:T(8,128)(2,1)S(1)}, u32[]{:S(2)}, u32[]{:S(2)}) collective-permute-start(bf16[192,256]{1,0:T(8,128)(2,1)S(1)} %get-tuple-element.149), channel_id=1, source_target_pairs={{0,1},{1,0},{2,3},{3,2},{4,5},{5,4},{6,7},{7,6},{8,9},{9,8},{10,11... | collective-permute-start | bytes 294920 | tf_op jit(solution)/shard_map/ppermute | solution.py:955
  110.3 18.0 %collective-permute-start.27 = (bf16[512,768]{1,0:T(8,128)(2,1)}, bf16[512,768]{1,0:T(8,128)(2,1)}, u32[]{:S(2)}, u32[]{:S(2)}) collective-permute-start(bf16[512,768]{1,0:T(8,128)(2,1)} %fence.16), channel_id=1, source_target_pairs={{0,1},{1,0},{2,3},{3,2},{4,5},{5,4},{6,7},{7,6},{8,9},{9,8},{10,11... | collective-permute-start | bytes 2359304 | tf_op jit(solution)/shard_map/ppermute | solution.py:955
  110.5 21.8 %collective-permute-start.28 = (bf16[512,768]{1,0:T(8,128)(2,1)}, bf16[512,768]{1,0:T(8,128)(2,1)S(1)}, u32[]{:S(2)}, u32[]{:S(2)}) collective-permute-start(bf16[512,768]{1,0:T(8,128)(2,1)} %fence.18), channel_id=1, source_target_pairs={{0,1},{1,0},{2,3},{3,2},{4,5},{5,4},{6,7},{7,6},{8,9},{9,8},{10,11... | collective-permute-start | bytes 2359304 | tf_op jit(solution)/shard_map/ppermute | solution.py:955
  117.4 163.5 %all-gather.2.cloned.1.call-start = ((), (), s32[]{:S(2)}) async-start(), calls=%async_computation.2 | async-start | bytes 2654208 | tf_op jit(solution)/shard_map/all_gather | solution.py:1110
  128.2 21.0 %collective-permute-start.20 = (bf16[192,256]{1,0:T(8,128)(2,1)S(1)}, bf16[192,256]{1,0:T(8,128)(2,1)S(1)}, u32[]{:S(2)}, u32[]{:S(2)}) collective-permute-start(bf16[192,256]{1,0:T(8,128)(2,1)S(1)} %get-tuple-element.142), channel_id=1, source_target_pairs={{0,1},{1,0},{2,3},{3,2},{4,5},{5,4},{6,7},{7,6},{8,9},{9,8},{10,11... | collective-permute-start | bytes 294920 | tf_op jit(solution)/shard_map/ppermute | solution.py:955
  130.1 19.8 %collective-permute-start.21 = (bf16[192,256]{1,0:T(8,128)(2,1)S(1)}, bf16[192,256]{1,0:T(8,128)(2,1)S(1)}, u32[]{:S(2)}, u32[]{:S(2)}) collective-permute-start(bf16[192,256]{1,0:T(8,128)(2,1)S(1)} %get-tuple-element.143), channel_id=1, source_target_pairs={{0,2},{2,0},{1,3},{3,1},{4,6},{6,4},{5,7},{7,5},{8,10},{10,8},{9,1... | collective-permute-start | bytes 294920 | tf_op jit(solution)/shard_map/ppermute | solution.py:959
  131.8 22.1 %collective-permute-start.29 = (bf16[192,768]{1,0:T(8,128)(2,1)S(1)}, bf16[192,768]{1,0:T(8,128)(2,1)S(1)}, u32[]{:S(2)}, u32[]{:S(2)}) collective-permute-start(bf16[192,768]{1,0:T(8,128)(2,1)S(1)} %get-tuple-element.163), channel_id=1, source_target_pairs={{0,1},{1,0},{2,3},{3,2},{4,5},{5,4},{6,7},{7,6},{8,9},{9,8},{10,11... | collective-permute-start | bytes 884744 | tf_op jit(solution)/shard_map/ppermute | solution.py:955
  132.3 21.6 %collective-permute-start.31 = (bf16[512,768]{1,0:T(8,128)(2,1)S(1)}, bf16[512,768]{1,0:T(8,128)(2,1)}, u32[]{:S(2)}, u32[]{:S(2)}) collective-permute-start(bf16[512,768]{1,0:T(8,128)(2,1)S(1)} %fence.17.refs_13_), channel_id=1, source_target_pairs={{0,2},{2,0},{1,3},{3,1},{4,6},{6,4},{5,7},{7,5},{8,10},{10,8},{9,1... | collective-permute-start | bytes 2359304 | tf_op jit(solution)/shard_map/ppermute | solution.py:959
  149.2 21.0 %collective-permute-start.32 = (bf16[192,768]{1,0:T(8,128)(2,1)S(1)}, bf16[192,768]{1,0:T(8,128)(2,1)S(1)}, u32[]{:S(2)}, u32[]{:S(2)}) collective-permute-start(bf16[192,768]{1,0:T(8,128)(2,1)S(1)} %add_convert_fusion.4.refs_17_), channel_id=1, source_target_pairs={{0,2},{2,0},{1,3},{3,1},{4,6},{6,4},{5,7},{7,5},{8,10},{10,8},{9,1... | collective-permute-start | bytes 884744 | tf_op jit(solution)/shard_map/ppermute | solution.py:959
  179.7 20.4 %collective-permute-start.34 = (bf16[512,768]{1,0:T(8,128)(2,1)S(1)}, bf16[512,768]{1,0:T(8,128)(2,1)S(1)}, u32[]{:S(2)}, u32[]{:S(2)}) collective-permute-start(bf16[512,768]{1,0:T(8,128)(2,1)S(1)} %fusion.3.p0_ref), channel_id=1, source_target_pairs={{0,2},{2,0},{1,3},{3,1},{4,6},{6,4},{5,7},{7,5},{8,10},{10,8},{9,1... | collective-permute-start | bytes 2359304 | tf_op jit(solution)/shard_map/ppermute | solution.py:959
  180.2 20.0 %collective-permute-start.33 = (bf16[512,768]{1,0:T(8,128)(2,1)S(1)}, bf16[512,768]{1,0:T(8,128)(2,1)S(1)}, u32[]{:S(2)}, u32[]{:S(2)}) collective-permute-start(bf16[512,768]{1,0:T(8,128)(2,1)S(1)} %fusion.3.p0_ref), channel_id=1, source_target_pairs={{0,1},{1,0},{2,3},{3,2},{4,5},{5,4},{6,7},{7,6},{8,9},{9,8},{10,11... | collective-permute-start | bytes 2359304 | tf_op jit(solution)/shard_map/ppermute | solution.py:955
  182.2 15.2 %collective-permute-start.36 = (bf16[384,768]{1,0:T(8,128)(2,1)S(1)}, bf16[384,768]{1,0:T(8,128)(2,1)S(1)}, u32[]{:S(2)}, u32[]{:S(2)}) collective-permute-start(bf16[384,768]{1,0:T(8,128)(2,1)S(1)} %copy-done.16), channel_id=1, source_target_pairs={{0,4},{4,0},{1,5},{5,1},{2,6},{6,2},{3,7},{7,3},{8,12},{12,8},{9,1... | collective-permute-start | bytes 1769480 | tf_op jit(solution)/shard_map/ppermute | solution.py:1105
  207.3 20.2 %collective-permute-start.41 = (bf16[528,768]{1,0:T(8,128)(2,1)S(1)}, bf16[528,768]{1,0:T(8,128)(2,1)S(1)}, u32[]{:S(2)}, u32[]{:S(2)}) collective-permute-start(bf16[528,768]{1,0:T(8,128)(2,1)S(1)} %chip_sum.1.refs_4_), channel_id=1, source_target_pairs={{0,2},{2,0},{1,3},{3,1},{4,6},{6,4},{5,7},{7,5},{8,10},{10,8},{9,1... | collective-permute-start | bytes 2433032 | tf_op jit(solution)/shard_map/ppermute | solution.py:959
  207.5 22.9 %collective-permute-start.37 = (bf16[96,768]{1,0:T(8,128)(2,1)S(1)}, bf16[96,768]{1,0:T(8,128)(2,1)S(1)}, u32[]{:S(2)}, u32[]{:S(2)}) collective-permute-start(bf16[96,768]{1,0:T(8,128)(2,1)S(1)} %copy-done.21), channel_id=1, source_target_pairs={{0,8},{8,16},{16,24},{24,0},{1,9},{9,17},{17,25},{25,1},{2,10},{10... | collective-permute-start | bytes 442376 | tf_op jit(solution)/shard_map/ppermute | solution.py:987
  208.2 22.2 %collective-permute-start.38 = (bf16[96,768]{1,0:T(8,128)(2,1)S(1)}, bf16[96,768]{1,0:T(8,128)(2,1)S(1)}, u32[]{:S(2)}, u32[]{:S(2)}) collective-permute-start(bf16[96,768]{1,0:T(8,128)(2,1)S(1)} %copy-done.20), channel_id=1, source_target_pairs={{0,16},{8,24},{16,0},{24,8},{1,17},{9,25},{17,1},{25,9},{2,18},{10... | collective-permute-start | bytes 442376 | tf_op jit(solution)/shard_map/ppermute | solution.py:987
  213.1 17.3 %collective-permute-start.39 = (bf16[96,768]{1,0:T(8,128)(2,1)S(1)}, bf16[96,768]{1,0:T(8,128)(2,1)S(1)}, u32[]{:S(2)}, u32[]{:S(2)}) collective-permute-start(bf16[96,768]{1,0:T(8,128)(2,1)S(1)} %copy-done.15), channel_id=1, source_target_pairs={{0,24},{8,0},{16,8},{24,16},{1,25},{9,1},{17,9},{25,17},{2,26},{10... | collective-permute-start | bytes 442376 | tf_op jit(solution)/shard_map/ppermute | solution.py:987
  213.1 27.0 %collective-permute-start.35 = (bf16[512,768]{1,0:T(8,128)(2,1)S(1)}, bf16[512,768]{1,0:T(8,128)(2,1)}, u32[]{:S(2)}, u32[]{:S(2)}) collective-permute-start(bf16[512,768]{1,0:T(8,128)(2,1)S(1)} %collective-permute-done.34.refs_4_.p2_ref), channel_id=1, source_target_pairs={{0,1},{1,0},{2,3},{3,2},{4,5},{5,4},{6,7},{7,6},{8,9},{9,8},{10,11... | collective-permute-start | bytes 2359304 | tf_op jit(solution)/shard_map/ppermute | solution.py:955
  232.2 41.3 %collective-permute-start.44 = (bf16[512,768]{1,0:T(8,128)(2,1)S(1)}, bf16[512,768]{1,0:T(8,128)(2,1)S(1)}, u32[]{:S(2)}, u32[]{:S(2)}) collective-permute-start(bf16[512,768]{1,0:T(8,128)(2,1)S(1)} %fence.23.p0_ref), channel_id=1, source_target_pairs={{0,2},{2,0},{1,3},{3,1},{4,6},{6,4},{5,7},{7,5},{8,10},{10,8},{9,1... | collective-permute-start | bytes 2359304 | tf_op jit(solution)/shard_map/ppermute | solution.py:959
  237.4 34.6 %collective-permute-start.46 = (bf16[112,768]{1,0:T(8,128)(2,1)}, bf16[112,768]{1,0:T(8,128)(2,1)S(1)}, u32[]{:S(2)}, u32[]{:S(2)}) collective-permute-start(bf16[112,768]{1,0:T(8,128)(2,1)} %second.1.rest_0_.refs_1_), channel_id=1, source_target_pairs={{0,16},{8,24},{16,0},{24,8},{1,17},{9,25},{17,1},{25,9},{2,18},{10... | collective-permute-start | bytes 516104 | tf_op jit(solution)/shard_map/ppermute | solution.py:987
  240.1 31.9 %collective-permute-start.45 = (bf16[112,768]{1,0:T(8,128)(2,1)}, bf16[112,768]{1,0:T(8,128)(2,1)S(1)}, u32[]{:S(2)}, u32[]{:S(2)}) collective-permute-start(bf16[112,768]{1,0:T(8,128)(2,1)} %second.1.rest_0_.refs_1_), channel_id=1, source_target_pairs={{0,8},{8,16},{16,24},{24,0},{1,9},{9,17},{17,25},{25,1},{2,10},{10... | collective-permute-start | bytes 516104 | tf_op jit(solution)/shard_map/ppermute | solution.py:987
  240.1 33.3 %collective-permute-start.43 = (bf16[512,768]{1,0:T(8,128)(2,1)S(1)}, bf16[512,768]{1,0:T(8,128)(2,1)}, u32[]{:S(2)}, u32[]{:S(2)}) collective-permute-start(bf16[512,768]{1,0:T(8,128)(2,1)S(1)} %fence.23.p0_ref), channel_id=1, source_target_pairs={{0,1},{1,0},{2,3},{3,2},{4,5},{5,4},{6,7},{7,6},{8,9},{9,8},{10,11... | collective-permute-start | bytes 2359304 | tf_op jit(solution)/shard_map/ppermute | solution.py:955
  273.5 16.5 %collective-permute-start.49 = (bf16[400,768]{1,0:T(8,128)(2,1)}, bf16[400,768]{1,0:T(8,128)(2,1)S(1)}, u32[]{:S(2)}, u32[]{:S(2)}) collective-permute-start(bf16[400,768]{1,0:T(8,128)(2,1)} %third.1.refs_1_.rest_0_.mine_ref), channel_id=1, source_target_pairs={{0,4},{4,0},{1,5},{5,1},{2,6},{6,2},{3,7},{7,3},{8,12},{12,8},{9,1... | collective-permute-start | bytes 1843208 | tf_op jit(solution)/shard_map/ppermute | solution.py:1129
  (50 other events, 386.8 us)
Sparse Core Ops, SparseCore 0:
  117.5 70.1 reduce-scatter.1
  203.6 71.2 all-gather.1

commit v10 on v9

--- a/solution.py
+++ b/solution.py
@@ -546,7 +546,8 @@
 
 
 def back_body(me_ref, b0_ref, b1_ref, b2_ref, residual_ref, g_ref, vec_ref, w0_ref, w1_ref, w2_ref, w3_ref,
-              grad_ref, low_ref, a0_ref, a1_ref, a2_ref, a3_ref, sum_ref):
+              *rest):
+    grad_ref, low_ref, a0_ref, a1_ref, a2_ref, a3_ref, sum_ref = rest[-7:]
     grad_mid = b0_ref[...].astype(F32) + b1_ref[...].astype(F32) + b2_ref[...].astype(F32)
     normed, scale, _ = stats(residual_ref[...])
     upstream = g_ref[...].astype(F32)
@@ -560,21 +561,21 @@
         sum_ref[8 * n:8 * n + 8] = fold(value)
 
 
-def middle_back(part, me, sums, residual, cot, vectors, weights):
+def middle_back(part, me, sums, residual, cot, vectors, weights, after):
     features = cot.shape[1]
     piece = const((TILE, features))
     width = weights[0].shape[0]
     return kernel_call(
         back_body,
-        (me, *sums, residual, cot, vectors, *weights),
-        free_in=(2, 3),
+        (me, *sums, residual, cot, vectors, *weights, *after),
+        free_in=(2, 3) + tuple(range(11, 11 + len(after))),
         free_out=(3, 4, 5),
         grid_spec=pltpu.PrefetchScalarGridSpec(
             num_scalar_prefetch=1,
             grid=(1,),
             in_specs=[piece] * 4
             + [pl.BlockSpec((TILE, features), lambda i, m: (4 * part + m[0], 0)), const(vectors.shape)]
-            + [const(v.shape) for v in weights],
+            + [const(v.shape) for v in weights] + [pl.BlockSpec(memory_space=pl.ANY)] * len(after),
             out_specs=[piece, piece] + [const((width, TILE))] * 4 + [const((32, features))],
         ),
         out_shape=[shape_of(TILE, features, dtype=F32), shape_of(TILE, features)]
@@ -1055,27 +1056,28 @@
         me, [pieces[p][n] for p in parts for n in (0, 1)], cot, inner_weight, vectors, outer_weight
     )
     backs[0, 0], backs[0, 1], backs[1, 0], backs[1, 1] = b00, b01, b10, b11
-    sums, kept, gathered, far_sums = [near_sum], (), [], [b00]
+    sums, kept, gathered, far_sums, behind = [near_sum], (), [], [], b00
     for p in parts:
-        far = fence(pieces[p][2], far_sums[-1], space=pltpu.VMEM)
+        far = fence(pieces[p][2], behind, space=pltpu.VMEM)
         *kept, backs[p, 2], backs[p, 3], far_sum = feed_far(
             p, me, far, other_core(far), cot, inner_weight, vectors, outer_weight, kept
         )
+        behind = backs[p, 2]
         sums.append(far_sum)
         if p:
             backs[p, 3] = fence(backs[p, 3], gathered[-1][2], space=pltpu.VMEM)
+            feed_sum = feed_grad(kept[0], kept[1], near_grad, ())
+            backs[p, 2] = fence(backs[p, 2], feed_sum)
         summed, far_sum = gather_sum([backs[p, n] for n in range(4)])
         gathered.append(summed)
         far_sums.append(far_sum)
-    far_sums = far_sums[1:]
     left, right, *far_outs = kept
     outs += far_outs
-    feed_sum = feed_grad(left, right, near_grad, far_sums).reshape(-1, features)
-    feed_sum = lax.psum_scatter(feed_sum, DP, scatter_dimension=0, tiled=True)
+    feed_sum = lax.psum_scatter(feed_sum.reshape(-1, features), DP, scatter_dimension=0, tiled=True)
     grad_residuals, lows, grads_attended, inner_sums = [], [], [], []
     for p in parts:
         grad, low, a0, a1, a2, a3, vector = middle_back(
-            p, me, gathered[p], residuals[p], cot, vectors, output_weights
+            p, me, gathered[p], residuals[p], cot, vectors, output_weights, far_sums[p + 1:]
         )
         grad_residuals.append(grad)
         lows.append(low)
@@ -1106,9 +1108,9 @@
     back_own, back_near, back_far, back_across, apart, summed = tail(
         me, grads, wq, wk, wv, tokens, stat, inner_sums, sums, (send,)
     )
+    feed_sum = lax.all_gather(fence(feed_sum, send), DP, axis=0, tiled=True)
+    feed_sum = (feed_sum[:features].astype(F32), feed_sum[features:].astype(F32))
     quarter = sum_first(xz, keep, got, (near, far, apart))
-    feed_sum = lax.all_gather(fence(feed_sum, quarter[-1]), DP, axis=0, tiled=True)
-    feed_sum = (feed_sum[:features].astype(F32), feed_sum[features:].astype(F32))
     back_across = other_core(fence(back_across, quarter[-1], space=pltpu.VMEM))
     back_far = chip_sum(back_far, back_across, summed, ())
     back_there = other_chip(back_far)

time: 302 us -> 288 us (0.954)
  waiting for transfers between devices: 80.8 us -> 67.8 us
  starting transfers between devices: 35.5 us -> 43 us
  Pallas kernels: 145 us -> 138 us
    ppermute x6, waiting for transfers between devices: 26.3 us -> 9.59 us  [turned(): lax.ppermute(values, 'z', [(n, (n + way) % size) for n in range(size)])]
    reduce_scatter x1, waiting for transfers between devices: 0.01 us -> 10.4 us  [local(): lax.psum_scatter(feed_sum.reshape(-1, features), DP, scatter_dimension=0,...]
    pallas_call x24, Pallas kernels: 145 us -> 138 us  [kernel_call(): pl.pallas_call(body, out_shape=shapes if many else shapes[0], compiler_pa...]
    ppermute x14, waiting for transfers between devices: 31.3 us -> 26.2 us  [other_chip(): return lax.ppermute(value, 'y', SWAP)]
    ppermute x6, starting transfers between devices: 13.2 us -> 17.8 us  [turned(): lax.ppermute(values, 'z', [(n, (n + way) % size) for n in range(size)])]
    ppermute x24, waiting for transfers between devices: 8.64 us -> 5.33 us  [other_core(): return lax.ppermute(value, 'core', SWAP)]
  transfers between devices with their start and end apart: 52 -> 52, of which waited for: 17 -> 14; matrix products, arithmetic and copies ran while one was open for 6% -> 7% of each run, Pallas kernels for 42% -> 43%
where the time goes in v10:
time: 288 us; the launch traced here: 287 us
  Pallas kernels  138 us (48%)
  waiting for transfers between devices  67.8 us (24%)
  starting transfers between devices  43 us (15%)
  between operations  14.5 us (5%)
  other arithmetic  12.5 us (4%)
  local copies, waits for them, and re-layouts  6.36 us (2%)
  matrix products  4.79 us (2%)
    pallas_call x24, Pallas kernels, kernel_call(): pl.pallas_call(body, out_shape=shapes if many else shapes[0], compiler_pa...  138 us
    ppermute x14, waiting for transfers between devices, other_chip(): return lax.ppermute(value, 'y', SWAP)  26.2 us
    ppermute x6, starting transfers between devices, turned(): lax.ppermute(values, 'z', [(n, (n + way) % size) for n in range(size)])  17.8 us
    ppermute x14, starting transfers between devices, other_chip(): return lax.ppermute(value, 'y', SWAP)  12.3 us
    reduce_scatter x1, waiting for transfers between devices, local(): lax.psum_scatter(feed_sum.reshape(-1, features), DP, scatter_dimension=0,...  10.4 us
    ppermute x6, waiting for transfers between devices, turned(): lax.ppermute(values, 'z', [(n, (n + way) % size) for n in range(size)])  9.59 us
    ppermute x1, waiting for transfers between devices, local(): got = lax.ppermute(send, 'x', SWAP)  6.36 us
  transfers between devices with their start and end apart: 52, of which 14 were waited for; matrix products, arithmetic and copies ran while one was open for 7% of the time, Pallas kernels for 43%

profile of v10, /device:TPU:0, one launch (start us, length us, event | category | flops | bytes accessed | tf_op | source)
XLA Modules:
  0.0 286.6 jit_solution(4028952567517610217)
XLA Ops:
  12.5 10.6 %project.1 = (bf16[2048,768]{1,0:T(8,128)(2,1)}, bf16[3,128,2048]{2,1,0:T(8,128)(2,1)}, bf16[192,2048]{1,0:T(8,128)(2,1)}, bf16[3,80,2048]{2,1,0:T(8,128)(2,1)},...) custom-call(bf16[2048,768]{1,0:T(8,128)(2,1)} %bitcast.19, ...), custom_call_target="tpu_custom_call" | custom-call | flops 6000000000 | bytes 14000000 | tf_op jit(solution)/shard_map/project/pallas_call | solution.py:83
  23.1 9.8 %attend_forward.2 = (bf16[4,192,256]{2,1,0:T(8,128)(2,1)}, bf16[3,16,1024]{2,1,0:T(8,128)(2,1)}, bf16[192,256]{1,0:T(8,128)(2,1)}, bf16[192,256]{1,0:T(8,128)(2,...) custom-call(s32[1]{0:T(128)} %bitcast.refs_0_.me_ref, s32[1,2048]{1,0:T(1,128)S(1)} %copy-done.11, ...), custom_call_target="tpu_custom_call" | custom-call | flops 8999999488 | bytes 5000000 | tf_op jit(solution)/shard_map/attend_forward/pallas_call | solution.py:83
  35.7 7.7 %attend_forward.3 = (bf16[4,192,256]{2,1,0:T(8,128)(2,1)}, bf16[3,16,1024]{2,1,0:T(8,128)(2,1)}, bf16[192,256]{1,0:T(8,128)(2,1)}, bf16[192,256]{1,0:T(8,128)(2,...) custom-call(s32[1]{0:T(128)} %bitcast.refs_0_.me_ref, s32[1,2048]{1,0:T(1,128)S(1)} %copy-done.12, ...), custom_call_target="tpu_custom_call" | custom-call | flops 8999999488 | bytes 5000000 | tf_op jit(solution)/shard_map/attend_forward/pallas_call | solution.py:83
  54.9 13.0 %feed_near.1 = (bf16[512,768]{1,0:T(8,128)(2,1)}, bf16[512,768]{1,0:T(8,128)(2,1)}, bf16[256,768]{1,0:T(8,128)(2,1)}, bf16[256,768]{1,0:T(8,128)(2,1)S(1)}, bf16...) custom-call(s32[1]{0:T(128)} %bitcast.refs_0_.me_ref, ...), custom_call_target="tpu_custom_call" | custom-call | flops 15000000512 | bytes 12000000 | tf_op jit(solution)/shard_map/feed_near/pallas_call | solution.py:83
  69.7 6.5 %feed_far.2 = (bf16[2,1024,768]{2,1,0:T(8,128)(2,1)}, bf16[2,1024,768]{2,1,0:T(8,128)(2,1)}, bf16[512,768]{1,0:T(8,128)(2,1)}, bf16[512,768]{1,0:T(8,128)(2,1)},...) custom-call(s32[1]{0:T(128)} %bitcast.refs_0_.me_ref, ...), custom_call_target="tpu_custom_call" | custom-call | flops 5000000000 | bytes 8000000 | tf_op jit(solution)/shard_map/feed_far/pallas_call | solution.py:83
  81.9 6.7 %feed_far.3 = (bf16[2,1024,768]{2,1,0:T(8,128)(2,1)}, bf16[2,1024,768]{2,1,0:T(8,128)(2,1)}, bf16[512,768]{1,0:T(8,128)(2,1)}, bf16[512,768]{1,0:T(8,128)(2,1)},...) custom-call(s32[1]{0:T(128)} %bitcast.refs_0_.me_ref, ...), custom_call_target="tpu_custom_call", output_to_operand_aliasing={{0}: (7, {}), {1}: (8, {}), {2}: (9, {}), {3}: (10, {})} | custom-call | flops 5000000000 | bytes 8000000 | tf_op jit(solution)/shard_map/feed_far/pallas_call | solution.py:83
  88.5 3.7 %collective-permute-done.17.refs_1_.b2_ref = bf16[256,768]{1,0:T(8,128)(2,1)S(1)} collective-permute-done((bf16[256,768]{1,0:T(8,128)(2,1)S(1)}, bf16[256,768]{1,0:T(8,128)(2,1)S(1)}, u32[]{:S(2)}, u32[]{:S(2)}) %collective-permute-start.17) | collective-permute-done | bytes 393248 | tf_op jit(solution)/shard_map/ppermute | solution.py:960
  93.0 6.1 %feed_grad.1.refs_1_ = bf16[2,768,768]{2,1,0:T(8,128)(2,1)} custom-call(bf16[2,1024,768]{2,1,0:T(8,128)(2,1)} %get-tuple-element.139.left_ref, bf16[2,1024,768]{2,1,0:T(8,128)(2,1)} %get-tuple-element.140.right_ref, bf16[2,768,768]{2,1,0:T(8,128)(2,1)} %get-tuple-element.141.before_ref), custom_call_target="tpu_custom_call" | custom-call | flops 5000000000 | bytes 10000000 | tf_op jit(solution)/shard_map/feed_grad/pallas_call | solution.py:83
  103.2 3.7 %middle_back.3 = (f32[256,768]{1,0:T(8,128)}, bf16[256,768]{1,0:T(8,128)(2,1)}, bf16[192,256]{1,0:T(8,128)(2,1)}, bf16[192,256]{1,0:T(8,128)(2,1)S(1)}, bf16[192...) custom-call(s32[1]{0:T(128)} %bitcast.refs_0_.me_ref, ...), custom_call_target="tpu_custom_call" | custom-call | flops 2000000000 | bytes 4000000 | tf_op jit(solution)/shard_map/middle_back/pallas_call | solution.py:83
  108.5 5.1 %collective-permute-done.19.b2_ref = bf16[256,768]{1,0:T(8,128)(2,1)S(1)} collective-permute-done((bf16[256,768]{1,0:T(8,128)(2,1)}, bf16[256,768]{1,0:T(8,128)(2,1)S(1)}, u32[]{:S(2)}, u32[]{:S(2)}) %collective-permute-start.19) | collective-permute-done | bytes 393248 | tf_op jit(solution)/shard_map/ppermute | solution.py:960
  124.8 14.2 %attend_backward.2 = (bf16[192,1024]{1,0:T(8,128)(2,1)}, f32[192,2048]{1,0:T(8,128)}, f32[192,2048]{1,0:T(8,128)}) custom-call(s32[1]{0:T(128)} %bitcast.refs_0_.me_ref, s32[1,2048]{1,0:T(1,128)S(1)} %copy-done.12, s32[1,2048]{1,0:T(1,128)S(1)} %copy-done.12, bf16[3,128,2048]{2,1,0:T(8,128)(2,1)} %get-tuple-element.110.refs_3_, ...), custom_call_target="tpu_custom_call" | custom-call | flops 16000000000 | bytes 10000000 | tf_op jit(solution)/shard_map/attend_backward/pallas_call | solution.py:83
  141.7 4.0 %collective-permute-done.22.refs_12_ = bf16[192,256]{1,0:T(8,128)(2,1)S(1)} collective-permute-done((bf16[192,256]{1,0:T(8,128)(2,1)S(1)}, bf16[192,256]{1,0:T(8,128)(2,1)S(1)}, u32[]{:S(2)}, u32[]{:S(2)}) %collective-permute-start.22) | collective-permute-done | bytes 98336 | tf_op jit(solution)/shard_map/ppermute | solution.py:964
  145.7 12.1 %attend_backward.3.refs_1_.g_ref = bf16[576,2048]{1,0:T(8,128)(2,1)} custom-call(s32[1]{0:T(128)} %bitcast.refs_0_.me_ref, s32[1,2048]{1,0:T(1,128)S(1)} %copy-done.12, s32[1,2048]{1,0:T(1,128)S(1)} %copy-done.12, bf16[3,128,2048]{2,1,0:T(8,128)(2,1)} %get-tuple-element.110.refs_3_, bf16[3,16,1024]{2,1,0:T(8,128)(2,1)} %get-tuple-element.117.rest_0_.refs_4_, ...), custom_call_target="tpu_custom_call" | custom-call | flops 16000000000 | bytes 10000000 | tf_op jit(solution)/shard_map/attend_backward/pallas_call | solution.py:83
  158.9 4.8 %convolution_convert_fusion.g_ref = bf16[576,768]{1,0:T(8,128)(2,1)S(1)} fusion(bf16[576,2048]{1,0:T(8,128)(2,1)} %attend_backward.3.refs_1_.g_ref, bf16[2048,768]{1,0:T(8,128)(2,1)} %get-tuple-element.169), kind=kOutput, calls=%fused_computation.6 | convolution fusion | flops 1812381696 | bytes 6389760 | tf_op jit(solution)/shard_map/dot_general | solution.py:23
  165.4 10.4 %reduce-scatter.2.cloned.1.call-done.refs_0_ = bf16[192,768]{1,0:T(8,128)(2,1)} async-done(((bf16[1536,768]{1,0:T(8,128)(2,1)}), bf16[192,768]{1,0:T(8,128)(2,1)}) %reduce-scatter.2.cloned.1.call-update) | async-done | bytes 294928 | tf_op jit(solution)/shard_map/reduce_scatter | solution.py:1076
  181.2 10.7 %tail.1 = (bf16[512,768]{1,0:T(8,128)(2,1)}, bf16[512,768]{1,0:T(8,128)(2,1)S(1)}, bf16[512,768]{1,0:T(8,128)(2,1)}, bf16[528,768]{1,0:T(8,128)(2,1)S(1)}, f32[8,768]{1,0:T(8,128)}, /*index=5*/f32[8,768]{1,0:T(8,128)}) custom-call(s32[1]{0:T(128)} %bitcast.refs_0_.me_ref, bf16[576,2048]{1,0:T(8,128)(2,1)} %attend_backward.3.refs_1_.g_ref, ...), custom_call_target="tpu_custom_call" | custom-call | flops 4000000000 | bytes 10000000 | tf_op jit(solution)/shard_map/tail/pallas_call | solution.py:83
  191.9 6.4 %collective-permute-done.36.refs_2_ = bf16[384,768]{1,0:T(8,128)(2,1)S(1)} collective-permute-done((bf16[384,768]{1,0:T(8,128)(2,1)S(1)}, bf16[384,768]{1,0:T(8,128)(2,1)S(1)}, u32[]{:S(2)}, u32[]{:S(2)}) %collective-permute-start.36) | collective-permute-done | bytes 589856 | tf_op jit(solution)/shard_map/ppermute | solution.py:1107
  211.2 14.3 %collective-permute-done.41.b2_ref.refs_5_ = bf16[528,768]{1,0:T(8,128)(2,1)S(1)} collective-permute-done((bf16[528,768]{1,0:T(8,128)(2,1)S(1)}, bf16[528,768]{1,0:T(8,128)(2,1)S(1)}, u32[]{:S(2)}, u32[]{:S(2)}) %collective-permute-start.41) | collective-permute-done | bytes 811040 | tf_op jit(solution)/shard_map/ppermute | solution.py:960
  230.8 11.2 %collective-permute-start.47 = (bf16[112,768]{1,0:T(8,128)(2,1)}, bf16[112,768]{1,0:T(8,128)(2,1)S(1)}, u32[]{:S(2)}, u32[]{:S(2)}) collective-permute-start(bf16[112,768]{1,0:T(8,128)(2,1)} %second.1.rest_0_.refs_1_), channel_id=1, source_target_pairs={{0,24},{8,0},{16,8},{24,16},{1,25},{9,1},{17,9},{25,17},{2,26},{10... | collective-permute-start | bytes 516104 | tf_op jit(solution)/shard_map/ppermute | solution.py:988
  244.6 4.4 %place.2.refs_5_ = bf16[2048,768]{1,0:T(8,128)(2,1)} custom-call(s32[1]{0:T(128)} %bitcast.refs_0_.me_ref, bf16[512,768]{1,0:T(8,128)(2,1)S(1)} %copy-done.3, bf16[512,768]{1,0:T(8,128)(2,1)S(1)} %copy-done.1, bf16[512,768]{1,0:T(8,128)(2,1)S(1)} %collective-permute-done.34.refs_4_.p2_ref, bf16[512,768]{1,0:T(8,128)(2,1)} %collective-permute-done.35.p3_ref, ...), custom_call_target="tpu_custom_call" | custom-call | flops 1000000 | bytes 9000000 | tf_op jit(solution)/shard_map/place/pallas_call | solution.py:83
  249.0 9.6 %collective-permute-done.46.refs_3_ = bf16[112,768]{1,0:T(8,128)(2,1)S(1)} collective-permute-done((bf16[112,768]{1,0:T(8,128)(2,1)}, bf16[112,768]{1,0:T(8,128)(2,1)S(1)}, u32[]{:S(2)}, u32[]{:S(2)}) %collective-permute-start.46) | collective-permute-done | bytes 172064 | tf_op jit(solution)/shard_map/ppermute | solution.py:988
  262.3 5.2 %place.3 = f32[2048,768]{1,0:T(8,128)} custom-call(s32[1]{0:T(128)} %bitcast.refs_0_.me_ref, bf16[512,768]{1,0:T(8,128)(2,1)S(1)} %fence.25.p0_ref, bf16[512,768]{1,0:T(8,128)(2,1)} %collective-permute-done.43.p1_ref, bf16[512,768]{1,0:T(8,128)(2,1)S(1)} %fence.26.p2_ref, bf16[512,768]{1,0:T(8,128)(2,1)S(1)} %collective-permute-done.48.p3_ref, ...), custom_call_target="tpu_custom_call" | custom-call | flops 1000000 | bytes 9000000 | tf_op jit(solution)/shard_map/place/pallas_call | solution.py:83
  267.5 4.2 %slice_convert_fusion = (f32[768,768]{1,0:T(8,128)}, f32[768,768]{1,0:T(8,128)}) fusion(bf16[1536,768]{1,0:T(8,128)(2,1)} %all-gather.2.cloned.1.call-done), kind=kLoop, calls=%fused_computation.7 | loop fusion | flops 1179648 | bytes 7077888 | tf_op jit(solution)/shard_map/convert_element_type | solution.py:1112
  271.6 4.9 %collective-permute-done.49.other_ref = bf16[400,768]{1,0:T(8,128)(2,1)S(1)} collective-permute-done((bf16[400,768]{1,0:T(8,128)(2,1)}, bf16[400,768]{1,0:T(8,128)(2,1)S(1)}, u32[]{:S(2)}, u32[]{:S(2)}) %collective-permute-start.49) | collective-permute-done | bytes 614432 | tf_op jit(solution)/shard_map/ppermute | solution.py:1131
  (178 shorter events, 83.1 us)
Async XLA Ops:
  7.2 168.6 %reduce-scatter.2.cloned.1.call-start = ((), (), s32[]{:S(2)}) async-start(), calls=%async_computation.1 | async-start | bytes 2654208 | tf_op jit(solution)/shard_map/reduce_scatter | solution.py:1076
  79.5 23.1 %collective-permute-start.23 = (bf16[256,768]{1,0:T(8,128)(2,1)S(1)}, bf16[256,768]{1,0:T(8,128)(2,1)S(1)}, u32[]{:S(2)}, u32[]{:S(2)}) collective-permute-start(bf16[256,768]{1,0:T(8,128)(2,1)S(1)} %get-tuple-element.150), channel_id=1, source_target_pairs={{0,1},{1,0},{2,3},{3,2},{4,5},{5,4},{6,7},{7,6},{8,9},{9,8},{10,11... | collective-permute-start | bytes 1179656 | tf_op jit(solution)/shard_map/ppermute | solution.py:956
  101.0 19.1 %collective-permute-start.27 = (bf16[512,768]{1,0:T(8,128)(2,1)}, bf16[512,768]{1,0:T(8,128)(2,1)}, u32[]{:S(2)}, u32[]{:S(2)}) collective-permute-start(bf16[512,768]{1,0:T(8,128)(2,1)} %fence.18), channel_id=1, source_target_pairs={{0,1},{1,0},{2,3},{3,2},{4,5},{5,4},{6,7},{7,6},{8,9},{9,8},{10,11... | collective-permute-start | bytes 2359304 | tf_op jit(solution)/shard_map/ppermute | solution.py:956
  102.2 165.2 %all-gather.2.cloned.1.call-start = ((), (), s32[]{:S(2)}) async-start(), calls=%async_computation.2 | async-start | bytes 2654208 | tf_op jit(solution)/shard_map/all_gather | solution.py:1111
  102.3 21.8 %collective-permute-start.28 = (bf16[512,768]{1,0:T(8,128)(2,1)}, bf16[512,768]{1,0:T(8,128)(2,1)S(1)}, u32[]{:S(2)}, u32[]{:S(2)}) collective-permute-start(bf16[512,768]{1,0:T(8,128)(2,1)} %fence.20), channel_id=1, source_target_pairs={{0,1},{1,0},{2,3},{3,2},{4,5},{5,4},{6,7},{7,6},{8,9},{9,8},{10,11... | collective-permute-start | bytes 2359304 | tf_op jit(solution)/shard_map/ppermute | solution.py:956
  107.1 16.5 %collective-permute-start.25 = (bf16[192,256]{1,0:T(8,128)(2,1)S(1)}, bf16[192,256]{1,0:T(8,128)(2,1)S(1)}, u32[]{:S(2)}, u32[]{:S(2)}) collective-permute-start(bf16[192,256]{1,0:T(8,128)(2,1)S(1)} %get-tuple-element.153), channel_id=1, source_target_pairs={{0,2},{2,0},{1,3},{3,1},{4,6},{6,4},{5,7},{7,5},{8,10},{10,8},{9,1... | collective-permute-start | bytes 294920 | tf_op jit(solution)/shard_map/ppermute | solution.py:960
  120.1 20.9 %collective-permute-start.20 = (bf16[192,256]{1,0:T(8,128)(2,1)S(1)}, bf16[192,256]{1,0:T(8,128)(2,1)S(1)}, u32[]{:S(2)}, u32[]{:S(2)}) collective-permute-start(bf16[192,256]{1,0:T(8,128)(2,1)S(1)} %get-tuple-element.145), channel_id=1, source_target_pairs={{0,1},{1,0},{2,3},{3,2},{4,5},{5,4},{6,7},{7,6},{8,9},{9,8},{10,11... | collective-permute-start | bytes 294920 | tf_op jit(solution)/shard_map/ppermute | solution.py:956
  122.1 19.6 %collective-permute-start.21 = (bf16[192,256]{1,0:T(8,128)(2,1)S(1)}, bf16[192,256]{1,0:T(8,128)(2,1)S(1)}, u32[]{:S(2)}, u32[]{:S(2)}) collective-permute-start(bf16[192,256]{1,0:T(8,128)(2,1)S(1)} %get-tuple-element.146), channel_id=1, source_target_pairs={{0,2},{2,0},{1,3},{3,1},{4,6},{6,4},{5,7},{7,5},{8,10},{10,8},{9,1... | collective-permute-start | bytes 294920 | tf_op jit(solution)/shard_map/ppermute | solution.py:960
  123.6 22.1 %collective-permute-start.29 = (bf16[192,768]{1,0:T(8,128)(2,1)S(1)}, bf16[192,768]{1,0:T(8,128)(2,1)S(1)}, u32[]{:S(2)}, u32[]{:S(2)}) collective-permute-start(bf16[192,768]{1,0:T(8,128)(2,1)S(1)} %get-tuple-element.166), channel_id=1, source_target_pairs={{0,1},{1,0},{2,3},{3,2},{4,5},{5,4},{6,7},{7,6},{8,9},{9,8},{10,11... | collective-permute-start | bytes 884744 | tf_op jit(solution)/shard_map/ppermute | solution.py:956
  124.1 21.6 %collective-permute-start.31 = (bf16[512,768]{1,0:T(8,128)(2,1)S(1)}, bf16[512,768]{1,0:T(8,128)(2,1)}, u32[]{:S(2)}, u32[]{:S(2)}) collective-permute-start(bf16[512,768]{1,0:T(8,128)(2,1)S(1)} %fence.19.refs_13_), channel_id=1, source_target_pairs={{0,2},{2,0},{1,3},{3,1},{4,6},{6,4},{5,7},{7,5},{8,10},{10,8},{9,1... | collective-permute-start | bytes 2359304 | tf_op jit(solution)/shard_map/ppermute | solution.py:960
  141.0 16.8 %collective-permute-start.32 = (bf16[192,768]{1,0:T(8,128)(2,1)S(1)}, bf16[192,768]{1,0:T(8,128)(2,1)S(1)}, u32[]{:S(2)}, u32[]{:S(2)}) collective-permute-start(bf16[192,768]{1,0:T(8,128)(2,1)S(1)} %add_convert_fusion.4.refs_17_), channel_id=1, source_target_pairs={{0,2},{2,0},{1,3},{3,1},{4,6},{6,4},{5,7},{7,5},{8,10},{10,8},{9,1... | collective-permute-start | bytes 884744 | tf_op jit(solution)/shard_map/ppermute | solution.py:960
  177.8 20.4 %collective-permute-start.34 = (bf16[512,768]{1,0:T(8,128)(2,1)S(1)}, bf16[512,768]{1,0:T(8,128)(2,1)S(1)}, u32[]{:S(2)}, u32[]{:S(2)}) collective-permute-start(bf16[512,768]{1,0:T(8,128)(2,1)S(1)} %fusion.3.p0_ref), channel_id=1, source_target_pairs={{0,2},{2,0},{1,3},{3,1},{4,6},{6,4},{5,7},{7,5},{8,10},{10,8},{9,1... | collective-permute-start | bytes 2359304 | tf_op jit(solution)/shard_map/ppermute | solution.py:960
  179.3 18.9 %collective-permute-start.33 = (bf16[512,768]{1,0:T(8,128)(2,1)S(1)}, bf16[512,768]{1,0:T(8,128)(2,1)S(1)}, u32[]{:S(2)}, u32[]{:S(2)}) collective-permute-start(bf16[512,768]{1,0:T(8,128)(2,1)S(1)} %fusion.3.p0_ref), channel_id=1, source_target_pairs={{0,1},{1,0},{2,3},{3,2},{4,5},{5,4},{6,7},{7,6},{8,9},{9,8},{10,11... | collective-permute-start | bytes 2359304 | tf_op jit(solution)/shard_map/ppermute | solution.py:956
  179.3 18.9 %collective-permute-start.36 = (bf16[384,768]{1,0:T(8,128)(2,1)S(1)}, bf16[384,768]{1,0:T(8,128)(2,1)S(1)}, u32[]{:S(2)}, u32[]{:S(2)}) collective-permute-start(bf16[384,768]{1,0:T(8,128)(2,1)S(1)} %copy-done.14), channel_id=1, source_target_pairs={{0,4},{4,0},{1,5},{5,1},{2,6},{6,2},{3,7},{7,3},{8,12},{12,8},{9,1... | collective-permute-start | bytes 1769480 | tf_op jit(solution)/shard_map/ppermute | solution.py:1107
  205.3 20.2 %collective-permute-start.41 = (bf16[528,768]{1,0:T(8,128)(2,1)S(1)}, bf16[528,768]{1,0:T(8,128)(2,1)S(1)}, u32[]{:S(2)}, u32[]{:S(2)}) collective-permute-start(bf16[528,768]{1,0:T(8,128)(2,1)S(1)} %chip_sum.1.refs_4_), channel_id=1, source_target_pairs={{0,2},{2,0},{1,3},{3,1},{4,6},{6,4},{5,7},{7,5},{8,10},{10,8},{9,1... | collective-permute-start | bytes 2433032 | tf_op jit(solution)/shard_map/ppermute | solution.py:960
  206.0 22.6 %collective-permute-start.37 = (bf16[96,768]{1,0:T(8,128)(2,1)S(1)}, bf16[96,768]{1,0:T(8,128)(2,1)S(1)}, u32[]{:S(2)}, u32[]{:S(2)}) collective-permute-start(bf16[96,768]{1,0:T(8,128)(2,1)S(1)} %copy-done.22), channel_id=1, source_target_pairs={{0,8},{8,16},{16,24},{24,0},{1,9},{9,17},{17,25},{25,1},{2,10},{10... | collective-permute-start | bytes 442376 | tf_op jit(solution)/shard_map/ppermute | solution.py:988
  206.9 21.6 %collective-permute-start.38 = (bf16[96,768]{1,0:T(8,128)(2,1)S(1)}, bf16[96,768]{1,0:T(8,128)(2,1)S(1)}, u32[]{:S(2)}, u32[]{:S(2)}) collective-permute-start(bf16[96,768]{1,0:T(8,128)(2,1)S(1)} %copy-done.21), channel_id=1, source_target_pairs={{0,16},{8,24},{16,0},{24,8},{1,17},{9,25},{17,1},{25,9},{2,18},{10... | collective-permute-start | bytes 442376 | tf_op jit(solution)/shard_map/ppermute | solution.py:988
  208.4 20.1 %collective-permute-start.39 = (bf16[96,768]{1,0:T(8,128)(2,1)S(1)}, bf16[96,768]{1,0:T(8,128)(2,1)S(1)}, u32[]{:S(2)}, u32[]{:S(2)}) collective-permute-start(bf16[96,768]{1,0:T(8,128)(2,1)S(1)} %copy-done.18), channel_id=1, source_target_pairs={{0,24},{8,0},{16,8},{24,16},{1,25},{9,1},{17,9},{25,17},{2,26},{10... | collective-permute-start | bytes 442376 | tf_op jit(solution)/shard_map/ppermute | solution.py:988
  211.2 32.3 %collective-permute-start.35 = (bf16[512,768]{1,0:T(8,128)(2,1)S(1)}, bf16[512,768]{1,0:T(8,128)(2,1)}, u32[]{:S(2)}, u32[]{:S(2)}) collective-permute-start(bf16[512,768]{1,0:T(8,128)(2,1)S(1)} %collective-permute-done.34.refs_4_.p2_ref), channel_id=1, source_target_pairs={{0,1},{1,0},{2,3},{3,2},{4,5},{5,4},{6,7},{7,6},{8,9},{9,8},{10,11... | collective-permute-start | bytes 2359304 | tf_op jit(solution)/shard_map/ppermute | solution.py:956
  230.3 29.7 %collective-permute-start.44 = (bf16[512,768]{1,0:T(8,128)(2,1)S(1)}, bf16[512,768]{1,0:T(8,128)(2,1)S(1)}, u32[]{:S(2)}, u32[]{:S(2)}) collective-permute-start(bf16[512,768]{1,0:T(8,128)(2,1)S(1)} %fence.25.p0_ref), channel_id=1, source_target_pairs={{0,2},{2,0},{1,3},{3,1},{4,6},{6,4},{5,7},{7,5},{8,10},{10,8},{9,1... | collective-permute-start | bytes 2359304 | tf_op jit(solution)/shard_map/ppermute | solution.py:960
  230.8 18.1 %collective-permute-start.47 = (bf16[112,768]{1,0:T(8,128)(2,1)}, bf16[112,768]{1,0:T(8,128)(2,1)S(1)}, u32[]{:S(2)}, u32[]{:S(2)}) collective-permute-start(bf16[112,768]{1,0:T(8,128)(2,1)} %second.1.rest_0_.refs_1_), channel_id=1, source_target_pairs={{0,24},{8,0},{16,8},{24,16},{1,25},{9,1},{17,9},{25,17},{2,26},{10... | collective-permute-start | bytes 516104 | tf_op jit(solution)/shard_map/ppermute | solution.py:988
  242.0 16.6 %collective-permute-start.46 = (bf16[112,768]{1,0:T(8,128)(2,1)}, bf16[112,768]{1,0:T(8,128)(2,1)S(1)}, u32[]{:S(2)}, u32[]{:S(2)}) collective-permute-start(bf16[112,768]{1,0:T(8,128)(2,1)} %second.1.rest_0_.refs_1_), channel_id=1, source_target_pairs={{0,16},{8,24},{16,0},{24,8},{1,17},{9,25},{17,1},{25,9},{2,18},{10... | collective-permute-start | bytes 516104 | tf_op jit(solution)/shard_map/ppermute | solution.py:988
  243.4 18.1 %collective-permute-start.43 = (bf16[512,768]{1,0:T(8,128)(2,1)S(1)}, bf16[512,768]{1,0:T(8,128)(2,1)}, u32[]{:S(2)}, u32[]{:S(2)}) collective-permute-start(bf16[512,768]{1,0:T(8,128)(2,1)S(1)} %fence.25.p0_ref), channel_id=1, source_target_pairs={{0,1},{1,0},{2,3},{3,2},{4,5},{5,4},{6,7},{7,6},{8,9},{9,8},{10,11... | collective-permute-start | bytes 2359304 | tf_op jit(solution)/shard_map/ppermute | solution.py:956
  260.0 16.5 %collective-permute-start.49 = (bf16[400,768]{1,0:T(8,128)(2,1)}, bf16[400,768]{1,0:T(8,128)(2,1)S(1)}, u32[]{:S(2)}, u32[]{:S(2)}) collective-permute-start(bf16[400,768]{1,0:T(8,128)(2,1)} %third.1.refs_1_.rest_0_.mine_ref), channel_id=1, source_target_pairs={{0,4},{4,0},{1,5},{5,1},{2,6},{6,2},{3,7},{7,3},{8,12},{12,8},{9,1... | collective-permute-start | bytes 1843208 | tf_op jit(solution)/shard_map/ppermute | solution.py:1131
  (51 other events, 415.4 us)
Sparse Core Ops, SparseCore 0:
  102.4 73.4 reduce-scatter.1
  178.0 64.2 all-gather.1

commit v11 on v10

--- a/solution.py
+++ b/solution.py
@@ -9,6 +9,7 @@
 HEAD = 64
 WIDE = 128
 TILE = 256
+LONG = 512
 PARTS = 2
 MASKED = 1e30
 SCALE = 1
@@ -125,20 +126,20 @@
     return kernel_call(
         project_body,
         (tokens, seg_row, vectors, wq, wk, wv),
-        grid=(length // TILE,),
+        grid=(length // LONG,),
         in_specs=[
-            pl.BlockSpec((TILE, features), lambda i: (i, 0)),
-            pl.BlockSpec((1, TILE), lambda i: (0, i)),
+            pl.BlockSpec((LONG, features), lambda i: (i, 0)),
+            pl.BlockSpec((1, LONG), lambda i: (0, i)),
             const(vectors.shape), const(wq.shape), const(wk.shape), const(wv.shape),
         ],
         out_specs=[
-            pl.BlockSpec((TILE, features), lambda i: (i, 0)),
-            pl.BlockSpec((heads, WIDE, TILE), lambda i: (0, 0, i)),
-            pl.BlockSpec((width, TILE), lambda i: (0, i)),
-            pl.BlockSpec((heads, HEAD + 16, TILE), lambda i: (0, 0, i)),
-            pl.BlockSpec((heads, TILE, WIDE), lambda i: (0, i, 0)),
-            pl.BlockSpec((heads, TILE, WIDE), lambda i: (0, i, 0)),
-            pl.BlockSpec((TILE, WIDE), lambda i: (i, 0)),
+            pl.BlockSpec((LONG, features), lambda i: (i, 0)),
+            pl.BlockSpec((heads, WIDE, LONG), lambda i: (0, 0, i)),
+            pl.BlockSpec((width, LONG), lambda i: (0, i)),
+            pl.BlockSpec((heads, HEAD + 16, LONG), lambda i: (0, 0, i)),
+            pl.BlockSpec((heads, LONG, WIDE), lambda i: (0, i, 0)),
+            pl.BlockSpec((heads, LONG, WIDE), lambda i: (0, i, 0)),
+            pl.BlockSpec((LONG, WIDE), lambda i: (i, 0)),
         ],
         out_shape=[
             shape_of(length, features),
@@ -162,11 +163,14 @@
     return before // TILE, (until + TILE - 1) // TILE
 
 
-def by_pairs(low, high, step, carry):
+def by_blocks(low, high, step, carry):
     keys = lambda kb: pl.ds(pl.multiple_of(kb * TILE, TILE), TILE)
-    pairs = (high - low) // 2
-    carry = lax.fori_loop(0, pairs, lambda n, c: step([keys(low + 2 * n), keys(low + 2 * n + 1)], c), carry)
-    return lax.fori_loop(low + 2 * pairs, high, lambda kb, c: step([keys(kb)], c), carry)
+    for many in (3, 2, 1):
+        rounds = (high - low) // many
+        run = lambda n, c, low=low, many=many: step([keys(low + many * n + k) for k in range(many)], c)
+        carry = lax.fori_loop(0, rounds, run, carry)
+        low = low + many * rounds
+    return carry
 
 
 def shifted(one_hot, pieces):
@@ -200,7 +204,7 @@
             acc_ref[h] = total
         return tuple(new_tops)
 
-    tops = by_pairs(low, high, step, (jnp.full((1, tile), -jnp.inf, F32),) * heads)
+    tops = by_blocks(low, high, step, (jnp.full((1, tile), -jnp.inf, F32),) * heads)
     for h in range(heads):
         total = acc_ref[h, HEAD:HEAD + 1, :]
         out_ref[0, h * HEAD:(h + 1) * HEAD, :] = (acc_ref[h, :HEAD, :] / total).astype(BF16)
@@ -309,7 +313,7 @@
             dq_ref[rows[h]] = total
         return carry
 
-    by_pairs(low, high, step, 0)
+    by_blocks(low, high, step, 0)
     dq = (dq_ref[...] * HEAD ** -0.5).astype(BF16)
     if part == 0:
         dq_out[...] = dq

time: 288 us -> 285 us (0.990)
  waiting for transfers between devices: 67.8 us -> 63.2 us
  Pallas kernels: 138 us -> 142 us
    reduce_scatter x1, waiting for transfers between devices: 10.4 us -> 2.25 us  [local(): lax.psum_scatter(feed_sum.reshape(-1, features), DP, scatter_dimension=0,...]
    pallas_call x24, Pallas kernels: 138 us -> 142 us  [kernel_call(): pl.pallas_call(body, out_shape=shapes if many else shapes[0], compiler_pa...]
  transfers between devices with their start and end apart: 52 -> 52, of which waited for: 14 -> 14; matrix products, arithmetic and copies ran while one was open for 7% -> 7% of each run, Pallas kernels for 43% -> 46%
where the time goes in v11:
time: 285 us; the launch traced here: 284 us
  Pallas kernels  142 us (50%)
  waiting for transfers between devices  63.2 us (22%)
  starting transfers between devices  40.7 us (14%)
  between operations  14.5 us (5%)
  other arithmetic  12.5 us (4%)
  local copies, waits for them, and re-layouts  6.36 us (2%)
  matrix products  4.6 us (2%)
    pallas_call x24, Pallas kernels, kernel_call(): pl.pallas_call(body, out_shape=shapes if many else shapes[0], compiler_pa...  142 us
    ppermute x14, waiting for transfers between devices, other_chip(): return lax.ppermute(value, 'y', SWAP)  27.1 us
    ppermute x6, starting transfers between devices, turned(): lax.ppermute(values, 'z', [(n, (n + way) % size) for n in range(size)])  17 us
    ppermute x14, starting transfers between devices, other_chip(): return lax.ppermute(value, 'y', SWAP)  12.5 us
    ppermute x6, waiting for transfers between devices, turned(): lax.ppermute(values, 'z', [(n, (n + way) % size) for n in range(size)])  9.65 us
    ppermute x1, waiting for transfers between devices, local(): got = lax.ppermute(send, 'x', SWAP)  7.45 us
    ppermute x4, waiting for transfers between devices, crosswise(): return lax.ppermute(value, MP, [(n, n ^ 3) for n in range(4)])  6.24 us
  transfers between devices with their start and end apart: 52, of which 14 were waited for; matrix products, arithmetic and copies ran while one was open for 7% of the time, Pallas kernels for 46%

profile of v11, /device:TPU:0, one launch (start us, length us, event | category | flops | bytes accessed | tf_op | source)
XLA Modules:
  0.0 283.9 jit_solution(4651836367912549915)
XLA Ops:
  12.5 8.6 %project.1 = (bf16[2048,768]{1,0:T(8,128)(2,1)}, bf16[3,128,2048]{2,1,0:T(8,128)(2,1)}, bf16[192,2048]{1,0:T(8,128)(2,1)}, bf16[3,80,2048]{2,1,0:T(8,128)(2,1)},...) custom-call(bf16[2048,768]{1,0:T(8,128)(2,1)} %bitcast.19, ...), custom_call_target="tpu_custom_call" | custom-call | flops 6000000000 | bytes 14000000 | tf_op jit(solution)/shard_map/project/pallas_call | solution.py:84
  21.1 9.0 %attend_forward.2 = (bf16[4,192,256]{2,1,0:T(8,128)(2,1)}, bf16[3,16,1024]{2,1,0:T(8,128)(2,1)}, bf16[192,256]{1,0:T(8,128)(2,1)}, bf16[192,256]{1,0:T(8,128)(2,...) custom-call(s32[1]{0:T(128)} %bitcast.refs_0_.me_ref, s32[1,2048]{1,0:T(1,128)S(1)} %copy-done.11, ...), custom_call_target="tpu_custom_call" | custom-call | flops 8999999488 | bytes 5000000 | tf_op jit(solution)/shard_map/attend_forward/pallas_call | solution.py:84
  32.9 11.1 %attend_forward.3 = (bf16[4,192,256]{2,1,0:T(8,128)(2,1)}, bf16[3,16,1024]{2,1,0:T(8,128)(2,1)}, bf16[192,256]{1,0:T(8,128)(2,1)}, bf16[192,256]{1,0:T(8,128)(2,...) custom-call(s32[1]{0:T(128)} %bitcast.refs_0_.me_ref, s32[1,2048]{1,0:T(1,128)S(1)} %copy-done.12, ...), custom_call_target="tpu_custom_call" | custom-call | flops 8999999488 | bytes 5000000 | tf_op jit(solution)/shard_map/attend_forward/pallas_call | solution.py:84
  55.5 13.0 %feed_near.1 = (bf16[512,768]{1,0:T(8,128)(2,1)}, bf16[512,768]{1,0:T(8,128)(2,1)}, bf16[256,768]{1,0:T(8,128)(2,1)}, bf16[256,768]{1,0:T(8,128)(2,1)S(1)}, bf16...) custom-call(s32[1]{0:T(128)} %bitcast.refs_0_.me_ref, ...), custom_call_target="tpu_custom_call" | custom-call | flops 15000000512 | bytes 12000000 | tf_op jit(solution)/shard_map/feed_near/pallas_call | solution.py:84
  70.3 6.5 %feed_far.2 = (bf16[2,1024,768]{2,1,0:T(8,128)(2,1)}, bf16[2,1024,768]{2,1,0:T(8,128)(2,1)}, bf16[512,768]{1,0:T(8,128)(2,1)}, bf16[512,768]{1,0:T(8,128)(2,1)},...) custom-call(s32[1]{0:T(128)} %bitcast.refs_0_.me_ref, ...), custom_call_target="tpu_custom_call" | custom-call | flops 5000000000 | bytes 8000000 | tf_op jit(solution)/shard_map/feed_far/pallas_call | solution.py:84
  82.5 6.5 %feed_far.3 = (bf16[2,1024,768]{2,1,0:T(8,128)(2,1)}, bf16[2,1024,768]{2,1,0:T(8,128)(2,1)}, bf16[512,768]{1,0:T(8,128)(2,1)}, bf16[512,768]{1,0:T(8,128)(2,1)},...) custom-call(s32[1]{0:T(128)} %bitcast.refs_0_.me_ref, ...), custom_call_target="tpu_custom_call", output_to_operand_aliasing={{0}: (7, {}), {1}: (8, {}), {2}: (9, {}), {3}: (10, {})} | custom-call | flops 5000000000 | bytes 8000000 | tf_op jit(solution)/shard_map/feed_far/pallas_call | solution.py:84
  89.0 3.9 %collective-permute-done.17.refs_1_.b2_ref = bf16[256,768]{1,0:T(8,128)(2,1)S(1)} collective-permute-done((bf16[256,768]{1,0:T(8,128)(2,1)S(1)}, bf16[256,768]{1,0:T(8,128)(2,1)S(1)}, u32[]{:S(2)}, u32[]{:S(2)}) %collective-permute-start.17) | collective-permute-done | bytes 393248 | tf_op jit(solution)/shard_map/ppermute | solution.py:964
  93.6 6.1 %feed_grad.1.refs_1_ = bf16[2,768,768]{2,1,0:T(8,128)(2,1)} custom-call(bf16[2,1024,768]{2,1,0:T(8,128)(2,1)} %get-tuple-element.139.left_ref, bf16[2,1024,768]{2,1,0:T(8,128)(2,1)} %get-tuple-element.140.right_ref, bf16[2,768,768]{2,1,0:T(8,128)(2,1)} %get-tuple-element.141.before_ref), custom_call_target="tpu_custom_call" | custom-call | flops 5000000000 | bytes 10000000 | tf_op jit(solution)/shard_map/feed_grad/pallas_call | solution.py:84
  103.8 3.7 %middle_back.3 = (f32[256,768]{1,0:T(8,128)}, bf16[256,768]{1,0:T(8,128)(2,1)}, bf16[192,256]{1,0:T(8,128)(2,1)}, bf16[192,256]{1,0:T(8,128)(2,1)S(1)}, bf16[192...) custom-call(s32[1]{0:T(128)} %bitcast.refs_0_.me_ref, ...), custom_call_target="tpu_custom_call" | custom-call | flops 2000000000 | bytes 4000000 | tf_op jit(solution)/shard_map/middle_back/pallas_call | solution.py:84
  109.1 5.1 %collective-permute-done.19.b2_ref = bf16[256,768]{1,0:T(8,128)(2,1)S(1)} collective-permute-done((bf16[256,768]{1,0:T(8,128)(2,1)}, bf16[256,768]{1,0:T(8,128)(2,1)S(1)}, u32[]{:S(2)}, u32[]{:S(2)}) %collective-permute-start.19) | collective-permute-done | bytes 393248 | tf_op jit(solution)/shard_map/ppermute | solution.py:964
  114.2 3.6 %middle_back.2 = (f32[256,768]{1,0:T(8,128)}, bf16[256,768]{1,0:T(8,128)(2,1)}, bf16[192,256]{1,0:T(8,128)(2,1)}, bf16[192,256]{1,0:T(8,128)(2,1)S(1)}, bf16[192...) custom-call(s32[1]{0:T(128)} %bitcast.refs_0_.me_ref, ...), custom_call_target="tpu_custom_call" | custom-call | flops 2000000000 | bytes 4000000 | tf_op jit(solution)/shard_map/middle_back/pallas_call | solution.py:84
  125.4 13.1 %attend_backward.2 = (bf16[192,1024]{1,0:T(8,128)(2,1)}, f32[192,2048]{1,0:T(8,128)}, f32[192,2048]{1,0:T(8,128)}) custom-call(s32[1]{0:T(128)} %bitcast.refs_0_.me_ref, s32[1,2048]{1,0:T(1,128)S(1)} %copy-done.12, s32[1,2048]{1,0:T(1,128)S(1)} %copy-done.12, bf16[3,128,2048]{2,1,0:T(8,128)(2,1)} %get-tuple-element.110.refs_3_, ...), custom_call_target="tpu_custom_call" | custom-call | flops 16000000000 | bytes 10000000 | tf_op jit(solution)/shard_map/attend_backward/pallas_call | solution.py:84
  141.1 5.2 %collective-permute-done.22.refs_12_ = bf16[192,256]{1,0:T(8,128)(2,1)S(1)} collective-permute-done((bf16[192,256]{1,0:T(8,128)(2,1)S(1)}, bf16[192,256]{1,0:T(8,128)(2,1)S(1)}, u32[]{:S(2)}, u32[]{:S(2)}) %collective-permute-start.22) | collective-permute-done | bytes 98336 | tf_op jit(solution)/shard_map/ppermute | solution.py:968
  146.3 17.2 %attend_backward.3.refs_1_.g_ref = bf16[576,2048]{1,0:T(8,128)(2,1)} custom-call(s32[1]{0:T(128)} %bitcast.refs_0_.me_ref, s32[1,2048]{1,0:T(1,128)S(1)} %copy-done.12, s32[1,2048]{1,0:T(1,128)S(1)} %copy-done.12, bf16[3,128,2048]{2,1,0:T(8,128)(2,1)} %get-tuple-element.110.refs_3_, bf16[3,16,1024]{2,1,0:T(8,128)(2,1)} %get-tuple-element.117.rest_0_.refs_4_, ...), custom_call_target="tpu_custom_call" | custom-call | flops 16000000000 | bytes 10000000 | tf_op jit(solution)/shard_map/attend_backward/pallas_call | solution.py:84
  164.6 4.6 %convolution_convert_fusion.g_ref = bf16[576,768]{1,0:T(8,128)(2,1)S(1)} fusion(bf16[576,2048]{1,0:T(8,128)(2,1)} %attend_backward.3.refs_1_.g_ref, bf16[2048,768]{1,0:T(8,128)(2,1)} %get-tuple-element.169), kind=kOutput, calls=%fused_computation.6 | convolution fusion | flops 1812381696 | bytes 6389760 | tf_op jit(solution)/shard_map/dot_general | solution.py:24
  177.3 10.7 %tail.1 = (bf16[512,768]{1,0:T(8,128)(2,1)}, bf16[512,768]{1,0:T(8,128)(2,1)S(1)}, bf16[512,768]{1,0:T(8,128)(2,1)}, bf16[528,768]{1,0:T(8,128)(2,1)S(1)}, f32[8,768]{1,0:T(8,128)}, /*index=5*/f32[8,768]{1,0:T(8,128)}) custom-call(s32[1]{0:T(128)} %bitcast.refs_0_.me_ref, bf16[576,2048]{1,0:T(8,128)(2,1)} %attend_backward.3.refs_1_.g_ref, ...), custom_call_target="tpu_custom_call" | custom-call | flops 4000000000 | bytes 10000000 | tf_op jit(solution)/shard_map/tail/pallas_call | solution.py:84
  188.0 7.5 %collective-permute-done.36.refs_2_ = bf16[384,768]{1,0:T(8,128)(2,1)S(1)} collective-permute-done((bf16[384,768]{1,0:T(8,128)(2,1)S(1)}, bf16[384,768]{1,0:T(8,128)(2,1)S(1)}, u32[]{:S(2)}, u32[]{:S(2)}) %collective-permute-start.36) | collective-permute-done | bytes 589856 | tf_op jit(solution)/shard_map/ppermute | solution.py:1111
  207.7 15.1 %collective-permute-done.41.b2_ref.refs_5_ = bf16[528,768]{1,0:T(8,128)(2,1)S(1)} collective-permute-done((bf16[528,768]{1,0:T(8,128)(2,1)S(1)}, bf16[528,768]{1,0:T(8,128)(2,1)S(1)}, u32[]{:S(2)}, u32[]{:S(2)}) %collective-permute-start.41) | collective-permute-done | bytes 811040 | tf_op jit(solution)/shard_map/ppermute | solution.py:964
  228.1 11.0 %collective-permute-start.47 = (bf16[112,768]{1,0:T(8,128)(2,1)}, bf16[112,768]{1,0:T(8,128)(2,1)S(1)}, u32[]{:S(2)}, u32[]{:S(2)}) collective-permute-start(bf16[112,768]{1,0:T(8,128)(2,1)} %second.1.rest_0_.refs_1_), channel_id=1, source_target_pairs={{0,24},{8,0},{16,8},{24,16},{1,25},{9,1},{17,9},{25,17},{2,26},{10... | collective-permute-start | bytes 516104 | tf_op jit(solution)/shard_map/ppermute | solution.py:992
  241.9 4.4 %place.2.refs_5_ = bf16[2048,768]{1,0:T(8,128)(2,1)} custom-call(s32[1]{0:T(128)} %bitcast.refs_0_.me_ref, bf16[512,768]{1,0:T(8,128)(2,1)S(1)} %copy-done.3, bf16[512,768]{1,0:T(8,128)(2,1)S(1)} %copy-done.1, bf16[512,768]{1,0:T(8,128)(2,1)S(1)} %collective-permute-done.34.refs_4_.p2_ref, bf16[512,768]{1,0:T(8,128)(2,1)} %collective-permute-done.35.p3_ref, ...), custom_call_target="tpu_custom_call" | custom-call | flops 1000000 | bytes 9000000 | tf_op jit(solution)/shard_map/place/pallas_call | solution.py:84
  246.2 9.6 %collective-permute-done.46.refs_3_ = bf16[112,768]{1,0:T(8,128)(2,1)S(1)} collective-permute-done((bf16[112,768]{1,0:T(8,128)(2,1)}, bf16[112,768]{1,0:T(8,128)(2,1)S(1)}, u32[]{:S(2)}, u32[]{:S(2)}) %collective-permute-start.46) | collective-permute-done | bytes 172064 | tf_op jit(solution)/shard_map/ppermute | solution.py:992
  259.6 5.2 %place.3 = f32[2048,768]{1,0:T(8,128)} custom-call(s32[1]{0:T(128)} %bitcast.refs_0_.me_ref, bf16[512,768]{1,0:T(8,128)(2,1)S(1)} %fence.25.p0_ref, bf16[512,768]{1,0:T(8,128)(2,1)} %collective-permute-done.43.p1_ref, bf16[512,768]{1,0:T(8,128)(2,1)S(1)} %fence.26.p2_ref, bf16[512,768]{1,0:T(8,128)(2,1)S(1)} %collective-permute-done.48.p3_ref, ...), custom_call_target="tpu_custom_call" | custom-call | flops 1000000 | bytes 9000000 | tf_op jit(solution)/shard_map/place/pallas_call | solution.py:84
  264.8 4.2 %slice_convert_fusion = (f32[768,768]{1,0:T(8,128)}, f32[768,768]{1,0:T(8,128)}) fusion(bf16[1536,768]{1,0:T(8,128)(2,1)} %all-gather.2.cloned.1.call-done), kind=kLoop, calls=%fused_computation.7 | loop fusion | flops 1179648 | bytes 7077888 | tf_op jit(solution)/shard_map/convert_element_type | solution.py:1116
  268.9 4.9 %collective-permute-done.49.other_ref = bf16[400,768]{1,0:T(8,128)(2,1)S(1)} collective-permute-done((bf16[400,768]{1,0:T(8,128)(2,1)}, bf16[400,768]{1,0:T(8,128)(2,1)S(1)}, u32[]{:S(2)}, u32[]{:S(2)}) %collective-permute-start.49) | collective-permute-done | bytes 614432 | tf_op jit(solution)/shard_map/ppermute | solution.py:1135
  (178 shorter events, 79.9 us)
Async XLA Ops:
  7.2 165.9 %reduce-scatter.2.cloned.1.call-start = ((), (), s32[]{:S(2)}) async-start(), calls=%async_computation.1 | async-start | bytes 2654208 | tf_op jit(solution)/shard_map/reduce_scatter | solution.py:1080
  80.1 23.1 %collective-permute-start.23 = (bf16[256,768]{1,0:T(8,128)(2,1)S(1)}, bf16[256,768]{1,0:T(8,128)(2,1)S(1)}, u32[]{:S(2)}, u32[]{:S(2)}) collective-permute-start(bf16[256,768]{1,0:T(8,128)(2,1)S(1)} %get-tuple-element.150), channel_id=1, source_target_pairs={{0,1},{1,0},{2,3},{3,2},{4,5},{5,4},{6,7},{7,6},{8,9},{9,8},{10,11... | collective-permute-start | bytes 1179656 | tf_op jit(solution)/shard_map/ppermute | solution.py:960
  101.6 19.0 %collective-permute-start.27 = (bf16[512,768]{1,0:T(8,128)(2,1)}, bf16[512,768]{1,0:T(8,128)(2,1)}, u32[]{:S(2)}, u32[]{:S(2)}) collective-permute-start(bf16[512,768]{1,0:T(8,128)(2,1)} %fence.18), channel_id=1, source_target_pairs={{0,1},{1,0},{2,3},{3,2},{4,5},{5,4},{6,7},{7,6},{8,9},{9,8},{10,11... | collective-permute-start | bytes 2359304 | tf_op jit(solution)/shard_map/ppermute | solution.py:960
  102.8 161.9 %all-gather.2.cloned.1.call-start = ((), (), s32[]{:S(2)}) async-start(), calls=%async_computation.2 | async-start | bytes 2654208 | tf_op jit(solution)/shard_map/all_gather | solution.py:1115
  102.9 21.8 %collective-permute-start.28 = (bf16[512,768]{1,0:T(8,128)(2,1)}, bf16[512,768]{1,0:T(8,128)(2,1)S(1)}, u32[]{:S(2)}, u32[]{:S(2)}) collective-permute-start(bf16[512,768]{1,0:T(8,128)(2,1)} %fence.20), channel_id=1, source_target_pairs={{0,1},{1,0},{2,3},{3,2},{4,5},{5,4},{6,7},{7,6},{8,9},{9,8},{10,11... | collective-permute-start | bytes 2359304 | tf_op jit(solution)/shard_map/ppermute | solution.py:960
  107.7 16.5 %collective-permute-start.25 = (bf16[192,256]{1,0:T(8,128)(2,1)S(1)}, bf16[192,256]{1,0:T(8,128)(2,1)S(1)}, u32[]{:S(2)}, u32[]{:S(2)}) collective-permute-start(bf16[192,256]{1,0:T(8,128)(2,1)S(1)} %get-tuple-element.153), channel_id=1, source_target_pairs={{0,2},{2,0},{1,3},{3,1},{4,6},{6,4},{5,7},{7,5},{8,10},{10,8},{9,1... | collective-permute-start | bytes 294920 | tf_op jit(solution)/shard_map/ppermute | solution.py:964
  120.6 19.6 %collective-permute-start.20 = (bf16[192,256]{1,0:T(8,128)(2,1)S(1)}, bf16[192,256]{1,0:T(8,128)(2,1)S(1)}, u32[]{:S(2)}, u32[]{:S(2)}) collective-permute-start(bf16[192,256]{1,0:T(8,128)(2,1)S(1)} %get-tuple-element.145), channel_id=1, source_target_pairs={{0,1},{1,0},{2,3},{3,2},{4,5},{5,4},{6,7},{7,6},{8,9},{9,8},{10,11... | collective-permute-start | bytes 294920 | tf_op jit(solution)/shard_map/ppermute | solution.py:960
  122.8 18.3 %collective-permute-start.21 = (bf16[192,256]{1,0:T(8,128)(2,1)S(1)}, bf16[192,256]{1,0:T(8,128)(2,1)S(1)}, u32[]{:S(2)}, u32[]{:S(2)}) collective-permute-start(bf16[192,256]{1,0:T(8,128)(2,1)S(1)} %get-tuple-element.146), channel_id=1, source_target_pairs={{0,2},{2,0},{1,3},{3,1},{4,6},{6,4},{5,7},{7,5},{8,10},{10,8},{9,1... | collective-permute-start | bytes 294920 | tf_op jit(solution)/shard_map/ppermute | solution.py:964
  124.2 22.1 %collective-permute-start.29 = (bf16[192,768]{1,0:T(8,128)(2,1)S(1)}, bf16[192,768]{1,0:T(8,128)(2,1)S(1)}, u32[]{:S(2)}, u32[]{:S(2)}) collective-permute-start(bf16[192,768]{1,0:T(8,128)(2,1)S(1)} %get-tuple-element.166), channel_id=1, source_target_pairs={{0,1},{1,0},{2,3},{3,2},{4,5},{5,4},{6,7},{7,6},{8,9},{9,8},{10,11... | collective-permute-start | bytes 884744 | tf_op jit(solution)/shard_map/ppermute | solution.py:960
  124.7 21.6 %collective-permute-start.31 = (bf16[512,768]{1,0:T(8,128)(2,1)S(1)}, bf16[512,768]{1,0:T(8,128)(2,1)}, u32[]{:S(2)}, u32[]{:S(2)}) collective-permute-start(bf16[512,768]{1,0:T(8,128)(2,1)S(1)} %fence.19.refs_13_), channel_id=1, source_target_pairs={{0,2},{2,0},{1,3},{3,1},{4,6},{6,4},{5,7},{7,5},{8,10},{10,8},{9,1... | collective-permute-start | bytes 2359304 | tf_op jit(solution)/shard_map/ppermute | solution.py:964
  140.3 23.2 %collective-permute-start.32 = (bf16[192,768]{1,0:T(8,128)(2,1)S(1)}, bf16[192,768]{1,0:T(8,128)(2,1)S(1)}, u32[]{:S(2)}, u32[]{:S(2)}) collective-permute-start(bf16[192,768]{1,0:T(8,128)(2,1)S(1)} %add_convert_fusion.4.refs_17_), channel_id=1, source_target_pairs={{0,2},{2,0},{1,3},{3,1},{4,6},{6,4},{5,7},{7,5},{8,10},{10,8},{9,1... | collective-permute-start | bytes 884744 | tf_op jit(solution)/shard_map/ppermute | solution.py:964
  175.1 20.4 %collective-permute-start.34 = (bf16[512,768]{1,0:T(8,128)(2,1)S(1)}, bf16[512,768]{1,0:T(8,128)(2,1)S(1)}, u32[]{:S(2)}, u32[]{:S(2)}) collective-permute-start(bf16[512,768]{1,0:T(8,128)(2,1)S(1)} %fusion.3.p0_ref), channel_id=1, source_target_pairs={{0,2},{2,0},{1,3},{3,1},{4,6},{6,4},{5,7},{7,5},{8,10},{10,8},{9,1... | collective-permute-start | bytes 2359304 | tf_op jit(solution)/shard_map/ppermute | solution.py:964
  176.6 18.9 %collective-permute-start.33 = (bf16[512,768]{1,0:T(8,128)(2,1)S(1)}, bf16[512,768]{1,0:T(8,128)(2,1)S(1)}, u32[]{:S(2)}, u32[]{:S(2)}) collective-permute-start(bf16[512,768]{1,0:T(8,128)(2,1)S(1)} %fusion.3.p0_ref), channel_id=1, source_target_pairs={{0,1},{1,0},{2,3},{3,2},{4,5},{5,4},{6,7},{7,6},{8,9},{9,8},{10,11... | collective-permute-start | bytes 2359304 | tf_op jit(solution)/shard_map/ppermute | solution.py:960
  176.6 18.9 %collective-permute-start.36 = (bf16[384,768]{1,0:T(8,128)(2,1)S(1)}, bf16[384,768]{1,0:T(8,128)(2,1)S(1)}, u32[]{:S(2)}, u32[]{:S(2)}) collective-permute-start(bf16[384,768]{1,0:T(8,128)(2,1)S(1)} %copy-done.14), channel_id=1, source_target_pairs={{0,4},{4,0},{1,5},{5,1},{2,6},{6,2},{3,7},{7,3},{8,12},{12,8},{9,1... | collective-permute-start | bytes 1769480 | tf_op jit(solution)/shard_map/ppermute | solution.py:1111
  202.6 20.2 %collective-permute-start.41 = (bf16[528,768]{1,0:T(8,128)(2,1)S(1)}, bf16[528,768]{1,0:T(8,128)(2,1)S(1)}, u32[]{:S(2)}, u32[]{:S(2)}) collective-permute-start(bf16[528,768]{1,0:T(8,128)(2,1)S(1)} %chip_sum.1.refs_4_), channel_id=1, source_target_pairs={{0,2},{2,0},{1,3},{3,1},{4,6},{6,4},{5,7},{7,5},{8,10},{10,8},{9,1... | collective-permute-start | bytes 2433032 | tf_op jit(solution)/shard_map/ppermute | solution.py:964
  203.2 22.5 %collective-permute-start.37 = (bf16[96,768]{1,0:T(8,128)(2,1)S(1)}, bf16[96,768]{1,0:T(8,128)(2,1)S(1)}, u32[]{:S(2)}, u32[]{:S(2)}) collective-permute-start(bf16[96,768]{1,0:T(8,128)(2,1)S(1)} %copy-done.22), channel_id=1, source_target_pairs={{0,8},{8,16},{16,24},{24,0},{1,9},{9,17},{17,25},{25,1},{2,10},{10... | collective-permute-start | bytes 442376 | tf_op jit(solution)/shard_map/ppermute | solution.py:992
  204.2 21.6 %collective-permute-start.38 = (bf16[96,768]{1,0:T(8,128)(2,1)S(1)}, bf16[96,768]{1,0:T(8,128)(2,1)S(1)}, u32[]{:S(2)}, u32[]{:S(2)}) collective-permute-start(bf16[96,768]{1,0:T(8,128)(2,1)S(1)} %copy-done.21), channel_id=1, source_target_pairs={{0,16},{8,24},{16,0},{24,8},{1,17},{9,25},{17,1},{25,9},{2,18},{10... | collective-permute-start | bytes 442376 | tf_op jit(solution)/shard_map/ppermute | solution.py:992
  205.7 20.1 %collective-permute-start.39 = (bf16[96,768]{1,0:T(8,128)(2,1)S(1)}, bf16[96,768]{1,0:T(8,128)(2,1)S(1)}, u32[]{:S(2)}, u32[]{:S(2)}) collective-permute-start(bf16[96,768]{1,0:T(8,128)(2,1)S(1)} %copy-done.18), channel_id=1, source_target_pairs={{0,24},{8,0},{16,8},{24,16},{1,25},{9,1},{17,9},{25,17},{2,26},{10... | collective-permute-start | bytes 442376 | tf_op jit(solution)/shard_map/ppermute | solution.py:992
  207.7 33.0 %collective-permute-start.35 = (bf16[512,768]{1,0:T(8,128)(2,1)S(1)}, bf16[512,768]{1,0:T(8,128)(2,1)}, u32[]{:S(2)}, u32[]{:S(2)}) collective-permute-start(bf16[512,768]{1,0:T(8,128)(2,1)S(1)} %collective-permute-done.34.refs_4_.p2_ref), channel_id=1, source_target_pairs={{0,1},{1,0},{2,3},{3,2},{4,5},{5,4},{6,7},{7,6},{8,9},{9,8},{10,11... | collective-permute-start | bytes 2359304 | tf_op jit(solution)/shard_map/ppermute | solution.py:960
  227.6 29.8 %collective-permute-start.44 = (bf16[512,768]{1,0:T(8,128)(2,1)S(1)}, bf16[512,768]{1,0:T(8,128)(2,1)S(1)}, u32[]{:S(2)}, u32[]{:S(2)}) collective-permute-start(bf16[512,768]{1,0:T(8,128)(2,1)S(1)} %fence.25.p0_ref), channel_id=1, source_target_pairs={{0,2},{2,0},{1,3},{3,1},{4,6},{6,4},{5,7},{7,5},{8,10},{10,8},{9,1... | collective-permute-start | bytes 2359304 | tf_op jit(solution)/shard_map/ppermute | solution.py:964
  228.1 18.1 %collective-permute-start.47 = (bf16[112,768]{1,0:T(8,128)(2,1)}, bf16[112,768]{1,0:T(8,128)(2,1)S(1)}, u32[]{:S(2)}, u32[]{:S(2)}) collective-permute-start(bf16[112,768]{1,0:T(8,128)(2,1)} %second.1.rest_0_.refs_1_), channel_id=1, source_target_pairs={{0,24},{8,0},{16,8},{24,16},{1,25},{9,1},{17,9},{25,17},{2,26},{10... | collective-permute-start | bytes 516104 | tf_op jit(solution)/shard_map/ppermute | solution.py:992
  239.1 16.8 %collective-permute-start.46 = (bf16[112,768]{1,0:T(8,128)(2,1)}, bf16[112,768]{1,0:T(8,128)(2,1)S(1)}, u32[]{:S(2)}, u32[]{:S(2)}) collective-permute-start(bf16[112,768]{1,0:T(8,128)(2,1)} %second.1.rest_0_.refs_1_), channel_id=1, source_target_pairs={{0,16},{8,24},{16,0},{24,8},{1,17},{9,25},{17,1},{25,9},{2,18},{10... | collective-permute-start | bytes 516104 | tf_op jit(solution)/shard_map/ppermute | solution.py:992
  240.7 17.9 %collective-permute-start.43 = (bf16[512,768]{1,0:T(8,128)(2,1)S(1)}, bf16[512,768]{1,0:T(8,128)(2,1)}, u32[]{:S(2)}, u32[]{:S(2)}) collective-permute-start(bf16[512,768]{1,0:T(8,128)(2,1)S(1)} %fence.25.p0_ref), channel_id=1, source_target_pairs={{0,1},{1,0},{2,3},{3,2},{4,5},{5,4},{6,7},{7,6},{8,9},{9,8},{10,11... | collective-permute-start | bytes 2359304 | tf_op jit(solution)/shard_map/ppermute | solution.py:960
  257.3 16.5 %collective-permute-start.49 = (bf16[400,768]{1,0:T(8,128)(2,1)}, bf16[400,768]{1,0:T(8,128)(2,1)S(1)}, u32[]{:S(2)}, u32[]{:S(2)}) collective-permute-start(bf16[400,768]{1,0:T(8,128)(2,1)} %third.1.refs_1_.rest_0_.mine_ref), channel_id=1, source_target_pairs={{0,4},{4,0},{1,5},{5,1},{2,6},{6,2},{3,7},{7,3},{8,12},{12,8},{9,1... | collective-permute-start | bytes 1843208 | tf_op jit(solution)/shard_map/ppermute | solution.py:1135
  (51 other events, 397.3 us)
Sparse Core Ops, SparseCore 0:
  103.0 70.0 reduce-scatter.1
  175.3 64.2 all-gather.1

commit v12 on v11

--- a/solution.py
+++ b/solution.py
@@ -528,25 +528,62 @@
     )
 
 
-def feed_grad_body(left_ref, right_ref, before_ref, *rest):
-    rest[-1][0] = (tn(left_ref[0], right_ref[0]) + before_ref[0].astype(F32)).astype(BF16)
-
-
-def feed_grad(left, right, before, after):
+def feed_grad_body(xz_ref, left_ref, right_ref, before_ref, keep_ref, send_ref):
+    value = (tn(left_ref[0], right_ref[0]) + before_ref[0].astype(F32)).astype(BF16)
+    mine = pl.program_id(0) == xz_ref[0]
+
+    @pl.when(mine)
+    def _():
+        keep_ref[...] = value
+
+    @pl.when(jnp.logical_not(mine))
+    def _():
+        send_ref[...] = value
+
+
+def feed_grad(xz, left, right, before):
     _, rows, features = left.shape
-    both = pl.BlockSpec((1, rows, features), lambda i: (i, 0, 0))
-    square = pl.BlockSpec((1, features, features), lambda i: (i, 0, 0))
+    both = pl.BlockSpec((1, rows, features), lambda i, m: (i, 0, 0))
     return kernel_call(
         feed_grad_body,
-        (left, right, before, *after),
-        free_in=tuple(range(3, 3 + len(after))),
-        grid=(2,),
-        in_specs=[both, both, square] + [pl.BlockSpec(memory_space=pl.ANY)] * len(after),
-        out_specs=[square],
-        out_shape=[shape_of(*before.shape)],
+        (xz, left, right, before),
+        grid_spec=pltpu.PrefetchScalarGridSpec(
+            num_scalar_prefetch=1,
+            grid=(2,),
+            in_specs=[both, both, pl.BlockSpec((1, features, features), lambda i, m: (i, 0, 0))],
+            out_specs=[const(before.shape[1:])] * 2,
+        ),
+        out_shape=[shape_of(*before.shape[1:])] * 2,
         cost_estimate=cost(5e9, 10e6),
         name="feed_grad",
-    )[0]
+    )
+
+
+def feed_ready_body(xz_ref, mine_ref, other_ref, outer_ref, inner_ref):
+    for from_ref, here in ((mine_ref, xz_ref[0]), (other_ref, 1 - xz_ref[0])):
+        for n, to_ref in enumerate((outer_ref, inner_ref)):
+            @pl.when(here == n)
+            def _(from_ref=from_ref, to_ref=to_ref):
+                to_ref[...] = from_ref[...].astype(F32)
+
+
+def feed_ready(xz, mine, other):
+    rows, features = mine.shape
+    block = pl.BlockSpec((TILE, features), lambda i, m: (i, 0))
+    return kernel_call(
+        feed_ready_body,
+        (xz, mine, other),
+        free_in=(1, 2),
+        grid_spec=pltpu.PrefetchScalarGridSpec(
+            num_scalar_prefetch=1,
+            grid=(rows // TILE,),
+            in_specs=[block, block],
+            out_specs=[block, block],
+        ),
+        out_shape=[shape_of(rows, features, dtype=F32)] * 2,
+        cost_estimate=cost(1e6, 7e6),
+        name="feed_ready",
+    )
 
 
 def back_body(me_ref, b0_ref, b1_ref, b2_ref, residual_ref, g_ref, vec_ref, w0_ref, w1_ref, w2_ref, w3_ref,
@@ -1033,6 +1070,7 @@
     cot = cotangent.reshape(length, features)
     at = lax.axis_index(MP).astype(jnp.int32)
     me = at[None]
+    xz = jnp.stack([lax.axis_index("x"), lax.axis_index("z")]).astype(jnp.int32)
     apart = jnp.concatenate([query_bias, value_bias, jnp.zeros((features - 2 * width,), F32)])
     vectors = jnp.concatenate([gain_one, bias_one, output_bias, gain_two, bias_two, outer_bias, apart, inner_bias])
     vectors = vectors.reshape(8, features)
@@ -1070,14 +1108,15 @@
         sums.append(far_sum)
         if p:
             backs[p, 3] = fence(backs[p, 3], gathered[-1][2], space=pltpu.VMEM)
-            feed_sum = feed_grad(kept[0], kept[1], near_grad, ())
-            backs[p, 2] = fence(backs[p, 2], feed_sum)
+            feed_keep, feed_send = feed_grad(xz, kept[0], kept[1], near_grad)
+            backs[p, 2] = fence(backs[p, 2], feed_send)
         summed, far_sum = gather_sum([backs[p, n] for n in range(4)])
         gathered.append(summed)
         far_sums.append(far_sum)
     left, right, *far_outs = kept
     outs += far_outs
-    feed_sum = lax.psum_scatter(feed_sum.reshape(-1, features), DP, scatter_dimension=0, tiled=True)
+    feed_sum = (feed_keep.astype(F32) + lax.ppermute(feed_send, "x", SWAP).astype(F32)).astype(BF16)
+    feed_sum = lax.psum_scatter(feed_sum, "z", scatter_dimension=0, tiled=True)
     grad_residuals, lows, grads_attended, inner_sums = [], [], [], []
     for p in parts:
         grad, low, a0, a1, a2, a3, vector = middle_back(
@@ -1101,7 +1140,6 @@
     grads = attend_backward(1, me, segment_ids, qt, extras[1], kn, kt, vn, attended[1], grads_attended[1], earlier,
                             (part_near, part_far, there))
 
-    xz = jnp.stack([lax.axis_index("x"), lax.axis_index("z")]).astype(jnp.int32)
     part_across = other_chip(part_far)
     grad_output = fence(part[0], grads).astype(F32) + part_near.astype(F32) + part_across.astype(F32)
     keep, send = halves(xz, nn(grads, attend_in).astype(BF16), grad_output.astype(BF16), ())
@@ -1112,13 +1150,13 @@
     back_own, back_near, back_far, back_across, apart, summed = tail(
         me, grads, wq, wk, wv, tokens, stat, inner_sums, sums, (send,)
     )
-    feed_sum = lax.all_gather(fence(feed_sum, send), DP, axis=0, tiled=True)
-    feed_sum = (feed_sum[:features].astype(F32), feed_sum[features:].astype(F32))
+    feed_sum = lax.all_gather(fence(feed_sum, send), "z", axis=0, tiled=True)
+    feed_other = lax.ppermute(feed_sum, "x", SWAP)
     quarter = sum_first(xz, keep, got, (near, far, apart))
     back_across = other_core(fence(back_across, quarter[-1], space=pltpu.VMEM))
     back_far = chip_sum(back_far, back_across, summed, ())
     back_there = other_chip(back_far)
-    share = final(me, [back_own, other_core(back_near), back_there], tokens, grad_residuals, vectors, ())
+    share = final(me, [back_own, other_core(back_near), back_there], tokens, grad_residuals, vectors, (feed_other,))
     if len(quarter) > 1:
         turns = [quarter[0]] + [turned(part, n + 1) for n, part in enumerate(quarter[1:])]
         held = second(turns, back_far, back_there, apart, (share,))
@@ -1131,8 +1169,9 @@
     share = fence(share, held if len(quarter) > 1 else mine, space=pltpu.VMEM)
     near, far = other_core(share), fence(other_chip(share), mine, space=pltpu.VMEM)
     input_grad = place(me, [share, near, far, other_core(far)], F32, (mine,))
+    feed_sum = feed_ready(xz, feed_sum, feed_other)
     *wide, two_gain, two_bias, output_sum, outer_bias, one_gain, one_bias, inner_bias, query, _, value = ready(
-        xz, mine, lax.ppermute(mine, "x", SWAP), width, feed_sum
+        xz, mine, lax.ppermute(mine, "x", SWAP), width, (*feed_sum, input_grad)
     )
     return (
         layer_out.reshape(1, length, features),

time: 285 us -> 295 us (1.035)
  Pallas kernels: 142 us -> 148 us
  local copies, waits for them, and re-layouts: 6.36 us -> 10.4 us
  waiting for transfers between devices: 63.2 us -> 66.9 us
    ppermute x0 -> x2, waiting for transfers between devices: none -> 10.3 us  [the longest x1 6.28 us: local(): lax.ppermute(feed_send, 'x', SWAP).astype(F32)]
    ppermute x6, starting transfers between devices: 17 us -> 8.59 us  [turned(): lax.ppermute(values, 'z', [(n, (n + way) % size) for n in range(size)])]
    pallas_call x24 -> x25, Pallas kernels: 142 us -> 148 us  [kernel_call(): pl.pallas_call(body, out_shape=shapes if many else shapes[0], compiler_pa...]
    all_gather x1, waiting for transfers between devices: 0.01 us -> 5.81 us  [local(): feed_sum = lax.all_gather(fence(feed_sum, send), 'z', axis=0, tiled=True)]
    ppermute x1, waiting for transfers between devices: 7.45 us -> 3 us  [local(): got = lax.ppermute(send, 'x', SWAP)]
    unnamed x46 -> x48, local copies, waits for them, and re-layouts: 4.87 us -> 8.89 us
    ppermute x24, waiting for transfers between devices: 5.56 us -> 2.24 us  [other_core(): return lax.ppermute(value, 'core', SWAP)]
  transfers between devices with their start and end apart: 52 -> 54, of which waited for: 14 -> 15; matrix products, arithmetic and copies ran while one was open for 7% -> 6% of each run, Pallas kernels for 46% -> 46%
where the time goes in v12:
time: 295 us; the launch traced here: 294 us
  Pallas kernels  148 us (50%)
  waiting for transfers between devices  66.9 us (23%)
  starting transfers between devices  38.3 us (13%)
  between operations  14.4 us (5%)
  other arithmetic  11.2 us (4%)
  local copies, waits for them, and re-layouts  10.4 us (4%)
  matrix products  4.59 us (2%)
    pallas_call x25, Pallas kernels, kernel_call(): pl.pallas_call(body, out_shape=shapes if many else shapes[0], compiler_pa...  148 us
    ppermute x14, waiting for transfers between devices, other_chip(): return lax.ppermute(value, 'y', SWAP)  30.1 us
    ppermute x14, starting transfers between devices, other_chip(): return lax.ppermute(value, 'y', SWAP)  14.1 us
    unnamed x48, local copies, waits for them, and re-layouts  8.89 us
    ppermute x6, starting transfers between devices, turned(): lax.ppermute(values, 'z', [(n, (n + way) % size) for n in range(size)])  8.59 us
    ppermute x6, waiting for transfers between devices, turned(): lax.ppermute(values, 'z', [(n, (n + way) % size) for n in range(size)])  7.52 us
    ppermute x1, waiting for transfers between devices, local(): lax.ppermute(feed_send, 'x', SWAP).astype(F32)  6.28 us
    ppermute x24, starting transfers between devices, other_core(): return lax.ppermute(value, 'core', SWAP)  6.11 us
  transfers between devices with their start and end apart: 54, of which 15 were waited for; matrix products, arithmetic and copies ran while one was open for 6% of the time, Pallas kernels for 46%

profile of v12, /device:TPU:0, one launch (start us, length us, event | category | flops | bytes accessed | tf_op | source)
XLA Modules:
  0.0 294.3 jit_solution(6506108110353062882)
XLA Ops:
  12.5 8.6 %project.1 = (bf16[2048,768]{1,0:T(8,128)(2,1)}, bf16[3,128,2048]{2,1,0:T(8,128)(2,1)}, bf16[192,2048]{1,0:T(8,128)(2,1)}, bf16[3,80,2048]{2,1,0:T(8,128)(2,1)},...) custom-call(bf16[2048,768]{1,0:T(8,128)(2,1)} %bitcast.17, ...), custom_call_target="tpu_custom_call" | custom-call | flops 6000000000 | bytes 14000000 | tf_op jit(solution)/shard_map/project/pallas_call | solution.py:84
  21.1 10.5 %attend_forward.2 = (bf16[4,192,256]{2,1,0:T(8,128)(2,1)}, bf16[3,16,1024]{2,1,0:T(8,128)(2,1)}, bf16[192,256]{1,0:T(8,128)(2,1)}, bf16[192,256]{1,0:T(8,128)(2,...) custom-call(s32[1]{0:T(128)} %bitcast.refs_0_.me_ref, s32[1,2048]{1,0:T(1,128)S(1)} %copy-done.12, ...), custom_call_target="tpu_custom_call" | custom-call | flops 8999999488 | bytes 5000000 | tf_op jit(solution)/shard_map/attend_forward/pallas_call | solution.py:84
  34.4 10.3 %attend_forward.3 = (bf16[4,192,256]{2,1,0:T(8,128)(2,1)}, bf16[3,16,1024]{2,1,0:T(8,128)(2,1)}, bf16[192,256]{1,0:T(8,128)(2,1)}, bf16[192,256]{1,0:T(8,128)(2,...) custom-call(s32[1]{0:T(128)} %bitcast.refs_0_.me_ref, s32[1,2048]{1,0:T(1,128)S(1)} %copy-done.12, ...), custom_call_target="tpu_custom_call" | custom-call | flops 8999999488 | bytes 5000000 | tf_op jit(solution)/shard_map/attend_forward/pallas_call | solution.py:84
  56.4 13.0 %feed_near.1 = (bf16[512,768]{1,0:T(8,128)(2,1)}, bf16[512,768]{1,0:T(8,128)(2,1)}, bf16[256,768]{1,0:T(8,128)(2,1)}, bf16[256,768]{1,0:T(8,128)(2,1)S(1)}, bf16...) custom-call(s32[1]{0:T(128)} %bitcast.refs_0_.me_ref, ...), custom_call_target="tpu_custom_call" | custom-call | flops 15000000512 | bytes 12000000 | tf_op jit(solution)/shard_map/feed_near/pallas_call | solution.py:84
  71.1 6.5 %feed_far.2 = (bf16[2,1024,768]{2,1,0:T(8,128)(2,1)}, bf16[2,1024,768]{2,1,0:T(8,128)(2,1)}, bf16[512,768]{1,0:T(8,128)(2,1)}, bf16[512,768]{1,0:T(8,128)(2,1)},...) custom-call(s32[1]{0:T(128)} %bitcast.refs_0_.me_ref, ...), custom_call_target="tpu_custom_call" | custom-call | flops 5000000000 | bytes 8000000 | tf_op jit(solution)/shard_map/feed_far/pallas_call | solution.py:84
  82.9 6.5 %feed_far.3 = (bf16[2,1024,768]{2,1,0:T(8,128)(2,1)}, bf16[2,1024,768]{2,1,0:T(8,128)(2,1)}, bf16[512,768]{1,0:T(8,128)(2,1)}, bf16[512,768]{1,0:T(8,128)(2,1)},...) custom-call(s32[1]{0:T(128)} %bitcast.refs_0_.me_ref, ...), custom_call_target="tpu_custom_call", output_to_operand_aliasing={{0}: (7, {}), {1}: (8, {}), {2}: (9, {}), {3}: (10, {})} | custom-call | flops 5000000000 | bytes 8000000 | tf_op jit(solution)/shard_map/feed_far/pallas_call | solution.py:84
  89.4 4.4 %collective-permute-done.17.refs_1_.b2_ref = bf16[256,768]{1,0:T(8,128)(2,1)S(1)} collective-permute-done((bf16[256,768]{1,0:T(8,128)(2,1)S(1)}, bf16[256,768]{1,0:T(8,128)(2,1)S(1)}, u32[]{:S(2)}, u32[]{:S(2)}) %collective-permute-start.17) | collective-permute-done | bytes 393248 | tf_op jit(solution)/shard_map/ppermute | solution.py:1001
  94.5 7.3 %feed_grad.1 = (bf16[768,768]{1,0:T(8,128)(2,1)}, bf16[768,768]{1,0:T(8,128)(2,1)}) custom-call(s32[2]{0:T(128)S(1)} %pad_add_fusion.xz_ref.refs_0_, bf16[2,1024,768]{2,1,0:T(8,128)(2,1)} %get-tuple-element.143.left_ref, bf16[2,1024,768]{2,1,0:T(8,128)(2,1)} %get-tuple-element.144.right_ref, bf16[2,768,768]{2,1,0:T(8,128)(2,1)} %get-tuple-element.145.before_ref), custom_call_target="tpu_custom_call" | custom-call | flops 5000000000 | bytes 10000000 | tf_op jit(solution)/shard_map/feed_grad/pallas_call | solution.py:84
  107.2 3.6 %middle_back.3 = (f32[256,768]{1,0:T(8,128)}, bf16[256,768]{1,0:T(8,128)(2,1)}, bf16[192,256]{1,0:T(8,128)(2,1)}, bf16[192,256]{1,0:T(8,128)(2,1)S(1)}, bf16[192...) custom-call(s32[1]{0:T(128)} %bitcast.refs_0_.me_ref, ...), custom_call_target="tpu_custom_call" | custom-call | flops 2000000000 | bytes 4000000 | tf_op jit(solution)/shard_map/middle_back/pallas_call | solution.py:84
  112.3 5.5 %collective-permute-done.19.b2_ref = bf16[256,768]{1,0:T(8,128)(2,1)S(1)} collective-permute-done((bf16[256,768]{1,0:T(8,128)(2,1)}, bf16[256,768]{1,0:T(8,128)(2,1)S(1)}, u32[]{:S(2)}, u32[]{:S(2)}) %collective-permute-start.19) | collective-permute-done | bytes 393248 | tf_op jit(solution)/shard_map/ppermute | solution.py:1001
  117.8 3.6 %middle_back.2 = (f32[256,768]{1,0:T(8,128)}, bf16[256,768]{1,0:T(8,128)(2,1)}, bf16[192,256]{1,0:T(8,128)(2,1)}, bf16[192,256]{1,0:T(8,128)(2,1)S(1)}, bf16[192...) custom-call(s32[1]{0:T(128)} %bitcast.refs_0_.me_ref, ...), custom_call_target="tpu_custom_call" | custom-call | flops 2000000000 | bytes 4000000 | tf_op jit(solution)/shard_map/middle_back/pallas_call | solution.py:84
  124.2 6.3 %collective-permute-done.43 = bf16[768,768]{1,0:T(8,128)(2,1)} collective-permute-done((bf16[768,768]{1,0:T(8,128)(2,1)}, bf16[768,768]{1,0:T(8,128)(2,1)}, u32[]{:S(2)}, u32[]{:S(2)}) %collective-permute-start.43) | collective-permute-done | bytes 1179680 | tf_op jit(solution)/shard_map/ppermute | solution.py:1118
  138.2 15.4 %attend_backward.2 = (bf16[192,1024]{1,0:T(8,128)(2,1)}, f32[192,2048]{1,0:T(8,128)}, f32[192,2048]{1,0:T(8,128)}) custom-call(s32[1]{0:T(128)} %bitcast.refs_0_.me_ref, s32[1,2048]{1,0:T(1,128)S(1)} %copy-done.12, s32[1,2048]{1,0:T(1,128)S(1)} %copy-done.12, bf16[3,128,2048]{2,1,0:T(8,128)(2,1)} %get-tuple-element.114.refs_3_, ...), custom_call_target="tpu_custom_call" | custom-call | flops 16000000000 | bytes 10000000 | tf_op jit(solution)/shard_map/attend_backward/pallas_call | solution.py:84
  158.8 16.1 %attend_backward.3.refs_1_.g_ref = bf16[576,2048]{1,0:T(8,128)(2,1)} custom-call(s32[1]{0:T(128)} %bitcast.refs_0_.me_ref, s32[1,2048]{1,0:T(1,128)S(1)} %copy-done.12, s32[1,2048]{1,0:T(1,128)S(1)} %copy-done.12, bf16[3,128,2048]{2,1,0:T(8,128)(2,1)} %get-tuple-element.114.refs_3_, bf16[3,16,1024]{2,1,0:T(8,128)(2,1)} %get-tuple-element.121.rest_0_.refs_4_, ...), custom_call_target="tpu_custom_call" | custom-call | flops 16000000000 | bytes 10000000 | tf_op jit(solution)/shard_map/attend_backward/pallas_call | solution.py:84
  176.1 4.6 %convolution_convert_fusion.g_ref = bf16[576,768]{1,0:T(8,128)(2,1)S(1)} fusion(bf16[576,2048]{1,0:T(8,128)(2,1)} %attend_backward.3.refs_1_.g_ref, bf16[2048,768]{1,0:T(8,128)(2,1)} %get-tuple-element.174), kind=kOutput, calls=%fused_computation.7 | convolution fusion | flops 1812381696 | bytes 6389760 | tf_op jit(solution)/shard_map/dot_general | solution.py:24
  189.6 10.6 %tail.1 = (bf16[512,768]{1,0:T(8,128)(2,1)}, bf16[512,768]{1,0:T(8,128)(2,1)S(1)}, bf16[512,768]{1,0:T(8,128)(2,1)}, bf16[528,768]{1,0:T(8,128)(2,1)S(1)}, f32[8,768]{1,0:T(8,128)}, /*index=5*/f32[8,768]{1,0:T(8,128)}) custom-call(s32[1]{0:T(128)} %bitcast.refs_0_.me_ref, bf16[576,2048]{1,0:T(8,128)(2,1)} %attend_backward.3.refs_1_.g_ref, ...), custom_call_target="tpu_custom_call" | custom-call | flops 4000000000 | bytes 10000000 | tf_op jit(solution)/shard_map/tail/pallas_call | solution.py:84
  209.7 5.8 %all-gather.2.cloned.1.call-done.mine_ref = bf16[768,768]{1,0:T(8,128)(2,1)} async-done(((bf16[192,768]{1,0:T(8,128)(2,1)}), bf16[768,768]{1,0:T(8,128)(2,1)}) %all-gather.2.cloned.1.call-update) | async-done | bytes 1179664 | tf_op jit(solution)/shard_map/all_gather | solution.py:1153
  224.3 14.5 %collective-permute-done.41.b2_ref.refs_5_ = bf16[528,768]{1,0:T(8,128)(2,1)S(1)} collective-permute-done((bf16[528,768]{1,0:T(8,128)(2,1)S(1)}, bf16[528,768]{1,0:T(8,128)(2,1)S(1)}, u32[]{:S(2)}, u32[]{:S(2)}) %collective-permute-start.41) | collective-permute-done | bytes 811040 | tf_op jit(solution)/shard_map/ppermute | solution.py:1001
  238.9 4.0 %collective-permute-done.44.rest_3_.other_ref = bf16[768,768]{1,0:T(8,128)(2,1)S(1)} collective-permute-done((bf16[768,768]{1,0:T(8,128)(2,1)}, bf16[768,768]{1,0:T(8,128)(2,1)S(1)}, u32[]{:S(2)}, u32[]{:S(2)}) %collective-permute-start.44) | collective-permute-done | bytes 1179680 | tf_op jit(solution)/shard_map/ppermute | solution.py:1154
  254.3 4.7 %place.2.refs_5_ = bf16[2048,768]{1,0:T(8,128)(2,1)} custom-call(s32[1]{0:T(128)} %bitcast.refs_0_.me_ref, bf16[512,768]{1,0:T(8,128)(2,1)S(1)} %copy-done.3, bf16[512,768]{1,0:T(8,128)(2,1)S(1)} %copy-done.1, bf16[512,768]{1,0:T(8,128)(2,1)} %collective-permute-done.34.refs_4_.p2_ref, bf16[512,768]{1,0:T(8,128)(2,1)} %collective-permute-done.35.p3_ref, ...), custom_call_target="tpu_custom_call" | custom-call | flops 1000000 | bytes 9000000 | tf_op jit(solution)/shard_map/place/pallas_call | solution.py:84
  259.0 7.5 %collective-permute-done.48.refs_3_ = bf16[112,768]{1,0:T(8,128)(2,1)S(1)} collective-permute-done((bf16[112,768]{1,0:T(8,128)(2,1)}, bf16[112,768]{1,0:T(8,128)(2,1)S(1)}, u32[]{:S(2)}, u32[]{:S(2)}) %collective-permute-start.48) | collective-permute-done | bytes 172064 | tf_op jit(solution)/shard_map/ppermute | solution.py:1029
  274.8 5.2 %place.3.rest_2_ = f32[2048,768]{1,0:T(8,128)} custom-call(s32[1]{0:T(128)} %bitcast.refs_0_.me_ref, bf16[512,768]{1,0:T(8,128)(2,1)S(1)} %fence.26.p0_ref, bf16[512,768]{1,0:T(8,128)(2,1)} %collective-permute-done.45.p1_ref, bf16[512,768]{1,0:T(8,128)(2,1)S(1)} %fence.27.p2_ref, bf16[512,768]{1,0:T(8,128)(2,1)S(1)} %collective-permute-done.50.p3_ref, ...), custom_call_target="tpu_custom_call" | custom-call | flops 1000000 | bytes 9000000 | tf_op jit(solution)/shard_map/place/pallas_call | solution.py:84
  280.0 4.2 %collective-permute-done.51.other_ref = bf16[400,768]{1,0:T(8,128)(2,1)S(1)} collective-permute-done((bf16[400,768]{1,0:T(8,128)(2,1)S(1)}, bf16[400,768]{1,0:T(8,128)(2,1)S(1)}, u32[]{:S(2)}, u32[]{:S(2)}) %collective-permute-start.51) | collective-permute-done | bytes 614432 | tf_op jit(solution)/shard_map/ppermute | solution.py:1174
  284.2 3.2 %ready.1 = (f32[192,768]{1,0:T(8,128)}, f32[192,768]{1,0:T(8,128)}, f32[192,768]{1,0:T(8,128)}, f32[192,768]{1,0:T(8,128)}, f32[768]{0:T(1024)}, /*index=5*/f32[...) custom-call(s32[2]{0:T(128)S(1)} %pad_add_fusion.xz_ref.refs_0_, ...), custom_call_target="tpu_custom_call" | custom-call | flops 1000000 | bytes 4000000 | tf_op jit(solution)/shard_map/ready/pallas_call | solution.py:84
  (185 shorter events, 97.9 us)
Async XLA Ops:
  7.2 175.1 %reduce-scatter.2.cloned.1.call-start = ((), (), s32[]{:S(2)}) async-start(), calls=%async_computation.1 | async-start | bytes 1474560 | tf_op jit(solution)/shard_map/reduce_scatter | solution.py:1119
  101.8 28.7 %collective-permute-start.43 = (bf16[768,768]{1,0:T(8,128)(2,1)}, bf16[768,768]{1,0:T(8,128)(2,1)}, u32[]{:S(2)}, u32[]{:S(2)}) collective-permute-start(bf16[768,768]{1,0:T(8,128)(2,1)} %get-tuple-element.146.refs_1_), channel_id=1, source_target_pairs={{0,4},{4,0},{1,5},{5,1},{2,6},{6,2},{3,7},{7,3},{8,12},{12,8},{9,1... | collective-permute-start | bytes 3538952 | tf_op jit(solution)/shard_map/ppermute | solution.py:1118
  106.2 26.9 %collective-permute-start.27 = (bf16[512,768]{1,0:T(8,128)(2,1)}, bf16[512,768]{1,0:T(8,128)(2,1)}, u32[]{:S(2)}, u32[]{:S(2)}) collective-permute-start(bf16[512,768]{1,0:T(8,128)(2,1)} %fence.18), channel_id=1, source_target_pairs={{0,1},{1,0},{2,3},{3,2},{4,5},{5,4},{6,7},{7,6},{8,9},{9,8},{10,11... | collective-permute-start | bytes 2359304 | tf_op jit(solution)/shard_map/ppermute | solution.py:997
  110.8 24.7 %collective-permute-start.24 = (bf16[192,256]{1,0:T(8,128)(2,1)S(1)}, bf16[192,256]{1,0:T(8,128)(2,1)S(1)}, u32[]{:S(2)}, u32[]{:S(2)}) collective-permute-start(bf16[192,256]{1,0:T(8,128)(2,1)S(1)} %get-tuple-element.157), channel_id=1, source_target_pairs={{0,1},{1,0},{2,3},{3,2},{4,5},{5,4},{6,7},{7,6},{8,9},{9,8},{10,11... | collective-permute-start | bytes 294920 | tf_op jit(solution)/shard_map/ppermute | solution.py:997
  110.8 26.2 %collective-permute-start.25 = (bf16[192,256]{1,0:T(8,128)(2,1)S(1)}, bf16[192,256]{1,0:T(8,128)(2,1)S(1)}, u32[]{:S(2)}, u32[]{:S(2)}) collective-permute-start(bf16[192,256]{1,0:T(8,128)(2,1)S(1)} %get-tuple-element.158), channel_id=1, source_target_pairs={{0,2},{2,0},{1,3},{3,1},{4,6},{6,4},{5,7},{7,5},{8,10},{10,8},{9,1... | collective-permute-start | bytes 294920 | tf_op jit(solution)/shard_map/ppermute | solution.py:1001
  117.8 19.8 %collective-permute-start.28 = (bf16[512,768]{1,0:T(8,128)(2,1)}, bf16[512,768]{1,0:T(8,128)(2,1)S(1)}, u32[]{:S(2)}, u32[]{:S(2)}) collective-permute-start(bf16[512,768]{1,0:T(8,128)(2,1)} %fence.20), channel_id=1, source_target_pairs={{0,1},{1,0},{2,3},{3,2},{4,5},{5,4},{6,7},{7,6},{8,9},{9,8},{10,11... | collective-permute-start | bytes 2359304 | tf_op jit(solution)/shard_map/ppermute | solution.py:997
  133.1 82.4 %all-gather.2.cloned.1.call-start = ((), (), s32[]{:S(2)}) async-start(), calls=%async_computation.2 | async-start | bytes 1474560 | tf_op jit(solution)/shard_map/all_gather | solution.py:1153
  133.2 22.2 %collective-permute-start.20 = (bf16[192,256]{1,0:T(8,128)(2,1)S(1)}, bf16[192,256]{1,0:T(8,128)(2,1)S(1)}, u32[]{:S(2)}, u32[]{:S(2)}) collective-permute-start(bf16[192,256]{1,0:T(8,128)(2,1)S(1)} %get-tuple-element.150), channel_id=1, source_target_pairs={{0,1},{1,0},{2,3},{3,2},{4,5},{5,4},{6,7},{7,6},{8,9},{9,8},{10,11... | collective-permute-start | bytes 294920 | tf_op jit(solution)/shard_map/ppermute | solution.py:997
  135.5 20.6 %collective-permute-start.21 = (bf16[192,256]{1,0:T(8,128)(2,1)S(1)}, bf16[192,256]{1,0:T(8,128)(2,1)S(1)}, u32[]{:S(2)}, u32[]{:S(2)}) collective-permute-start(bf16[192,256]{1,0:T(8,128)(2,1)S(1)} %get-tuple-element.151), channel_id=1, source_target_pairs={{0,2},{2,0},{1,3},{3,1},{4,6},{6,4},{5,7},{7,5},{8,10},{10,8},{9,1... | collective-permute-start | bytes 294920 | tf_op jit(solution)/shard_map/ppermute | solution.py:1001
  137.0 21.8 %collective-permute-start.29 = (bf16[192,768]{1,0:T(8,128)(2,1)S(1)}, bf16[192,768]{1,0:T(8,128)(2,1)S(1)}, u32[]{:S(2)}, u32[]{:S(2)}) collective-permute-start(bf16[192,768]{1,0:T(8,128)(2,1)S(1)} %get-tuple-element.171), channel_id=1, source_target_pairs={{0,1},{1,0},{2,3},{3,2},{4,5},{5,4},{6,7},{7,6},{8,9},{9,8},{10,11... | collective-permute-start | bytes 884744 | tf_op jit(solution)/shard_map/ppermute | solution.py:997
  137.0 16.5 %collective-permute-start.30 = (bf16[192,768]{1,0:T(8,128)(2,1)S(1)}, bf16[192,768]{1,0:T(8,128)(2,1)}, u32[]{:S(2)}, u32[]{:S(2)}) collective-permute-start(bf16[192,768]{1,0:T(8,128)(2,1)S(1)} %get-tuple-element.173), channel_id=1, source_target_pairs={{0,1},{1,0},{2,3},{3,2},{4,5},{5,4},{6,7},{7,6},{8,9},{9,8},{10,11... | collective-permute-start | bytes 884744 | tf_op jit(solution)/shard_map/ppermute | solution.py:997
  137.5 21.3 %collective-permute-start.31 = (bf16[512,768]{1,0:T(8,128)(2,1)S(1)}, bf16[512,768]{1,0:T(8,128)(2,1)}, u32[]{:S(2)}, u32[]{:S(2)}) collective-permute-start(bf16[512,768]{1,0:T(8,128)(2,1)S(1)} %fence.19.refs_13_), channel_id=1, source_target_pairs={{0,2},{2,0},{1,3},{3,1},{4,6},{6,4},{5,7},{7,5},{8,10},{10,8},{9,1... | collective-permute-start | bytes 2359304 | tf_op jit(solution)/shard_map/ppermute | solution.py:1001
  155.3 19.7 %collective-permute-start.32 = (bf16[192,768]{1,0:T(8,128)(2,1)S(1)}, bf16[192,768]{1,0:T(8,128)(2,1)S(1)}, u32[]{:S(2)}, u32[]{:S(2)}) collective-permute-start(bf16[192,768]{1,0:T(8,128)(2,1)S(1)} %add_convert_fusion.5.refs_17_), channel_id=1, source_target_pairs={{0,2},{2,0},{1,3},{3,1},{4,6},{6,4},{5,7},{7,5},{8,10},{10,8},{9,1... | collective-permute-start | bytes 884744 | tf_op jit(solution)/shard_map/ppermute | solution.py:1001
  185.6 20.5 %collective-permute-start.34 = (bf16[512,768]{1,0:T(8,128)(2,1)S(1)}, bf16[512,768]{1,0:T(8,128)(2,1)}, u32[]{:S(2)}, u32[]{:S(2)}) collective-permute-start(bf16[512,768]{1,0:T(8,128)(2,1)S(1)} %fusion.3.p0_ref), channel_id=1, source_target_pairs={{0,2},{2,0},{1,3},{3,1},{4,6},{6,4},{5,7},{7,5},{8,10},{10,8},{9,1... | collective-permute-start | bytes 2359304 | tf_op jit(solution)/shard_map/ppermute | solution.py:1001
  186.8 19.2 %collective-permute-start.33 = (bf16[512,768]{1,0:T(8,128)(2,1)S(1)}, bf16[512,768]{1,0:T(8,128)(2,1)S(1)}, u32[]{:S(2)}, u32[]{:S(2)}) collective-permute-start(bf16[512,768]{1,0:T(8,128)(2,1)S(1)} %fusion.3.p0_ref), channel_id=1, source_target_pairs={{0,1},{1,0},{2,3},{3,2},{4,5},{5,4},{6,7},{7,6},{8,9},{9,8},{10,11... | collective-permute-start | bytes 2359304 | tf_op jit(solution)/shard_map/ppermute | solution.py:997
  188.1 15.2 %collective-permute-start.36 = (bf16[384,768]{1,0:T(8,128)(2,1)S(1)}, bf16[384,768]{1,0:T(8,128)(2,1)S(1)}, u32[]{:S(2)}, u32[]{:S(2)}) collective-permute-start(bf16[384,768]{1,0:T(8,128)(2,1)S(1)} %copy-done.15), channel_id=1, source_target_pairs={{0,4},{4,0},{1,5},{5,1},{2,6},{6,2},{3,7},{7,3},{8,12},{12,8},{9,1... | collective-permute-start | bytes 1769480 | tf_op jit(solution)/shard_map/ppermute | solution.py:1149
  215.5 27.3 %collective-permute-start.44 = (bf16[768,768]{1,0:T(8,128)(2,1)}, bf16[768,768]{1,0:T(8,128)(2,1)S(1)}, u32[]{:S(2)}, u32[]{:S(2)}) collective-permute-start(bf16[768,768]{1,0:T(8,128)(2,1)} %all-gather.2.cloned.1.call-done.mine_ref), channel_id=1, source_target_pairs={{0,4},{4,0},{1,5},{5,1},{2,6},{6,2},{3,7},{7,3},{8,12},{12,8},{9,1... | collective-permute-start | bytes 3538952 | tf_op jit(solution)/shard_map/ppermute | solution.py:1154
  218.3 20.5 %collective-permute-start.41 = (bf16[528,768]{1,0:T(8,128)(2,1)S(1)}, bf16[528,768]{1,0:T(8,128)(2,1)S(1)}, u32[]{:S(2)}, u32[]{:S(2)}) collective-permute-start(bf16[528,768]{1,0:T(8,128)(2,1)S(1)} %chip_sum.1.refs_4_), channel_id=1, source_target_pairs={{0,2},{2,0},{1,3},{3,1},{4,6},{6,4},{5,7},{7,5},{8,10},{10,8},{9,1... | collective-permute-start | bytes 2433032 | tf_op jit(solution)/shard_map/ppermute | solution.py:1001
  219.9 26.0 %collective-permute-start.37 = (bf16[96,768]{1,0:T(8,128)(2,1)S(1)}, bf16[96,768]{1,0:T(8,128)(2,1)S(1)}, u32[]{:S(2)}, u32[]{:S(2)}) collective-permute-start(bf16[96,768]{1,0:T(8,128)(2,1)S(1)} %copy-done.23), channel_id=1, source_target_pairs={{0,8},{8,16},{16,24},{24,0},{1,9},{9,17},{17,25},{25,1},{2,10},{10... | collective-permute-start | bytes 442376 | tf_op jit(solution)/shard_map/ppermute | solution.py:1029
  220.8 25.0 %collective-permute-start.38 = (bf16[96,768]{1,0:T(8,128)(2,1)S(1)}, bf16[96,768]{1,0:T(8,128)(2,1)S(1)}, u32[]{:S(2)}, u32[]{:S(2)}) collective-permute-start(bf16[96,768]{1,0:T(8,128)(2,1)S(1)} %copy-done.22), channel_id=1, source_target_pairs={{0,16},{8,24},{16,0},{24,8},{1,17},{9,25},{17,1},{25,9},{2,18},{10... | collective-permute-start | bytes 442376 | tf_op jit(solution)/shard_map/ppermute | solution.py:1029
  221.9 23.9 %collective-permute-start.39 = (bf16[96,768]{1,0:T(8,128)(2,1)S(1)}, bf16[96,768]{1,0:T(8,128)(2,1)S(1)}, u32[]{:S(2)}, u32[]{:S(2)}) collective-permute-start(bf16[96,768]{1,0:T(8,128)(2,1)S(1)} %copy-done.19), channel_id=1, source_target_pairs={{0,24},{8,0},{16,8},{24,16},{1,25},{9,1},{17,9},{25,17},{2,26},{10... | collective-permute-start | bytes 442376 | tf_op jit(solution)/shard_map/ppermute | solution.py:1029
  247.6 20.4 %collective-permute-start.46 = (bf16[512,768]{1,0:T(8,128)(2,1)S(1)}, bf16[512,768]{1,0:T(8,128)(2,1)S(1)}, u32[]{:S(2)}, u32[]{:S(2)}) collective-permute-start(bf16[512,768]{1,0:T(8,128)(2,1)S(1)} %fence.26.p0_ref), channel_id=1, source_target_pairs={{0,2},{2,0},{1,3},{3,1},{4,6},{6,4},{5,7},{7,5},{8,10},{10,8},{9,1... | collective-permute-start | bytes 2359304 | tf_op jit(solution)/shard_map/ppermute | solution.py:1001
  253.2 21.6 %collective-permute-start.45 = (bf16[512,768]{1,0:T(8,128)(2,1)S(1)}, bf16[512,768]{1,0:T(8,128)(2,1)}, u32[]{:S(2)}, u32[]{:S(2)}) collective-permute-start(bf16[512,768]{1,0:T(8,128)(2,1)S(1)} %fence.26.p0_ref), channel_id=1, source_target_pairs={{0,1},{1,0},{2,3},{3,2},{4,5},{5,4},{6,7},{7,6},{8,9},{9,8},{10,11... | collective-permute-start | bytes 2359304 | tf_op jit(solution)/shard_map/ppermute | solution.py:997
  269.0 15.2 %collective-permute-start.51 = (bf16[400,768]{1,0:T(8,128)(2,1)S(1)}, bf16[400,768]{1,0:T(8,128)(2,1)S(1)}, u32[]{:S(2)}, u32[]{:S(2)}) collective-permute-start(bf16[400,768]{1,0:T(8,128)(2,1)S(1)} %copy-done.13), channel_id=1, source_target_pairs={{0,4},{4,0},{1,5},{5,1},{2,6},{6,2},{3,7},{7,3},{8,12},{12,8},{9,1... | collective-permute-start | bytes 1843208 | tf_op jit(solution)/shard_map/ppermute | solution.py:1174
  (54 other events, 404.7 us)
Sparse Core Ops, SparseCore 0:
  133.2 29.8 reduce-scatter.1
  182.5 32.9 all-gather.1

commit v13 on v12

--- a/solution.py
+++ b/solution.py
@@ -1115,8 +1115,6 @@
         far_sums.append(far_sum)
     left, right, *far_outs = kept
     outs += far_outs
-    feed_sum = (feed_keep.astype(F32) + lax.ppermute(feed_send, "x", SWAP).astype(F32)).astype(BF16)
-    feed_sum = lax.psum_scatter(feed_sum, "z", scatter_dimension=0, tiled=True)
     grad_residuals, lows, grads_attended, inner_sums = [], [], [], []
     for p in parts:
         grad, low, a0, a1, a2, a3, vector = middle_back(
@@ -1134,6 +1132,8 @@
     earlier = attend_backward(0, me, segment_ids, qt, extras[0], kn, kt, vn, attended[0], grads_attended[0], (),
                               (far, near, part[0]))
     there = other_chip(far)
+    feed_sum = fence(feed_keep, earlier[0]).astype(F32) + lax.ppermute(feed_send, "x", SWAP).astype(F32)
+    feed_sum = lax.psum_scatter(feed_sum.astype(BF16), "z", scatter_dimension=0, tiled=True)
     part_far = fence(part[2], earlier[0])
     part_far = (part_far.astype(F32) + other_core(part[3]).astype(F32)).astype(BF16)
     part_near = other_core(part[1])
@@ -1156,11 +1156,11 @@
     back_across = other_core(fence(back_across, quarter[-1], space=pltpu.VMEM))
     back_far = chip_sum(back_far, back_across, summed, ())
     back_there = other_chip(back_far)
-    share = final(me, [back_own, other_core(back_near), back_there], tokens, grad_residuals, vectors, (feed_other,))
+    share = final(me, [back_own, other_core(back_near), back_there], tokens, grad_residuals, vectors, ())
     if len(quarter) > 1:
         turns = [quarter[0]] + [turned(part, n + 1) for n, part in enumerate(quarter[1:])]
         held = second(turns, back_far, back_there, apart, (share,))
-        layer_out = place(me, [result, near, far, other_core(far)], BF16, (held,))
+        layer_out = place(me, [result, near, far, other_core(far)], BF16, (held, feed_other))
         mine = third(xz, gather_z(held), 16, (layer_out,))
     else:
         small = joined(back_far[-16:]) + joined(back_there[-16:]) + apart

time: 295 us -> 282 us (0.956)
  waiting for transfers between devices: 66.9 us -> 48.3 us
  starting transfers between devices: 38.3 us -> 49 us
  Pallas kernels: 148 us -> 143 us
    ppermute x14, waiting for transfers between devices: 30.1 us -> 15.7 us  [other_chip(): return lax.ppermute(value, 'y', SWAP)]
    ppermute x1, waiting for transfers between devices: 6.28 us -> 0.01 us  [local(): lax.ppermute(feed_send, 'x', SWAP).astype(F32)]
    pallas_call x25, Pallas kernels: 148 us -> 143 us  [kernel_call(): pl.pallas_call(body, out_shape=shapes if many else shapes[0], compiler_pa...]
    all_gather x1, waiting for transfers between devices: 5.81 us -> 10.2 us  [local(): feed_sum = lax.all_gather(fence(feed_sum, send), 'z', axis=0, tiled=True)]
    ppermute x1, starting transfers between devices: 1.57 us -> 5.81 us  [local(): got = lax.ppermute(send, 'x', SWAP)]
    ppermute x1, waiting for transfers between devices: 4 us -> 0.99 us  [local(): feed_other = lax.ppermute(feed_sum, 'x', SWAP)]
    ppermute x6, waiting for transfers between devices: 7.52 us -> 4.51 us  [turned(): lax.ppermute(values, 'z', [(n, (n + way) % size) for n in range(size)])]
    unnamed x48 -> x58, local copies, waits for them, and re-layouts: 8.89 us -> 9.89 us
  transfers between devices with their start and end apart: 54 -> 54, of which waited for: 15 -> 16; matrix products, arithmetic and copies ran while one was open for 6% -> 6% of each run, Pallas kernels for 46% -> 46%
where the time goes in v13:
time: 282 us
  Pallas kernels  143 us (51%)
  starting transfers between devices  49 us (17%)
  waiting for transfers between devices  48.3 us (17%)
  between operations  14.4 us (5%)
  local copies, waits for them, and re-layouts  11.4 us (4%)
  other arithmetic  11.1 us (4%)
  matrix products  4.62 us (2%)
    pallas_call x25, Pallas kernels, kernel_call(): pl.pallas_call(body, out_shape=shapes if many else shapes[0], compiler_pa...  143 us
    ppermute x14, waiting for transfers between devices, other_chip(): return lax.ppermute(value, 'y', SWAP)  15.7 us
    ppermute x14, starting transfers between devices, other_chip(): return lax.ppermute(value, 'y', SWAP)  12.4 us
    ppermute x6, starting transfers between devices, turned(): lax.ppermute(values, 'z', [(n, (n + way) % size) for n in range(size)])  11.4 us
    all_gather x1, waiting for transfers between devices, local(): feed_sum = lax.all_gather(fence(feed_sum, send), 'z', axis=0, tiled=True)  10.2 us
    unnamed x58, local copies, waits for them, and re-layouts  9.89 us
    ppermute x24, starting transfers between devices, other_core(): return lax.ppermute(value, 'core', SWAP)  6.03 us
    ppermute x1, starting transfers between devices, local(): got = lax.ppermute(send, 'x', SWAP)  5.81 us
  transfers between devices with their start and end apart: 54, of which 16 were waited for; matrix products, arithmetic and copies ran while one was open for 6% of the time, Pallas kernels for 46%

profile of v13, /device:TPU:0, one launch (start us, length us, event | category | flops | bytes accessed | tf_op | source)
XLA Modules:
  0.0 281.9 jit_solution(16011683639685856651)
XLA Ops:
  12.5 8.7 %project.1 = (bf16[2048,768]{1,0:T(8,128)(2,1)}, bf16[3,128,2048]{2,1,0:T(8,128)(2,1)}, bf16[192,2048]{1,0:T(8,128)(2,1)}, bf16[3,80,2048]{2,1,0:T(8,128)(2,1)},...) custom-call(bf16[2048,768]{1,0:T(8,128)(2,1)} %bitcast.17, ...), custom_call_target="tpu_custom_call" | custom-call | flops 6000000000 | bytes 14000000 | tf_op jit(solution)/shard_map/project/pallas_call | solution.py:84
  21.2 10.2 %attend_forward.2 = (bf16[4,192,256]{2,1,0:T(8,128)(2,1)}, bf16[3,16,1024]{2,1,0:T(8,128)(2,1)}, bf16[192,256]{1,0:T(8,128)(2,1)}, bf16[192,256]{1,0:T(8,128)(2,...) custom-call(s32[1]{0:T(128)} %bitcast.refs_0_.me_ref, s32[1,2048]{1,0:T(1,128)S(1)} %copy-done.18, ...), custom_call_target="tpu_custom_call" | custom-call | flops 8999999488 | bytes 5000000 | tf_op jit(solution)/shard_map/attend_forward/pallas_call | solution.py:84
  34.1 8.2 %attend_forward.3 = (bf16[4,192,256]{2,1,0:T(8,128)(2,1)}, bf16[3,16,1024]{2,1,0:T(8,128)(2,1)}, bf16[192,256]{1,0:T(8,128)(2,1)}, bf16[192,256]{1,0:T(8,128)(2,...) custom-call(s32[1]{0:T(128)} %bitcast.refs_0_.me_ref, s32[1,2048]{1,0:T(1,128)S(1)} %copy-done.18, ...), custom_call_target="tpu_custom_call" | custom-call | flops 8999999488 | bytes 5000000 | tf_op jit(solution)/shard_map/attend_forward/pallas_call | solution.py:84
  53.8 13.0 %feed_near.1 = (bf16[512,768]{1,0:T(8,128)(2,1)}, bf16[512,768]{1,0:T(8,128)(2,1)}, bf16[256,768]{1,0:T(8,128)(2,1)}, bf16[256,768]{1,0:T(8,128)(2,1)S(1)}, bf16...) custom-call(s32[1]{0:T(128)} %bitcast.refs_0_.me_ref, ...), custom_call_target="tpu_custom_call" | custom-call | flops 15000000512 | bytes 12000000 | tf_op jit(solution)/shard_map/feed_near/pallas_call | solution.py:84
  68.6 6.5 %feed_far.2 = (bf16[2,1024,768]{2,1,0:T(8,128)(2,1)}, bf16[2,1024,768]{2,1,0:T(8,128)(2,1)}, bf16[512,768]{1,0:T(8,128)(2,1)}, bf16[512,768]{1,0:T(8,128)(2,1)},...) custom-call(s32[1]{0:T(128)} %bitcast.refs_0_.me_ref, ...), custom_call_target="tpu_custom_call" | custom-call | flops 5000000000 | bytes 8000000 | tf_op jit(solution)/shard_map/feed_far/pallas_call | solution.py:84
  80.8 6.5 %feed_far.3 = (bf16[2,1024,768]{2,1,0:T(8,128)(2,1)}, bf16[2,1024,768]{2,1,0:T(8,128)(2,1)}, bf16[512,768]{1,0:T(8,128)(2,1)}, bf16[512,768]{1,0:T(8,128)(2,1)},...) custom-call(s32[1]{0:T(128)} %bitcast.refs_0_.me_ref, ...), custom_call_target="tpu_custom_call", output_to_operand_aliasing={{0}: (7, {}), {1}: (8, {}), {2}: (9, {}), {3}: (10, {})} | custom-call | flops 5000000000 | bytes 8000000 | tf_op jit(solution)/shard_map/feed_far/pallas_call | solution.py:84
  87.3 3.9 %collective-permute-done.17.refs_1_.b2_ref = bf16[256,768]{1,0:T(8,128)(2,1)S(1)} collective-permute-done((bf16[256,768]{1,0:T(8,128)(2,1)S(1)}, bf16[256,768]{1,0:T(8,128)(2,1)S(1)}, u32[]{:S(2)}, u32[]{:S(2)}) %collective-permute-start.17) | collective-permute-done | bytes 393248 | tf_op jit(solution)/shard_map/ppermute | solution.py:1001
  92.0 7.4 %feed_grad.1 = (bf16[768,768]{1,0:T(8,128)(2,1)}, bf16[768,768]{1,0:T(8,128)(2,1)}) custom-call(s32[2]{0:T(128)S(1)} %pad_add_fusion.xz_ref.refs_0_, bf16[2,1024,768]{2,1,0:T(8,128)(2,1)} %get-tuple-element.143.left_ref, bf16[2,1024,768]{2,1,0:T(8,128)(2,1)} %get-tuple-element.144.right_ref, bf16[2,768,768]{2,1,0:T(8,128)(2,1)} %get-tuple-element.145.before_ref), custom_call_target="tpu_custom_call" | custom-call | flops 5000000000 | bytes 10000000 | tf_op jit(solution)/shard_map/feed_grad/pallas_call | solution.py:84
  105.9 3.7 %middle_back.3 = (f32[256,768]{1,0:T(8,128)}, bf16[256,768]{1,0:T(8,128)(2,1)}, bf16[192,256]{1,0:T(8,128)(2,1)}, bf16[192,256]{1,0:T(8,128)(2,1)}, bf16[192,256...) custom-call(s32[1]{0:T(128)} %bitcast.refs_0_.me_ref, ...), custom_call_target="tpu_custom_call" | custom-call | flops 2000000000 | bytes 4000000 | tf_op jit(solution)/shard_map/middle_back/pallas_call | solution.py:84
  110.2 3.5 %collective-permute-done.19.b2_ref = bf16[256,768]{1,0:T(8,128)(2,1)S(1)} collective-permute-done((bf16[256,768]{1,0:T(8,128)(2,1)S(1)}, bf16[256,768]{1,0:T(8,128)(2,1)S(1)}, u32[]{:S(2)}, u32[]{:S(2)}) %collective-permute-start.19) | collective-permute-done | bytes 393248 | tf_op jit(solution)/shard_map/ppermute | solution.py:1001
  114.3 3.6 %middle_back.2 = (f32[256,768]{1,0:T(8,128)}, bf16[256,768]{1,0:T(8,128)(2,1)}, bf16[192,256]{1,0:T(8,128)(2,1)}, bf16[192,256]{1,0:T(8,128)(2,1)S(1)}, bf16[192...) custom-call(s32[1]{0:T(128)} %bitcast.refs_0_.me_ref, ...), custom_call_target="tpu_custom_call" | custom-call | flops 2000000000 | bytes 4000000 | tf_op jit(solution)/shard_map/middle_back/pallas_call | solution.py:84
  127.2 14.3 %attend_backward.2 = (bf16[192,1024]{1,0:T(8,128)(2,1)}, f32[192,2048]{1,0:T(8,128)}, f32[192,2048]{1,0:T(8,128)}) custom-call(s32[1]{0:T(128)} %bitcast.refs_0_.me_ref, s32[1,2048]{1,0:T(1,128)S(1)} %copy-done.18, s32[1,2048]{1,0:T(1,128)S(1)} %copy-done.18, bf16[3,128,2048]{2,1,0:T(8,128)(2,1)} %get-tuple-element.114.refs_3_, ...), custom_call_target="tpu_custom_call" | custom-call | flops 16000000000 | bytes 10000000 | tf_op jit(solution)/shard_map/attend_backward/pallas_call | solution.py:84
  149.6 12.8 %attend_backward.3.refs_1_.g_ref = bf16[576,2048]{1,0:T(8,128)(2,1)} custom-call(s32[1]{0:T(128)} %bitcast.refs_0_.me_ref, s32[1,2048]{1,0:T(1,128)S(1)} %copy-done.18, s32[1,2048]{1,0:T(1,128)S(1)} %copy-done.18, bf16[3,128,2048]{2,1,0:T(8,128)(2,1)} %get-tuple-element.114.refs_3_, bf16[3,16,1024]{2,1,0:T(8,128)(2,1)} %get-tuple-element.121.rest_0_.refs_4_, ...), custom_call_target="tpu_custom_call" | custom-call | flops 16000000000 | bytes 10000000 | tf_op jit(solution)/shard_map/attend_backward/pallas_call | solution.py:84
  163.5 4.6 %convolution_convert_fusion.g_ref = bf16[576,768]{1,0:T(8,128)(2,1)S(1)} fusion(bf16[576,2048]{1,0:T(8,128)(2,1)} %attend_backward.3.refs_1_.g_ref, bf16[2048,768]{1,0:T(8,128)(2,1)} %get-tuple-element.174), kind=kOutput, calls=%fused_computation.7 | convolution fusion | flops 1812381696 | bytes 6389760 | tf_op jit(solution)/shard_map/dot_general | solution.py:24
  172.5 5.8 %collective-permute-start.36 = (bf16[384,768]{1,0:T(8,128)(2,1)}, bf16[384,768]{1,0:T(8,128)(2,1)S(1)}, u32[]{:S(2)}, u32[]{:S(2)}) collective-permute-start(bf16[384,768]{1,0:T(8,128)(2,1)} %get-tuple-element.175.refs_1_.rest_5_), channel_id=1, source_target_pairs={{0,4},{4,0},{1,5},{5,1},{2,6},{6,2},{3,7},{7,3},{8,12},{12,8},{9,1... | collective-permute-start | bytes 1769480 | tf_op jit(solution)/shard_map/ppermute | solution.py:1149
  178.4 11.0 %tail.1 = (bf16[512,768]{1,0:T(8,128)(2,1)}, bf16[512,768]{1,0:T(8,128)(2,1)}, bf16[512,768]{1,0:T(8,128)(2,1)}, bf16[528,768]{1,0:T(8,128)(2,1)S(1)}, f32[8,768]{1,0:T(8,128)}, /*index=5*/f32[8,768]{1,0:T(8,128)}) custom-call(s32[1]{0:T(128)} %bitcast.refs_0_.me_ref, bf16[576,2048]{1,0:T(8,128)(2,1)} %attend_backward.3.refs_1_.g_ref, ...), custom_call_target="tpu_custom_call" | custom-call | flops 4000000000 | bytes 10000000 | tf_op jit(solution)/shard_map/tail/pallas_call | solution.py:84
  201.6 10.2 %all-gather.2.cloned.1.call-done.mine_ref = bf16[768,768]{1,0:T(8,128)(2,1)} async-done(((bf16[192,768]{1,0:T(8,128)(2,1)}), bf16[768,768]{1,0:T(8,128)(2,1)}) %all-gather.2.cloned.1.call-update) | async-done | bytes 1179664 | tf_op jit(solution)/shard_map/all_gather | solution.py:1153
  215.3 5.2 %collective-permute-done.41.b2_ref.refs_5_ = bf16[528,768]{1,0:T(8,128)(2,1)S(1)} collective-permute-done((bf16[528,768]{1,0:T(8,128)(2,1)}, bf16[528,768]{1,0:T(8,128)(2,1)S(1)}, u32[]{:S(2)}, u32[]{:S(2)}) %collective-permute-start.41) | collective-permute-done | bytes 811040 | tf_op jit(solution)/shard_map/ppermute | solution.py:1001
  221.5 6.1 %collective-permute-start.39 = (bf16[96,768]{1,0:T(8,128)(2,1)S(1)}, bf16[96,768]{1,0:T(8,128)(2,1)S(1)}, u32[]{:S(2)}, u32[]{:S(2)}) collective-permute-start(bf16[96,768]{1,0:T(8,128)(2,1)S(1)} %copy-done.24), channel_id=1, source_target_pairs={{0,24},{8,0},{16,8},{24,16},{1,25},{9,1},{17,9},{25,17},{2,26},{10... | collective-permute-start | bytes 442376 | tf_op jit(solution)/shard_map/ppermute | solution.py:1029
  241.3 4.7 %place.2.refs_5_ = bf16[2048,768]{1,0:T(8,128)(2,1)} custom-call(s32[1]{0:T(128)} %bitcast.refs_0_.me_ref, bf16[512,768]{1,0:T(8,128)(2,1)S(1)} %copy-done.10, bf16[512,768]{1,0:T(8,128)(2,1)S(1)} %copy-done.8, bf16[512,768]{1,0:T(8,128)(2,1)} %collective-permute-done.34.refs_4_.p2_ref, bf16[512,768]{1,0:T(8,128)(2,1)} %collective-permute-done.35.p3_ref, ...), custom_call_target="tpu_custom_call" | custom-call | flops 1000000 | bytes 9000000 | tf_op jit(solution)/shard_map/place/pallas_call | solution.py:84
  246.0 4.5 %collective-permute-done.48.refs_3_ = bf16[112,768]{1,0:T(8,128)(2,1)S(1)} collective-permute-done((bf16[112,768]{1,0:T(8,128)(2,1)}, bf16[112,768]{1,0:T(8,128)(2,1)S(1)}, u32[]{:S(2)}, u32[]{:S(2)}) %collective-permute-start.48) | collective-permute-done | bytes 172064 | tf_op jit(solution)/shard_map/ppermute | solution.py:1029
  253.0 4.3 %collective-permute-start.51 = (bf16[400,768]{1,0:T(8,128)(2,1)S(1)}, bf16[400,768]{1,0:T(8,128)(2,1)S(1)}, u32[]{:S(2)}, u32[]{:S(2)}) collective-permute-start(bf16[400,768]{1,0:T(8,128)(2,1)S(1)} %copy-done.19), channel_id=1, source_target_pairs={{0,4},{4,0},{1,5},{5,1},{2,6},{6,2},{3,7},{7,3},{8,12},{12,8},{9,1... | collective-permute-start | bytes 1843208 | tf_op jit(solution)/shard_map/ppermute | solution.py:1174
  261.6 5.2 %place.3.rest_2_ = f32[2048,768]{1,0:T(8,128)} custom-call(s32[1]{0:T(128)} %bitcast.refs_0_.me_ref, bf16[512,768]{1,0:T(8,128)(2,1)S(1)} %fence.28.p0_ref, bf16[512,768]{1,0:T(8,128)(2,1)} %collective-permute-done.45.p1_ref, bf16[512,768]{1,0:T(8,128)(2,1)S(1)} %fence.29.p2_ref, bf16[512,768]{1,0:T(8,128)(2,1)S(1)} %collective-permute-done.50.p3_ref, ...), custom_call_target="tpu_custom_call" | custom-call | flops 1000000 | bytes 9000000 | tf_op jit(solution)/shard_map/place/pallas_call | solution.py:84
  266.8 5.0 %collective-permute-done.51.other_ref = bf16[400,768]{1,0:T(8,128)(2,1)S(1)} collective-permute-done((bf16[400,768]{1,0:T(8,128)(2,1)S(1)}, bf16[400,768]{1,0:T(8,128)(2,1)S(1)}, u32[]{:S(2)}, u32[]{:S(2)}) %collective-permute-start.51) | collective-permute-done | bytes 614432 | tf_op jit(solution)/shard_map/ppermute | solution.py:1174
  (196 shorter events, 98.7 us)
Async XLA Ops:
  7.2 171.1 %reduce-scatter.2.cloned.1.call-start = ((), (), s32[]{:S(2)}) async-start(), calls=%async_computation.1 | async-start | bytes 1474560 | tf_op jit(solution)/shard_map/reduce_scatter | solution.py:1136
  7.2 13.9 %collective-permute-start.1 = (bf16[192,768]{1,0:T(8,128)(2,1)}, bf16[192,768]{1,0:T(8,128)(2,1)S(1)}, u32[]{:S(2)}, u32[]{:S(2)}) collective-permute-start(bf16[192,768]{1,0:T(8,128)(2,1)} %w0_ref.7), channel_id=1, source_target_pairs={{0,2},{2,0},{1,3},{3,1},{4,6},{6,4},{5,7},{7,5},{8,10},{10,8},{9,1... | collective-permute-start | bytes 884744 | tf_op jit(solution)/shard_map/ppermute | solution.py:1001
  52.4 14.4 %collective-permute-start.13 = (bf16[256,768]{1,0:T(8,128)(2,1)S(1)}, bf16[256,768]{1,0:T(8,128)(2,1)S(1)}, u32[]{:S(2)}, u32[]{:S(2)}) collective-permute-start(bf16[256,768]{1,0:T(8,128)(2,1)S(1)} %get-tuple-element.128.refs_0_), channel_id=1, source_target_pairs={{0,2},{2,0},{1,3},{3,1},{4,6},{6,4},{5,7},{7,5},{8,10},{10,8},{9,1... | collective-permute-start | bytes 1179656 | tf_op jit(solution)/shard_map/ppermute | solution.py:1001
  78.5 27.4 %collective-permute-start.23 = (bf16[256,768]{1,0:T(8,128)(2,1)S(1)}, bf16[256,768]{1,0:T(8,128)(2,1)S(1)}, u32[]{:S(2)}, u32[]{:S(2)}) collective-permute-start(bf16[256,768]{1,0:T(8,128)(2,1)S(1)} %get-tuple-element.155), channel_id=1, source_target_pairs={{0,1},{1,0},{2,3},{3,2},{4,5},{5,4},{6,7},{7,6},{8,9},{9,8},{10,11... | collective-permute-start | bytes 1179656 | tf_op jit(solution)/shard_map/ppermute | solution.py:997
  101.2 19.6 %collective-permute-start.27 = (bf16[512,768]{1,0:T(8,128)(2,1)}, bf16[512,768]{1,0:T(8,128)(2,1)}, u32[]{:S(2)}, u32[]{:S(2)}) collective-permute-start(bf16[512,768]{1,0:T(8,128)(2,1)} %fence.19), channel_id=1, source_target_pairs={{0,1},{1,0},{2,3},{3,2},{4,5},{5,4},{6,7},{7,6},{8,9},{9,8},{10,11... | collective-permute-start | bytes 2359304 | tf_op jit(solution)/shard_map/ppermute | solution.py:997
  102.8 38.7 %collective-permute-start.43 = (bf16[768,768]{1,0:T(8,128)(2,1)}, bf16[768,768]{1,0:T(8,128)(2,1)}, u32[]{:S(2)}, u32[]{:S(2)}) collective-permute-start(bf16[768,768]{1,0:T(8,128)(2,1)} %get-tuple-element.146.refs_1_), channel_id=1, source_target_pairs={{0,4},{4,0},{1,5},{5,1},{2,6},{6,2},{3,7},{7,3},{8,12},{12,8},{9,1... | collective-permute-start | bytes 3538952 | tf_op jit(solution)/shard_map/ppermute | solution.py:1135
  105.9 20.2 %collective-permute-start.28 = (bf16[512,768]{1,0:T(8,128)(2,1)}, bf16[512,768]{1,0:T(8,128)(2,1)S(1)}, u32[]{:S(2)}, u32[]{:S(2)}) collective-permute-start(bf16[512,768]{1,0:T(8,128)(2,1)} %fence.21), channel_id=1, source_target_pairs={{0,1},{1,0},{2,3},{3,2},{4,5},{5,4},{6,7},{7,6},{8,9},{9,8},{10,11... | collective-permute-start | bytes 2359304 | tf_op jit(solution)/shard_map/ppermute | solution.py:997
  122.6 24.2 %collective-permute-start.20 = (bf16[192,256]{1,0:T(8,128)(2,1)S(1)}, bf16[192,256]{1,0:T(8,128)(2,1)S(1)}, u32[]{:S(2)}, u32[]{:S(2)}) collective-permute-start(bf16[192,256]{1,0:T(8,128)(2,1)S(1)} %get-tuple-element.150), channel_id=1, source_target_pairs={{0,1},{1,0},{2,3},{3,2},{4,5},{5,4},{6,7},{7,6},{8,9},{9,8},{10,11... | collective-permute-start | bytes 294920 | tf_op jit(solution)/shard_map/ppermute | solution.py:997
  123.7 24.3 %collective-permute-start.21 = (bf16[192,256]{1,0:T(8,128)(2,1)S(1)}, bf16[192,256]{1,0:T(8,128)(2,1)S(1)}, u32[]{:S(2)}, u32[]{:S(2)}) collective-permute-start(bf16[192,256]{1,0:T(8,128)(2,1)S(1)} %get-tuple-element.151), channel_id=1, source_target_pairs={{0,2},{2,0},{1,3},{3,1},{4,6},{6,4},{5,7},{7,5},{8,10},{10,8},{9,1... | collective-permute-start | bytes 294920 | tf_op jit(solution)/shard_map/ppermute | solution.py:1001
  126.0 23.6 %collective-permute-start.29 = (bf16[192,768]{1,0:T(8,128)(2,1)S(1)}, bf16[192,768]{1,0:T(8,128)(2,1)S(1)}, u32[]{:S(2)}, u32[]{:S(2)}) collective-permute-start(bf16[192,768]{1,0:T(8,128)(2,1)S(1)} %get-tuple-element.171), channel_id=1, source_target_pairs={{0,1},{1,0},{2,3},{3,2},{4,5},{5,4},{6,7},{7,6},{8,9},{9,8},{10,11... | collective-permute-start | bytes 884744 | tf_op jit(solution)/shard_map/ppermute | solution.py:997
  126.1 23.4 %collective-permute-start.31 = (bf16[512,768]{1,0:T(8,128)(2,1)S(1)}, bf16[512,768]{1,0:T(8,128)(2,1)}, u32[]{:S(2)}, u32[]{:S(2)}) collective-permute-start(bf16[512,768]{1,0:T(8,128)(2,1)S(1)} %fence.20.refs_13_), channel_id=1, source_target_pairs={{0,2},{2,0},{1,3},{3,1},{4,6},{6,4},{5,7},{7,5},{8,10},{10,8},{9,1... | collective-permute-start | bytes 2359304 | tf_op jit(solution)/shard_map/ppermute | solution.py:1001
  144.7 67.0 %all-gather.2.cloned.1.call-start = ((), (), s32[]{:S(2)}) async-start(), calls=%async_computation.2 | async-start | bytes 1474560 | tf_op jit(solution)/shard_map/all_gather | solution.py:1153
  146.8 15.6 %collective-permute-start.32 = (bf16[192,768]{1,0:T(8,128)(2,1)S(1)}, bf16[192,768]{1,0:T(8,128)(2,1)S(1)}, u32[]{:S(2)}, u32[]{:S(2)}) collective-permute-start(bf16[192,768]{1,0:T(8,128)(2,1)S(1)} %add_convert_fusion.5.refs_17_), channel_id=1, source_target_pairs={{0,2},{2,0},{1,3},{3,1},{4,6},{6,4},{5,7},{7,5},{8,10},{10,8},{9,1... | collective-permute-start | bytes 884744 | tf_op jit(solution)/shard_map/ppermute | solution.py:1001
  171.6 20.8 %collective-permute-start.34 = (bf16[512,768]{1,0:T(8,128)(2,1)S(1)}, bf16[512,768]{1,0:T(8,128)(2,1)}, u32[]{:S(2)}, u32[]{:S(2)}) collective-permute-start(bf16[512,768]{1,0:T(8,128)(2,1)S(1)} %fusion.3.p0_ref), channel_id=1, source_target_pairs={{0,2},{2,0},{1,3},{3,1},{4,6},{6,4},{5,7},{7,5},{8,10},{10,8},{9,1... | collective-permute-start | bytes 2359304 | tf_op jit(solution)/shard_map/ppermute | solution.py:1001
  172.4 20.0 %collective-permute-start.33 = (bf16[512,768]{1,0:T(8,128)(2,1)S(1)}, bf16[512,768]{1,0:T(8,128)(2,1)S(1)}, u32[]{:S(2)}, u32[]{:S(2)}) collective-permute-start(bf16[512,768]{1,0:T(8,128)(2,1)S(1)} %fusion.3.p0_ref), channel_id=1, source_target_pairs={{0,1},{1,0},{2,3},{3,2},{4,5},{5,4},{6,7},{7,6},{8,9},{9,8},{10,11... | collective-permute-start | bytes 2359304 | tf_op jit(solution)/shard_map/ppermute | solution.py:997
  172.5 19.9 %collective-permute-start.36 = (bf16[384,768]{1,0:T(8,128)(2,1)}, bf16[384,768]{1,0:T(8,128)(2,1)S(1)}, u32[]{:S(2)}, u32[]{:S(2)}) collective-permute-start(bf16[384,768]{1,0:T(8,128)(2,1)} %get-tuple-element.175.refs_1_.rest_5_), channel_id=1, source_target_pairs={{0,4},{4,0},{1,5},{5,1},{2,6},{6,2},{3,7},{7,3},{8,12},{12,8},{9,1... | collective-permute-start | bytes 1769480 | tf_op jit(solution)/shard_map/ppermute | solution.py:1149
  200.3 20.3 %collective-permute-start.41 = (bf16[528,768]{1,0:T(8,128)(2,1)}, bf16[528,768]{1,0:T(8,128)(2,1)S(1)}, u32[]{:S(2)}, u32[]{:S(2)}) collective-permute-start(bf16[528,768]{1,0:T(8,128)(2,1)} %chip_sum.1.refs_4_), channel_id=1, source_target_pairs={{0,2},{2,0},{1,3},{3,1},{4,6},{6,4},{5,7},{7,5},{8,10},{10,8},{9,1... | collective-permute-start | bytes 2433032 | tf_op jit(solution)/shard_map/ppermute | solution.py:1001
  211.8 27.4 %collective-permute-start.44 = (bf16[768,768]{1,0:T(8,128)(2,1)}, bf16[768,768]{1,0:T(8,128)(2,1)S(1)}, u32[]{:S(2)}, u32[]{:S(2)}) collective-permute-start(bf16[768,768]{1,0:T(8,128)(2,1)} %all-gather.2.cloned.1.call-done.mine_ref), channel_id=1, source_target_pairs={{0,4},{4,0},{1,5},{5,1},{2,6},{6,2},{3,7},{7,3},{8,12},{12,8},{9,1... | collective-permute-start | bytes 3538952 | tf_op jit(solution)/shard_map/ppermute | solution.py:1154
  213.3 24.3 %collective-permute-start.35 = (bf16[512,768]{1,0:T(8,128)(2,1)}, bf16[512,768]{1,0:T(8,128)(2,1)}, u32[]{:S(2)}, u32[]{:S(2)}) collective-permute-start(bf16[512,768]{1,0:T(8,128)(2,1)} %collective-permute-done.34.refs_4_.p2_ref), channel_id=1, source_target_pairs={{0,1},{1,0},{2,3},{3,2},{4,5},{5,4},{6,7},{7,6},{8,9},{9,8},{10,11... | collective-permute-start | bytes 2359304 | tf_op jit(solution)/shard_map/ppermute | solution.py:997
  213.3 18.5 %collective-permute-start.37 = (bf16[96,768]{1,0:T(8,128)(2,1)S(1)}, bf16[96,768]{1,0:T(8,128)(2,1)S(1)}, u32[]{:S(2)}, u32[]{:S(2)}) collective-permute-start(bf16[96,768]{1,0:T(8,128)(2,1)S(1)} %copy-done.28), channel_id=1, source_target_pairs={{0,8},{8,16},{16,24},{24,0},{1,9},{9,17},{17,25},{25,1},{2,10},{10... | collective-permute-start | bytes 442376 | tf_op jit(solution)/shard_map/ppermute | solution.py:1029
  214.3 17.5 %collective-permute-start.38 = (bf16[96,768]{1,0:T(8,128)(2,1)S(1)}, bf16[96,768]{1,0:T(8,128)(2,1)S(1)}, u32[]{:S(2)}, u32[]{:S(2)}) collective-permute-start(bf16[96,768]{1,0:T(8,128)(2,1)S(1)} %copy-done.27), channel_id=1, source_target_pairs={{0,16},{8,24},{16,0},{24,8},{1,17},{9,25},{17,1},{25,9},{2,18},{10... | collective-permute-start | bytes 442376 | tf_op jit(solution)/shard_map/ppermute | solution.py:1029
  233.5 18.5 %collective-permute-start.46 = (bf16[512,768]{1,0:T(8,128)(2,1)S(1)}, bf16[512,768]{1,0:T(8,128)(2,1)S(1)}, u32[]{:S(2)}, u32[]{:S(2)}) collective-permute-start(bf16[512,768]{1,0:T(8,128)(2,1)S(1)} %fence.28.p0_ref), channel_id=1, source_target_pairs={{0,2},{2,0},{1,3},{3,1},{4,6},{6,4},{5,7},{7,5},{8,10},{10,8},{9,1... | collective-permute-start | bytes 2359304 | tf_op jit(solution)/shard_map/ppermute | solution.py:1001
  239.1 22.5 %collective-permute-start.45 = (bf16[512,768]{1,0:T(8,128)(2,1)S(1)}, bf16[512,768]{1,0:T(8,128)(2,1)}, u32[]{:S(2)}, u32[]{:S(2)}) collective-permute-start(bf16[512,768]{1,0:T(8,128)(2,1)S(1)} %fence.28.p0_ref), channel_id=1, source_target_pairs={{0,1},{1,0},{2,3},{3,2},{4,5},{5,4},{6,7},{7,6},{8,9},{9,8},{10,11... | collective-permute-start | bytes 2359304 | tf_op jit(solution)/shard_map/ppermute | solution.py:997
  253.0 18.8 %collective-permute-start.51 = (bf16[400,768]{1,0:T(8,128)(2,1)S(1)}, bf16[400,768]{1,0:T(8,128)(2,1)S(1)}, u32[]{:S(2)}, u32[]{:S(2)}) collective-permute-start(bf16[400,768]{1,0:T(8,128)(2,1)S(1)} %copy-done.19), channel_id=1, source_target_pairs={{0,4},{4,0},{1,5},{5,1},{2,6},{6,2},{3,7},{7,3},{8,12},{12,8},{9,1... | collective-permute-start | bytes 1843208 | tf_op jit(solution)/shard_map/ppermute | solution.py:1174
  (59 other events, 416.6 us)
Sparse Core Ops, SparseCore 0:
  144.9 32.3 reduce-scatter.1
  178.8 32.9 all-gather.1

commit v14 on v13

--- a/solution.py
+++ b/solution.py
@@ -834,7 +834,7 @@
     return kernel_call(
         body,
         (*parts, one, two, apart, *after),
-        free_in=tuple(range(1, count + 2)) + tuple(range(count + 3, count + 3 + len(after))),
+        free_in=tuple(range(1, count)) + tuple(range(count + 3, count + 3 + len(after))),
         grid=(1,),
         in_specs=[const((rows, features))] * count + [last, last, const(apart.shape)]
         + [pl.BlockSpec(memory_space=pl.ANY)] * len(after),
@@ -934,7 +934,6 @@
     return kernel_call(
         final_body,
         (me, *sums, tokens, *grads, vectors, *after),
-        free_in=(2, 3) + tuple(range(6 + PARTS, 6 + PARTS + len(after))),
         free_out=(0,),
         grid_spec=pltpu.PrefetchScalarGridSpec(
             num_scalar_prefetch=1,

time: 282 us -> 279 us (0.989)
  starting transfers between devices: 49 us -> 37.4 us
  waiting for transfers between devices: 48.3 us -> 53.5 us
  Pallas kernels: 143 us -> 146 us
    ppermute x14, waiting for transfers between devices: 15.7 us -> 26.7 us  [other_chip(): return lax.ppermute(value, 'y', SWAP)]
    all_gather x1, waiting for transfers between devices: 10.2 us -> 5.65 us  [local(): feed_sum = lax.all_gather(fence(feed_sum, send), 'z', axis=0, tiled=True)]
    ppermute x1, starting transfers between devices: 5.81 us -> 1.65 us  [local(): got = lax.ppermute(send, 'x', SWAP)]
    pallas_call x25, Pallas kernels: 143 us -> 146 us  [kernel_call(): pl.pallas_call(body, out_shape=shapes if many else shapes[0], compiler_pa...]
    ppermute x1, starting transfers between devices: 4.32 us -> 1.43 us  [local(): lax.ppermute(mine, 'x', SWAP)]
    unnamed x58 -> x56, local copies, waits for them, and re-layouts: 9.89 us -> 8.12 us
  transfers between devices with their start and end apart: 54 -> 54, of which waited for: 16 -> 16; matrix products, arithmetic and copies ran while one was open for 6% -> 6% of each run, Pallas kernels for 46% -> 48%
where the time goes in v14:
time: 279 us; the launch traced here: 277 us
  Pallas kernels  146 us (52%)
  waiting for transfers between devices  53.5 us (19%)
  starting transfers between devices  37.4 us (13%)
  between operations  14.4 us (5%)
  other arithmetic  11.1 us (4%)
  local copies, waits for them, and re-layouts  9.62 us (3%)
  matrix products  4.62 us (2%)
    pallas_call x25, Pallas kernels, kernel_call(): pl.pallas_call(body, out_shape=shapes if many else shapes[0], compiler_pa...  146 us
    ppermute x14, waiting for transfers between devices, other_chip(): return lax.ppermute(value, 'y', SWAP)  26.7 us
    ppermute x14, starting transfers between devices, other_chip(): return lax.ppermute(value, 'y', SWAP)  10.7 us
    ppermute x6, starting transfers between devices, turned(): lax.ppermute(values, 'z', [(n, (n + way) % size) for n in range(size)])  10.2 us
    unnamed x56, local copies, waits for them, and re-layouts  8.12 us
    ppermute x24, starting transfers between devices, other_core(): return lax.ppermute(value, 'core', SWAP)  6.09 us
    all_gather x1, waiting for transfers between devices, local(): feed_sum = lax.all_gather(fence(feed_sum, send), 'z', axis=0, tiled=True)  5.65 us
  transfers between devices with their start and end apart: 54, of which 16 were waited for; matrix products, arithmetic and copies ran while one was open for 6% of the time, Pallas kernels for 48%

profile of v14, /device:TPU:0, one launch (start us, length us, event | category | flops | bytes accessed | tf_op | source)
XLA Modules:
  0.0 277.0 jit_solution(4170354965697212720)
XLA Ops:
  12.5 8.6 %project.1 = (bf16[2048,768]{1,0:T(8,128)(2,1)}, bf16[3,128,2048]{2,1,0:T(8,128)(2,1)}, bf16[192,2048]{1,0:T(8,128)(2,1)}, bf16[3,80,2048]{2,1,0:T(8,128)(2,1)},...) custom-call(bf16[2048,768]{1,0:T(8,128)(2,1)} %bitcast.17, ...), custom_call_target="tpu_custom_call" | custom-call | flops 6000000000 | bytes 14000000 | tf_op jit(solution)/shard_map/project/pallas_call | solution.py:84
  21.2 9.0 %attend_forward.2 = (bf16[4,192,256]{2,1,0:T(8,128)(2,1)}, bf16[3,16,1024]{2,1,0:T(8,128)(2,1)}, bf16[192,256]{1,0:T(8,128)(2,1)}, bf16[192,256]{1,0:T(8,128)(2,...) custom-call(s32[1]{0:T(128)} %bitcast.refs_0_.me_ref, s32[1,2048]{1,0:T(1,128)S(1)} %copy-done.18, ...), custom_call_target="tpu_custom_call" | custom-call | flops 8999999488 | bytes 5000000 | tf_op jit(solution)/shard_map/attend_forward/pallas_call | solution.py:84
  32.8 11.1 %attend_forward.3 = (bf16[4,192,256]{2,1,0:T(8,128)(2,1)}, bf16[3,16,1024]{2,1,0:T(8,128)(2,1)}, bf16[192,256]{1,0:T(8,128)(2,1)}, bf16[192,256]{1,0:T(8,128)(2,...) custom-call(s32[1]{0:T(128)} %bitcast.refs_0_.me_ref, s32[1,2048]{1,0:T(1,128)S(1)} %copy-done.18, ...), custom_call_target="tpu_custom_call" | custom-call | flops 8999999488 | bytes 5000000 | tf_op jit(solution)/shard_map/attend_forward/pallas_call | solution.py:84
  55.5 13.0 %feed_near.1 = (bf16[512,768]{1,0:T(8,128)(2,1)}, bf16[512,768]{1,0:T(8,128)(2,1)}, bf16[256,768]{1,0:T(8,128)(2,1)}, bf16[256,768]{1,0:T(8,128)(2,1)S(1)}, bf16...) custom-call(s32[1]{0:T(128)} %bitcast.refs_0_.me_ref, ...), custom_call_target="tpu_custom_call" | custom-call | flops 15000000512 | bytes 12000000 | tf_op jit(solution)/shard_map/feed_near/pallas_call | solution.py:84
  70.2 6.5 %feed_far.2 = (bf16[2,1024,768]{2,1,0:T(8,128)(2,1)}, bf16[2,1024,768]{2,1,0:T(8,128)(2,1)}, bf16[512,768]{1,0:T(8,128)(2,1)}, bf16[512,768]{1,0:T(8,128)(2,1)},...) custom-call(s32[1]{0:T(128)} %bitcast.refs_0_.me_ref, ...), custom_call_target="tpu_custom_call" | custom-call | flops 5000000000 | bytes 8000000 | tf_op jit(solution)/shard_map/feed_far/pallas_call | solution.py:84
  82.4 6.5 %feed_far.3 = (bf16[2,1024,768]{2,1,0:T(8,128)(2,1)}, bf16[2,1024,768]{2,1,0:T(8,128)(2,1)}, bf16[512,768]{1,0:T(8,128)(2,1)}, bf16[512,768]{1,0:T(8,128)(2,1)},...) custom-call(s32[1]{0:T(128)} %bitcast.refs_0_.me_ref, ...), custom_call_target="tpu_custom_call", output_to_operand_aliasing={{0}: (7, {}), {1}: (8, {}), {2}: (9, {}), {3}: (10, {})} | custom-call | flops 5000000000 | bytes 8000000 | tf_op jit(solution)/shard_map/feed_far/pallas_call | solution.py:84
  88.9 3.9 %collective-permute-done.17.refs_1_.b2_ref = bf16[256,768]{1,0:T(8,128)(2,1)S(1)} collective-permute-done((bf16[256,768]{1,0:T(8,128)(2,1)S(1)}, bf16[256,768]{1,0:T(8,128)(2,1)S(1)}, u32[]{:S(2)}, u32[]{:S(2)}) %collective-permute-start.17) | collective-permute-done | bytes 393248 | tf_op jit(solution)/shard_map/ppermute | solution.py:1000
  93.6 7.4 %feed_grad.1 = (bf16[768,768]{1,0:T(8,128)(2,1)}, bf16[768,768]{1,0:T(8,128)(2,1)}) custom-call(s32[2]{0:T(128)S(1)} %pad_add_fusion.xz_ref.refs_0_, bf16[2,1024,768]{2,1,0:T(8,128)(2,1)} %get-tuple-element.143.left_ref, bf16[2,1024,768]{2,1,0:T(8,128)(2,1)} %get-tuple-element.144.right_ref, bf16[2,768,768]{2,1,0:T(8,128)(2,1)} %get-tuple-element.145.before_ref), custom_call_target="tpu_custom_call" | custom-call | flops 5000000000 | bytes 10000000 | tf_op jit(solution)/shard_map/feed_grad/pallas_call | solution.py:84
  105.9 3.7 %middle_back.3 = (f32[256,768]{1,0:T(8,128)}, bf16[256,768]{1,0:T(8,128)(2,1)}, bf16[192,256]{1,0:T(8,128)(2,1)}, bf16[192,256]{1,0:T(8,128)(2,1)}, bf16[192,256...) custom-call(s32[1]{0:T(128)} %bitcast.refs_0_.me_ref, ...), custom_call_target="tpu_custom_call" | custom-call | flops 2000000000 | bytes 4000000 | tf_op jit(solution)/shard_map/middle_back/pallas_call | solution.py:84
  110.1 5.1 %collective-permute-done.19.b2_ref = bf16[256,768]{1,0:T(8,128)(2,1)S(1)} collective-permute-done((bf16[256,768]{1,0:T(8,128)(2,1)S(1)}, bf16[256,768]{1,0:T(8,128)(2,1)S(1)}, u32[]{:S(2)}, u32[]{:S(2)}) %collective-permute-start.19) | collective-permute-done | bytes 393248 | tf_op jit(solution)/shard_map/ppermute | solution.py:1000
  115.9 3.6 %middle_back.2 = (f32[256,768]{1,0:T(8,128)}, bf16[256,768]{1,0:T(8,128)(2,1)}, bf16[192,256]{1,0:T(8,128)(2,1)}, bf16[192,256]{1,0:T(8,128)(2,1)S(1)}, bf16[192...) custom-call(s32[1]{0:T(128)} %bitcast.refs_0_.me_ref, ...), custom_call_target="tpu_custom_call" | custom-call | flops 2000000000 | bytes 4000000 | tf_op jit(solution)/shard_map/middle_back/pallas_call | solution.py:84
  128.7 12.8 %attend_backward.2 = (bf16[192,1024]{1,0:T(8,128)(2,1)}, f32[192,2048]{1,0:T(8,128)}, f32[192,2048]{1,0:T(8,128)}) custom-call(s32[1]{0:T(128)} %bitcast.refs_0_.me_ref, s32[1,2048]{1,0:T(1,128)S(1)} %copy-done.18, s32[1,2048]{1,0:T(1,128)S(1)} %copy-done.18, bf16[3,128,2048]{2,1,0:T(8,128)(2,1)} %get-tuple-element.114.refs_3_, ...), custom_call_target="tpu_custom_call" | custom-call | flops 16000000000 | bytes 10000000 | tf_op jit(solution)/shard_map/attend_backward/pallas_call | solution.py:84
  149.6 17.0 %attend_backward.3.refs_1_.g_ref = bf16[576,2048]{1,0:T(8,128)(2,1)} custom-call(s32[1]{0:T(128)} %bitcast.refs_0_.me_ref, s32[1,2048]{1,0:T(1,128)S(1)} %copy-done.18, s32[1,2048]{1,0:T(1,128)S(1)} %copy-done.18, bf16[3,128,2048]{2,1,0:T(8,128)(2,1)} %get-tuple-element.114.refs_3_, bf16[3,16,1024]{2,1,0:T(8,128)(2,1)} %get-tuple-element.121.rest_0_.refs_4_, ...), custom_call_target="tpu_custom_call" | custom-call | flops 16000000000 | bytes 10000000 | tf_op jit(solution)/shard_map/attend_backward/pallas_call | solution.py:84
  167.8 4.6 %convolution_convert_fusion.g_ref = bf16[576,768]{1,0:T(8,128)(2,1)S(1)} fusion(bf16[576,2048]{1,0:T(8,128)(2,1)} %attend_backward.3.refs_1_.g_ref, bf16[2048,768]{1,0:T(8,128)(2,1)} %get-tuple-element.174), kind=kOutput, calls=%fused_computation.7 | convolution fusion | flops 1812381696 | bytes 6389760 | tf_op jit(solution)/shard_map/dot_general | solution.py:24
  178.5 10.7 %tail.1 = (bf16[512,768]{1,0:T(8,128)(2,1)}, bf16[512,768]{1,0:T(8,128)(2,1)S(1)}, bf16[512,768]{1,0:T(8,128)(2,1)}, bf16[528,768]{1,0:T(8,128)(2,1)S(1)}, f32[8,768]{1,0:T(8,128)}, /*index=5*/f32[8,768]{1,0:T(8,128)}) custom-call(s32[1]{0:T(128)} %bitcast.refs_0_.me_ref, bf16[576,2048]{1,0:T(8,128)(2,1)} %attend_backward.3.refs_1_.g_ref, ...), custom_call_target="tpu_custom_call" | custom-call | flops 4000000000 | bytes 10000000 | tf_op jit(solution)/shard_map/tail/pallas_call | solution.py:84
  192.6 3.5 %collective-permute-done.34.refs_4_.p2_ref = bf16[512,768]{1,0:T(8,128)(2,1)} collective-permute-done((bf16[512,768]{1,0:T(8,128)(2,1)S(1)}, bf16[512,768]{1,0:T(8,128)(2,1)}, u32[]{:S(2)}, u32[]{:S(2)}) %collective-permute-start.34) | collective-permute-done | bytes 786464 | tf_op jit(solution)/shard_map/ppermute | solution.py:1000
  203.7 5.6 %all-gather.2.cloned.1.call-done.mine_ref = bf16[768,768]{1,0:T(8,128)(2,1)} async-done(((bf16[192,768]{1,0:T(8,128)(2,1)}), bf16[768,768]{1,0:T(8,128)(2,1)}) %all-gather.2.cloned.1.call-update) | async-done | bytes 1179664 | tf_op jit(solution)/shard_map/all_gather | solution.py:1152
  213.0 10.4 %collective-permute-done.41.b2_ref.refs_5_ = bf16[528,768]{1,0:T(8,128)(2,1)} collective-permute-done((bf16[528,768]{1,0:T(8,128)(2,1)S(1)}, bf16[528,768]{1,0:T(8,128)(2,1)}, u32[]{:S(2)}, u32[]{:S(2)}) %collective-permute-start.41) | collective-permute-done | bytes 811040 | tf_op jit(solution)/shard_map/ppermute | solution.py:1000
  223.4 3.8 %collective-permute-start.39 = (bf16[96,768]{1,0:T(8,128)(2,1)S(1)}, bf16[96,768]{1,0:T(8,128)(2,1)S(1)}, u32[]{:S(2)}, u32[]{:S(2)}) collective-permute-start(bf16[96,768]{1,0:T(8,128)(2,1)S(1)} %copy-done.24), channel_id=1, source_target_pairs={{0,24},{8,0},{16,8},{24,16},{1,25},{9,1},{17,9},{25,17},{2,26},{10... | collective-permute-start | bytes 442376 | tf_op jit(solution)/shard_map/ppermute | solution.py:1028
  232.6 3.7 %collective-permute-start.49 = (bf16[112,768]{1,0:T(8,128)(2,1)}, bf16[112,768]{1,0:T(8,128)(2,1)S(1)}, u32[]{:S(2)}, u32[]{:S(2)}) collective-permute-start(bf16[112,768]{1,0:T(8,128)(2,1)} %second.1.rest_0_.refs_1_), channel_id=1, source_target_pairs={{0,24},{8,0},{16,8},{24,16},{1,25},{9,1},{17,9},{25,17},{2,26},{10... | collective-permute-start | bytes 516104 | tf_op jit(solution)/shard_map/ppermute | solution.py:1028
  239.0 4.7 %place.2.refs_5_ = bf16[2048,768]{1,0:T(8,128)(2,1)} custom-call(s32[1]{0:T(128)} %bitcast.refs_0_.me_ref, bf16[512,768]{1,0:T(8,128)(2,1)S(1)} %copy-done.8, bf16[512,768]{1,0:T(8,128)(2,1)S(1)} %copy-done.6, bf16[512,768]{1,0:T(8,128)(2,1)} %collective-permute-done.34.refs_4_.p2_ref, bf16[512,768]{1,0:T(8,128)(2,1)} %collective-permute-done.35.p3_ref, ...), custom_call_target="tpu_custom_call" | custom-call | flops 1000000 | bytes 9000000 | tf_op jit(solution)/shard_map/place/pallas_call | solution.py:84
  243.7 4.8 %collective-permute-done.48.refs_3_ = bf16[112,768]{1,0:T(8,128)(2,1)S(1)} collective-permute-done((bf16[112,768]{1,0:T(8,128)(2,1)}, bf16[112,768]{1,0:T(8,128)(2,1)S(1)}, u32[]{:S(2)}, u32[]{:S(2)}) %collective-permute-start.48) | collective-permute-done | bytes 172064 | tf_op jit(solution)/shard_map/ppermute | solution.py:1028
  256.8 5.2 %place.3.rest_2_ = f32[2048,768]{1,0:T(8,128)} custom-call(s32[1]{0:T(128)} %bitcast.refs_0_.me_ref, bf16[512,768]{1,0:T(8,128)(2,1)S(1)} %fence.28.p0_ref, bf16[512,768]{1,0:T(8,128)(2,1)} %collective-permute-done.45.p1_ref, bf16[512,768]{1,0:T(8,128)(2,1)S(1)} %fence.29.p2_ref, bf16[512,768]{1,0:T(8,128)(2,1)S(1)} %collective-permute-done.50.p3_ref, ...), custom_call_target="tpu_custom_call" | custom-call | flops 1000000 | bytes 9000000 | tf_op jit(solution)/shard_map/place/pallas_call | solution.py:84
  261.9 5.0 %collective-permute-done.51.other_ref = bf16[400,768]{1,0:T(8,128)(2,1)S(1)} collective-permute-done((bf16[400,768]{1,0:T(8,128)(2,1)S(1)}, bf16[400,768]{1,0:T(8,128)(2,1)S(1)}, u32[]{:S(2)}, u32[]{:S(2)}) %collective-permute-start.51) | collective-permute-done | bytes 614432 | tf_op jit(solution)/shard_map/ppermute | solution.py:1173
  (194 shorter events, 92.5 us)
Async XLA Ops:
  7.2 171.3 %reduce-scatter.2.cloned.1.call-start = ((), (), s32[]{:S(2)}) async-start(), calls=%async_computation.1 | async-start | bytes 1474560 | tf_op jit(solution)/shard_map/reduce_scatter | solution.py:1135
  30.8 15.1 %collective-permute-start.4 = (bf16[192,256]{1,0:T(8,128)(2,1)S(1)}, bf16[192,256]{1,0:T(8,128)(2,1)S(1)}, u32[]{:S(2)}, u32[]{:S(2)}) collective-permute-start(bf16[192,256]{1,0:T(8,128)(2,1)S(1)} %get-tuple-element.120), channel_id=1, source_target_pairs={{0,3},{1,2},{2,1},{3,0},{4,7},{5,6},{6,5},{7,4},{8,11},{9,10},{10,... | collective-permute-start | bytes 294920 | tf_op jit(solution)/shard_map/ppermute | solution.py:1004
  80.1 25.8 %collective-permute-start.23 = (bf16[256,768]{1,0:T(8,128)(2,1)S(1)}, bf16[256,768]{1,0:T(8,128)(2,1)S(1)}, u32[]{:S(2)}, u32[]{:S(2)}) collective-permute-start(bf16[256,768]{1,0:T(8,128)(2,1)S(1)} %get-tuple-element.155), channel_id=1, source_target_pairs={{0,1},{1,0},{2,3},{3,2},{4,5},{5,4},{6,7},{7,6},{8,9},{9,8},{10,11... | collective-permute-start | bytes 1179656 | tf_op jit(solution)/shard_map/ppermute | solution.py:996
  102.8 19.5 %collective-permute-start.27 = (bf16[512,768]{1,0:T(8,128)(2,1)}, bf16[512,768]{1,0:T(8,128)(2,1)}, u32[]{:S(2)}, u32[]{:S(2)}) collective-permute-start(bf16[512,768]{1,0:T(8,128)(2,1)} %fence.19), channel_id=1, source_target_pairs={{0,1},{1,0},{2,3},{3,2},{4,5},{5,4},{6,7},{7,6},{8,9},{9,8},{10,11... | collective-permute-start | bytes 2359304 | tf_op jit(solution)/shard_map/ppermute | solution.py:996
  104.4 37.1 %collective-permute-start.43 = (bf16[768,768]{1,0:T(8,128)(2,1)}, bf16[768,768]{1,0:T(8,128)(2,1)}, u32[]{:S(2)}, u32[]{:S(2)}) collective-permute-start(bf16[768,768]{1,0:T(8,128)(2,1)} %get-tuple-element.146.refs_1_), channel_id=1, source_target_pairs={{0,4},{4,0},{1,5},{5,1},{2,6},{6,2},{3,7},{7,3},{8,12},{12,8},{9,1... | collective-permute-start | bytes 3538952 | tf_op jit(solution)/shard_map/ppermute | solution.py:1134
  105.9 21.8 %collective-permute-start.28 = (bf16[512,768]{1,0:T(8,128)(2,1)}, bf16[512,768]{1,0:T(8,128)(2,1)S(1)}, u32[]{:S(2)}, u32[]{:S(2)}) collective-permute-start(bf16[512,768]{1,0:T(8,128)(2,1)} %fence.21), channel_id=1, source_target_pairs={{0,1},{1,0},{2,3},{3,2},{4,5},{5,4},{6,7},{7,6},{8,9},{9,8},{10,11... | collective-permute-start | bytes 2359304 | tf_op jit(solution)/shard_map/ppermute | solution.py:996
  109.6 14.6 %collective-permute-start.24 = (bf16[192,256]{1,0:T(8,128)(2,1)}, bf16[192,256]{1,0:T(8,128)(2,1)S(1)}, u32[]{:S(2)}, u32[]{:S(2)}) collective-permute-start(bf16[192,256]{1,0:T(8,128)(2,1)} %get-tuple-element.157), channel_id=1, source_target_pairs={{0,1},{1,0},{2,3},{3,2},{4,5},{5,4},{6,7},{7,6},{8,9},{9,8},{10,11... | collective-permute-start | bytes 294920 | tf_op jit(solution)/shard_map/ppermute | solution.py:996
  124.2 22.7 %collective-permute-start.20 = (bf16[192,256]{1,0:T(8,128)(2,1)S(1)}, bf16[192,256]{1,0:T(8,128)(2,1)S(1)}, u32[]{:S(2)}, u32[]{:S(2)}) collective-permute-start(bf16[192,256]{1,0:T(8,128)(2,1)S(1)} %get-tuple-element.150), channel_id=1, source_target_pairs={{0,1},{1,0},{2,3},{3,2},{4,5},{5,4},{6,7},{7,6},{8,9},{9,8},{10,11... | collective-permute-start | bytes 294920 | tf_op jit(solution)/shard_map/ppermute | solution.py:996
  125.2 22.7 %collective-permute-start.21 = (bf16[192,256]{1,0:T(8,128)(2,1)S(1)}, bf16[192,256]{1,0:T(8,128)(2,1)S(1)}, u32[]{:S(2)}, u32[]{:S(2)}) collective-permute-start(bf16[192,256]{1,0:T(8,128)(2,1)S(1)} %get-tuple-element.151), channel_id=1, source_target_pairs={{0,2},{2,0},{1,3},{3,1},{4,6},{6,4},{5,7},{7,5},{8,10},{10,8},{9,1... | collective-permute-start | bytes 294920 | tf_op jit(solution)/shard_map/ppermute | solution.py:1000
  127.5 22.1 %collective-permute-start.29 = (bf16[192,768]{1,0:T(8,128)(2,1)S(1)}, bf16[192,768]{1,0:T(8,128)(2,1)S(1)}, u32[]{:S(2)}, u32[]{:S(2)}) collective-permute-start(bf16[192,768]{1,0:T(8,128)(2,1)S(1)} %get-tuple-element.171), channel_id=1, source_target_pairs={{0,1},{1,0},{2,3},{3,2},{4,5},{5,4},{6,7},{7,6},{8,9},{9,8},{10,11... | collective-permute-start | bytes 884744 | tf_op jit(solution)/shard_map/ppermute | solution.py:996
  127.7 21.9 %collective-permute-start.31 = (bf16[512,768]{1,0:T(8,128)(2,1)S(1)}, bf16[512,768]{1,0:T(8,128)(2,1)}, u32[]{:S(2)}, u32[]{:S(2)}) collective-permute-start(bf16[512,768]{1,0:T(8,128)(2,1)S(1)} %fence.20.refs_13_), channel_id=1, source_target_pairs={{0,2},{2,0},{1,3},{3,1},{4,6},{6,4},{5,7},{7,5},{8,10},{10,8},{9,1... | collective-permute-start | bytes 2359304 | tf_op jit(solution)/shard_map/ppermute | solution.py:1000
  144.8 64.6 %all-gather.2.cloned.1.call-start = ((), (), s32[]{:S(2)}) async-start(), calls=%async_computation.2 | async-start | bytes 1474560 | tf_op jit(solution)/shard_map/all_gather | solution.py:1152
  146.9 19.8 %collective-permute-start.32 = (bf16[192,768]{1,0:T(8,128)(2,1)S(1)}, bf16[192,768]{1,0:T(8,128)(2,1)S(1)}, u32[]{:S(2)}, u32[]{:S(2)}) collective-permute-start(bf16[192,768]{1,0:T(8,128)(2,1)S(1)} %add_convert_fusion.5.refs_17_), channel_id=1, source_target_pairs={{0,2},{2,0},{1,3},{3,1},{4,6},{6,4},{5,7},{7,5},{8,10},{10,8},{9,1... | collective-permute-start | bytes 884744 | tf_op jit(solution)/shard_map/ppermute | solution.py:1000
  175.9 20.2 %collective-permute-start.34 = (bf16[512,768]{1,0:T(8,128)(2,1)S(1)}, bf16[512,768]{1,0:T(8,128)(2,1)}, u32[]{:S(2)}, u32[]{:S(2)}) collective-permute-start(bf16[512,768]{1,0:T(8,128)(2,1)S(1)} %fusion.3.p0_ref), channel_id=1, source_target_pairs={{0,2},{2,0},{1,3},{3,1},{4,6},{6,4},{5,7},{7,5},{8,10},{10,8},{9,1... | collective-permute-start | bytes 2359304 | tf_op jit(solution)/shard_map/ppermute | solution.py:1000
  176.6 19.5 %collective-permute-start.33 = (bf16[512,768]{1,0:T(8,128)(2,1)S(1)}, bf16[512,768]{1,0:T(8,128)(2,1)S(1)}, u32[]{:S(2)}, u32[]{:S(2)}) collective-permute-start(bf16[512,768]{1,0:T(8,128)(2,1)S(1)} %fusion.3.p0_ref), channel_id=1, source_target_pairs={{0,1},{1,0},{2,3},{3,2},{4,5},{5,4},{6,7},{7,6},{8,9},{9,8},{10,11... | collective-permute-start | bytes 2359304 | tf_op jit(solution)/shard_map/ppermute | solution.py:996
  176.8 15.8 %collective-permute-start.36 = (bf16[384,768]{1,0:T(8,128)(2,1)}, bf16[384,768]{1,0:T(8,128)(2,1)S(1)}, u32[]{:S(2)}, u32[]{:S(2)}) collective-permute-start(bf16[384,768]{1,0:T(8,128)(2,1)} %get-tuple-element.175.refs_1_.rest_5_), channel_id=1, source_target_pairs={{0,4},{4,0},{1,5},{5,1},{2,6},{6,2},{3,7},{7,3},{8,12},{12,8},{9,1... | collective-permute-start | bytes 1769480 | tf_op jit(solution)/shard_map/ppermute | solution.py:1148
  203.1 20.3 %collective-permute-start.41 = (bf16[528,768]{1,0:T(8,128)(2,1)S(1)}, bf16[528,768]{1,0:T(8,128)(2,1)}, u32[]{:S(2)}, u32[]{:S(2)}) collective-permute-start(bf16[528,768]{1,0:T(8,128)(2,1)S(1)} %chip_sum.1.refs_4_), channel_id=1, source_target_pairs={{0,2},{2,0},{1,3},{3,1},{4,6},{6,4},{5,7},{7,5},{8,10},{10,8},{9,1... | collective-permute-start | bytes 2433032 | tf_op jit(solution)/shard_map/ppermute | solution.py:1000
  209.4 27.5 %collective-permute-start.44 = (bf16[768,768]{1,0:T(8,128)(2,1)}, bf16[768,768]{1,0:T(8,128)(2,1)S(1)}, u32[]{:S(2)}, u32[]{:S(2)}) collective-permute-start(bf16[768,768]{1,0:T(8,128)(2,1)} %all-gather.2.cloned.1.call-done.mine_ref), channel_id=1, source_target_pairs={{0,4},{4,0},{1,5},{5,1},{2,6},{6,2},{3,7},{7,3},{8,12},{12,8},{9,1... | collective-permute-start | bytes 3538952 | tf_op jit(solution)/shard_map/ppermute | solution.py:1153
  210.9 25.4 %collective-permute-start.35 = (bf16[512,768]{1,0:T(8,128)(2,1)}, bf16[512,768]{1,0:T(8,128)(2,1)}, u32[]{:S(2)}, u32[]{:S(2)}) collective-permute-start(bf16[512,768]{1,0:T(8,128)(2,1)} %collective-permute-done.34.refs_4_.p2_ref), channel_id=1, source_target_pairs={{0,1},{1,0},{2,3},{3,2},{4,5},{5,4},{6,7},{7,6},{8,9},{9,8},{10,11... | collective-permute-start | bytes 2359304 | tf_op jit(solution)/shard_map/ppermute | solution.py:996
  210.9 19.6 %collective-permute-start.37 = (bf16[96,768]{1,0:T(8,128)(2,1)}, bf16[96,768]{1,0:T(8,128)(2,1)S(1)}, u32[]{:S(2)}, u32[]{:S(2)}) collective-permute-start(bf16[96,768]{1,0:T(8,128)(2,1)} %get-tuple-element.185), channel_id=1, source_target_pairs={{0,8},{8,16},{16,24},{24,0},{1,9},{9,17},{17,25},{25,1},{2,10},{10... | collective-permute-start | bytes 442376 | tf_op jit(solution)/shard_map/ppermute | solution.py:1028
  211.9 18.6 %collective-permute-start.38 = (bf16[96,768]{1,0:T(8,128)(2,1)S(1)}, bf16[96,768]{1,0:T(8,128)(2,1)S(1)}, u32[]{:S(2)}, u32[]{:S(2)}) collective-permute-start(bf16[96,768]{1,0:T(8,128)(2,1)S(1)} %copy-done.27), channel_id=1, source_target_pairs={{0,16},{8,24},{16,0},{24,8},{1,17},{9,25},{17,1},{25,9},{2,18},{10... | collective-permute-start | bytes 442376 | tf_op jit(solution)/shard_map/ppermute | solution.py:1028
  232.2 18.5 %collective-permute-start.46 = (bf16[512,768]{1,0:T(8,128)(2,1)S(1)}, bf16[512,768]{1,0:T(8,128)(2,1)S(1)}, u32[]{:S(2)}, u32[]{:S(2)}) collective-permute-start(bf16[512,768]{1,0:T(8,128)(2,1)S(1)} %fence.28.p0_ref), channel_id=1, source_target_pairs={{0,2},{2,0},{1,3},{3,1},{4,6},{6,4},{5,7},{7,5},{8,10},{10,8},{9,1... | collective-permute-start | bytes 2359304 | tf_op jit(solution)/shard_map/ppermute | solution.py:1000
  236.9 19.9 %collective-permute-start.45 = (bf16[512,768]{1,0:T(8,128)(2,1)S(1)}, bf16[512,768]{1,0:T(8,128)(2,1)}, u32[]{:S(2)}, u32[]{:S(2)}) collective-permute-start(bf16[512,768]{1,0:T(8,128)(2,1)S(1)} %fence.28.p0_ref), channel_id=1, source_target_pairs={{0,1},{1,0},{2,3},{3,2},{4,5},{5,4},{6,7},{7,6},{8,9},{9,8},{10,11... | collective-permute-start | bytes 2359304 | tf_op jit(solution)/shard_map/ppermute | solution.py:996
  251.0 16.0 %collective-permute-start.51 = (bf16[400,768]{1,0:T(8,128)(2,1)S(1)}, bf16[400,768]{1,0:T(8,128)(2,1)S(1)}, u32[]{:S(2)}, u32[]{:S(2)}) collective-permute-start(bf16[400,768]{1,0:T(8,128)(2,1)S(1)} %copy-done.19), channel_id=1, source_target_pairs={{0,4},{4,0},{1,5},{5,1},{2,6},{6,2},{3,7},{7,3},{8,12},{12,8},{9,1... | collective-permute-start | bytes 1843208 | tf_op jit(solution)/shard_map/ppermute | solution.py:1173
  (58 other events, 398.9 us)
Sparse Core Ops, SparseCore 0:
  144.9 33.0 reduce-scatter.1
  179.6 29.7 all-gather.1
